TPU v7x, 256 devices: a whole 4x4x8 slice. The times are simulated.
256 devices in a mesh: grp: 16 (over y_hi, x, core), dev: 16 (over y_lo, z).
Axes of the slice: x: 4, y: 4 (y_hi: 2, y_lo: 2; y = y_hi * 2 + y_lo), z: 8, core: 2. Of those that a mesh axis runs over, the one named last changes fastest.
Arguments:
- images: float32 [16384, 1152], P(('grp', 'dev')), may hold values from -0.2 to 0.2
- texts: float32 [16384, 1152], P(('grp', 'dev')), may hold values from -0.2 to 0.2
- log_temp: float32 [1], replicated, may hold values from 1.6 to 3
- bias: float32 [1], replicated, may hold values from -3 to -1
Outputs:
- grad_images: float32 [16384, 1152], P(('grp', 'dev'))
- grad_texts: float32 [16384, 1152], P(('grp', 'dev'))
All inputs are finite; a program needn't handle non-finite values.
Results may differ from a plain program's by a relative error of at most 0.0063.
Values may be sent and summed in bfloat16 or wider, within the bound.
No kernel may reach another device: no remote copies, remote signals or barrier semaphores. Data moves between devices by JAX's collectives and lax.ppermute only.
A program may use at most 64 MiB of HBM per device.

v0:
```python
import jax
import jax.numpy as jnp
from jax import lax
from jax.sharding import PartitionSpec as P


def passed_along(block, axis, distance):
    devices = range(lax.axis_size(axis))
    route = [((i - distance) % len(devices), i) for i in devices]
    return lax.ppermute(block, axis, route)


def to_unit(raw):
    norm = jnp.sqrt(jnp.sum(raw * raw, axis=1, keepdims=True) + 1e-06)
    return (raw / norm, norm)


def from_unit(grad, unit, norm):
    return (grad - unit * jnp.sum(unit * grad, axis=1, keepdims=True)) / norm


def on_device(images, texts, log_temp, bias):
    temp = jnp.exp(log_temp[0])
    offset = bias[0]
    groups = lax.axis_size("grp")
    my_group = lax.axis_index("grp")
    my_member = lax.axis_index("dev")
    rows, width = images.shape
    img_unit, img_norm = to_unit(images)
    txt_unit, txt_norm = to_unit(texts)
    gathered = lax.all_gather(img_unit.astype(jnp.bfloat16), "dev", axis=0, tiled=True)
    pooled = gathered.shape[0]
    spans = ((0, rows, 1),)
    text_bf = txt_unit.astype(jnp.bfloat16)
    blocks = tuple((text_bf for start, count, _ in spans))
    columns = lax.broadcasted_iota(jnp.int32, (1, pooled), 1)

    def score(block, start, anchor):
        dots = lax.dot_general(
            block, gathered, (((1,), (1,)), ((), ())), preferred_element_type=jnp.float32
        )
        logits = temp * dots + offset
        diag_rows = (
            my_member * rows + start + lax.broadcasted_iota(jnp.int32, (block.shape[0], 1), 0)
        )
        hits = jnp.logical_and(diag_rows == columns, anchor == my_group)
        coeff = (jax.nn.sigmoid(logits) - hits.astype(jnp.float32)).astype(jnp.bfloat16)
        text_part = jnp.dot(coeff, gathered, preferred_element_type=jnp.float32)
        image_part = lax.dot_general(
            coeff, block, (((0,), (0,)), ((), ())), preferred_element_type=jnp.float32
        )
        return (text_part, image_part)

    def visit(step, blocks, grads, image_acc):
        for index, (start, count, direction) in enumerate(spans):
            anchor = jnp.mod(my_group - direction * step, groups)
            text_part, image_part = score(blocks[index], start, anchor)
            image_acc = image_acc + image_part
            grads = grads[:index] + (grads[index] + text_part,) + grads[index + 1 :]
        return (grads, image_acc)

    def advance(step, state):
        blocks, grads, image_acc = state
        grads, image_acc = visit(step, blocks, grads, image_acc)
        blocks = tuple(
            (passed_along(blocks[index], "grp", spans[index][2]) for index in range(len(spans)))
        )
        grads = tuple(
            (passed_along(grads[index], "grp", spans[index][2]) for index in range(len(spans)))
        )
        return (blocks, grads, image_acc)

    grads = tuple((jnp.zeros((count, width), jnp.float32) for _, count, _ in spans))
    image_acc = jnp.zeros((pooled, width), jnp.float32)
    blocks, grads, image_acc = lax.fori_loop(0, groups - 1, advance, (blocks, grads, image_acc))
    grads, image_acc = visit(groups - 1, blocks, grads, image_acc)
    homed = tuple(
        (passed_along(grads[index], "grp", spans[index][2]) for index in range(len(spans)))
    )
    text_sum = homed[0]
    image_sum = lax.psum_scatter(image_acc, "dev", scatter_dimension=0, tiled=True)
    grad_images = from_unit(temp * image_sum, img_unit, img_norm)
    grad_texts = from_unit(temp * text_sum, txt_unit, txt_norm)
    return (grad_images, grad_texts)


def solution(mesh):
    placed = (P(("grp", "dev"), None), P(("grp", "dev"), None), P(), P())
    return jax.shard_map(
        on_device,
        mesh=mesh,
        in_specs=placed,
        out_specs=(P(("grp", "dev"), None), P(("grp", "dev"), None)),
        check_vma=False,
    )
```

profile of v0, /device:TPU:8, one launch (start us, length us, event | category | flops | bytes accessed | tf_op | source)
XLA Modules:
  0.0 412.3 jit_solution(9192721153694918468)
XLA Ops:
  13.7 70.9 %all-gather.2.cloned.1.call-done = bf16[1024,1152]{1,0:T(8,128)(2,1)} async-done(((bf16[64,1152]{1,0:T(8,128)(2,1)}), bf16[1024,1152]{1,0:T(8,128)(2,1)}) %all-gather.2.cloned.1.call-update) | async-done | bytes 2359312 | tf_op jit(solution)/shard_map/all_gather | solution.py:31
  84.6 230.8 %while.20 = (s32[]{:T(128)}, bf16[64,1152]{1,0:T(8,128)(2,1)S(1)}, f32[64,1152]{1,0:T(8,128)S(1)}, f32[1024,1152]{1,0:T(8,128)}, f32[]{:T(128)}, /*index=5*/bf16...) while((s32[]{:T(128)}, bf16[64,1152]{1,0:T(8,128)(2,1)S(1)}, ...), condition=%wide.region_3.4_spmd.clone, body=%wide.region_2.3_spmd.clone.sunk | while | flops 456073280 | bytes 17498980 | solution.py:75
  94.7 5.3 %collective-permute-done.1 = f32[64,1152]{1,0:T(8,128)S(1)} collective-permute-done((f32[64,1152]{1,0:T(8,128)S(1)}, f32[64,1152]{1,0:T(8,128)S(1)}, u32[]{:S(2)}, u32[]{:S(2)}) %collective-permute-start.1) | collective-permute-done | bytes 294944 | tf_op jit(solution)/shard_map/while/body/eval_jaxpr/ppermute | solution.py:10
  105.7 5.3 %convolution_add_fusion.7 = f32[1024,1152]{1,0:T(8,128)} fusion(bf16[64,1024]{1,0:T(8,128)(2,1)S(1)} %fusion.45, bf16[64,1152]{1,0:T(8,128)(2,1)S(1)} %copy.11, f32[1024,1152]{1,0:T(8,128)} %get-tuple-element.373, pred[]{:T(512)S(6)} %compare.5), kind=kOutput, calls=%fused_computation.1.clone.1 | convolution fusion | flops 153354240 | bytes 9715713 | tf_op jit(solution)/shard_map/while/body/eval_jaxpr/dot_general | solution.py:49
  110.9 4.5 %collective-permute-done.1 = f32[64,1152]{1,0:T(8,128)S(1)} collective-permute-done((f32[64,1152]{1,0:T(8,128)S(1)}, f32[64,1152]{1,0:T(8,128)S(1)}, u32[]{:S(2)}, u32[]{:S(2)}) %collective-permute-start.1) | collective-permute-done | bytes 294944 | tf_op jit(solution)/shard_map/while/body/eval_jaxpr/ppermute | solution.py:10
  121.1 5.3 %convolution_add_fusion.7 = f32[1024,1152]{1,0:T(8,128)} fusion(bf16[64,1024]{1,0:T(8,128)(2,1)S(1)} %fusion.45, bf16[64,1152]{1,0:T(8,128)(2,1)S(1)} %copy.11, f32[1024,1152]{1,0:T(8,128)} %get-tuple-element.373, pred[]{:T(512)S(6)} %compare.5), kind=kOutput, calls=%fused_computation.1.clone.1 | convolution fusion | flops 153354240 | bytes 9715713 | tf_op jit(solution)/shard_map/while/body/eval_jaxpr/dot_general | solution.py:49
  126.3 4.5 %collective-permute-done.1 = f32[64,1152]{1,0:T(8,128)S(1)} collective-permute-done((f32[64,1152]{1,0:T(8,128)S(1)}, f32[64,1152]{1,0:T(8,128)S(1)}, u32[]{:S(2)}, u32[]{:S(2)}) %collective-permute-start.1) | collective-permute-done | bytes 294944 | tf_op jit(solution)/shard_map/while/body/eval_jaxpr/ppermute | solution.py:10
  136.4 5.3 %convolution_add_fusion.7 = f32[1024,1152]{1,0:T(8,128)} fusion(bf16[64,1024]{1,0:T(8,128)(2,1)S(1)} %fusion.45, bf16[64,1152]{1,0:T(8,128)(2,1)S(1)} %copy.11, f32[1024,1152]{1,0:T(8,128)} %get-tuple-element.373, pred[]{:T(512)S(6)} %compare.5), kind=kOutput, calls=%fused_computation.1.clone.1 | convolution fusion | flops 153354240 | bytes 9715713 | tf_op jit(solution)/shard_map/while/body/eval_jaxpr/dot_general | solution.py:49
  151.8 5.3 %convolution_add_fusion.7 = f32[1024,1152]{1,0:T(8,128)} fusion(bf16[64,1024]{1,0:T(8,128)(2,1)S(1)} %fusion.45, bf16[64,1152]{1,0:T(8,128)(2,1)S(1)} %copy.11, f32[1024,1152]{1,0:T(8,128)} %get-tuple-element.373, pred[]{:T(512)S(6)} %compare.5), kind=kOutput, calls=%fused_computation.1.clone.1 | convolution fusion | flops 153354240 | bytes 9715713 | tf_op jit(solution)/shard_map/while/body/eval_jaxpr/dot_general | solution.py:49
  167.2 5.3 %convolution_add_fusion.7 = f32[1024,1152]{1,0:T(8,128)} fusion(bf16[64,1024]{1,0:T(8,128)(2,1)S(1)} %fusion.45, bf16[64,1152]{1,0:T(8,128)(2,1)S(1)} %copy.11, f32[1024,1152]{1,0:T(8,128)} %get-tuple-element.373, pred[]{:T(512)S(6)} %compare.5), kind=kOutput, calls=%fused_computation.1.clone.1 | convolution fusion | flops 153354240 | bytes 9715713 | tf_op jit(solution)/shard_map/while/body/eval_jaxpr/dot_general | solution.py:49
  182.6 5.3 %convolution_add_fusion.7 = f32[1024,1152]{1,0:T(8,128)} fusion(bf16[64,1024]{1,0:T(8,128)(2,1)S(1)} %fusion.45, bf16[64,1152]{1,0:T(8,128)(2,1)S(1)} %copy.11, f32[1024,1152]{1,0:T(8,128)} %get-tuple-element.373, pred[]{:T(512)S(6)} %compare.5), kind=kOutput, calls=%fused_computation.1.clone.1 | convolution fusion | flops 153354240 | bytes 9715713 | tf_op jit(solution)/shard_map/while/body/eval_jaxpr/dot_general | solution.py:49
  198.0 5.3 %convolution_add_fusion.7 = f32[1024,1152]{1,0:T(8,128)} fusion(bf16[64,1024]{1,0:T(8,128)(2,1)S(1)} %fusion.45, bf16[64,1152]{1,0:T(8,128)(2,1)S(1)} %copy.11, f32[1024,1152]{1,0:T(8,128)} %get-tuple-element.373, pred[]{:T(512)S(6)} %compare.5), kind=kOutput, calls=%fused_computation.1.clone.1 | convolution fusion | flops 153354240 | bytes 9715713 | tf_op jit(solution)/shard_map/while/body/eval_jaxpr/dot_general | solution.py:49
  213.4 5.3 %convolution_add_fusion.7 = f32[1024,1152]{1,0:T(8,128)} fusion(bf16[64,1024]{1,0:T(8,128)(2,1)S(1)} %fusion.45, bf16[64,1152]{1,0:T(8,128)(2,1)S(1)} %copy.11, f32[1024,1152]{1,0:T(8,128)} %get-tuple-element.373, pred[]{:T(512)S(6)} %compare.5), kind=kOutput, calls=%fused_computation.1.clone.1 | convolution fusion | flops 153354240 | bytes 9715713 | tf_op jit(solution)/shard_map/while/body/eval_jaxpr/dot_general | solution.py:49
  218.6 4.5 %collective-permute-done.1 = f32[64,1152]{1,0:T(8,128)S(1)} collective-permute-done((f32[64,1152]{1,0:T(8,128)S(1)}, f32[64,1152]{1,0:T(8,128)S(1)}, u32[]{:S(2)}, u32[]{:S(2)}) %collective-permute-start.1) | collective-permute-done | bytes 294944 | tf_op jit(solution)/shard_map/while/body/eval_jaxpr/ppermute | solution.py:10
  228.8 5.3 %convolution_add_fusion.7 = f32[1024,1152]{1,0:T(8,128)} fusion(bf16[64,1024]{1,0:T(8,128)(2,1)S(1)} %fusion.45, bf16[64,1152]{1,0:T(8,128)(2,1)S(1)} %copy.11, f32[1024,1152]{1,0:T(8,128)} %get-tuple-element.373, pred[]{:T(512)S(6)} %compare.5), kind=kOutput, calls=%fused_computation.1.clone.1 | convolution fusion | flops 153354240 | bytes 9715713 | tf_op jit(solution)/shard_map/while/body/eval_jaxpr/dot_general | solution.py:49
  244.1 5.3 %convolution_add_fusion.7 = f32[1024,1152]{1,0:T(8,128)} fusion(bf16[64,1024]{1,0:T(8,128)(2,1)S(1)} %fusion.45, bf16[64,1152]{1,0:T(8,128)(2,1)S(1)} %copy.11, f32[1024,1152]{1,0:T(8,128)} %get-tuple-element.373, pred[]{:T(512)S(6)} %compare.5), kind=kOutput, calls=%fused_computation.1.clone.1 | convolution fusion | flops 153354240 | bytes 9715713 | tf_op jit(solution)/shard_map/while/body/eval_jaxpr/dot_general | solution.py:49
  259.5 5.3 %convolution_add_fusion.7 = f32[1024,1152]{1,0:T(8,128)} fusion(bf16[64,1024]{1,0:T(8,128)(2,1)S(1)} %fusion.45, bf16[64,1152]{1,0:T(8,128)(2,1)S(1)} %copy.11, f32[1024,1152]{1,0:T(8,128)} %get-tuple-element.373, pred[]{:T(512)S(6)} %compare.5), kind=kOutput, calls=%fused_computation.1.clone.1 | convolution fusion | flops 153354240 | bytes 9715713 | tf_op jit(solution)/shard_map/while/body/eval_jaxpr/dot_general | solution.py:49
  274.9 5.3 %convolution_add_fusion.7 = f32[1024,1152]{1,0:T(8,128)} fusion(bf16[64,1024]{1,0:T(8,128)(2,1)S(1)} %fusion.45, bf16[64,1152]{1,0:T(8,128)(2,1)S(1)} %copy.11, f32[1024,1152]{1,0:T(8,128)} %get-tuple-element.373, pred[]{:T(512)S(6)} %compare.5), kind=kOutput, calls=%fused_computation.1.clone.1 | convolution fusion | flops 153354240 | bytes 9715713 | tf_op jit(solution)/shard_map/while/body/eval_jaxpr/dot_general | solution.py:49
  290.3 5.3 %convolution_add_fusion.7 = f32[1024,1152]{1,0:T(8,128)} fusion(bf16[64,1024]{1,0:T(8,128)(2,1)S(1)} %fusion.45, bf16[64,1152]{1,0:T(8,128)(2,1)S(1)} %copy.11, f32[1024,1152]{1,0:T(8,128)} %get-tuple-element.373, pred[]{:T(512)S(6)} %compare.5), kind=kOutput, calls=%fused_computation.1.clone.1 | convolution fusion | flops 153354240 | bytes 9715713 | tf_op jit(solution)/shard_map/while/body/eval_jaxpr/dot_general | solution.py:49
  305.7 5.3 %convolution_add_fusion.7 = f32[1024,1152]{1,0:T(8,128)} fusion(bf16[64,1024]{1,0:T(8,128)(2,1)S(1)} %fusion.45, bf16[64,1152]{1,0:T(8,128)(2,1)S(1)} %copy.11, f32[1024,1152]{1,0:T(8,128)} %get-tuple-element.373, pred[]{:T(512)S(6)} %compare.5), kind=kOutput, calls=%fused_computation.1.clone.1 | convolution fusion | flops 153354240 | bytes 9715713 | tf_op jit(solution)/shard_map/while/body/eval_jaxpr/dot_general | solution.py:49
  311.0 4.5 %collective-permute-done.1 = f32[64,1152]{1,0:T(8,128)S(1)} collective-permute-done((f32[64,1152]{1,0:T(8,128)S(1)}, f32[64,1152]{1,0:T(8,128)S(1)}, u32[]{:S(2)}, u32[]{:S(2)}) %collective-permute-start.1) | collective-permute-done | bytes 294944 | tf_op jit(solution)/shard_map/while/body/eval_jaxpr/ppermute | solution.py:10
  318.0 5.3 %convolution_add_fusion.2 = f32[1024,1152]{1,0:T(8,128)} fusion(f32[1024,1152]{1,0:T(8,128)} %get-tuple-element.249, bf16[64,1024]{1,0:T(8,128)(2,1)S(1)} %fusion.16, bf16[64,1152]{1,0:T(8,128)(2,1)S(1)} %get-tuple-element.250), kind=kOutput, calls=%fused_computation.14 | convolution fusion | flops 152174592 | bytes 9715712 | tf_op jit(solution)/shard_map/dot_general | solution.py:49
  325.6 9.7 %collective-permute-done.2 = f32[64,1152]{1,0:T(8,128)S(1)} collective-permute-done((f32[64,1152]{1,0:T(8,128)S(1)}, f32[64,1152]{1,0:T(8,128)S(1)}, u32[]{:S(2)}, u32[]{:S(2)}) %collective-permute-start.2) | collective-permute-done | bytes 294944 | tf_op jit(solution)/shard_map/ppermute | solution.py:10
  336.4 66.1 %reduce-scatter.2.cloned.1.call-done = f32[64,1152]{1,0:T(8,128)} async-done(((f32[1024,1152]{1,0:T(8,128)}), f32[64,1152]{1,0:T(8,128)}) %reduce-scatter.2.cloned.1.call-update) | async-done | bytes 294928 | tf_op jit(solution)/shard_map/reduce_scatter | solution.py:81
  (142 shorter events, 146.5 us)
Async XLA Ops:
  7.2 77.4 %all-gather.2.cloned.1.call-start = ((), (), s32[]{:S(2)}) async-start(), calls=%async_computation.1 | async-start | bytes 2506752 | tf_op jit(solution)/shard_map/all_gather | solution.py:31
  10.1 392.4 %reduce-scatter.2.cloned.1.call-start = ((), (), s32[]{:S(2)}) async-start(), calls=%async_computation.2 | async-start | bytes 5013504 | tf_op jit(solution)/shard_map/reduce_scatter | solution.py:81
  84.7 10.1 %collective-permute-start = (bf16[64,1152]{1,0:T(8,128)(2,1)S(1)}, bf16[64,1152]{1,0:T(8,128)(2,1)S(1)}, u32[]{:S(2)}, u32[]{:S(2)}) collective-permute-start(bf16[64,1152]{1,0:T(8,128)(2,1)S(1)} %copy.11), channel_id=1, source_target_pairs={{240,0},{0,16},{16,32},{32,48},{48,64},{64,80},{80,96},{96,112},{1... | collective-permute-start | bytes 442376 | tf_op jit(solution)/shard_map/while/body/eval_jaxpr/ppermute | solution.py:10
  100.0 10.9 %collective-permute-start = (bf16[64,1152]{1,0:T(8,128)(2,1)S(1)}, bf16[64,1152]{1,0:T(8,128)(2,1)S(1)}, u32[]{:S(2)}, u32[]{:S(2)}) collective-permute-start(bf16[64,1152]{1,0:T(8,128)(2,1)S(1)} %copy.11), channel_id=1, source_target_pairs={{240,0},{0,16},{16,32},{32,48},{48,64},{64,80},{80,96},{96,112},{1... | collective-permute-start | bytes 442376 | tf_op jit(solution)/shard_map/while/body/eval_jaxpr/ppermute | solution.py:10
  105.6 9.8 %collective-permute-start.1 = (f32[64,1152]{1,0:T(8,128)S(1)}, f32[64,1152]{1,0:T(8,128)S(1)}, u32[]{:S(2)}, u32[]{:S(2)}) collective-permute-start(f32[64,1152]{1,0:T(8,128)S(1)} %convolution_add_fusion.6), channel_id=1, source_target_pairs={{240,0},{0,16},{16,32},{32,48},{48,64},{64,80},{80,96},{96,112},{1... | collective-permute-start | bytes 884744 | tf_op jit(solution)/shard_map/while/body/eval_jaxpr/ppermute | solution.py:10
  115.4 10.9 %collective-permute-start = (bf16[64,1152]{1,0:T(8,128)(2,1)S(1)}, bf16[64,1152]{1,0:T(8,128)(2,1)S(1)}, u32[]{:S(2)}, u32[]{:S(2)}) collective-permute-start(bf16[64,1152]{1,0:T(8,128)(2,1)S(1)} %copy.11), channel_id=1, source_target_pairs={{240,0},{0,16},{16,32},{32,48},{48,64},{64,80},{80,96},{96,112},{1... | collective-permute-start | bytes 442376 | tf_op jit(solution)/shard_map/while/body/eval_jaxpr/ppermute | solution.py:10
  121.0 9.8 %collective-permute-start.1 = (f32[64,1152]{1,0:T(8,128)S(1)}, f32[64,1152]{1,0:T(8,128)S(1)}, u32[]{:S(2)}, u32[]{:S(2)}) collective-permute-start(f32[64,1152]{1,0:T(8,128)S(1)} %convolution_add_fusion.6), channel_id=1, source_target_pairs={{240,0},{0,16},{16,32},{32,48},{48,64},{64,80},{80,96},{96,112},{1... | collective-permute-start | bytes 884744 | tf_op jit(solution)/shard_map/while/body/eval_jaxpr/ppermute | solution.py:10
  130.8 10.9 %collective-permute-start = (bf16[64,1152]{1,0:T(8,128)(2,1)S(1)}, bf16[64,1152]{1,0:T(8,128)(2,1)S(1)}, u32[]{:S(2)}, u32[]{:S(2)}) collective-permute-start(bf16[64,1152]{1,0:T(8,128)(2,1)S(1)} %copy.11), channel_id=1, source_target_pairs={{240,0},{0,16},{16,32},{32,48},{48,64},{64,80},{80,96},{96,112},{1... | collective-permute-start | bytes 442376 | tf_op jit(solution)/shard_map/while/body/eval_jaxpr/ppermute | solution.py:10
  136.3 9.8 %collective-permute-start.1 = (f32[64,1152]{1,0:T(8,128)S(1)}, f32[64,1152]{1,0:T(8,128)S(1)}, u32[]{:S(2)}, u32[]{:S(2)}) collective-permute-start(f32[64,1152]{1,0:T(8,128)S(1)} %convolution_add_fusion.6), channel_id=1, source_target_pairs={{240,0},{0,16},{16,32},{32,48},{48,64},{64,80},{80,96},{96,112},{1... | collective-permute-start | bytes 884744 | tf_op jit(solution)/shard_map/while/body/eval_jaxpr/ppermute | solution.py:10
  146.2 10.9 %collective-permute-start = (bf16[64,1152]{1,0:T(8,128)(2,1)S(1)}, bf16[64,1152]{1,0:T(8,128)(2,1)S(1)}, u32[]{:S(2)}, u32[]{:S(2)}) collective-permute-start(bf16[64,1152]{1,0:T(8,128)(2,1)S(1)} %copy.11), channel_id=1, source_target_pairs={{240,0},{0,16},{16,32},{32,48},{48,64},{64,80},{80,96},{96,112},{1... | collective-permute-start | bytes 442376 | tf_op jit(solution)/shard_map/while/body/eval_jaxpr/ppermute | solution.py:10
  151.7 9.8 %collective-permute-start.1 = (f32[64,1152]{1,0:T(8,128)S(1)}, f32[64,1152]{1,0:T(8,128)S(1)}, u32[]{:S(2)}, u32[]{:S(2)}) collective-permute-start(f32[64,1152]{1,0:T(8,128)S(1)} %convolution_add_fusion.6), channel_id=1, source_target_pairs={{240,0},{0,16},{16,32},{32,48},{48,64},{64,80},{80,96},{96,112},{1... | collective-permute-start | bytes 884744 | tf_op jit(solution)/shard_map/while/body/eval_jaxpr/ppermute | solution.py:10
  161.6 10.9 %collective-permute-start = (bf16[64,1152]{1,0:T(8,128)(2,1)S(1)}, bf16[64,1152]{1,0:T(8,128)(2,1)S(1)}, u32[]{:S(2)}, u32[]{:S(2)}) collective-permute-start(bf16[64,1152]{1,0:T(8,128)(2,1)S(1)} %copy.11), channel_id=1, source_target_pairs={{240,0},{0,16},{16,32},{32,48},{48,64},{64,80},{80,96},{96,112},{1... | collective-permute-start | bytes 442376 | tf_op jit(solution)/shard_map/while/body/eval_jaxpr/ppermute | solution.py:10
  167.1 9.8 %collective-permute-start.1 = (f32[64,1152]{1,0:T(8,128)S(1)}, f32[64,1152]{1,0:T(8,128)S(1)}, u32[]{:S(2)}, u32[]{:S(2)}) collective-permute-start(f32[64,1152]{1,0:T(8,128)S(1)} %convolution_add_fusion.6), channel_id=1, source_target_pairs={{240,0},{0,16},{16,32},{32,48},{48,64},{64,80},{80,96},{96,112},{1... | collective-permute-start | bytes 884744 | tf_op jit(solution)/shard_map/while/body/eval_jaxpr/ppermute | solution.py:10
  177.0 10.9 %collective-permute-start = (bf16[64,1152]{1,0:T(8,128)(2,1)S(1)}, bf16[64,1152]{1,0:T(8,128)(2,1)S(1)}, u32[]{:S(2)}, u32[]{:S(2)}) collective-permute-start(bf16[64,1152]{1,0:T(8,128)(2,1)S(1)} %copy.11), channel_id=1, source_target_pairs={{240,0},{0,16},{16,32},{32,48},{48,64},{64,80},{80,96},{96,112},{1... | collective-permute-start | bytes 442376 | tf_op jit(solution)/shard_map/while/body/eval_jaxpr/ppermute | solution.py:10
  192.4 10.9 %collective-permute-start = (bf16[64,1152]{1,0:T(8,128)(2,1)S(1)}, bf16[64,1152]{1,0:T(8,128)(2,1)S(1)}, u32[]{:S(2)}, u32[]{:S(2)}) collective-permute-start(bf16[64,1152]{1,0:T(8,128)(2,1)S(1)} %copy.11), channel_id=1, source_target_pairs={{240,0},{0,16},{16,32},{32,48},{48,64},{64,80},{80,96},{96,112},{1... | collective-permute-start | bytes 442376 | tf_op jit(solution)/shard_map/while/body/eval_jaxpr/ppermute | solution.py:10
  207.7 10.9 %collective-permute-start = (bf16[64,1152]{1,0:T(8,128)(2,1)S(1)}, bf16[64,1152]{1,0:T(8,128)(2,1)S(1)}, u32[]{:S(2)}, u32[]{:S(2)}) collective-permute-start(bf16[64,1152]{1,0:T(8,128)(2,1)S(1)} %copy.11), channel_id=1, source_target_pairs={{240,0},{0,16},{16,32},{32,48},{48,64},{64,80},{80,96},{96,112},{1... | collective-permute-start | bytes 442376 | tf_op jit(solution)/shard_map/while/body/eval_jaxpr/ppermute | solution.py:10
  213.3 9.8 %collective-permute-start.1 = (f32[64,1152]{1,0:T(8,128)S(1)}, f32[64,1152]{1,0:T(8,128)S(1)}, u32[]{:S(2)}, u32[]{:S(2)}) collective-permute-start(f32[64,1152]{1,0:T(8,128)S(1)} %convolution_add_fusion.6), channel_id=1, source_target_pairs={{240,0},{0,16},{16,32},{32,48},{48,64},{64,80},{80,96},{96,112},{1... | collective-permute-start | bytes 884744 | tf_op jit(solution)/shard_map/while/body/eval_jaxpr/ppermute | solution.py:10
  223.1 10.9 %collective-permute-start = (bf16[64,1152]{1,0:T(8,128)(2,1)S(1)}, bf16[64,1152]{1,0:T(8,128)(2,1)S(1)}, u32[]{:S(2)}, u32[]{:S(2)}) collective-permute-start(bf16[64,1152]{1,0:T(8,128)(2,1)S(1)} %copy.11), channel_id=1, source_target_pairs={{240,0},{0,16},{16,32},{32,48},{48,64},{64,80},{80,96},{96,112},{1... | collective-permute-start | bytes 442376 | tf_op jit(solution)/shard_map/while/body/eval_jaxpr/ppermute | solution.py:10
  228.7 9.8 %collective-permute-start.1 = (f32[64,1152]{1,0:T(8,128)S(1)}, f32[64,1152]{1,0:T(8,128)S(1)}, u32[]{:S(2)}, u32[]{:S(2)}) collective-permute-start(f32[64,1152]{1,0:T(8,128)S(1)} %convolution_add_fusion.6), channel_id=1, source_target_pairs={{240,0},{0,16},{16,32},{32,48},{48,64},{64,80},{80,96},{96,112},{1... | collective-permute-start | bytes 884744 | tf_op jit(solution)/shard_map/while/body/eval_jaxpr/ppermute | solution.py:10
  238.5 10.9 %collective-permute-start = (bf16[64,1152]{1,0:T(8,128)(2,1)S(1)}, bf16[64,1152]{1,0:T(8,128)(2,1)S(1)}, u32[]{:S(2)}, u32[]{:S(2)}) collective-permute-start(bf16[64,1152]{1,0:T(8,128)(2,1)S(1)} %copy.11), channel_id=1, source_target_pairs={{240,0},{0,16},{16,32},{32,48},{48,64},{64,80},{80,96},{96,112},{1... | collective-permute-start | bytes 442376 | tf_op jit(solution)/shard_map/while/body/eval_jaxpr/ppermute | solution.py:10
  253.9 10.9 %collective-permute-start = (bf16[64,1152]{1,0:T(8,128)(2,1)S(1)}, bf16[64,1152]{1,0:T(8,128)(2,1)S(1)}, u32[]{:S(2)}, u32[]{:S(2)}) collective-permute-start(bf16[64,1152]{1,0:T(8,128)(2,1)S(1)} %copy.11), channel_id=1, source_target_pairs={{240,0},{0,16},{16,32},{32,48},{48,64},{64,80},{80,96},{96,112},{1... | collective-permute-start | bytes 442376 | tf_op jit(solution)/shard_map/while/body/eval_jaxpr/ppermute | solution.py:10
  269.3 10.9 %collective-permute-start = (bf16[64,1152]{1,0:T(8,128)(2,1)S(1)}, bf16[64,1152]{1,0:T(8,128)(2,1)S(1)}, u32[]{:S(2)}, u32[]{:S(2)}) collective-permute-start(bf16[64,1152]{1,0:T(8,128)(2,1)S(1)} %copy.11), channel_id=1, source_target_pairs={{240,0},{0,16},{16,32},{32,48},{48,64},{64,80},{80,96},{96,112},{1... | collective-permute-start | bytes 442376 | tf_op jit(solution)/shard_map/while/body/eval_jaxpr/ppermute | solution.py:10
  284.7 10.9 %collective-permute-start = (bf16[64,1152]{1,0:T(8,128)(2,1)S(1)}, bf16[64,1152]{1,0:T(8,128)(2,1)S(1)}, u32[]{:S(2)}, u32[]{:S(2)}) collective-permute-start(bf16[64,1152]{1,0:T(8,128)(2,1)S(1)} %copy.11), channel_id=1, source_target_pairs={{240,0},{0,16},{16,32},{32,48},{48,64},{64,80},{80,96},{96,112},{1... | collective-permute-start | bytes 442376 | tf_op jit(solution)/shard_map/while/body/eval_jaxpr/ppermute | solution.py:10
  300.1 10.9 %collective-permute-start = (bf16[64,1152]{1,0:T(8,128)(2,1)S(1)}, bf16[64,1152]{1,0:T(8,128)(2,1)S(1)}, u32[]{:S(2)}, u32[]{:S(2)}) collective-permute-start(bf16[64,1152]{1,0:T(8,128)(2,1)S(1)} %copy.11), channel_id=1, source_target_pairs={{240,0},{0,16},{16,32},{32,48},{48,64},{64,80},{80,96},{96,112},{1... | collective-permute-start | bytes 442376 | tf_op jit(solution)/shard_map/while/body/eval_jaxpr/ppermute | solution.py:10
  (12 other events, 181.5 us)
Sparse Core Ops, SparseCore 0:
  10.4 74.1 all-gather.1
  323.4 79.0 reduce-scatter.1
where the time goes:
time: 414 us; the launch traced here: 412 us
  waiting for transfers between devices  215 us (52%)
  matrix products  166 us (40%)
  between operations  15.5 us (4%)
  other arithmetic  9.08 us (2%)
  starting transfers between devices  4.17 us (1%)
    dot_general x16, matrix products, score(): lax.dot_general(coeff, block, (((0,), (0,)), ((), ())), preferred_element...  82.1 us
    ppermute x31, waiting for transfers between devices, passed_along(): return lax.ppermute(block, axis, route)  77.6 us
    all_gather x1, waiting for transfers between devices, on_device(): lax.all_gather(img_unit.astype(jnp.bfloat16), 'dev', axis=0, tiled=True)  70.9 us
    reduce_scatter x1, waiting for transfers between devices, on_device(): lax.psum_scatter(image_acc, 'dev', scatter_dimension=0, tiled=True)  66.1 us
    dot_general x16, matrix products, score(): lax.dot_general(block, gathered, (((1,), (1,)), ((), ())), preferred_elem...  50.3 us
    dot_general x16, matrix products, score(): text_part = jnp.dot(coeff, gathered, preferred_element_type=jnp.float32)  33.4 us
  transfers between devices with their start and end apart: 33, of which 18 were waited for; matrix products, arithmetic and copies ran while one was open for 39% of the time, Pallas kernels for 0%

commit v1 on v0

v1 whole, which is shorter than its diff:
```python
import jax
import jax.numpy as jnp
from jax import lax
from jax.experimental import pallas as pl
from jax.experimental.pallas import tpu as pltpu
from jax.sharding import Mesh, PartitionSpec as P

AXES = ("yh", "x", "core", "yl", "z")
PLANE = ("yh", "x", "yl")
BF = jnp.bfloat16
F32 = jnp.float32
NT = (((1,), (1,)), ((), ()))
TN = (((0,), (0,)), ((), ()))


def shifted(block, axis, distance):
    n = lax.axis_size(axis)
    return lax.ppermute(block, axis, [(i, (i + distance) % n) for i in range(n)])


def to_unit(raw):
    norm = jnp.sqrt(jnp.sum(raw * raw, axis=1, keepdims=True) + 1e-06)
    return (raw / norm, norm)


def from_unit(grad, unit, norm):
    return (grad - unit * jnp.sum(unit * grad, axis=1, keepdims=True)) / norm


def add(a, b):
    return (a.astype(F32) + b.astype(F32)).astype(BF)


def pair_kernel(place, scal, xs, xo, ts, dxs, dxo, dy, x, coeff):
    temp = scal[0]
    offset = scal[1]
    rows = 64
    half = xs.shape[0]
    pooled = ts.shape[0]
    x[0:half] = xs[...]
    x[half:] = xo[...]
    step = 256
    for j in range(pooled // step):
        sl = pl.ds(j * step, step)
        dots = lax.dot_general(ts[sl], x[...], NT, preferred_element_type=F32)
        coeff[sl] = jax.nn.sigmoid(temp * dots + offset).astype(BF)
    at = pl.multiple_of(place[0] * rows, rows)
    dots = lax.dot_general(ts[pl.ds(at, rows)], x[0:rows], NT, preferred_element_type=F32)
    eye = lax.broadcasted_iota(jnp.int32, (rows, rows), 0) == lax.broadcasted_iota(
        jnp.int32, (rows, rows), 1
    )
    own = jax.nn.sigmoid(temp * dots + offset) - eye.astype(F32)
    coeff[pl.ds(at, rows), 0:rows] = own.astype(BF)
    for i in range(half // step):
        part = lax.dot_general(
            coeff[:, half + i * step : half + (i + 1) * step], ts[...], TN, preferred_element_type=F32
        )
        dxo[pl.ds(i * step, step)] = part.astype(BF)
    for i in range(half // step):
        part = lax.dot_general(
            coeff[:, i * step : (i + 1) * step], ts[...], TN, preferred_element_type=F32
        )
        dxs[pl.ds(i * step, step)] = part
    for j in range(pooled // step):
        sl = pl.ds(j * step, step)
        dy[sl] = jnp.dot(coeff[sl], x[...], preferred_element_type=F32).astype(BF)


def pairs(place, scal, xs, xo, ts):
    half, width = xs.shape
    pooled = ts.shape[0]
    smem = pl.BlockSpec(memory_space=pltpu.SMEM)
    vmem = pl.BlockSpec(memory_space=pltpu.VMEM)
    return pl.pallas_call(
        pair_kernel,
        out_shape=(
            jax.ShapeDtypeStruct((half, width), F32),
            jax.ShapeDtypeStruct((half, width), BF),
            jax.ShapeDtypeStruct((pooled, width), BF),
        ),
        in_specs=[smem, smem, vmem, vmem, vmem],
        out_specs=(vmem, vmem, vmem),
        scratch_shapes=[
            pltpu.VMEM((2 * half, width), BF),
            pltpu.VMEM((pooled, 2 * half), BF),
        ],
        compiler_params=pltpu.CompilerParams(vmem_limit_bytes=48 * 2**20),
        cost_estimate=pl.CostEstimate(
            flops=6 * 2 * half * pooled * width, bytes_accessed=12 * 2**20, transcendentals=2 * half * pooled
        ),
    )(place, scal, xs, xo, ts)


def ring_gather(block):
    rows = block.shape[0]
    cut = rows // 2
    up = down = block
    held = [block]
    for _ in range(3):
        up = shifted(up, "z", 1)
        down = shifted(down, "z", -1)
        held += [up, down]
    far = jnp.concatenate([shifted(up[:cut], "z", 1), shifted(down[cut:], "z", -1)], 0)
    return jnp.concatenate(held + [far], 0)


def ring_reduce(parts):
    cut = parts.shape[1] // 2
    up = shifted(parts[7, :cut], "z", 1)
    down = shifted(parts[7, cut:], "z", -1)
    up = jnp.concatenate([add(parts[6, :cut], up), parts[6, cut:]], 0)
    down = jnp.concatenate([parts[5, :cut], add(parts[5, cut:], down)], 0)
    up, down = shifted(up, "z", 1), shifted(down, "z", -1)
    up, down = add(parts[4], up), add(parts[3], down)
    up, down = shifted(up, "z", 1), shifted(down, "z", -1)
    up, down = add(parts[2], up), add(parts[1], down)
    up, down = shifted(up, "z", 1), shifted(down, "z", -1)
    return parts[0].astype(F32) + up.astype(F32) + down.astype(F32)


def on_device(images, texts, log_temp, bias):
    temp = jnp.exp(log_temp[0])
    rows, width = images.shape
    img_unit, img_norm = to_unit(images)
    txt_unit, txt_norm = to_unit(texts)
    n_plane = lax.axis_size(PLANE)
    spread = jnp.broadcast_to(txt_unit.astype(BF)[None], (n_plane, rows, width))
    ts = lax.all_to_all(spread, PLANE, 0, 0, tiled=True).reshape(n_plane * rows, width)
    xs = ring_gather(img_unit.astype(BF))
    xo = shifted(xs, "core", 1)
    place = lax.axis_index(PLANE).astype(jnp.int32).reshape(1)
    scal = jnp.stack([temp, bias[0]])
    dxs, dxo, dy = pairs(place, scal, xs, xo, ts)
    dyr = lax.all_to_all(dy.reshape(n_plane, rows, width), PLANE, 0, 0, tiled=True)
    mine = add(dxs, shifted(dxo, "core", 1)).reshape(-1, rows, width)
    image_sum = ring_reduce(mine)
    text_sum = jnp.sum(dyr.astype(F32), axis=0)
    grad_images = from_unit(temp * image_sum, img_unit, img_norm)
    grad_texts = from_unit(temp * text_sum, txt_unit, txt_norm)
    return (grad_images, grad_texts)


def solution(mesh):
    fine = Mesh(mesh.devices.reshape(2, 4, 2, 2, 8), AXES)
    split = P(AXES, None)
    return jax.shard_map(
        on_device,
        mesh=fine,
        in_specs=(split, split, P(), P()),
        out_specs=(split, split),
        check_vma=False,
    )
```

time: 414 us -> 112 us (0.27)
  waiting for transfers between devices: 215 us -> 45.4 us
  matrix products: 166 us -> 0 us
  starting transfers between devices: 4.17 us -> 39.1 us
  between operations: 15.5 us -> 2.18 us
  Pallas kernels: 0 us -> 11.8 us
    dot_general x48 -> x0, matrix products: 166 us -> none  [the longest x16 82.1 us: score(): lax.dot_general(coeff, block, (((0,), (0,)), ((), ())), preferred_element...]
    all_gather x1 -> x0, waiting for transfers between devices: 70.9 us -> none  [on_device(): lax.all_gather(img_unit.astype(jnp.bfloat16), 'dev', axis=0, tiled=True)]
    reduce_scatter x1 -> x0, waiting for transfers between devices: 66.1 us -> none  [on_device(): lax.psum_scatter(image_acc, 'dev', scatter_dimension=0, tiled=True)]
    ppermute x31 -> x18, waiting for transfers between devices: 77.6 us -> 31.7 us  [shifted(): lax.ppermute(block, axis, [(i, (i + distance) % n) for i in range(n)])]
    ppermute x31 -> x18, starting transfers between devices: 4.09 us -> 26.7 us  [shifted(): lax.ppermute(block, axis, [(i, (i + distance) % n) for i in range(n)])]
    all_to_all x0 -> x2, waiting for transfers between devices: none -> 13.8 us  [the longest x1 7.93 us: on_device(): lax.all_to_all(spread, PLANE, 0, 0, tiled=True)]
    all_to_all x0 -> x2, starting transfers between devices: none -> 12.4 us  [the longest x1 7.39 us: on_device(): lax.all_to_all(spread, PLANE, 0, 0, tiled=True)]
    pallas_call x0 -> x1, Pallas kernels: none -> 11.8 us  [pairs(): pl.pallas_call(pair_kernel, out_shape=(jax.ShapeDtypeStruct((half, width)...]
  transfers between devices with their start and end apart: 33 -> 20, of which waited for: 18 -> 12; matrix products, arithmetic and copies ran while one was open for 39% -> 6% of each run, Pallas kernels for 0% -> 0%
where the time goes in v1:
time: 112 us; the launch traced here: 110 us
  waiting for transfers between devices  45.4 us (41%)
  starting transfers between devices  39.1 us (35%)
  Pallas kernels  11.8 us (11%)
  other arithmetic  9.02 us (8%)
  local copies, waits for them, and re-layouts  2.61 us (2%)
  between operations  2.18 us (2%)
    ppermute x18, waiting for transfers between devices, shifted(): lax.ppermute(block, axis, [(i, (i + distance) % n) for i in range(n)])  31.7 us
    ppermute x18, starting transfers between devices, shifted(): lax.ppermute(block, axis, [(i, (i + distance) % n) for i in range(n)])  26.7 us
    pallas_call x1, Pallas kernels, pairs(): pl.pallas_call(pair_kernel, out_shape=(jax.ShapeDtypeStruct((half, width)...  11.8 us
    all_to_all x1, waiting for transfers between devices, on_device(): lax.all_to_all(spread, PLANE, 0, 0, tiled=True)  7.93 us
    all_to_all x1, starting transfers between devices, on_device(): lax.all_to_all(spread, PLANE, 0, 0, tiled=True)  7.39 us
    all_to_all x1, waiting for transfers between devices, on_device(): lax.all_to_all(dy.reshape(n_plane, rows, width), PLANE, 0, 0, tiled=True)  5.83 us
    all_to_all x1, starting transfers between devices, on_device(): lax.all_to_all(dy.reshape(n_plane, rows, width), PLANE, 0, 0, tiled=True)  4.98 us
  transfers between devices with their start and end apart: 20, of which 12 were waited for; matrix products, arithmetic and copies ran while one was open for 6% of the time, Pallas kernels for 0%

profile of v1, /device:TPU:8, one launch (start us, length us, event | category | flops | bytes accessed | tf_op | source)
XLA Modules:
  0.0 110.2 jit_solution(594361256500531738)
XLA Ops:
  0.6 1.1 %multiply_reduce_fusion.3 = f32[64]{0:T(128)S(1)} fusion(f32[64,1152]{1,0:T(8,128)} %param.4), kind=kLoop, calls=%fused_computation.12 | loop fusion | flops 147392 | bytes 295168 | tf_op jit(solution)/shard_map/reduce_sum | solution.py:22
  2.9 5.9 %collective-permute-start.1 = (bf16[64,1152]{1,0:T(8,128)(2,1)S(1)}, bf16[64,1152]{1,0:T(8,128)(2,1)S(1)}, u32[]{:S(2)}, u32[]{:S(2)}) collective-permute-start(bf16[64,1152]{1,0:T(8,128)(2,1)S(1)} %get-tuple-element.9), channel_id=1, source_target_pairs={{0,7},{1,0},{2,1},{3,2},{4,3},{5,4},{6,5},{7,6},{8,15},{9,8},{10,9... | collective-permute-start | bytes 442376 | tf_op jit(solution)/shard_map/ppermute | solution.py:18
  8.8 1.1 multiply_reduce_fusion.2
  10.0 1.7 %broadcast_in_dim.2 = bf16[16,64,1152]{2,1,0:T(8,128)(2,1)} broadcast(bf16[64,1152]{1,0:T(8,128)(2,1)S(1)} %fusion.3), dimensions={1,2} | broadcast | bytes 2506752 | tf_op jit(solution)/shard_map/broadcast_in_dim | solution.py:127
  11.7 7.4 %all-to-all-start = ((bf16[16,64,1152]{2,1,0:T(8,128)(2,1)}), bf16[16,64,1152]{2,1,0:T(8,128)(2,1)}, u32[]{:S(2)}, u32[]{:S(2)}) async-start(bf16[16,64,1152]{2,1,0:T(8,128)(2,1)} %broadcast_in_dim.2), calls=%async_computation | async-start | bytes 4718592 | tf_op jit(solution)/shard_map/all_to_all | solution.py:128
  19.1 3.3 %collective-permute-start.3 = (bf16[64,1152]{1,0:T(8,128)(2,1)S(1)}, bf16[64,1152]{1,0:T(8,128)(2,1)S(1)}, u32[]{:S(2)}, u32[]{:S(2)}) collective-permute-start(bf16[64,1152]{1,0:T(8,128)(2,1)S(1)} %collective-permute-done.1), channel_id=1, source_target_pairs={{0,7},{1,0},{2,1},{3,2},{4,3},{5,4},{6,5},{7,6},{8,15},{9,8},{10,9... | collective-permute-start | bytes 442376 | tf_op jit(solution)/shard_map/ppermute | solution.py:18
  22.5 2.6 %collective-permute-done.3 = bf16[64,1152]{1,0:T(8,128)(2,1)S(1)} collective-permute-done((bf16[64,1152]{1,0:T(8,128)(2,1)S(1)}, bf16[64,1152]{1,0:T(8,128)(2,1)S(1)}, u32[]{:S(2)}, u32[]{:S(2)}) %collective-permute-start.3) | collective-permute-done | bytes 147488 | tf_op jit(solution)/shard_map/ppermute | solution.py:18
  25.1 3.7 %collective-permute-start.5 = (bf16[64,1152]{1,0:T(8,128)(2,1)S(1)}, bf16[64,1152]{1,0:T(8,128)(2,1)S(1)}, u32[]{:S(2)}, u32[]{:S(2)}) collective-permute-start(bf16[64,1152]{1,0:T(8,128)(2,1)S(1)} %collective-permute-done.3), channel_id=1, source_target_pairs={{0,7},{1,0},{2,1},{3,2},{4,3},{5,4},{6,5},{7,6},{8,15},{9,8},{10,9... | collective-permute-start | bytes 442376 | tf_op jit(solution)/shard_map/ppermute | solution.py:18
  28.9 2.6 %collective-permute-done.5 = bf16[64,1152]{1,0:T(8,128)(2,1)S(1)} collective-permute-done((bf16[64,1152]{1,0:T(8,128)(2,1)S(1)}, bf16[64,1152]{1,0:T(8,128)(2,1)S(1)}, u32[]{:S(2)}, u32[]{:S(2)}) %collective-permute-start.5) | collective-permute-done | bytes 147488 | tf_op jit(solution)/shard_map/ppermute | solution.py:18
  31.5 3.7 %collective-permute-start.7 = (bf16[32,1152]{1,0:T(8,128)(2,1)S(1)}, bf16[32,1152]{1,0:T(8,128)(2,1)S(1)}, u32[]{:S(2)}, u32[]{:S(2)}) collective-permute-start(bf16[32,1152]{1,0:T(8,128)(2,1)S(1)} %slice.58), channel_id=1, source_target_pairs={{0,7},{1,0},{2,1},{3,2},{4,3},{5,4},{6,5},{7,6},{8,15},{9,8},{10,9... | collective-permute-start | bytes 221192 | tf_op jit(solution)/shard_map/ppermute | solution.py:18
  35.3 5.5 %collective-permute-done.6 = bf16[32,1152]{1,0:T(8,128)(2,1)S(1)} collective-permute-done((bf16[32,1152]{1,0:T(8,128)(2,1)S(1)}, bf16[32,1152]{1,0:T(8,128)(2,1)S(1)}, u32[]{:S(2)}, u32[]{:S(2)}) %collective-permute-start.6) | collective-permute-done | bytes 73760 | tf_op jit(solution)/shard_map/ppermute | solution.py:18
  42.6 1.4 %collective-permute-done.8.xo = bf16[512,1152]{1,0:T(8,128)(2,1)S(1)} collective-permute-done((bf16[512,1152]{1,0:T(8,128)(2,1)S(1)}, bf16[512,1152]{1,0:T(8,128)(2,1)S(1)}, u32[]{:S(2)}, u32[]{:S(2)}) %collective-permute-start.8) | collective-permute-done | bytes 1179680 | tf_op jit(solution)/shard_map/ppermute | solution.py:18
  44.0 7.9 %all-to-all-done = bf16[16,64,1152]{2,1,0:T(8,128)(2,1)} async-done(((bf16[16,64,1152]{2,1,0:T(8,128)(2,1)}), bf16[16,64,1152]{2,1,0:T(8,128)(2,1)}, u32[]{:S(2)}, u32[]{:S(2)}) %all-to-all-start) | async-done | bytes 2359328 | tf_op jit(solution)/shard_map/all_to_all | solution.py:128
  51.9 11.8 %shard_map.59 = (f32[512,1152]{1,0:T(8,128)S(1)}, bf16[512,1152]{1,0:T(8,128)(2,1)S(1)}, bf16[1024,1152]{1,0:T(8,128)(2,1)}) custom-call(s32[1]{0:T(128)} %bitcast.1.place, f32[2]{0:T(128)S(1)} %pad_maximum_fusion.2.scal, bf16[512,1152]{1,0:T(8,128)(2,1)S(1)} %constant_dynamic-update-slice_fusion.xs, bf16[512,1152]{1,0:T(8,128)(2,1)S(1)} %collective-permute-done.8.xo, ...), custom_call_target="tpu_custom_call" | custom-call | flops 7247757312 | bytes 12582912 | tf_op jit(solution)/shard_map/pallas_call | solution.py:74
  63.7 2.8 %collective-permute-done.9 = bf16[512,1152]{1,0:T(8,128)(2,1)S(1)} collective-permute-done((bf16[512,1152]{1,0:T(8,128)(2,1)S(1)}, bf16[512,1152]{1,0:T(8,128)(2,1)S(1)}, u32[]{:S(2)}, u32[]{:S(2)}) %collective-permute-start.9) | collective-permute-done | bytes 1179680 | tf_op jit(solution)/shard_map/ppermute | solution.py:18
  67.5 3.2 %collective-permute-start.14 = (bf16[32,1152]{1,0:T(8,128)(2,1)}, bf16[32,1152]{1,0:T(8,128)(2,1)}, u32[]{:S(2)}, u32[]{:S(2)}) collective-permute-start(bf16[32,1152]{1,0:T(8,128)(2,1)} %get-tuple-element.15), channel_id=1, source_target_pairs={{0,7},{1,0},{2,1},{3,2},{4,3},{5,4},{6,5},{7,6},{8,15},{9,8},{10,9... | collective-permute-start | bytes 221192 | tf_op jit(solution)/shard_map/ppermute | solution.py:18
  70.7 5.0 %all-to-all-start.1 = ((bf16[16,64,1152]{2,1,0:T(8,128)(2,1)}), bf16[16,64,1152]{2,1,0:T(8,128)(2,1)S(1)}, u32[]{:S(2)}, u32[]{:S(2)}) async-start(bf16[16,64,1152]{2,1,0:T(8,128)(2,1)} %bitcast.25), calls=%async_computation.1 | async-start | bytes 4718592 | tf_op jit(solution)/shard_map/all_to_all | solution.py:134
  78.6 3.3 %collective-permute-start.15 = (bf16[64,1152]{1,0:T(8,128)(2,1)S(1)}, bf16[64,1152]{1,0:T(8,128)(2,1)S(1)}, u32[]{:S(2)}, u32[]{:S(2)}) collective-permute-start(bf16[64,1152]{1,0:T(8,128)(2,1)S(1)} %pad_maximum_fusion.1), channel_id=1, source_target_pairs={{0,7},{1,0},{2,1},{3,2},{4,3},{5,4},{6,5},{7,6},{8,15},{9,8},{10,9... | collective-permute-start | bytes 442376 | tf_op jit(solution)/shard_map/ppermute | solution.py:18
  81.9 2.1 %collective-permute-done.11 = bf16[64,1152]{1,0:T(8,128)(2,1)S(1)} collective-permute-done((bf16[64,1152]{1,0:T(8,128)(2,1)S(1)}, bf16[64,1152]{1,0:T(8,128)(2,1)S(1)}, u32[]{:S(2)}, u32[]{:S(2)}) %collective-permute-start.11) | collective-permute-done | bytes 147488 | tf_op jit(solution)/shard_map/ppermute | solution.py:18
  84.6 6.2 %collective-permute-done.12 = bf16[64,1152]{1,0:T(8,128)(2,1)S(1)} collective-permute-done((bf16[64,1152]{1,0:T(8,128)(2,1)S(1)}, bf16[64,1152]{1,0:T(8,128)(2,1)S(1)}, u32[]{:S(2)}, u32[]{:S(2)}) %collective-permute-start.12) | collective-permute-done | bytes 147488 | tf_op jit(solution)/shard_map/ppermute | solution.py:18
  91.0 2.0 %collective-permute-start.13 = (bf16[64,1152]{1,0:T(8,128)(2,1)S(1)}, bf16[64,1152]{1,0:T(8,128)(2,1)S(1)}, u32[]{:S(2)}, u32[]{:S(2)}) collective-permute-start(bf16[64,1152]{1,0:T(8,128)(2,1)S(1)} %get-tuple-element.10), channel_id=1, source_target_pairs={{0,1},{1,2},{2,3},{3,4},{4,5},{5,6},{6,7},{7,0},{8,9},{9,10},{10,1... | collective-permute-start | bytes 442376 | tf_op jit(solution)/shard_map/ppermute | solution.py:18
  93.0 3.7 %collective-permute-done.16 = bf16[64,1152]{1,0:T(8,128)(2,1)S(1)} collective-permute-done((bf16[64,1152]{1,0:T(8,128)(2,1)S(1)}, bf16[64,1152]{1,0:T(8,128)(2,1)S(1)}, u32[]{:S(2)}, u32[]{:S(2)}) %collective-permute-start.16) | collective-permute-done | bytes 147488 | tf_op jit(solution)/shard_map/ppermute | solution.py:18
  97.4 4.5 %collective-permute-done.17 = bf16[64,1152]{1,0:T(8,128)(2,1)S(1)} collective-permute-done((bf16[64,1152]{1,0:T(8,128)(2,1)S(1)}, bf16[64,1152]{1,0:T(8,128)(2,1)S(1)}, u32[]{:S(2)}, u32[]{:S(2)}) %collective-permute-start.17) | collective-permute-done | bytes 147488 | tf_op jit(solution)/shard_map/ppermute | solution.py:18
  103.0 5.8 %all-to-all-done.1 = bf16[16,64,1152]{2,1,0:T(8,128)(2,1)S(1)} async-done(((bf16[16,64,1152]{2,1,0:T(8,128)(2,1)}), bf16[16,64,1152]{2,1,0:T(8,128)(2,1)S(1)}, u32[]{:S(2)}, u32[]{:S(2)}) %all-to-all-start.1) | async-done | bytes 2359328 | tf_op jit(solution)/shard_map/all_to_all | solution.py:134
  (54 shorter events, 9.5 us)
Async XLA Ops:
  0.6 9.3 %copy-start.1 = (f32[64,1152]{1,0:T(8,128)S(1)}, f32[64,1152]{1,0:T(8,128)}, u32[]{:S(2)}) copy-start(f32[64,1152]{1,0:T(8,128)} %param.5) | copy-start | bytes 884740
  2.9 16.3 %collective-permute-start.1 = (bf16[64,1152]{1,0:T(8,128)(2,1)S(1)}, bf16[64,1152]{1,0:T(8,128)(2,1)S(1)}, u32[]{:S(2)}, u32[]{:S(2)}) collective-permute-start(bf16[64,1152]{1,0:T(8,128)(2,1)S(1)} %get-tuple-element.9), channel_id=1, source_target_pairs={{0,7},{1,0},{2,1},{3,2},{4,3},{5,4},{6,5},{7,6},{8,15},{9,8},{10,9... | collective-permute-start | bytes 442376 | tf_op jit(solution)/shard_map/ppermute | solution.py:18
  8.8 13.7 %collective-permute-start = (bf16[64,1152]{1,0:T(8,128)(2,1)S(1)}, bf16[64,1152]{1,0:T(8,128)(2,1)S(1)}, u32[]{:S(2)}, u32[]{:S(2)}) collective-permute-start(bf16[64,1152]{1,0:T(8,128)(2,1)S(1)} %get-tuple-element.9), channel_id=1, source_target_pairs={{0,1},{1,2},{2,3},{3,4},{4,5},{5,6},{6,7},{7,0},{8,9},{9,10},{10,1... | collective-permute-start | bytes 442376 | tf_op jit(solution)/shard_map/ppermute | solution.py:18
  11.7 40.2 %all-to-all-start = ((bf16[16,64,1152]{2,1,0:T(8,128)(2,1)}), bf16[16,64,1152]{2,1,0:T(8,128)(2,1)}, u32[]{:S(2)}, u32[]{:S(2)}) async-start(bf16[16,64,1152]{2,1,0:T(8,128)(2,1)} %broadcast_in_dim.2), calls=%async_computation | async-start | bytes 4718592 | tf_op jit(solution)/shard_map/all_to_all | solution.py:128
  19.1 6.0 %collective-permute-start.3 = (bf16[64,1152]{1,0:T(8,128)(2,1)S(1)}, bf16[64,1152]{1,0:T(8,128)(2,1)S(1)}, u32[]{:S(2)}, u32[]{:S(2)}) collective-permute-start(bf16[64,1152]{1,0:T(8,128)(2,1)S(1)} %collective-permute-done.1), channel_id=1, source_target_pairs={{0,7},{1,0},{2,1},{3,2},{4,3},{5,4},{6,5},{7,6},{8,15},{9,8},{10,9... | collective-permute-start | bytes 442376 | tf_op jit(solution)/shard_map/ppermute | solution.py:18
  22.5 6.4 %collective-permute-start.2 = (bf16[64,1152]{1,0:T(8,128)(2,1)S(1)}, bf16[64,1152]{1,0:T(8,128)(2,1)S(1)}, u32[]{:S(2)}, u32[]{:S(2)}) collective-permute-start(bf16[64,1152]{1,0:T(8,128)(2,1)S(1)} %collective-permute-done), channel_id=1, source_target_pairs={{0,1},{1,2},{2,3},{3,4},{4,5},{5,6},{6,7},{7,0},{8,9},{9,10},{10,1... | collective-permute-start | bytes 442376 | tf_op jit(solution)/shard_map/ppermute | solution.py:18
  25.1 6.4 %collective-permute-start.5 = (bf16[64,1152]{1,0:T(8,128)(2,1)S(1)}, bf16[64,1152]{1,0:T(8,128)(2,1)S(1)}, u32[]{:S(2)}, u32[]{:S(2)}) collective-permute-start(bf16[64,1152]{1,0:T(8,128)(2,1)S(1)} %collective-permute-done.3), channel_id=1, source_target_pairs={{0,7},{1,0},{2,1},{3,2},{4,3},{5,4},{6,5},{7,6},{8,15},{9,8},{10,9... | collective-permute-start | bytes 442376 | tf_op jit(solution)/shard_map/ppermute | solution.py:18
  28.8 6.4 %collective-permute-start.4 = (bf16[64,1152]{1,0:T(8,128)(2,1)S(1)}, bf16[64,1152]{1,0:T(8,128)(2,1)S(1)}, u32[]{:S(2)}, u32[]{:S(2)}) collective-permute-start(bf16[64,1152]{1,0:T(8,128)(2,1)S(1)} %collective-permute-done.2), channel_id=1, source_target_pairs={{0,1},{1,2},{2,3},{3,4},{4,5},{5,6},{6,7},{7,0},{8,9},{9,10},{10,1... | collective-permute-start | bytes 442376 | tf_op jit(solution)/shard_map/ppermute | solution.py:18
  31.5 9.3 %collective-permute-start.7 = (bf16[32,1152]{1,0:T(8,128)(2,1)S(1)}, bf16[32,1152]{1,0:T(8,128)(2,1)S(1)}, u32[]{:S(2)}, u32[]{:S(2)}) collective-permute-start(bf16[32,1152]{1,0:T(8,128)(2,1)S(1)} %slice.58), channel_id=1, source_target_pairs={{0,7},{1,0},{2,1},{3,2},{4,3},{5,4},{6,5},{7,6},{8,15},{9,8},{10,9... | collective-permute-start | bytes 221192 | tf_op jit(solution)/shard_map/ppermute | solution.py:18
  35.2 5.6 %collective-permute-start.6 = (bf16[32,1152]{1,0:T(8,128)(2,1)S(1)}, bf16[32,1152]{1,0:T(8,128)(2,1)S(1)}, u32[]{:S(2)}, u32[]{:S(2)}) collective-permute-start(bf16[32,1152]{1,0:T(8,128)(2,1)S(1)} %slice.57), channel_id=1, source_target_pairs={{0,1},{1,2},{2,3},{3,4},{4,5},{5,6},{6,7},{7,0},{8,9},{9,10},{10,1... | collective-permute-start | bytes 221192 | tf_op jit(solution)/shard_map/ppermute | solution.py:18
  40.9 3.1 %collective-permute-start.8 = (bf16[512,1152]{1,0:T(8,128)(2,1)S(1)}, bf16[512,1152]{1,0:T(8,128)(2,1)S(1)}, u32[]{:S(2)}, u32[]{:S(2)}) collective-permute-start(bf16[512,1152]{1,0:T(8,128)(2,1)S(1)} %constant_dynamic-update-slice_fusion.xs), channel_id=1, source_target_pairs={{0,16},{16,0},{1,17},{17,1},{2,18},{18,2},{3,19},{19,3},{4,20},{20... | collective-permute-start | bytes 3538952 | tf_op jit(solution)/shard_map/ppermute | solution.py:18
  63.7 2.8 %collective-permute-start.9 = (bf16[512,1152]{1,0:T(8,128)(2,1)S(1)}, bf16[512,1152]{1,0:T(8,128)(2,1)S(1)}, u32[]{:S(2)}, u32[]{:S(2)}) collective-permute-start(bf16[512,1152]{1,0:T(8,128)(2,1)S(1)} %get-tuple-element.6), channel_id=1, source_target_pairs={{0,16},{16,0},{1,17},{17,1},{2,18},{18,2},{3,19},{19,3},{4,20},{20... | collective-permute-start | bytes 3538952 | tf_op jit(solution)/shard_map/ppermute | solution.py:18
  67.5 8.2 %collective-permute-start.10 = (bf16[32,1152]{1,0:T(8,128)(2,1)}, bf16[32,1152]{1,0:T(8,128)(2,1)}, u32[]{:S(2)}, u32[]{:S(2)}) collective-permute-start(bf16[32,1152]{1,0:T(8,128)(2,1)} %get-tuple-element.14), channel_id=1, source_target_pairs={{0,1},{1,2},{2,3},{3,4},{4,5},{5,6},{6,7},{7,0},{8,9},{9,10},{10,1... | collective-permute-start | bytes 221192 | tf_op jit(solution)/shard_map/ppermute | solution.py:18
  67.5 8.2 %collective-permute-start.14 = (bf16[32,1152]{1,0:T(8,128)(2,1)}, bf16[32,1152]{1,0:T(8,128)(2,1)}, u32[]{:S(2)}, u32[]{:S(2)}) collective-permute-start(bf16[32,1152]{1,0:T(8,128)(2,1)} %get-tuple-element.15), channel_id=1, source_target_pairs={{0,7},{1,0},{2,1},{3,2},{4,3},{5,4},{6,5},{7,6},{8,15},{9,8},{10,9... | collective-permute-start | bytes 221192 | tf_op jit(solution)/shard_map/ppermute | solution.py:18
  70.7 38.0 %all-to-all-start.1 = ((bf16[16,64,1152]{2,1,0:T(8,128)(2,1)}), bf16[16,64,1152]{2,1,0:T(8,128)(2,1)S(1)}, u32[]{:S(2)}, u32[]{:S(2)}) async-start(bf16[16,64,1152]{2,1,0:T(8,128)(2,1)} %bitcast.25), calls=%async_computation.1 | async-start | bytes 4718592 | tf_op jit(solution)/shard_map/all_to_all | solution.py:134
  76.7 25.2 %copy-start = (f32[64,1152]{1,0:T(8,128)S(1)}, f32[64,1152]{1,0:T(8,128)}, u32[]{:S(2)}) copy-start(f32[64,1152]{1,0:T(8,128)} %param.4) | copy-start | bytes 884740
  77.7 6.4 %collective-permute-start.11 = (bf16[64,1152]{1,0:T(8,128)(2,1)S(1)}, bf16[64,1152]{1,0:T(8,128)(2,1)S(1)}, u32[]{:S(2)}, u32[]{:S(2)}) collective-permute-start(bf16[64,1152]{1,0:T(8,128)(2,1)S(1)} %pad_maximum_fusion), channel_id=1, source_target_pairs={{0,1},{1,2},{2,3},{3,4},{4,5},{5,6},{6,7},{7,0},{8,9},{9,10},{10,1... | collective-permute-start | bytes 442376 | tf_op jit(solution)/shard_map/ppermute | solution.py:18
  78.6 6.0 %collective-permute-start.15 = (bf16[64,1152]{1,0:T(8,128)(2,1)S(1)}, bf16[64,1152]{1,0:T(8,128)(2,1)S(1)}, u32[]{:S(2)}, u32[]{:S(2)}) collective-permute-start(bf16[64,1152]{1,0:T(8,128)(2,1)S(1)} %pad_maximum_fusion.1), channel_id=1, source_target_pairs={{0,7},{1,0},{2,1},{3,2},{4,3},{5,4},{6,5},{7,6},{8,15},{9,8},{10,9... | collective-permute-start | bytes 442376 | tf_op jit(solution)/shard_map/ppermute | solution.py:18
  84.1 6.7 %collective-permute-start.12 = (bf16[64,1152]{1,0:T(8,128)(2,1)S(1)}, bf16[64,1152]{1,0:T(8,128)(2,1)S(1)}, u32[]{:S(2)}, u32[]{:S(2)}) collective-permute-start(bf16[64,1152]{1,0:T(8,128)(2,1)S(1)} %add_convert_fusion.4), channel_id=1, source_target_pairs={{0,1},{1,2},{2,3},{3,4},{4,5},{5,6},{6,7},{7,0},{8,9},{9,10},{10,1... | collective-permute-start | bytes 442376 | tf_op jit(solution)/shard_map/ppermute | solution.py:18
  90.9 5.8 %collective-permute-start.16 = (bf16[64,1152]{1,0:T(8,128)(2,1)S(1)}, bf16[64,1152]{1,0:T(8,128)(2,1)S(1)}, u32[]{:S(2)}, u32[]{:S(2)}) collective-permute-start(bf16[64,1152]{1,0:T(8,128)(2,1)S(1)} %get-tuple-element.11), channel_id=1, source_target_pairs={{0,7},{1,0},{2,1},{3,2},{4,3},{5,4},{6,5},{7,6},{8,15},{9,8},{10,9... | collective-permute-start | bytes 442376 | tf_op jit(solution)/shard_map/ppermute | solution.py:18
  91.0 6.5 %collective-permute-start.13 = (bf16[64,1152]{1,0:T(8,128)(2,1)S(1)}, bf16[64,1152]{1,0:T(8,128)(2,1)S(1)}, u32[]{:S(2)}, u32[]{:S(2)}) collective-permute-start(bf16[64,1152]{1,0:T(8,128)(2,1)S(1)} %get-tuple-element.10), channel_id=1, source_target_pairs={{0,1},{1,2},{2,3},{3,4},{4,5},{5,6},{6,7},{7,0},{8,9},{9,10},{10,1... | collective-permute-start | bytes 442376 | tf_op jit(solution)/shard_map/ppermute | solution.py:18
  96.7 5.2 %collective-permute-start.17 = (bf16[64,1152]{1,0:T(8,128)(2,1)S(1)}, bf16[64,1152]{1,0:T(8,128)(2,1)S(1)}, u32[]{:S(2)}, u32[]{:S(2)}) collective-permute-start(bf16[64,1152]{1,0:T(8,128)(2,1)S(1)} %add_convert_fusion.1), channel_id=1, source_target_pairs={{0,7},{1,0},{2,1},{3,2},{4,3},{5,4},{6,5},{7,6},{8,15},{9,8},{10,9... | collective-permute-start | bytes 442376 | tf_op jit(solution)/shard_map/ppermute | solution.py:18
  103.0 6.2 %copy-start.2 = (f32[64,1152]{1,0:T(8,128)S(1)}, f32[64,1152]{1,0:T(8,128)}, u32[]{:S(2)}) copy-start(f32[64,1152]{1,0:T(8,128)} %param.5) | copy-start | bytes 884740

commit v2 on v1

v2 whole, which is shorter than its diff:
```python
import jax
import jax.numpy as jnp
from jax import lax
from jax.experimental import pallas as pl
from jax.experimental.pallas import tpu as pltpu
from jax.sharding import Mesh, PartitionSpec as P

AXES = ("yh", "x", "core", "yl", "z")
PLANE = ("yh", "x", "yl")
BF = jnp.bfloat16
F32 = jnp.float32
ROWS = 64
NT = (((1,), (1,)), ((), ()))
TN = (((0,), (0,)), ((), ()))


def shifted(block, axis, distance):
    n = lax.axis_size(axis)
    return lax.ppermute(block, axis, [(i, (i + distance) % n) for i in range(n)])


def to_unit(raw):
    norm = jnp.sqrt(jnp.sum(raw * raw, axis=1, keepdims=True) + 1e-06)
    return (raw / norm, norm)


def from_unit(grad, unit, norm):
    return (grad - unit * jnp.sum(unit * grad, axis=1, keepdims=True)) / norm


def add(a, b):
    return (a.astype(F32) + b.astype(F32)).astype(BF)


def unit_rows(raw):
    norm = jnp.sqrt(jnp.sum(raw * raw, axis=1, keepdims=True) + 1e-06)
    return (raw / norm).astype(BF)


def spread_kernel(raw, out):
    unit = unit_rows(raw[...])
    for k in range(out.shape[0]):
        out[k] = unit


def unit_kernel(raw, out):
    out[...] = unit_rows(raw[...])


def coeff_kernel(place, scal, xs, xo, ts, dxo, coeff):
    temp = scal[0]
    offset = scal[1]
    rows = ROWS
    half = xs.shape[0]
    pooled = ts.shape[0]
    step = 256
    for j in range(pooled // step):
        sl = pl.ds(j * step, step)
        for h, x in ((0, xs), (half, xo)):
            dots = lax.dot_general(ts[sl], x[...], NT, preferred_element_type=F32)
            coeff[sl, h : h + half] = jax.nn.sigmoid(temp * dots + offset).astype(BF)
    at = pl.multiple_of(place[0] * rows, rows)
    dots = lax.dot_general(ts[pl.ds(at, rows)], xs[0:rows], NT, preferred_element_type=F32)
    eye = lax.broadcasted_iota(jnp.int32, (rows, rows), 0) == lax.broadcasted_iota(
        jnp.int32, (rows, rows), 1
    )
    own = jax.nn.sigmoid(temp * dots + offset) - eye.astype(F32)
    coeff[pl.ds(at, rows), 0:rows] = own.astype(BF)
    for i in range(half // step):
        cols = slice(half + i * step, half + (i + 1) * step)
        part = lax.dot_general(coeff[:, cols], ts[...], TN, preferred_element_type=F32)
        dxo[pl.ds(i * step, step)] = part.astype(BF)


def text_kernel(coeff, xs, xo, dy):
    half = xs.shape[0]
    step = 256
    for j in range(coeff.shape[0] // step):
        sl = pl.ds(j * step, step)
        part = jnp.dot(coeff[sl, 0:half], xs[...], preferred_element_type=F32)
        part += jnp.dot(coeff[sl, half:], xo[...], preferred_element_type=F32)
        dy[sl] = part.astype(BF)


def image_kernel(coeff, ts, other, dxs):
    step = 256
    for i in range(dxs.shape[0] // step):
        sl = pl.ds(i * step, step)
        part = lax.dot_general(coeff[:, i * step : (i + 1) * step], ts[...], TN, preferred_element_type=F32)
        dxs[sl] = (part + other[sl].astype(F32)).astype(BF)


def local(kernel, outs, args, smem=0, flops=0, nbytes=2**20, trans=0):
    specs = [pl.BlockSpec(memory_space=pltpu.SMEM)] * smem
    specs += [pl.BlockSpec(memory_space=pltpu.VMEM)] * (len(args) - smem)
    shapes = tuple(jax.ShapeDtypeStruct(shape, BF) for shape in outs)
    return pl.pallas_call(
        kernel,
        out_shape=shapes,
        in_specs=specs,
        out_specs=tuple(pl.BlockSpec(memory_space=pltpu.VMEM) for _ in outs),
        compiler_params=pltpu.CompilerParams(vmem_limit_bytes=40 * 2**20),
        cost_estimate=pl.CostEstimate(flops=flops, bytes_accessed=nbytes, transcendentals=trans),
    )(*args)


def ring_gather(block):
    up = down = block
    held = [block]
    for _ in range(3):
        up = shifted(up, "z", 1)
        down = shifted(down, "z", -1)
        held += [up, down]
    return jnp.concatenate(held + [shifted(up, "z", 1)], 0)


def ring_reduce(parts):
    up, down = shifted(parts[7], "z", 1), shifted(parts[5], "z", -1)
    up, down = shifted(add(parts[6], up), "z", 1), shifted(add(parts[3], down), "z", -1)
    up, down = shifted(add(parts[4], up), "z", 1), shifted(add(parts[1], down), "z", -1)
    up = shifted(add(parts[2], up), "z", 1)
    return parts[0].astype(F32) + up.astype(F32) + down.astype(F32)


def on_device(images, texts, log_temp, bias):
    temp = jnp.exp(log_temp[0])
    rows, width = images.shape
    n_plane = lax.axis_size(PLANE)
    half = ROWS * lax.axis_size("z")
    pooled = ROWS * n_plane
    (spread,) = local(spread_kernel, [(n_plane, rows, width)], [texts])
    spread, images = lax.optimization_barrier((spread, images))
    ts = lax.all_to_all(spread, PLANE, 0, 0, tiled=True).reshape(pooled, width)
    (x,) = local(unit_kernel, [(rows, width)], [images])
    xs = ring_gather(x)
    xo = shifted(xs, "core", 1)
    img_unit, img_norm = to_unit(images)
    txt_unit, txt_norm = to_unit(texts)
    place = lax.axis_index(PLANE).astype(jnp.int32).reshape(1)
    scal = jnp.stack([temp, bias[0]])
    unit_flops = 2 * half * pooled * width
    dxo, coeff = local(
        coeff_kernel, [(half, width), (pooled, 2 * half)], [place, scal, xs, xo, ts],
        smem=2, flops=3 * unit_flops, nbytes=8 * 2**20, trans=4 * half * pooled,
    )
    (dy,) = local(text_kernel, [(pooled, width)], [coeff, xs, xo], flops=2 * unit_flops, nbytes=7 * 2**20)
    dyr = lax.all_to_all(dy.reshape(n_plane, rows, width), PLANE, 0, 0, tiled=True)
    other = shifted(dxo, "core", 1)
    (mine,) = local(image_kernel, [(half, width)], [coeff, ts, other], flops=unit_flops, nbytes=6 * 2**20)
    image_sum = ring_reduce(mine.reshape(-1, rows, width))
    text_sum = jnp.sum(dyr.astype(F32), axis=0)
    grad_images = from_unit(temp * image_sum, img_unit, img_norm)
    grad_texts = from_unit(temp * text_sum, txt_unit, txt_norm)
    return (grad_images, grad_texts)


def solution(mesh):
    fine = Mesh(mesh.devices.reshape(2, 4, 2, 2, 8), AXES)
    split = P(AXES, None)
    return jax.shard_map(
        on_device,
        mesh=fine,
        in_specs=(split, split, P(), P()),
        out_specs=(split, split),
        check_vma=False,
    )
```

time: 112 us -> 120 us (1.071); the launches traced: 110 us -> 120 us
  waiting for transfers between devices: 45.4 us -> 55.1 us
  local copies, waits for them, and re-layouts: 2.61 us -> 9.25 us
  other arithmetic: 9.02 us -> 4.61 us
  starting transfers between devices: 39.1 us -> 36.5 us
    all_to_all x1, waiting for transfers between devices: 5.83 us -> 17.5 us  [on_device(): lax.all_to_all(dy.reshape(n_plane, rows, width), PLANE, 0, 0, tiled=True)]
    unnamed x13 -> x23, local copies, waits for them, and re-layouts: 0.14 us -> 8.56 us
    ppermute x18 -> x16, starting transfers between devices: 26.7 us -> 23.4 us  [shifted(): lax.ppermute(block, axis, [(i, (i + distance) % n) for i in range(n)])]
    ppermute x18 -> x16, waiting for transfers between devices: 31.7 us -> 28.4 us  [shifted(): lax.ppermute(block, axis, [(i, (i + distance) % n) for i in range(n)])]
    reduce_sum x2, other arithmetic: 2.21 us -> 0.24 us  [to_unit(): norm = jnp.sqrt(jnp.sum(raw * raw, axis=1, keepdims=True) + 1e-06)]
    concatenate x2 -> x0, other arithmetic: 1.84 us -> none  [the longest x1 0.94 us: ring_reduce(): up = jnp.concatenate([add(parts[6, :cut], up), parts[6, cut:]], 0)]
    broadcast_in_dim x1 -> x0, local copies, waits for them, and re-layouts: 1.74 us -> none  [on_device(): spread = jnp.broadcast_to(txt_unit.astype(BF)[None], (n_plane, rows, width))]
    reduce_sum x1, other arithmetic: 0.32 us -> 2.02 us  [on_device(): text_sum = jnp.sum(dyr.astype(F32), axis=0)]
  transfers between devices with their start and end apart: 20 -> 18, of which waited for: 12 -> 12; matrix products, arithmetic and copies ran while one was open for 6% -> 6% of each run, Pallas kernels for 0% -> 3%
where the time goes in v2:
time: 120 us
  waiting for transfers between devices  55.1 us (46%)
  starting transfers between devices  36.5 us (30%)
  Pallas kernels  12 us (10%)
  local copies, waits for them, and re-layouts  9.25 us (8%)
  other arithmetic  4.61 us (4%)
  between operations  2.16 us (2%)
    ppermute x16, waiting for transfers between devices, shifted(): lax.ppermute(block, axis, [(i, (i + distance) % n) for i in range(n)])  28.4 us
    ppermute x16, starting transfers between devices, shifted(): lax.ppermute(block, axis, [(i, (i + distance) % n) for i in range(n)])  23.4 us
    all_to_all x1, waiting for transfers between devices, on_device(): lax.all_to_all(dy.reshape(n_plane, rows, width), PLANE, 0, 0, tiled=True)  17.5 us
    pallas_call x5, Pallas kernels, local(): pl.pallas_call(kernel, out_shape=shapes, in_specs=specs, out_specs=tuple(...  12 us
    all_to_all x1, waiting for transfers between devices, on_device(): ts = lax.all_to_all(spread, PLANE, 0, 0, tiled=True).reshape(pooled, width)  9.22 us
    unnamed x23, local copies, waits for them, and re-layouts  8.56 us
    all_to_all x1, starting transfers between devices, on_device(): ts = lax.all_to_all(spread, PLANE, 0, 0, tiled=True).reshape(pooled, width)  7.39 us
    all_to_all x1, starting transfers between devices, on_device(): lax.all_to_all(dy.reshape(n_plane, rows, width), PLANE, 0, 0, tiled=True)  5.77 us
  transfers between devices with their start and end apart: 18, of which 12 were waited for; matrix products, arithmetic and copies ran while one was open for 6% of the time, Pallas kernels for 3%

profile of v2, /device:TPU:8, one launch (start us, length us, event | category | flops | bytes accessed | tf_op | source)
XLA Modules:
  0.0 119.6 jit_solution(9547307884608345771)
XLA Ops:
  3.5 2.0 %collective-permute-start = (bf16[64,1152]{1,0:T(8,128)(2,1)S(1)}, bf16[64,1152]{1,0:T(8,128)(2,1)S(1)}, u32[]{:S(2)}, u32[]{:S(2)}) collective-permute-start(bf16[64,1152]{1,0:T(8,128)(2,1)S(1)} %shard_map.60), channel_id=1, source_target_pairs={{0,1},{1,2},{2,3},{3,4},{4,5},{5,6},{6,7},{7,0},{8,9},{9,10},{10,1... | collective-permute-start | bytes 442376 | tf_op jit(solution)/shard_map/ppermute | solution.py:19
  5.5 4.0 %collective-permute-start.1 = (bf16[64,1152]{1,0:T(8,128)(2,1)S(1)}, bf16[64,1152]{1,0:T(8,128)(2,1)S(1)}, u32[]{:S(2)}, u32[]{:S(2)}) collective-permute-start(bf16[64,1152]{1,0:T(8,128)(2,1)S(1)} %shard_map.60), channel_id=1, source_target_pairs={{0,7},{1,0},{2,1},{3,2},{4,3},{5,4},{6,5},{7,6},{8,15},{9,8},{10,9... | collective-permute-start | bytes 442376 | tf_op jit(solution)/shard_map/ppermute | solution.py:19
  9.5 7.4 %all-to-all-start = ((bf16[16,64,1152]{2,1,0:T(8,128)(2,1)}), bf16[16,64,1152]{2,1,0:T(8,128)(2,1)S(1)}, u32[]{:S(2)}, u32[]{:S(2)}) async-start(bf16[16,64,1152]{2,1,0:T(8,128)(2,1)} %copy-done), calls=%async_computation | async-start | bytes 4718592 | tf_op jit(solution)/shard_map/all_to_all | solution.py:133
  18.3 3.2 %collective-permute-start.3 = (bf16[64,1152]{1,0:T(8,128)(2,1)S(1)}, bf16[64,1152]{1,0:T(8,128)(2,1)S(1)}, u32[]{:S(2)}, u32[]{:S(2)}) collective-permute-start(bf16[64,1152]{1,0:T(8,128)(2,1)S(1)} %collective-permute-done.1), channel_id=1, source_target_pairs={{0,7},{1,0},{2,1},{3,2},{4,3},{5,4},{6,5},{7,6},{8,15},{9,8},{10,9... | collective-permute-start | bytes 442376 | tf_op jit(solution)/shard_map/ppermute | solution.py:19
  22.2 1.8 %collective-permute-done.2 = bf16[64,1152]{1,0:T(8,128)(2,1)S(1)} collective-permute-done((bf16[64,1152]{1,0:T(8,128)(2,1)S(1)}, bf16[64,1152]{1,0:T(8,128)(2,1)S(1)}, u32[]{:S(2)}, u32[]{:S(2)}) %collective-permute-start.2) | collective-permute-done | bytes 147488 | tf_op jit(solution)/shard_map/ppermute | solution.py:19
  24.6 3.2 %collective-permute-start.5 = (bf16[64,1152]{1,0:T(8,128)(2,1)S(1)}, bf16[64,1152]{1,0:T(8,128)(2,1)S(1)}, u32[]{:S(2)}, u32[]{:S(2)}) collective-permute-start(bf16[64,1152]{1,0:T(8,128)(2,1)S(1)} %collective-permute-done.3), channel_id=1, source_target_pairs={{0,7},{1,0},{2,1},{3,2},{4,3},{5,4},{6,5},{7,6},{8,15},{9,8},{10,9... | collective-permute-start | bytes 442376 | tf_op jit(solution)/shard_map/ppermute | solution.py:19
  28.5 1.8 %collective-permute-done.4 = bf16[64,1152]{1,0:T(8,128)(2,1)S(1)} collective-permute-done((bf16[64,1152]{1,0:T(8,128)(2,1)S(1)}, bf16[64,1152]{1,0:T(8,128)(2,1)S(1)}, u32[]{:S(2)}, u32[]{:S(2)}) %collective-permute-start.4) | collective-permute-done | bytes 147488 | tf_op jit(solution)/shard_map/ppermute | solution.py:19
  31.6 5.0 %collective-permute-done.6 = bf16[64,1152]{1,0:T(8,128)(2,1)S(1)} collective-permute-done((bf16[64,1152]{1,0:T(8,128)(2,1)S(1)}, bf16[64,1152]{1,0:T(8,128)(2,1)S(1)}, u32[]{:S(2)}, u32[]{:S(2)}) %collective-permute-start.6) | collective-permute-done | bytes 147488 | tf_op jit(solution)/shard_map/ppermute | solution.py:19
  38.7 1.6 %collective-permute-done.7.xo = bf16[512,1152]{1,0:T(8,128)(2,1)S(1)} collective-permute-done((bf16[512,1152]{1,0:T(8,128)(2,1)}, bf16[512,1152]{1,0:T(8,128)(2,1)S(1)}, u32[]{:S(2)}, u32[]{:S(2)}) %collective-permute-start.7) | collective-permute-done | bytes 1179680 | tf_op jit(solution)/shard_map/ppermute | solution.py:19
  40.4 9.2 %all-to-all-done = bf16[16,64,1152]{2,1,0:T(8,128)(2,1)S(1)} async-done(((bf16[16,64,1152]{2,1,0:T(8,128)(2,1)}), bf16[16,64,1152]{2,1,0:T(8,128)(2,1)S(1)}, u32[]{:S(2)}, u32[]{:S(2)}) %all-to-all-start) | async-done | bytes 2359328 | tf_op jit(solution)/shard_map/all_to_all | solution.py:133
  49.6 5.9 %shard_map.61 = (bf16[512,1152]{1,0:T(8,128)(2,1)S(1)}, bf16[1024,1024]{1,0:T(8,128)(2,1)S(1)}) custom-call(s32[1]{0:T(128)} %bitcast.1.place, f32[2]{0:T(128)S(1)} %pad_maximum_fusion.scal, bf16[512,1152]{1,0:T(8,128)(2,1)} %constant_dynamic-update-slice_fusion.xs, bf16[512,1152]{1,0:T(8,128)(2,1)S(1)} %collective-permute-done.7.xo, ...), custom_call_target="tpu_custom_call" | custom-call | flops 3623878656 | bytes 8388608 | tf_op jit(solution)/shard_map/pallas_call | solution.py:97
  55.6 2.8 %collective-permute-done.8.other = bf16[512,1152]{1,0:T(8,128)(2,1)S(1)} collective-permute-done((bf16[512,1152]{1,0:T(8,128)(2,1)S(1)}, bf16[512,1152]{1,0:T(8,128)(2,1)S(1)}, u32[]{:S(2)}, u32[]{:S(2)}) %collective-permute-start.8) | collective-permute-done | bytes 1179680 | tf_op jit(solution)/shard_map/ppermute | solution.py:19
  58.4 1.6 %shard_map.62 = bf16[512,1152]{1,0:T(8,128)(2,1)S(1)} custom-call(bf16[1024,1024]{1,0:T(8,128)(2,1)S(1)} %get-tuple-element.8.coeff, bf16[1024,1152]{1,0:T(8,128)(2,1)S(1)} %bitcast.5, bf16[512,1152]{1,0:T(8,128)(2,1)S(1)} %collective-permute-done.8.other), custom_call_target="tpu_custom_call" | custom-call | flops 1207959552 | bytes 6291456 | tf_op jit(solution)/shard_map/pallas_call | solution.py:97
  60.3 7.1 %collective-permute-done.9 = bf16[64,1152]{1,0:T(8,128)(2,1)S(1)} collective-permute-done((bf16[64,1152]{1,0:T(8,128)(2,1)S(1)}, bf16[64,1152]{1,0:T(8,128)(2,1)S(1)}, u32[]{:S(2)}, u32[]{:S(2)}) %collective-permute-start.9) | collective-permute-done | bytes 147488 | tf_op jit(solution)/shard_map/ppermute | solution.py:19
  67.5 3.2 %collective-permute-start.13 = (bf16[64,1152]{1,0:T(8,128)(2,1)S(1)}, bf16[64,1152]{1,0:T(8,128)(2,1)S(1)}, u32[]{:S(2)}, u32[]{:S(2)}) collective-permute-start(bf16[64,1152]{1,0:T(8,128)(2,1)S(1)} %get-tuple-element.13), channel_id=1, source_target_pairs={{0,7},{1,0},{2,1},{3,2},{4,3},{5,4},{6,5},{7,6},{8,15},{9,8},{10,9... | collective-permute-start | bytes 442376 | tf_op jit(solution)/shard_map/ppermute | solution.py:19
  70.7 3.1 %collective-permute-done.10 = bf16[64,1152]{1,0:T(8,128)(2,1)S(1)} collective-permute-done((bf16[64,1152]{1,0:T(8,128)(2,1)S(1)}, bf16[64,1152]{1,0:T(8,128)(2,1)S(1)}, u32[]{:S(2)}, u32[]{:S(2)}) %collective-permute-start.10) | collective-permute-done | bytes 147488 | tf_op jit(solution)/shard_map/ppermute | solution.py:19
  74.0 4.2 %shard_map.63 = bf16[1024,1152]{1,0:T(8,128)(2,1)S(1)} custom-call(bf16[1024,1024]{1,0:T(8,128)(2,1)S(1)} %get-tuple-element.8.coeff, bf16[512,1152]{1,0:T(8,128)(2,1)} %constant_dynamic-update-slice_fusion.xs, bf16[512,1152]{1,0:T(8,128)(2,1)S(1)} %copy-done.7), custom_call_target="tpu_custom_call" | custom-call | flops 2415919104 | bytes 7340032 | tf_op jit(solution)/shard_map/pallas_call | solution.py:97
  79.6 5.8 %all-to-all-start.1 = ((bf16[16,64,1152]{2,1,0:T(8,128)(2,1)}), bf16[16,64,1152]{2,1,0:T(8,128)(2,1)}, u32[]{:S(2)}, u32[]{:S(2)}) async-start(bf16[16,64,1152]{2,1,0:T(8,128)(2,1)} %bitcast.6), calls=%async_computation.1 | async-start | bytes 4718592 | tf_op jit(solution)/shard_map/all_to_all | solution.py:147
  85.6 3.3 %collective-permute-start.14 = (bf16[64,1152]{1,0:T(8,128)(2,1)S(1)}, bf16[64,1152]{1,0:T(8,128)(2,1)S(1)}, u32[]{:S(2)}, u32[]{:S(2)}) collective-permute-start(bf16[64,1152]{1,0:T(8,128)(2,1)S(1)} %get-tuple-element.11), channel_id=1, source_target_pairs={{0,7},{1,0},{2,1},{3,2},{4,3},{5,4},{6,5},{7,6},{8,15},{9,8},{10,9... | collective-permute-start | bytes 442376 | tf_op jit(solution)/shard_map/ppermute | solution.py:19
  89.1 2.5 %collective-permute-done.14 = bf16[64,1152]{1,0:T(8,128)(2,1)S(1)} collective-permute-done((bf16[64,1152]{1,0:T(8,128)(2,1)S(1)}, bf16[64,1152]{1,0:T(8,128)(2,1)S(1)}, u32[]{:S(2)}, u32[]{:S(2)}) %collective-permute-start.14) | collective-permute-done | bytes 147488 | tf_op jit(solution)/shard_map/ppermute | solution.py:19
  91.6 3.8 %collective-permute-start.15 = (bf16[64,1152]{1,0:T(8,128)(2,1)S(1)}, bf16[64,1152]{1,0:T(8,128)(2,1)S(1)}, u32[]{:S(2)}, u32[]{:S(2)}) collective-permute-start(bf16[64,1152]{1,0:T(8,128)(2,1)S(1)} %add_convert_fusion), channel_id=1, source_target_pairs={{0,7},{1,0},{2,1},{3,2},{4,3},{5,4},{6,5},{7,6},{8,15},{9,8},{10,9... | collective-permute-start | bytes 442376 | tf_op jit(solution)/shard_map/ppermute | solution.py:19
  95.4 2.6 %collective-permute-done.15 = bf16[64,1152]{1,0:T(8,128)(2,1)S(1)} collective-permute-done((bf16[64,1152]{1,0:T(8,128)(2,1)S(1)}, bf16[64,1152]{1,0:T(8,128)(2,1)S(1)}, u32[]{:S(2)}, u32[]{:S(2)}) %collective-permute-start.15) | collective-permute-done | bytes 147488 | tf_op jit(solution)/shard_map/ppermute | solution.py:19
  99.0 17.5 %all-to-all-done.1 = bf16[16,64,1152]{2,1,0:T(8,128)(2,1)} async-done(((bf16[16,64,1152]{2,1,0:T(8,128)(2,1)}), bf16[16,64,1152]{2,1,0:T(8,128)(2,1)}, u32[]{:S(2)}, u32[]{:S(2)}) %all-to-all-start.1) | async-done | bytes 2359328 | tf_op jit(solution)/shard_map/all_to_all | solution.py:147
  116.6 2.0 %convert_reduce_fusion = f32[64,1152]{1,0:T(8,128)S(1)} fusion(bf16[16,64,1152]{2,1,0:T(8,128)(2,1)} %all-to-all-done.1), kind=kLoop, calls=%fused_computation | loop fusion | flops 2285568 | bytes 2654208 | tf_op jit(solution)/shard_map/reduce_sum | solution.py:151
  (56 shorter events, 13.0 us)
Async XLA Ops:
  0.6 2.7 %copy-start.1 = (f32[64,1152]{1,0:T(8,128)S(1)}, f32[64,1152]{1,0:T(8,128)}, u32[]{:S(2)}) copy-start(f32[64,1152]{1,0:T(8,128)} %raw.2) | copy-start | bytes 884740
  1.9 1.4 %copy-start = (bf16[16,64,1152]{2,1,0:T(8,128)(2,1)}, bf16[16,64,1152]{2,1,0:T(8,128)(2,1)S(1)}, u32[]{:S(2)}) copy-start(bf16[16,64,1152]{2,1,0:T(8,128)(2,1)S(1)} %shard_map.59) | copy-start | bytes 7077892
  3.5 14.1 %collective-permute-start = (bf16[64,1152]{1,0:T(8,128)(2,1)S(1)}, bf16[64,1152]{1,0:T(8,128)(2,1)S(1)}, u32[]{:S(2)}, u32[]{:S(2)}) collective-permute-start(bf16[64,1152]{1,0:T(8,128)(2,1)S(1)} %shard_map.60), channel_id=1, source_target_pairs={{0,1},{1,2},{2,3},{3,4},{4,5},{5,6},{6,7},{7,0},{8,9},{9,10},{10,1... | collective-permute-start | bytes 442376 | tf_op jit(solution)/shard_map/ppermute | solution.py:19
  5.5 12.8 %collective-permute-start.1 = (bf16[64,1152]{1,0:T(8,128)(2,1)S(1)}, bf16[64,1152]{1,0:T(8,128)(2,1)S(1)}, u32[]{:S(2)}, u32[]{:S(2)}) collective-permute-start(bf16[64,1152]{1,0:T(8,128)(2,1)S(1)} %shard_map.60), channel_id=1, source_target_pairs={{0,7},{1,0},{2,1},{3,2},{4,3},{5,4},{6,5},{7,6},{8,15},{9,8},{10,9... | collective-permute-start | bytes 442376 | tf_op jit(solution)/shard_map/ppermute | solution.py:19
  9.5 40.1 %all-to-all-start = ((bf16[16,64,1152]{2,1,0:T(8,128)(2,1)}), bf16[16,64,1152]{2,1,0:T(8,128)(2,1)S(1)}, u32[]{:S(2)}, u32[]{:S(2)}) async-start(bf16[16,64,1152]{2,1,0:T(8,128)(2,1)} %copy-done), calls=%async_computation | async-start | bytes 4718592 | tf_op jit(solution)/shard_map/all_to_all | solution.py:133
  17.6 6.4 %collective-permute-start.2 = (bf16[64,1152]{1,0:T(8,128)(2,1)S(1)}, bf16[64,1152]{1,0:T(8,128)(2,1)S(1)}, u32[]{:S(2)}, u32[]{:S(2)}) collective-permute-start(bf16[64,1152]{1,0:T(8,128)(2,1)S(1)} %collective-permute-done), channel_id=1, source_target_pairs={{0,1},{1,2},{2,3},{3,4},{4,5},{5,6},{6,7},{7,0},{8,9},{9,10},{10,1... | collective-permute-start | bytes 442376 | tf_op jit(solution)/shard_map/ppermute | solution.py:19
  18.3 6.4 %collective-permute-start.3 = (bf16[64,1152]{1,0:T(8,128)(2,1)S(1)}, bf16[64,1152]{1,0:T(8,128)(2,1)S(1)}, u32[]{:S(2)}, u32[]{:S(2)}) collective-permute-start(bf16[64,1152]{1,0:T(8,128)(2,1)S(1)} %collective-permute-done.1), channel_id=1, source_target_pairs={{0,7},{1,0},{2,1},{3,2},{4,3},{5,4},{6,5},{7,6},{8,15},{9,8},{10,9... | collective-permute-start | bytes 442376 | tf_op jit(solution)/shard_map/ppermute | solution.py:19
  23.9 6.4 %collective-permute-start.4 = (bf16[64,1152]{1,0:T(8,128)(2,1)S(1)}, bf16[64,1152]{1,0:T(8,128)(2,1)S(1)}, u32[]{:S(2)}, u32[]{:S(2)}) collective-permute-start(bf16[64,1152]{1,0:T(8,128)(2,1)S(1)} %collective-permute-done.2), channel_id=1, source_target_pairs={{0,1},{1,2},{2,3},{3,4},{4,5},{5,6},{6,7},{7,0},{8,9},{9,10},{10,1... | collective-permute-start | bytes 442376 | tf_op jit(solution)/shard_map/ppermute | solution.py:19
  24.6 6.4 %collective-permute-start.5 = (bf16[64,1152]{1,0:T(8,128)(2,1)S(1)}, bf16[64,1152]{1,0:T(8,128)(2,1)S(1)}, u32[]{:S(2)}, u32[]{:S(2)}) collective-permute-start(bf16[64,1152]{1,0:T(8,128)(2,1)S(1)} %collective-permute-done.3), channel_id=1, source_target_pairs={{0,7},{1,0},{2,1},{3,2},{4,3},{5,4},{6,5},{7,6},{8,15},{9,8},{10,9... | collective-permute-start | bytes 442376 | tf_op jit(solution)/shard_map/ppermute | solution.py:19
  30.3 6.4 %collective-permute-start.6 = (bf16[64,1152]{1,0:T(8,128)(2,1)S(1)}, bf16[64,1152]{1,0:T(8,128)(2,1)S(1)}, u32[]{:S(2)}, u32[]{:S(2)}) collective-permute-start(bf16[64,1152]{1,0:T(8,128)(2,1)S(1)} %collective-permute-done.4), channel_id=1, source_target_pairs={{0,1},{1,2},{2,3},{3,4},{4,5},{5,6},{6,7},{7,0},{8,9},{9,10},{10,1... | collective-permute-start | bytes 442376 | tf_op jit(solution)/shard_map/ppermute | solution.py:19
  37.3 3.1 %collective-permute-start.7 = (bf16[512,1152]{1,0:T(8,128)(2,1)}, bf16[512,1152]{1,0:T(8,128)(2,1)S(1)}, u32[]{:S(2)}, u32[]{:S(2)}) collective-permute-start(bf16[512,1152]{1,0:T(8,128)(2,1)} %constant_dynamic-update-slice_fusion.xs), channel_id=1, source_target_pairs={{0,16},{16,0},{1,17},{17,1},{2,18},{18,2},{3,19},{19,3},{4,20},{20... | collective-permute-start | bytes 3538952 | tf_op jit(solution)/shard_map/ppermute | solution.py:19
  40.4 15.1 %copy-start.6 = (bf16[512,1152]{1,0:T(8,128)(2,1)}, bf16[512,1152]{1,0:T(8,128)(2,1)S(1)}, u32[]{:S(2)}) copy-start(bf16[512,1152]{1,0:T(8,128)(2,1)S(1)} %collective-permute-done.7.xo) | copy-start | bytes 3538948
  55.5 2.9 %collective-permute-start.8 = (bf16[512,1152]{1,0:T(8,128)(2,1)S(1)}, bf16[512,1152]{1,0:T(8,128)(2,1)S(1)}, u32[]{:S(2)}, u32[]{:S(2)}) collective-permute-start(bf16[512,1152]{1,0:T(8,128)(2,1)S(1)} %get-tuple-element.9), channel_id=1, source_target_pairs={{0,16},{16,0},{1,17},{17,1},{2,18},{18,2},{3,19},{19,3},{4,20},{20... | collective-permute-start | bytes 3538952 | tf_op jit(solution)/shard_map/ppermute | solution.py:19
  60.0 14.0 %copy-start.7 = (bf16[512,1152]{1,0:T(8,128)(2,1)S(1)}, bf16[512,1152]{1,0:T(8,128)(2,1)}, u32[]{:S(2)}) copy-start(bf16[512,1152]{1,0:T(8,128)(2,1)} %copy-done.6) | copy-start | bytes 3538948
  60.0 7.4 %collective-permute-start.9 = (bf16[64,1152]{1,0:T(8,128)(2,1)S(1)}, bf16[64,1152]{1,0:T(8,128)(2,1)S(1)}, u32[]{:S(2)}, u32[]{:S(2)}) collective-permute-start(bf16[64,1152]{1,0:T(8,128)(2,1)S(1)} %get-tuple-element.12), channel_id=1, source_target_pairs={{0,1},{1,2},{2,3},{3,4},{4,5},{5,6},{6,7},{7,0},{8,9},{9,10},{10,1... | collective-permute-start | bytes 442376 | tf_op jit(solution)/shard_map/ppermute | solution.py:19
  67.4 6.4 %collective-permute-start.10 = (bf16[64,1152]{1,0:T(8,128)(2,1)S(1)}, bf16[64,1152]{1,0:T(8,128)(2,1)S(1)}, u32[]{:S(2)}, u32[]{:S(2)}) collective-permute-start(bf16[64,1152]{1,0:T(8,128)(2,1)S(1)} %add_convert_fusion.4), channel_id=1, source_target_pairs={{0,1},{1,2},{2,3},{3,4},{4,5},{5,6},{6,7},{7,0},{8,9},{9,10},{10,1... | collective-permute-start | bytes 442376 | tf_op jit(solution)/shard_map/ppermute | solution.py:19
  67.5 18.0 %collective-permute-start.13 = (bf16[64,1152]{1,0:T(8,128)(2,1)S(1)}, bf16[64,1152]{1,0:T(8,128)(2,1)S(1)}, u32[]{:S(2)}, u32[]{:S(2)}) collective-permute-start(bf16[64,1152]{1,0:T(8,128)(2,1)S(1)} %get-tuple-element.13), channel_id=1, source_target_pairs={{0,7},{1,0},{2,1},{3,2},{4,3},{5,4},{6,5},{7,6},{8,15},{9,8},{10,9... | collective-permute-start | bytes 442376 | tf_op jit(solution)/shard_map/ppermute | solution.py:19
  73.9 11.6 %collective-permute-start.11 = (bf16[64,1152]{1,0:T(8,128)(2,1)S(1)}, bf16[64,1152]{1,0:T(8,128)(2,1)S(1)}, u32[]{:S(2)}, u32[]{:S(2)}) collective-permute-start(bf16[64,1152]{1,0:T(8,128)(2,1)S(1)} %add_convert_fusion.3), channel_id=1, source_target_pairs={{0,1},{1,2},{2,3},{3,4},{4,5},{5,6},{6,7},{7,0},{8,9},{9,10},{10,1... | collective-permute-start | bytes 442376 | tf_op jit(solution)/shard_map/ppermute | solution.py:19
  79.6 5.8 %copy-start.2 = (f32[64,1152]{1,0:T(8,128)S(1)}, f32[64,1152]{1,0:T(8,128)}, u32[]{:S(2)}) copy-start(f32[64,1152]{1,0:T(8,128)} %raw.2) | copy-start | bytes 884740
  79.6 37.0 %all-to-all-start.1 = ((bf16[16,64,1152]{2,1,0:T(8,128)(2,1)}), bf16[16,64,1152]{2,1,0:T(8,128)(2,1)}, u32[]{:S(2)}, u32[]{:S(2)}) async-start(bf16[16,64,1152]{2,1,0:T(8,128)(2,1)} %bitcast.6), calls=%async_computation.1 | async-start | bytes 4718592 | tf_op jit(solution)/shard_map/all_to_all | solution.py:147
  85.3 3.5 %copy-start.4 = (f32[64,1152]{1,0:T(8,128)S(1)}, f32[64,1152]{1,0:T(8,128)}, u32[]{:S(2)}) copy-start(f32[64,1152]{1,0:T(8,128)} %raw.1) | copy-start | bytes 884740
  85.6 6.0 %collective-permute-start.14 = (bf16[64,1152]{1,0:T(8,128)(2,1)S(1)}, bf16[64,1152]{1,0:T(8,128)(2,1)S(1)}, u32[]{:S(2)}, u32[]{:S(2)}) collective-permute-start(bf16[64,1152]{1,0:T(8,128)(2,1)S(1)} %get-tuple-element.11), channel_id=1, source_target_pairs={{0,7},{1,0},{2,1},{3,2},{4,3},{5,4},{6,5},{7,6},{8,15},{9,8},{10,9... | collective-permute-start | bytes 442376 | tf_op jit(solution)/shard_map/ppermute | solution.py:19
  89.0 6.4 %collective-permute-start.12 = (bf16[64,1152]{1,0:T(8,128)(2,1)S(1)}, bf16[64,1152]{1,0:T(8,128)(2,1)S(1)}, u32[]{:S(2)}, u32[]{:S(2)}) collective-permute-start(bf16[64,1152]{1,0:T(8,128)(2,1)S(1)} %get-tuple-element.10), channel_id=1, source_target_pairs={{0,1},{1,2},{2,3},{3,4},{4,5},{5,6},{6,7},{7,0},{8,9},{9,10},{10,1... | collective-permute-start | bytes 442376 | tf_op jit(solution)/shard_map/ppermute | solution.py:19
  91.6 6.4 %collective-permute-start.15 = (bf16[64,1152]{1,0:T(8,128)(2,1)S(1)}, bf16[64,1152]{1,0:T(8,128)(2,1)S(1)}, u32[]{:S(2)}, u32[]{:S(2)}) collective-permute-start(bf16[64,1152]{1,0:T(8,128)(2,1)S(1)} %add_convert_fusion), channel_id=1, source_target_pairs={{0,7},{1,0},{2,1},{3,2},{4,3},{5,4},{6,5},{7,6},{8,15},{9,8},{10,9... | collective-permute-start | bytes 442376 | tf_op jit(solution)/shard_map/ppermute | solution.py:19
  (2 other events, 2.4 us)

commit v3 on v2

--- a/solution.py
+++ b/solution.py
@@ -37,49 +37,56 @@
     return (raw / norm).astype(BF)
 
 
-def spread_kernel(raw, out):
-    unit = unit_rows(raw[...])
-    for k in range(out.shape[0]):
-        out[k] = unit
+def spread_kernel(raw, out, unit, sems):
+    unit[...] = unit_rows(raw[...])
+    copies = [pltpu.make_async_copy(unit, out.at[k], sems.at[k]) for k in range(out.shape[0])]
+    for copy in copies:
+        copy.start()
+    for copy in copies:
+        copy.wait()
 
 
 def unit_kernel(raw, out):
     out[...] = unit_rows(raw[...])
 
 
-def coeff_kernel(place, scal, xs, xo, ts, dxo, coeff):
+def text_kernel(place, scal, xs, xo, ts, coeff, dy, part, sems):
     temp = scal[0]
     offset = scal[1]
-    rows = ROWS
     half = xs.shape[0]
     pooled = ts.shape[0]
-    step = 256
+    step = pooled // sems.shape[0]
     for j in range(pooled // step):
         sl = pl.ds(j * step, step)
         for h, x in ((0, xs), (half, xo)):
             dots = lax.dot_general(ts[sl], x[...], NT, preferred_element_type=F32)
             coeff[sl, h : h + half] = jax.nn.sigmoid(temp * dots + offset).astype(BF)
-    at = pl.multiple_of(place[0] * rows, rows)
-    dots = lax.dot_general(ts[pl.ds(at, rows)], xs[0:rows], NT, preferred_element_type=F32)
-    eye = lax.broadcasted_iota(jnp.int32, (rows, rows), 0) == lax.broadcasted_iota(
-        jnp.int32, (rows, rows), 1
+    at = pl.multiple_of(place[0] * ROWS, ROWS)
+    dots = lax.dot_general(ts[pl.ds(at, ROWS)], xs[0:ROWS], NT, preferred_element_type=F32)
+    eye = lax.broadcasted_iota(jnp.int32, (ROWS, ROWS), 0) == lax.broadcasted_iota(
+        jnp.int32, (ROWS, ROWS), 1
     )
     own = jax.nn.sigmoid(temp * dots + offset) - eye.astype(F32)
-    coeff[pl.ds(at, rows), 0:rows] = own.astype(BF)
+    coeff[pl.ds(at, ROWS), 0:ROWS] = own.astype(BF)
+    copies = []
+    for j in range(pooled // step):
+        sl = pl.ds(j * step, step)
+        dots = jnp.dot(coeff[sl, 0:half], xs[...], preferred_element_type=F32)
+        dots += jnp.dot(coeff[sl, half:], xo[...], preferred_element_type=F32)
+        part[sl] = dots.astype(BF)
+        copies.append(pltpu.make_async_copy(part.at[sl], dy.at[sl], sems.at[j]))
+        copies[-1].start()
+    for copy in copies:
+        copy.wait()
+
+
+def other_kernel(coeff, ts, dxo):
+    half = dxo.shape[0]
+    step = 256
     for i in range(half // step):
         cols = slice(half + i * step, half + (i + 1) * step)
         part = lax.dot_general(coeff[:, cols], ts[...], TN, preferred_element_type=F32)
         dxo[pl.ds(i * step, step)] = part.astype(BF)
-
-
-def text_kernel(coeff, xs, xo, dy):
-    half = xs.shape[0]
-    step = 256
-    for j in range(coeff.shape[0] // step):
-        sl = pl.ds(j * step, step)
-        part = jnp.dot(coeff[sl, 0:half], xs[...], preferred_element_type=F32)
-        part += jnp.dot(coeff[sl, half:], xo[...], preferred_element_type=F32)
-        dy[sl] = part.astype(BF)
 
 
 def image_kernel(coeff, ts, other, dxs):
@@ -90,15 +97,18 @@
         dxs[sl] = (part + other[sl].astype(F32)).astype(BF)
 
 
-def local(kernel, outs, args, smem=0, flops=0, nbytes=2**20, trans=0):
-    specs = [pl.BlockSpec(memory_space=pltpu.SMEM)] * smem
-    specs += [pl.BlockSpec(memory_space=pltpu.VMEM)] * (len(args) - smem)
-    shapes = tuple(jax.ShapeDtypeStruct(shape, BF) for shape in outs)
+VMEM = pl.BlockSpec(memory_space=pltpu.VMEM)
+SMEM = pl.BlockSpec(memory_space=pltpu.SMEM)
+HBM = pl.BlockSpec(memory_space=pltpu.HBM)
+
+
+def local(kernel, outs, args, smem=0, scratch=(), flops=0, nbytes=2**20, trans=0):
     return pl.pallas_call(
         kernel,
-        out_shape=shapes,
-        in_specs=specs,
-        out_specs=tuple(pl.BlockSpec(memory_space=pltpu.VMEM) for _ in outs),
+        out_shape=tuple(jax.ShapeDtypeStruct(shape, BF) for shape, _ in outs),
+        in_specs=[SMEM] * smem + [VMEM] * (len(args) - smem),
+        out_specs=tuple(spec for _, spec in outs),
+        scratch_shapes=list(scratch),
         compiler_params=pltpu.CompilerParams(vmem_limit_bytes=40 * 2**20),
         cost_estimate=pl.CostEstimate(flops=flops, bytes_accessed=nbytes, transcendentals=trans),
     )(*args)
@@ -128,10 +138,13 @@
     n_plane = lax.axis_size(PLANE)
     half = ROWS * lax.axis_size("z")
     pooled = ROWS * n_plane
-    (spread,) = local(spread_kernel, [(n_plane, rows, width)], [texts])
+    (spread,) = local(
+        spread_kernel, [((n_plane, rows, width), HBM)], [texts],
+        scratch=[pltpu.VMEM((rows, width), BF), pltpu.SemaphoreType.DMA((n_plane,))],
+    )
     spread, images = lax.optimization_barrier((spread, images))
     ts = lax.all_to_all(spread, PLANE, 0, 0, tiled=True).reshape(pooled, width)
-    (x,) = local(unit_kernel, [(rows, width)], [images])
+    (x,) = local(unit_kernel, [((rows, width), VMEM)], [images])
     xs = ring_gather(x)
     xo = shifted(xs, "core", 1)
     img_unit, img_norm = to_unit(images)
@@ -139,14 +152,15 @@
     place = lax.axis_index(PLANE).astype(jnp.int32).reshape(1)
     scal = jnp.stack([temp, bias[0]])
     unit_flops = 2 * half * pooled * width
-    dxo, coeff = local(
-        coeff_kernel, [(half, width), (pooled, 2 * half)], [place, scal, xs, xo, ts],
-        smem=2, flops=3 * unit_flops, nbytes=8 * 2**20, trans=4 * half * pooled,
+    coeff, dy = local(
+        text_kernel, [((pooled, 2 * half), VMEM), ((pooled, width), HBM)], [place, scal, xs, xo, ts], smem=2,
+        scratch=[pltpu.VMEM((pooled, width), BF), pltpu.SemaphoreType.DMA((4,))],
+        flops=4 * unit_flops, nbytes=9 * 2**20, trans=4 * half * pooled,
     )
-    (dy,) = local(text_kernel, [(pooled, width)], [coeff, xs, xo], flops=2 * unit_flops, nbytes=7 * 2**20)
     dyr = lax.all_to_all(dy.reshape(n_plane, rows, width), PLANE, 0, 0, tiled=True)
+    (dxo,) = local(other_kernel, [((half, width), VMEM)], [coeff, ts], flops=unit_flops, nbytes=5 * 2**20)
     other = shifted(dxo, "core", 1)
-    (mine,) = local(image_kernel, [(half, width)], [coeff, ts, other], flops=unit_flops, nbytes=6 * 2**20)
+    (mine,) = local(image_kernel, [((half, width), VMEM)], [coeff, ts, other], flops=unit_flops, nbytes=6 * 2**20)
     image_sum = ring_reduce(mine.reshape(-1, rows, width))
     text_sum = jnp.sum(dyr.astype(F32), axis=0)
     grad_images = from_unit(temp * image_sum, img_unit, img_norm)

time: 120 us -> 123 us (1.025)
  Pallas kernels: 12 us -> 14.7 us
    pallas_call x5, Pallas kernels: 12 us -> 14.7 us  [local(): pl.pallas_call(kernel, out_shape=tuple((jax.ShapeDtypeStruct(shape, BF) f...]
    unnamed x23 -> x19, local copies, waits for them, and re-layouts: 8.56 us -> 8.51 us
  transfers between devices with their start and end apart: 18 -> 18, of which waited for: 12 -> 13; matrix products, arithmetic and copies ran while one was open for 6% -> 6% of each run, Pallas kernels for 3% -> 0%
where the time goes in v3:
time: 123 us; the launch traced here: 122 us
  waiting for transfers between devices  55.5 us (45%)
  starting transfers between devices  36 us (29%)
  Pallas kernels  14.7 us (12%)
  local copies, waits for them, and re-layouts  9.18 us (7%)
  other arithmetic  4.61 us (4%)
  between operations  2.14 us (2%)
    ppermute x16, waiting for transfers between devices, shifted(): lax.ppermute(block, axis, [(i, (i + distance) % n) for i in range(n)])  28.8 us
    ppermute x16, starting transfers between devices, shifted(): lax.ppermute(block, axis, [(i, (i + distance) % n) for i in range(n)])  22.8 us
    all_to_all x1, waiting for transfers between devices, on_device(): lax.all_to_all(dy.reshape(n_plane, rows, width), PLANE, 0, 0, tiled=True)  17.5 us
    pallas_call x5, Pallas kernels, local(): pl.pallas_call(kernel, out_shape=tuple((jax.ShapeDtypeStruct(shape, BF) f...  14.7 us
    all_to_all x1, waiting for transfers between devices, on_device(): ts = lax.all_to_all(spread, PLANE, 0, 0, tiled=True).reshape(pooled, width)  9.23 us
    unnamed x19, local copies, waits for them, and re-layouts  8.51 us
    all_to_all x1, starting transfers between devices, on_device(): ts = lax.all_to_all(spread, PLANE, 0, 0, tiled=True).reshape(pooled, width)  7.39 us
    all_to_all x1, starting transfers between devices, on_device(): lax.all_to_all(dy.reshape(n_plane, rows, width), PLANE, 0, 0, tiled=True)  5.79 us
  transfers between devices with their start and end apart: 18, of which 13 were waited for; matrix products, arithmetic and copies ran while one was open for 6% of the time, Pallas kernels for 0%

profile of v3, /device:TPU:8, one launch (start us, length us, event | category | flops | bytes accessed | tf_op | source)
XLA Modules:
  0.0 122.2 jit_solution(15589690466235231543)
XLA Ops:
  1.6 3.3 %shard_map.59 = bf16[16,64,1152]{2,1,0:T(8,128)(2,1)S(1)} custom-call(f32[64,1152]{1,0:T(8,128)S(1)} %copy-done.3), custom_call_target="tpu_custom_call" | custom-call | bytes 1048576 | tf_op jit(solution)/shard_map/pallas_call | solution.py:106
  6.6 2.0 %collective-permute-start = (bf16[64,1152]{1,0:T(8,128)(2,1)S(1)}, bf16[64,1152]{1,0:T(8,128)(2,1)S(1)}, u32[]{:S(2)}, u32[]{:S(2)}) collective-permute-start(bf16[64,1152]{1,0:T(8,128)(2,1)S(1)} %shard_map.60), channel_id=1, source_target_pairs={{0,1},{1,2},{2,3},{3,4},{4,5},{5,6},{6,7},{7,0},{8,9},{9,10},{10,1... | collective-permute-start | bytes 442376 | tf_op jit(solution)/shard_map/ppermute | solution.py:19
  8.5 4.0 %collective-permute-start.1 = (bf16[64,1152]{1,0:T(8,128)(2,1)S(1)}, bf16[64,1152]{1,0:T(8,128)(2,1)S(1)}, u32[]{:S(2)}, u32[]{:S(2)}) collective-permute-start(bf16[64,1152]{1,0:T(8,128)(2,1)S(1)} %shard_map.60), channel_id=1, source_target_pairs={{0,7},{1,0},{2,1},{3,2},{4,3},{5,4},{6,5},{7,6},{8,15},{9,8},{10,9... | collective-permute-start | bytes 442376 | tf_op jit(solution)/shard_map/ppermute | solution.py:19
  12.6 7.4 %all-to-all-start = ((bf16[16,64,1152]{2,1,0:T(8,128)(2,1)}), bf16[16,64,1152]{2,1,0:T(8,128)(2,1)S(1)}, u32[]{:S(2)}, u32[]{:S(2)}) async-start(bf16[16,64,1152]{2,1,0:T(8,128)(2,1)} %copy-done), calls=%async_computation | async-start | bytes 4718592 | tf_op jit(solution)/shard_map/all_to_all | solution.py:146
  21.3 3.2 %collective-permute-start.3 = (bf16[64,1152]{1,0:T(8,128)(2,1)S(1)}, bf16[64,1152]{1,0:T(8,128)(2,1)S(1)}, u32[]{:S(2)}, u32[]{:S(2)}) collective-permute-start(bf16[64,1152]{1,0:T(8,128)(2,1)S(1)} %collective-permute-done.1), channel_id=1, source_target_pairs={{0,7},{1,0},{2,1},{3,2},{4,3},{5,4},{6,5},{7,6},{8,15},{9,8},{10,9... | collective-permute-start | bytes 442376 | tf_op jit(solution)/shard_map/ppermute | solution.py:19
  25.2 1.8 %collective-permute-done.2 = bf16[64,1152]{1,0:T(8,128)(2,1)S(1)} collective-permute-done((bf16[64,1152]{1,0:T(8,128)(2,1)S(1)}, bf16[64,1152]{1,0:T(8,128)(2,1)S(1)}, u32[]{:S(2)}, u32[]{:S(2)}) %collective-permute-start.2) | collective-permute-done | bytes 147488 | tf_op jit(solution)/shard_map/ppermute | solution.py:19
  27.7 3.2 %collective-permute-start.5 = (bf16[64,1152]{1,0:T(8,128)(2,1)S(1)}, bf16[64,1152]{1,0:T(8,128)(2,1)S(1)}, u32[]{:S(2)}, u32[]{:S(2)}) collective-permute-start(bf16[64,1152]{1,0:T(8,128)(2,1)S(1)} %collective-permute-done.3), channel_id=1, source_target_pairs={{0,7},{1,0},{2,1},{3,2},{4,3},{5,4},{6,5},{7,6},{8,15},{9,8},{10,9... | collective-permute-start | bytes 442376 | tf_op jit(solution)/shard_map/ppermute | solution.py:19
  31.6 1.8 %collective-permute-done.4 = bf16[64,1152]{1,0:T(8,128)(2,1)S(1)} collective-permute-done((bf16[64,1152]{1,0:T(8,128)(2,1)S(1)}, bf16[64,1152]{1,0:T(8,128)(2,1)S(1)}, u32[]{:S(2)}, u32[]{:S(2)}) %collective-permute-start.4) | collective-permute-done | bytes 147488 | tf_op jit(solution)/shard_map/ppermute | solution.py:19
  34.7 5.0 %collective-permute-done.6 = bf16[64,1152]{1,0:T(8,128)(2,1)S(1)} collective-permute-done((bf16[64,1152]{1,0:T(8,128)(2,1)S(1)}, bf16[64,1152]{1,0:T(8,128)(2,1)S(1)}, u32[]{:S(2)}, u32[]{:S(2)}) %collective-permute-start.6) | collective-permute-done | bytes 147488 | tf_op jit(solution)/shard_map/ppermute | solution.py:19
  41.8 1.6 %collective-permute-done.7.xo = bf16[512,1152]{1,0:T(8,128)(2,1)S(1)} collective-permute-done((bf16[512,1152]{1,0:T(8,128)(2,1)}, bf16[512,1152]{1,0:T(8,128)(2,1)S(1)}, u32[]{:S(2)}, u32[]{:S(2)}) %collective-permute-start.7) | collective-permute-done | bytes 1179680 | tf_op jit(solution)/shard_map/ppermute | solution.py:19
  43.4 9.2 %all-to-all-done = bf16[16,64,1152]{2,1,0:T(8,128)(2,1)S(1)} async-done(((bf16[16,64,1152]{2,1,0:T(8,128)(2,1)}), bf16[16,64,1152]{2,1,0:T(8,128)(2,1)S(1)}, u32[]{:S(2)}, u32[]{:S(2)}) %all-to-all-start) | async-done | bytes 2359328 | tf_op jit(solution)/shard_map/all_to_all | solution.py:146
  52.6 8.2 %shard_map.61 = (bf16[1024,1024]{1,0:T(8,128)(2,1)S(1)}, bf16[1024,1152]{1,0:T(8,128)(2,1)S(1)}) custom-call(s32[1]{0:T(128)} %bitcast.1.place, f32[2]{0:T(128)S(1)} %pad_maximum_fusion.scal, bf16[512,1152]{1,0:T(8,128)(2,1)} %constant_dynamic-update-slice_fusion.xs, bf16[512,1152]{1,0:T(8,128)(2,1)S(1)} %collective-permute-done.7.xo, ...), custom_call_target="tpu_custom_call" | custom-call | flops 4831838208 | bytes 9437184 | tf_op jit(solution)/shard_map/pallas_call | solution.py:106
  63.9 2.8 %collective-permute-done.8.other = bf16[512,1152]{1,0:T(8,128)(2,1)S(1)} collective-permute-done((bf16[512,1152]{1,0:T(8,128)(2,1)S(1)}, bf16[512,1152]{1,0:T(8,128)(2,1)S(1)}, u32[]{:S(2)}, u32[]{:S(2)}) %collective-permute-start.8) | collective-permute-done | bytes 1179680 | tf_op jit(solution)/shard_map/ppermute | solution.py:19
  66.7 1.6 %shard_map.63 = bf16[512,1152]{1,0:T(8,128)(2,1)S(1)} custom-call(bf16[1024,1024]{1,0:T(8,128)(2,1)S(1)} %get-tuple-element.8.coeff, bf16[1024,1152]{1,0:T(8,128)(2,1)S(1)} %bitcast.6, bf16[512,1152]{1,0:T(8,128)(2,1)S(1)} %collective-permute-done.8.other), custom_call_target="tpu_custom_call" | custom-call | flops 1207959552 | bytes 6291456 | tf_op jit(solution)/shard_map/pallas_call | solution.py:106
  68.4 7.1 %collective-permute-done.9 = bf16[64,1152]{1,0:T(8,128)(2,1)S(1)} collective-permute-done((bf16[64,1152]{1,0:T(8,128)(2,1)S(1)}, bf16[64,1152]{1,0:T(8,128)(2,1)S(1)}, u32[]{:S(2)}, u32[]{:S(2)}) %collective-permute-start.9) | collective-permute-done | bytes 147488 | tf_op jit(solution)/shard_map/ppermute | solution.py:19
  75.6 3.2 %collective-permute-start.13 = (bf16[64,1152]{1,0:T(8,128)(2,1)S(1)}, bf16[64,1152]{1,0:T(8,128)(2,1)S(1)}, u32[]{:S(2)}, u32[]{:S(2)}) collective-permute-start(bf16[64,1152]{1,0:T(8,128)(2,1)S(1)} %get-tuple-element.13), channel_id=1, source_target_pairs={{0,7},{1,0},{2,1},{3,2},{4,3},{5,4},{6,5},{7,6},{8,15},{9,8},{10,9... | collective-permute-start | bytes 442376 | tf_op jit(solution)/shard_map/ppermute | solution.py:19
  78.9 3.1 %collective-permute-done.10 = bf16[64,1152]{1,0:T(8,128)(2,1)S(1)} collective-permute-done((bf16[64,1152]{1,0:T(8,128)(2,1)S(1)}, bf16[64,1152]{1,0:T(8,128)(2,1)S(1)}, u32[]{:S(2)}, u32[]{:S(2)}) %collective-permute-start.10) | collective-permute-done | bytes 147488 | tf_op jit(solution)/shard_map/ppermute | solution.py:19
  82.1 5.8 %all-to-all-start.1 = ((bf16[16,64,1152]{2,1,0:T(8,128)(2,1)}), bf16[16,64,1152]{2,1,0:T(8,128)(2,1)}, u32[]{:S(2)}, u32[]{:S(2)}) async-start(bf16[16,64,1152]{2,1,0:T(8,128)(2,1)} %bitcast.7), calls=%async_computation.1 | async-start | bytes 4718592 | tf_op jit(solution)/shard_map/all_to_all | solution.py:160
  88.5 2.9 %collective-permute-start.14 = (bf16[64,1152]{1,0:T(8,128)(2,1)S(1)}, bf16[64,1152]{1,0:T(8,128)(2,1)S(1)}, u32[]{:S(2)}, u32[]{:S(2)}) collective-permute-start(bf16[64,1152]{1,0:T(8,128)(2,1)S(1)} %get-tuple-element.11), channel_id=1, source_target_pairs={{0,7},{1,0},{2,1},{3,2},{4,3},{5,4},{6,5},{7,6},{8,15},{9,8},{10,9... | collective-permute-start | bytes 442376 | tf_op jit(solution)/shard_map/ppermute | solution.py:19
  91.6 2.5 %collective-permute-done.14 = bf16[64,1152]{1,0:T(8,128)(2,1)S(1)} collective-permute-done((bf16[64,1152]{1,0:T(8,128)(2,1)S(1)}, bf16[64,1152]{1,0:T(8,128)(2,1)S(1)}, u32[]{:S(2)}, u32[]{:S(2)}) %collective-permute-start.14) | collective-permute-done | bytes 147488 | tf_op jit(solution)/shard_map/ppermute | solution.py:19
  94.1 3.8 %collective-permute-start.15 = (bf16[64,1152]{1,0:T(8,128)(2,1)S(1)}, bf16[64,1152]{1,0:T(8,128)(2,1)S(1)}, u32[]{:S(2)}, u32[]{:S(2)}) collective-permute-start(bf16[64,1152]{1,0:T(8,128)(2,1)S(1)} %add_convert_fusion), channel_id=1, source_target_pairs={{0,7},{1,0},{2,1},{3,2},{4,3},{5,4},{6,5},{7,6},{8,15},{9,8},{10,9... | collective-permute-start | bytes 442376 | tf_op jit(solution)/shard_map/ppermute | solution.py:19
  98.0 2.6 %collective-permute-done.15 = bf16[64,1152]{1,0:T(8,128)(2,1)S(1)} collective-permute-done((bf16[64,1152]{1,0:T(8,128)(2,1)S(1)}, bf16[64,1152]{1,0:T(8,128)(2,1)S(1)}, u32[]{:S(2)}, u32[]{:S(2)}) %collective-permute-start.15) | collective-permute-done | bytes 147488 | tf_op jit(solution)/shard_map/ppermute | solution.py:19
  101.6 17.5 %all-to-all-done.1 = bf16[16,64,1152]{2,1,0:T(8,128)(2,1)} async-done(((bf16[16,64,1152]{2,1,0:T(8,128)(2,1)}), bf16[16,64,1152]{2,1,0:T(8,128)(2,1)}, u32[]{:S(2)}, u32[]{:S(2)}) %all-to-all-start.1) | async-done | bytes 2359328 | tf_op jit(solution)/shard_map/all_to_all | solution.py:160
  119.1 2.0 %convert_reduce_fusion = f32[64,1152]{1,0:T(8,128)S(1)} fusion(bf16[16,64,1152]{2,1,0:T(8,128)(2,1)} %all-to-all-done.1), kind=kLoop, calls=%fused_computation | loop fusion | flops 2285568 | bytes 2654208 | tf_op jit(solution)/shard_map/reduce_sum | solution.py:165
  (52 shorter events, 14.4 us)
Async XLA Ops:
  0.6 5.8 %copy-start.1 = (f32[64,1152]{1,0:T(8,128)S(1)}, f32[64,1152]{1,0:T(8,128)}, u32[]{:S(2)}) copy-start(f32[64,1152]{1,0:T(8,128)} %raw.2) | copy-start | bytes 884740
  0.6 1.0 copy-start.3
  5.0 1.4 %copy-start = (bf16[16,64,1152]{2,1,0:T(8,128)(2,1)}, bf16[16,64,1152]{2,1,0:T(8,128)(2,1)S(1)}, u32[]{:S(2)}) copy-start(bf16[16,64,1152]{2,1,0:T(8,128)(2,1)S(1)} %shard_map.59) | copy-start | bytes 7077892
  6.6 14.1 %collective-permute-start = (bf16[64,1152]{1,0:T(8,128)(2,1)S(1)}, bf16[64,1152]{1,0:T(8,128)(2,1)S(1)}, u32[]{:S(2)}, u32[]{:S(2)}) collective-permute-start(bf16[64,1152]{1,0:T(8,128)(2,1)S(1)} %shard_map.60), channel_id=1, source_target_pairs={{0,1},{1,2},{2,3},{3,4},{4,5},{5,6},{6,7},{7,0},{8,9},{9,10},{10,1... | collective-permute-start | bytes 442376 | tf_op jit(solution)/shard_map/ppermute | solution.py:19
  8.5 12.8 %collective-permute-start.1 = (bf16[64,1152]{1,0:T(8,128)(2,1)S(1)}, bf16[64,1152]{1,0:T(8,128)(2,1)S(1)}, u32[]{:S(2)}, u32[]{:S(2)}) collective-permute-start(bf16[64,1152]{1,0:T(8,128)(2,1)S(1)} %shard_map.60), channel_id=1, source_target_pairs={{0,7},{1,0},{2,1},{3,2},{4,3},{5,4},{6,5},{7,6},{8,15},{9,8},{10,9... | collective-permute-start | bytes 442376 | tf_op jit(solution)/shard_map/ppermute | solution.py:19
  12.6 40.1 %all-to-all-start = ((bf16[16,64,1152]{2,1,0:T(8,128)(2,1)}), bf16[16,64,1152]{2,1,0:T(8,128)(2,1)S(1)}, u32[]{:S(2)}, u32[]{:S(2)}) async-start(bf16[16,64,1152]{2,1,0:T(8,128)(2,1)} %copy-done), calls=%async_computation | async-start | bytes 4718592 | tf_op jit(solution)/shard_map/all_to_all | solution.py:146
  20.6 6.4 %collective-permute-start.2 = (bf16[64,1152]{1,0:T(8,128)(2,1)S(1)}, bf16[64,1152]{1,0:T(8,128)(2,1)S(1)}, u32[]{:S(2)}, u32[]{:S(2)}) collective-permute-start(bf16[64,1152]{1,0:T(8,128)(2,1)S(1)} %collective-permute-done), channel_id=1, source_target_pairs={{0,1},{1,2},{2,3},{3,4},{4,5},{5,6},{6,7},{7,0},{8,9},{9,10},{10,1... | collective-permute-start | bytes 442376 | tf_op jit(solution)/shard_map/ppermute | solution.py:19
  21.3 6.4 %collective-permute-start.3 = (bf16[64,1152]{1,0:T(8,128)(2,1)S(1)}, bf16[64,1152]{1,0:T(8,128)(2,1)S(1)}, u32[]{:S(2)}, u32[]{:S(2)}) collective-permute-start(bf16[64,1152]{1,0:T(8,128)(2,1)S(1)} %collective-permute-done.1), channel_id=1, source_target_pairs={{0,7},{1,0},{2,1},{3,2},{4,3},{5,4},{6,5},{7,6},{8,15},{9,8},{10,9... | collective-permute-start | bytes 442376 | tf_op jit(solution)/shard_map/ppermute | solution.py:19
  27.0 6.4 %collective-permute-start.4 = (bf16[64,1152]{1,0:T(8,128)(2,1)S(1)}, bf16[64,1152]{1,0:T(8,128)(2,1)S(1)}, u32[]{:S(2)}, u32[]{:S(2)}) collective-permute-start(bf16[64,1152]{1,0:T(8,128)(2,1)S(1)} %collective-permute-done.2), channel_id=1, source_target_pairs={{0,1},{1,2},{2,3},{3,4},{4,5},{5,6},{6,7},{7,0},{8,9},{9,10},{10,1... | collective-permute-start | bytes 442376 | tf_op jit(solution)/shard_map/ppermute | solution.py:19
  27.7 6.3 %collective-permute-start.5 = (bf16[64,1152]{1,0:T(8,128)(2,1)S(1)}, bf16[64,1152]{1,0:T(8,128)(2,1)S(1)}, u32[]{:S(2)}, u32[]{:S(2)}) collective-permute-start(bf16[64,1152]{1,0:T(8,128)(2,1)S(1)} %collective-permute-done.3), channel_id=1, source_target_pairs={{0,7},{1,0},{2,1},{3,2},{4,3},{5,4},{6,5},{7,6},{8,15},{9,8},{10,9... | collective-permute-start | bytes 442376 | tf_op jit(solution)/shard_map/ppermute | solution.py:19
  33.3 6.4 %collective-permute-start.6 = (bf16[64,1152]{1,0:T(8,128)(2,1)S(1)}, bf16[64,1152]{1,0:T(8,128)(2,1)S(1)}, u32[]{:S(2)}, u32[]{:S(2)}) collective-permute-start(bf16[64,1152]{1,0:T(8,128)(2,1)S(1)} %collective-permute-done.4), channel_id=1, source_target_pairs={{0,1},{1,2},{2,3},{3,4},{4,5},{5,6},{6,7},{7,0},{8,9},{9,10},{10,1... | collective-permute-start | bytes 442376 | tf_op jit(solution)/shard_map/ppermute | solution.py:19
  40.3 3.1 %collective-permute-start.7 = (bf16[512,1152]{1,0:T(8,128)(2,1)}, bf16[512,1152]{1,0:T(8,128)(2,1)S(1)}, u32[]{:S(2)}, u32[]{:S(2)}) collective-permute-start(bf16[512,1152]{1,0:T(8,128)(2,1)} %constant_dynamic-update-slice_fusion.xs), channel_id=1, source_target_pairs={{0,16},{16,0},{1,17},{17,1},{2,18},{18,2},{3,19},{19,3},{4,20},{20... | collective-permute-start | bytes 3538952 | tf_op jit(solution)/shard_map/ppermute | solution.py:19
  60.8 1.4 %copy-start.5 = (bf16[1024,1152]{1,0:T(8,128)(2,1)}, bf16[1024,1152]{1,0:T(8,128)(2,1)S(1)}, u32[]{:S(2)}) copy-start(bf16[1024,1152]{1,0:T(8,128)(2,1)S(1)} %get-tuple-element.9) | copy-start | bytes 7077892
  63.8 2.9 %collective-permute-start.8 = (bf16[512,1152]{1,0:T(8,128)(2,1)S(1)}, bf16[512,1152]{1,0:T(8,128)(2,1)S(1)}, u32[]{:S(2)}, u32[]{:S(2)}) collective-permute-start(bf16[512,1152]{1,0:T(8,128)(2,1)S(1)} %shard_map.62), channel_id=1, source_target_pairs={{0,16},{16,0},{1,17},{17,1},{2,18},{18,2},{3,19},{19,3},{4,20},{20... | collective-permute-start | bytes 3538952 | tf_op jit(solution)/shard_map/ppermute | solution.py:19
  68.3 7.2 %collective-permute-start.9 = (bf16[64,1152]{1,0:T(8,128)(2,1)S(1)}, bf16[64,1152]{1,0:T(8,128)(2,1)S(1)}, u32[]{:S(2)}, u32[]{:S(2)}) collective-permute-start(bf16[64,1152]{1,0:T(8,128)(2,1)S(1)} %get-tuple-element.12), channel_id=1, source_target_pairs={{0,1},{1,2},{2,3},{3,4},{4,5},{5,6},{6,7},{7,0},{8,9},{9,10},{10,1... | collective-permute-start | bytes 442376 | tf_op jit(solution)/shard_map/ppermute | solution.py:19
  75.5 6.4 %collective-permute-start.10 = (bf16[64,1152]{1,0:T(8,128)(2,1)S(1)}, bf16[64,1152]{1,0:T(8,128)(2,1)S(1)}, u32[]{:S(2)}, u32[]{:S(2)}) collective-permute-start(bf16[64,1152]{1,0:T(8,128)(2,1)S(1)} %add_convert_fusion.4), channel_id=1, source_target_pairs={{0,1},{1,2},{2,3},{3,4},{4,5},{5,6},{6,7},{7,0},{8,9},{9,10},{10,1... | collective-permute-start | bytes 442376 | tf_op jit(solution)/shard_map/ppermute | solution.py:19
  75.6 12.4 %collective-permute-start.13 = (bf16[64,1152]{1,0:T(8,128)(2,1)S(1)}, bf16[64,1152]{1,0:T(8,128)(2,1)S(1)}, u32[]{:S(2)}, u32[]{:S(2)}) collective-permute-start(bf16[64,1152]{1,0:T(8,128)(2,1)S(1)} %get-tuple-element.13), channel_id=1, source_target_pairs={{0,7},{1,0},{2,1},{3,2},{4,3},{5,4},{6,5},{7,6},{8,15},{9,8},{10,9... | collective-permute-start | bytes 442376 | tf_op jit(solution)/shard_map/ppermute | solution.py:19
  82.0 6.4 %collective-permute-start.11 = (bf16[64,1152]{1,0:T(8,128)(2,1)S(1)}, bf16[64,1152]{1,0:T(8,128)(2,1)S(1)}, u32[]{:S(2)}, u32[]{:S(2)}) collective-permute-start(bf16[64,1152]{1,0:T(8,128)(2,1)S(1)} %add_convert_fusion.3), channel_id=1, source_target_pairs={{0,1},{1,2},{2,3},{3,4},{4,5},{5,6},{6,7},{7,0},{8,9},{9,10},{10,1... | collective-permute-start | bytes 442376 | tf_op jit(solution)/shard_map/ppermute | solution.py:19
  82.1 5.8 %copy-start.2 = (f32[64,1152]{1,0:T(8,128)S(1)}, f32[64,1152]{1,0:T(8,128)}, u32[]{:S(2)}) copy-start(f32[64,1152]{1,0:T(8,128)} %raw.2) | copy-start | bytes 884740
  82.1 37.0 %all-to-all-start.1 = ((bf16[16,64,1152]{2,1,0:T(8,128)(2,1)}), bf16[16,64,1152]{2,1,0:T(8,128)(2,1)}, u32[]{:S(2)}, u32[]{:S(2)}) async-start(bf16[16,64,1152]{2,1,0:T(8,128)(2,1)} %bitcast.7), calls=%async_computation.1 | async-start | bytes 4718592 | tf_op jit(solution)/shard_map/all_to_all | solution.py:160
  87.9 3.5 %copy-start.4 = (f32[64,1152]{1,0:T(8,128)S(1)}, f32[64,1152]{1,0:T(8,128)}, u32[]{:S(2)}) copy-start(f32[64,1152]{1,0:T(8,128)} %raw.1) | copy-start | bytes 884740
  88.5 5.6 %collective-permute-start.14 = (bf16[64,1152]{1,0:T(8,128)(2,1)S(1)}, bf16[64,1152]{1,0:T(8,128)(2,1)S(1)}, u32[]{:S(2)}, u32[]{:S(2)}) collective-permute-start(bf16[64,1152]{1,0:T(8,128)(2,1)S(1)} %get-tuple-element.11), channel_id=1, source_target_pairs={{0,7},{1,0},{2,1},{3,2},{4,3},{5,4},{6,5},{7,6},{8,15},{9,8},{10,9... | collective-permute-start | bytes 442376 | tf_op jit(solution)/shard_map/ppermute | solution.py:19
  91.5 6.4 %collective-permute-start.12 = (bf16[64,1152]{1,0:T(8,128)(2,1)S(1)}, bf16[64,1152]{1,0:T(8,128)(2,1)S(1)}, u32[]{:S(2)}, u32[]{:S(2)}) collective-permute-start(bf16[64,1152]{1,0:T(8,128)(2,1)S(1)} %get-tuple-element.10), channel_id=1, source_target_pairs={{0,1},{1,2},{2,3},{3,4},{4,5},{5,6},{6,7},{7,0},{8,9},{9,10},{10,1... | collective-permute-start | bytes 442376 | tf_op jit(solution)/shard_map/ppermute | solution.py:19
  94.1 6.4 %collective-permute-start.15 = (bf16[64,1152]{1,0:T(8,128)(2,1)S(1)}, bf16[64,1152]{1,0:T(8,128)(2,1)S(1)}, u32[]{:S(2)}, u32[]{:S(2)}) collective-permute-start(bf16[64,1152]{1,0:T(8,128)(2,1)S(1)} %add_convert_fusion), channel_id=1, source_target_pairs={{0,7},{1,0},{2,1},{3,2},{4,3},{5,4},{6,5},{7,6},{8,15},{9,8},{10,9... | collective-permute-start | bytes 442376 | tf_op jit(solution)/shard_map/ppermute | solution.py:19

commit v4 on v3

v4 whole, which is shorter than its diff:
```python
import jax
import jax.numpy as jnp
from jax import lax
from jax.experimental import pallas as pl
from jax.experimental.pallas import tpu as pltpu
from jax.sharding import Mesh, PartitionSpec as P

AXES = ("yh", "x", "core", "yl", "z")
PLANE = ("yh", "x", "yl")
BF = jnp.bfloat16
F32 = jnp.float32
ROWS = 64
NT = (((1,), (1,)), ((), ()))
TN = (((0,), (0,)), ((), ()))


def shifted(block, axis, distance):
    n = lax.axis_size(axis)
    return lax.ppermute(block, axis, [(i, (i + distance) % n) for i in range(n)])


def to_unit(raw):
    norm = jnp.sqrt(jnp.sum(raw * raw, axis=1, keepdims=True) + 1e-06)
    return (raw / norm, norm)


def from_unit(grad, unit, norm):
    return (grad - unit * jnp.sum(unit * grad, axis=1, keepdims=True)) / norm


def unit_rows(raw):
    norm = jnp.sqrt(jnp.sum(raw * raw, axis=1, keepdims=True) + 1e-06)
    return (raw / norm).astype(BF)


def spread_kernel(raw, out):
    unit = unit_rows(raw[...])
    for k in range(out.shape[0]):
        out[k] = unit


def unit_kernel(raw, out):
    out[...] = unit_rows(raw[...])


def text_kernel(place, scal, xs, ts, coeff, dy, part, sems):
    temp = scal[0]
    offset = scal[1]
    pooled = ts.shape[0]
    step = pooled // sems.shape[0]
    for j in range(pooled // step):
        sl = pl.ds(j * step, step)
        dots = lax.dot_general(ts[sl], xs[...], NT, preferred_element_type=F32)
        coeff[sl] = jax.nn.sigmoid(temp * dots + offset).astype(BF)
    at = pl.multiple_of(place[0] * ROWS, ROWS)
    wide = pl.multiple_of(place[1] // 2 * 2 * ROWS, 2 * ROWS)
    dots = lax.dot_general(ts[pl.ds(at, ROWS)], xs[pl.ds(wide, 2 * ROWS)], NT, preferred_element_type=F32)
    row = lax.broadcasted_iota(jnp.int32, dots.shape, 0) + place[1] % 2 * ROWS
    eye = row == lax.broadcasted_iota(jnp.int32, dots.shape, 1)
    own = jax.nn.sigmoid(temp * dots + offset) - eye.astype(F32)
    coeff[pl.ds(at, ROWS), pl.ds(wide, 2 * ROWS)] = own.astype(BF)
    copies = []
    for j in range(pooled // step):
        sl = pl.ds(j * step, step)
        part[sl] = jnp.dot(coeff[sl], xs[...], preferred_element_type=F32).astype(BF)
        copies.append(pltpu.make_async_copy(part.at[sl], dy.at[sl], sems.at[j]))
        copies[-1].start()
    for copy in copies:
        copy.wait()


def other_kernel(place, coeff, ts, dxo):
    half = dxo.shape[0]
    cols = pl.ds(pl.multiple_of((1 - place[2]) * half, half), half)
    part = lax.dot_general(coeff[:, cols], ts[...], TN, preferred_element_type=F32)
    dxo[...] = part.astype(BF)


def image_kernel(place, coeff, ts, other, dxs):
    half = dxs.shape[0]
    cols = pl.ds(pl.multiple_of(place[2] * half, half), half)
    part = lax.dot_general(coeff[:, cols], ts[...], TN, preferred_element_type=F32)
    part = (part + other[...].astype(F32)).astype(BF)
    n = half // ROWS
    for k in range(n):
        at = pl.multiple_of((k + n - place[3]) % n * ROWS, ROWS)
        dxs[pl.ds(at, ROWS)] = part[k * ROWS : (k + 1) * ROWS]


VMEM = pl.BlockSpec(memory_space=pltpu.VMEM)
SMEM = pl.BlockSpec(memory_space=pltpu.SMEM)
HBM = pl.BlockSpec(memory_space=pltpu.HBM)


def local(kernel, outs, args, smem=0, scratch=(), flops=0, nbytes=2**20, trans=0):
    return pl.pallas_call(
        kernel,
        out_shape=tuple((pltpu.HBM if spec is HBM else jax.ShapeDtypeStruct)(shape, BF) for shape, spec in outs),
        in_specs=[SMEM] * smem + [VMEM] * (len(args) - smem),
        out_specs=tuple(spec for _, spec in outs),
        scratch_shapes=list(scratch),
        compiler_params=pltpu.CompilerParams(vmem_limit_bytes=40 * 2**20),
        cost_estimate=pl.CostEstimate(flops=flops, bytes_accessed=nbytes, transcendentals=trans),
    )(*args)


def direct_reduce(parts):
    total = parts[0].astype(F32)
    for got in [shifted(parts[k], "z", k) for k in (4, 3, 5, 2, 6, 1, 7)]:
        total = total + got.astype(F32)
    return total


def on_device(images, texts, log_temp, bias):
    temp = jnp.exp(log_temp[0])
    rows, width = images.shape
    n_plane = lax.axis_size(PLANE)
    half = ROWS * lax.axis_size("z")
    pooled = ROWS * n_plane
    (x,) = local(unit_kernel, [((rows, width), VMEM)], [images])
    (spread,) = local(spread_kernel, [((n_plane, rows, width), VMEM)], [texts])
    xs = lax.all_gather(x, ("core", "z"), axis=0, tiled=True)
    ts = lax.all_to_all(spread, PLANE, 0, 0, tiled=True).reshape(pooled, width)
    img_unit, img_norm = to_unit(images)
    txt_unit, txt_norm = to_unit(texts)
    place = jnp.stack([lax.axis_index(a).astype(jnp.int32) for a in (PLANE, ("core", "z"), "core", "z")])
    scal = jnp.stack([temp, bias[0]])
    unit_flops = 2 * half * pooled * width
    coeff, dy = local(
        text_kernel, [((pooled, 2 * half), VMEM), ((pooled, width), HBM)], [place, scal, xs, ts], smem=2,
        scratch=[pltpu.VMEM((pooled, width), BF), pltpu.SemaphoreType.DMA((4,))],
        flops=4 * unit_flops, nbytes=9 * 2**20, trans=4 * half * pooled,
    )
    dyr = lax.all_to_all(dy.reshape(n_plane, rows, width), PLANE, 0, 0, tiled=True)
    (dxo,) = local(
        other_kernel, [((half, width), VMEM)], [place, coeff, ts], smem=1, flops=unit_flops, nbytes=5 * 2**20
    )
    other = shifted(dxo, "core", 1)
    (mine,) = local(
        image_kernel, [((half, width), VMEM)], [place, coeff, ts, other], smem=1, flops=unit_flops, nbytes=6 * 2**20
    )
    image_sum = direct_reduce(mine.reshape(-1, rows, width))
    text_sum = jnp.sum(dyr.astype(F32), axis=0)
    grad_images = from_unit(temp * image_sum, img_unit, img_norm)
    grad_texts = from_unit(temp * text_sum, txt_unit, txt_norm)
    return (grad_images, grad_texts)


def solution(mesh):
    fine = Mesh(mesh.devices.reshape(2, 4, 2, 2, 8), AXES)
    split = P(AXES, None)
    return jax.shard_map(
        on_device,
        mesh=fine,
        in_specs=(split, split, P(), P()),
        out_specs=(split, split),
        check_vma=False,
    )
```

time: 123 us -> 122 us (level)
  between operations: 2.14 us -> 15.5 us
  starting transfers between devices: 36 us -> 29.5 us
  waiting for transfers between devices: 55.5 us -> 50.4 us
  local copies, waits for them, and re-layouts: 9.18 us -> 6.66 us
    all_to_all x1, waiting for transfers between devices: 9.23 us -> 31.5 us  [on_device(): ts = lax.all_to_all(spread, PLANE, 0, 0, tiled=True).reshape(pooled, width)]
    all_to_all x1, waiting for transfers between devices: 17.5 us -> 0.01 us  [on_device(): lax.all_to_all(dy.reshape(n_plane, rows, width), PLANE, 0, 0, tiled=True)]
    ppermute x16 -> x8, waiting for transfers between devices: 28.8 us -> 17.6 us  [shifted(): lax.ppermute(block, axis, [(i, (i + distance) % n) for i in range(n)])]
    ppermute x16 -> x8, starting transfers between devices: 22.8 us -> 14.6 us  [shifted(): lax.ppermute(block, axis, [(i, (i + distance) % n) for i in range(n)])]
    unnamed x19 -> x16, local copies, waits for them, and re-layouts: 8.51 us -> 6.57 us
    all_to_all x1, starting transfers between devices: 5.79 us -> 7.39 us  [on_device(): lax.all_to_all(dy.reshape(n_plane, rows, width), PLANE, 0, 0, tiled=True)]
    all_gather x0 -> x1, waiting for transfers between devices: none -> 1.3 us  [on_device(): xs = lax.all_gather(x, ('core', 'z'), axis=0, tiled=True)]
  transfers between devices with their start and end apart: 18 -> 11, of which waited for: 13 -> 7; matrix products, arithmetic and copies ran while one was open for 6% -> 1% of each run, Pallas kernels for 0% -> 3%
where the time goes in v4:
time: 122 us; the launch traced here: 121 us
  waiting for transfers between devices  50.4 us (41%)
  starting transfers between devices  29.5 us (24%)
  between operations  15.5 us (13%)
  Pallas kernels  14.6 us (12%)
  local copies, waits for them, and re-layouts  6.66 us (5%)
  other arithmetic  4.59 us (4%)
    all_to_all x1, waiting for transfers between devices, on_device(): ts = lax.all_to_all(spread, PLANE, 0, 0, tiled=True).reshape(pooled, width)  31.5 us
    ppermute x8, waiting for transfers between devices, shifted(): lax.ppermute(block, axis, [(i, (i + distance) % n) for i in range(n)])  17.6 us
    ppermute x8, starting transfers between devices, shifted(): lax.ppermute(block, axis, [(i, (i + distance) % n) for i in range(n)])  14.6 us
    pallas_call x5, Pallas kernels, local(): pl.pallas_call(kernel, out_shape=tuple(((pltpu.HBM if spec is HBM else ja...  14.6 us
    all_to_all x1, starting transfers between devices, on_device(): ts = lax.all_to_all(spread, PLANE, 0, 0, tiled=True).reshape(pooled, width)  7.39 us
    all_to_all x1, starting transfers between devices, on_device(): lax.all_to_all(dy.reshape(n_plane, rows, width), PLANE, 0, 0, tiled=True)  7.39 us
    unnamed x16, local copies, waits for them, and re-layouts  6.57 us
  transfers between devices with their start and end apart: 11, of which 7 were waited for; matrix products, arithmetic and copies ran while one was open for 1% of the time, Pallas kernels for 3%

profile of v4, /device:TPU:8, one launch (start us, length us, event | category | flops | bytes accessed | tf_op | source)
XLA Modules:
  0.0 121.1 jit_solution(16909443638568655144)
XLA Ops:
  7.2 1.0 copy-done.3
  9.0 1.0 copy-done.5
  10.2 1.4 %copy-done = bf16[16,64,1152]{2,1,0:T(8,128)(2,1)} copy-done((bf16[16,64,1152]{2,1,0:T(8,128)(2,1)}, bf16[16,64,1152]{2,1,0:T(8,128)(2,1)S(1)}, u32[]{:S(2)}) %copy-start) | copy-done | bytes 2359320
  11.6 7.4 %all-to-all-start = ((bf16[16,64,1152]{2,1,0:T(8,128)(2,1)}), bf16[16,64,1152]{2,1,0:T(8,128)(2,1)S(1)}, u32[]{:S(2)}, u32[]{:S(2)}) async-start(bf16[16,64,1152]{2,1,0:T(8,128)(2,1)} %copy-done), calls=%async_computation | async-start | bytes 4718592 | tf_op jit(solution)/shard_map/all_to_all | solution.py:123
  20.5 31.5 %all-to-all-done = bf16[16,64,1152]{2,1,0:T(8,128)(2,1)S(1)} async-done(((bf16[16,64,1152]{2,1,0:T(8,128)(2,1)}), bf16[16,64,1152]{2,1,0:T(8,128)(2,1)S(1)}, u32[]{:S(2)}, u32[]{:S(2)}) %all-to-all-start) | async-done | bytes 2359328 | tf_op jit(solution)/shard_map/all_to_all | solution.py:123
  52.0 1.3 %all-gather.2.cloned.1.call-done.xs = bf16[1024,1152]{1,0:T(8,128)(2,1)} async-done(((bf16[64,1152]{1,0:T(8,128)(2,1)}), bf16[1024,1152]{1,0:T(8,128)(2,1)}) %all-gather.2.cloned.1.call-update) | async-done | bytes 2359312 | tf_op jit(solution)/shard_map/all_gather | solution.py:122
  53.3 1.7 %copy-done.7 = bf16[1024,1152]{1,0:T(8,128)(2,1)S(1)} copy-done((bf16[1024,1152]{1,0:T(8,128)(2,1)S(1)}, bf16[1024,1152]{1,0:T(8,128)(2,1)}, u32[]{:S(2)}) %copy-start.7) | copy-done | bytes 2359320
  54.9 7.3 %shard_map.61 = (bf16[1024,1024]{1,0:T(8,128)(2,1)S(1)}, bf16[1024,1152]{1,0:T(8,128)(2,1)}) custom-call(s32[4]{0:T(128)S(1)} %pad_add_fusion.place, f32[2]{0:T(128)S(1)} %pad_maximum_fusion.scal, bf16[1024,1152]{1,0:T(8,128)(2,1)S(1)} %copy-done.7, bf16[1024,1152]{1,0:T(8,128)(2,1)S(1)} %bitcast.7), custom_call_target="tpu_custom_call" | custom-call | flops 4831838208 | bytes 9437184 | tf_op jit(solution)/shard_map/pallas_call | solution.py:96
  62.3 3.2 %shard_map.62 = bf16[512,1152]{1,0:T(8,128)(2,1)} custom-call(s32[4]{0:T(128)S(1)} %pad_add_fusion.place, bf16[1024,1024]{1,0:T(8,128)(2,1)S(1)} %get-tuple-element.4.coeff, bf16[1024,1152]{1,0:T(8,128)(2,1)S(1)} %bitcast.8), custom_call_target="tpu_custom_call" | custom-call | flops 1207959552 | bytes 5242880 | tf_op jit(solution)/shard_map/pallas_call | solution.py:96
  65.8 7.4 %all-to-all-start.1 = ((bf16[16,64,1152]{2,1,0:T(8,128)(2,1)}), bf16[16,64,1152]{2,1,0:T(8,128)(2,1)}, u32[]{:S(2)}, u32[]{:S(2)}) async-start(bf16[16,64,1152]{2,1,0:T(8,128)(2,1)} %bitcast.10), calls=%async_computation.1 | async-start | bytes 4718592 | tf_op jit(solution)/shard_map/all_to_all | solution.py:134
  73.3 1.6 %copy-done.2 = bf16[1024,1024]{1,0:T(8,128)(2,1)S(1)} copy-done((bf16[1024,1024]{1,0:T(8,128)(2,1)S(1)}, bf16[1024,1024]{1,0:T(8,128)(2,1)}, u32[]{:S(2)}) %copy-start.2) | copy-done | bytes 2097176
  74.9 2.9 %shard_map.63 = bf16[512,1152]{1,0:T(8,128)(2,1)S(1)} custom-call(s32[4]{0:T(128)S(1)} %pad_add_fusion.place, bf16[1024,1024]{1,0:T(8,128)(2,1)S(1)} %copy-done.2, bf16[1024,1152]{1,0:T(8,128)(2,1)S(1)} %bitcast.9, bf16[512,1152]{1,0:T(8,128)(2,1)} %collective-permute-done.other), custom_call_target="tpu_custom_call" | custom-call | flops 1207959552 | bytes 6291456 | tf_op jit(solution)/shard_map/pallas_call | solution.py:96
  77.9 4.1 %collective-permute-start.1 = (bf16[64,1152]{1,0:T(8,128)(2,1)S(1)}, bf16[64,1152]{1,0:T(8,128)(2,1)S(1)}, u32[]{:S(2)}, u32[]{:S(2)}) collective-permute-start(bf16[64,1152]{1,0:T(8,128)(2,1)S(1)} %get-tuple-element.8), channel_id=1, source_target_pairs={{0,4},{1,5},{2,6},{3,7},{4,0},{5,1},{6,2},{7,3},{8,12},{9,13},{10,... | collective-permute-start | bytes 442376 | tf_op jit(solution)/shard_map/ppermute | solution.py:19
  82.0 1.9 %collective-permute-start.2 = (bf16[64,1152]{1,0:T(8,128)(2,1)S(1)}, bf16[64,1152]{1,0:T(8,128)(2,1)S(1)}, u32[]{:S(2)}, u32[]{:S(2)}) collective-permute-start(bf16[64,1152]{1,0:T(8,128)(2,1)S(1)} %get-tuple-element.14), channel_id=1, source_target_pairs={{0,3},{1,4},{2,5},{3,6},{4,7},{5,0},{6,1},{7,2},{8,11},{9,12},{10,... | collective-permute-start | bytes 442376 | tf_op jit(solution)/shard_map/ppermute | solution.py:19
  84.1 3.2 %collective-permute-start.3 = (bf16[64,1152]{1,0:T(8,128)(2,1)S(1)}, bf16[64,1152]{1,0:T(8,128)(2,1)S(1)}, u32[]{:S(2)}, u32[]{:S(2)}) collective-permute-start(bf16[64,1152]{1,0:T(8,128)(2,1)S(1)} %get-tuple-element.13), channel_id=1, source_target_pairs={{0,5},{1,6},{2,7},{3,0},{4,1},{5,2},{6,3},{7,4},{8,13},{9,14},{10,... | collective-permute-start | bytes 442376 | tf_op jit(solution)/shard_map/ppermute | solution.py:19
  87.3 1.5 %collective-permute-start.4 = (bf16[64,1152]{1,0:T(8,128)(2,1)S(1)}, bf16[64,1152]{1,0:T(8,128)(2,1)S(1)}, u32[]{:S(2)}, u32[]{:S(2)}) collective-permute-start(bf16[64,1152]{1,0:T(8,128)(2,1)S(1)} %get-tuple-element.12), channel_id=1, source_target_pairs={{0,2},{1,3},{2,4},{3,5},{4,6},{5,7},{6,0},{7,1},{8,10},{9,11},{10,... | collective-permute-start | bytes 442376 | tf_op jit(solution)/shard_map/ppermute | solution.py:19
  88.8 2.7 %collective-permute-start.5 = (bf16[64,1152]{1,0:T(8,128)(2,1)S(1)}, bf16[64,1152]{1,0:T(8,128)(2,1)S(1)}, u32[]{:S(2)}, u32[]{:S(2)}) collective-permute-start(bf16[64,1152]{1,0:T(8,128)(2,1)S(1)} %get-tuple-element.11), channel_id=1, source_target_pairs={{0,6},{1,7},{2,0},{3,1},{4,2},{5,3},{6,4},{7,5},{8,14},{9,15},{10,... | collective-permute-start | bytes 442376 | tf_op jit(solution)/shard_map/ppermute | solution.py:19
  91.4 1.0 collective-permute-start.6
  92.4 10.4 %collective-permute-done.2 = bf16[64,1152]{1,0:T(8,128)(2,1)S(1)} collective-permute-done((bf16[64,1152]{1,0:T(8,128)(2,1)S(1)}, bf16[64,1152]{1,0:T(8,128)(2,1)S(1)}, u32[]{:S(2)}, u32[]{:S(2)}) %collective-permute-start.2) | collective-permute-done | bytes 147488 | tf_op jit(solution)/shard_map/ppermute | solution.py:19
  102.8 3.5 %collective-permute-done.4 = bf16[64,1152]{1,0:T(8,128)(2,1)S(1)} collective-permute-done((bf16[64,1152]{1,0:T(8,128)(2,1)S(1)}, bf16[64,1152]{1,0:T(8,128)(2,1)S(1)}, u32[]{:S(2)}, u32[]{:S(2)}) %collective-permute-start.4) | collective-permute-done | bytes 147488 | tf_op jit(solution)/shard_map/ppermute | solution.py:19
  107.1 1.3 %collective-permute-done.6 = bf16[64,1152]{1,0:T(8,128)(2,1)S(1)} collective-permute-done((bf16[64,1152]{1,0:T(8,128)(2,1)S(1)}, bf16[64,1152]{1,0:T(8,128)(2,1)S(1)}, u32[]{:S(2)}, u32[]{:S(2)}) %collective-permute-start.6) | collective-permute-done | bytes 147488 | tf_op jit(solution)/shard_map/ppermute | solution.py:19
  108.4 1.7 %collective-permute-done.7 = bf16[64,1152]{1,0:T(8,128)(2,1)S(1)} collective-permute-done((bf16[64,1152]{1,0:T(8,128)(2,1)S(1)}, bf16[64,1152]{1,0:T(8,128)(2,1)S(1)}, u32[]{:S(2)}, u32[]{:S(2)}) %collective-permute-start.7) | collective-permute-done | bytes 147488 | tf_op jit(solution)/shard_map/ppermute | solution.py:19
  111.2 2.0 %convert_reduce_fusion = f32[64,1152]{1,0:T(8,128)S(1)} fusion(bf16[16,64,1152]{2,1,0:T(8,128)(2,1)} %all-to-all-done.1), kind=kLoop, calls=%fused_computation | loop fusion | flops 2285568 | bytes 2654208 | tf_op jit(solution)/shard_map/reduce_sum | solution.py:143
  113.4 0.8 subtract_divide_fusion
  (32 shorter events, 3.9 us)
Async XLA Ops:
  7.2 46.1 %all-gather.2.cloned.1.call-start = ((), (), s32[]{:S(2)}) async-start(), calls=%async_computation.2 | async-start | bytes 2506752 | tf_op jit(solution)/shard_map/all_gather | solution.py:122
  7.2 1.0 copy-start.3
  9.0 1.0 copy-start.5
  10.2 1.4 %copy-start = (bf16[16,64,1152]{2,1,0:T(8,128)(2,1)}, bf16[16,64,1152]{2,1,0:T(8,128)(2,1)S(1)}, u32[]{:S(2)}) copy-start(bf16[16,64,1152]{2,1,0:T(8,128)(2,1)S(1)} %shard_map.60) | copy-start | bytes 7077892
  11.6 40.3 %all-to-all-start = ((bf16[16,64,1152]{2,1,0:T(8,128)(2,1)}), bf16[16,64,1152]{2,1,0:T(8,128)(2,1)S(1)}, u32[]{:S(2)}, u32[]{:S(2)}) async-start(bf16[16,64,1152]{2,1,0:T(8,128)(2,1)} %copy-done), calls=%async_computation | async-start | bytes 4718592 | tf_op jit(solution)/shard_map/all_to_all | solution.py:123
  53.3 1.7 %copy-start.7 = (bf16[1024,1152]{1,0:T(8,128)(2,1)S(1)}, bf16[1024,1152]{1,0:T(8,128)(2,1)}, u32[]{:S(2)}) copy-start(bf16[1024,1152]{1,0:T(8,128)(2,1)} %all-gather.2.cloned.1.call-done.xs) | copy-start | bytes 7077892
  62.3 3.2 %copy-start.1 = (bf16[1024,1024]{1,0:T(8,128)(2,1)}, bf16[1024,1024]{1,0:T(8,128)(2,1)S(1)}, u32[]{:S(2)}) copy-start(bf16[1024,1024]{1,0:T(8,128)(2,1)S(1)} %get-tuple-element.4.coeff) | copy-start | bytes 6291460
  65.5 7.8 %collective-permute-start = (bf16[512,1152]{1,0:T(8,128)(2,1)}, bf16[512,1152]{1,0:T(8,128)(2,1)}, u32[]{:S(2)}, u32[]{:S(2)}) collective-permute-start(bf16[512,1152]{1,0:T(8,128)(2,1)} %shard_map.62), channel_id=1, source_target_pairs={{0,16},{16,0},{1,17},{17,1},{2,18},{18,2},{3,19},{19,3},{4,20},{20... | collective-permute-start | bytes 3538952 | tf_op jit(solution)/shard_map/ppermute | solution.py:19
  65.8 7.4 %copy-start.4 = (f32[64,1152]{1,0:T(8,128)S(1)}, f32[64,1152]{1,0:T(8,128)}, u32[]{:S(2)}) copy-start(f32[64,1152]{1,0:T(8,128)} %raw.2) | copy-start | bytes 884740
  65.8 45.4 %all-to-all-start.1 = ((bf16[16,64,1152]{2,1,0:T(8,128)(2,1)}), bf16[16,64,1152]{2,1,0:T(8,128)(2,1)}, u32[]{:S(2)}, u32[]{:S(2)}) async-start(bf16[16,64,1152]{2,1,0:T(8,128)(2,1)} %bitcast.10), calls=%async_computation.1 | async-start | bytes 4718592 | tf_op jit(solution)/shard_map/all_to_all | solution.py:134
  73.3 1.6 %copy-start.2 = (bf16[1024,1024]{1,0:T(8,128)(2,1)S(1)}, bf16[1024,1024]{1,0:T(8,128)(2,1)}, u32[]{:S(2)}) copy-start(bf16[1024,1024]{1,0:T(8,128)(2,1)} %copy-done.1) | copy-start | bytes 6291460
  74.9 9.1 %copy-start.6 = (f32[64,1152]{1,0:T(8,128)S(1)}, f32[64,1152]{1,0:T(8,128)}, u32[]{:S(2)}) copy-start(f32[64,1152]{1,0:T(8,128)} %raw.3) | copy-start | bytes 884740
  77.9 13.5 %collective-permute-start.1 = (bf16[64,1152]{1,0:T(8,128)(2,1)S(1)}, bf16[64,1152]{1,0:T(8,128)(2,1)S(1)}, u32[]{:S(2)}, u32[]{:S(2)}) collective-permute-start(bf16[64,1152]{1,0:T(8,128)(2,1)S(1)} %get-tuple-element.8), channel_id=1, source_target_pairs={{0,4},{1,5},{2,6},{3,7},{4,0},{5,1},{6,2},{7,3},{8,12},{9,13},{10,... | collective-permute-start | bytes 442376 | tf_op jit(solution)/shard_map/ppermute | solution.py:19
  82.0 20.8 %collective-permute-start.2 = (bf16[64,1152]{1,0:T(8,128)(2,1)S(1)}, bf16[64,1152]{1,0:T(8,128)(2,1)S(1)}, u32[]{:S(2)}, u32[]{:S(2)}) collective-permute-start(bf16[64,1152]{1,0:T(8,128)(2,1)S(1)} %get-tuple-element.14), channel_id=1, source_target_pairs={{0,3},{1,4},{2,5},{3,6},{4,7},{5,0},{6,1},{7,2},{8,11},{9,12},{10,... | collective-permute-start | bytes 442376 | tf_op jit(solution)/shard_map/ppermute | solution.py:19
  84.1 18.7 %collective-permute-start.3 = (bf16[64,1152]{1,0:T(8,128)(2,1)S(1)}, bf16[64,1152]{1,0:T(8,128)(2,1)S(1)}, u32[]{:S(2)}, u32[]{:S(2)}) collective-permute-start(bf16[64,1152]{1,0:T(8,128)(2,1)S(1)} %get-tuple-element.13), channel_id=1, source_target_pairs={{0,5},{1,6},{2,7},{3,0},{4,1},{5,2},{6,3},{7,4},{8,13},{9,14},{10,... | collective-permute-start | bytes 442376 | tf_op jit(solution)/shard_map/ppermute | solution.py:19
  87.3 19.1 %collective-permute-start.4 = (bf16[64,1152]{1,0:T(8,128)(2,1)S(1)}, bf16[64,1152]{1,0:T(8,128)(2,1)S(1)}, u32[]{:S(2)}, u32[]{:S(2)}) collective-permute-start(bf16[64,1152]{1,0:T(8,128)(2,1)S(1)} %get-tuple-element.12), channel_id=1, source_target_pairs={{0,2},{1,3},{2,4},{3,5},{4,6},{5,7},{6,0},{7,1},{8,10},{9,11},{10,... | collective-permute-start | bytes 442376 | tf_op jit(solution)/shard_map/ppermute | solution.py:19
  88.8 18.3 %collective-permute-start.5 = (bf16[64,1152]{1,0:T(8,128)(2,1)S(1)}, bf16[64,1152]{1,0:T(8,128)(2,1)S(1)}, u32[]{:S(2)}, u32[]{:S(2)}) collective-permute-start(bf16[64,1152]{1,0:T(8,128)(2,1)S(1)} %get-tuple-element.11), channel_id=1, source_target_pairs={{0,6},{1,7},{2,0},{3,1},{4,2},{5,3},{6,4},{7,5},{8,14},{9,15},{10,... | collective-permute-start | bytes 442376 | tf_op jit(solution)/shard_map/ppermute | solution.py:19
  91.4 16.9 %collective-permute-start.6 = (bf16[64,1152]{1,0:T(8,128)(2,1)S(1)}, bf16[64,1152]{1,0:T(8,128)(2,1)S(1)}, u32[]{:S(2)}, u32[]{:S(2)}) collective-permute-start(bf16[64,1152]{1,0:T(8,128)(2,1)S(1)} %get-tuple-element.10), channel_id=1, source_target_pairs={{0,1},{1,2},{2,3},{3,4},{4,5},{5,6},{6,7},{7,0},{8,9},{9,10},{10,1... | collective-permute-start | bytes 442376 | tf_op jit(solution)/shard_map/ppermute | solution.py:19
  102.8 7.3 %collective-permute-start.7 = (bf16[64,1152]{1,0:T(8,128)(2,1)S(1)}, bf16[64,1152]{1,0:T(8,128)(2,1)S(1)}, u32[]{:S(2)}, u32[]{:S(2)}) collective-permute-start(bf16[64,1152]{1,0:T(8,128)(2,1)S(1)} %get-tuple-element.9), channel_id=1, source_target_pairs={{0,7},{1,0},{2,1},{3,2},{4,3},{5,4},{6,5},{7,6},{8,15},{9,8},{10,9... | collective-permute-start | bytes 442376 | tf_op jit(solution)/shard_map/ppermute | solution.py:19
Sparse Core Ops, SparseCore 0:
  10.4 42.8 all-gather.1

commit v5 on v3

--- a/solution.py
+++ b/solution.py
@@ -28,10 +28,6 @@
     return (grad - unit * jnp.sum(unit * grad, axis=1, keepdims=True)) / norm
 
 
-def add(a, b):
-    return (a.astype(F32) + b.astype(F32)).astype(BF)
-
-
 def unit_rows(raw):
     norm = jnp.sqrt(jnp.sum(raw * raw, axis=1, keepdims=True) + 1e-06)
     return (raw / norm).astype(BF)
@@ -50,7 +46,12 @@
     out[...] = unit_rows(raw[...])
 
 
-def text_kernel(place, scal, xs, xo, ts, coeff, dy, part, sems):
+def pack_kernel(*refs):
+    for k, block in enumerate(refs[:-1]):
+        refs[-1][k * ROWS : (k + 1) * ROWS] = block[...]
+
+
+def pair_kernel(place, scal, xs, xo, ts, coeff, dxo, dy, part, sems):
     temp = scal[0]
     offset = scal[1]
     half = xs.shape[0]
@@ -76,17 +77,12 @@
         part[sl] = dots.astype(BF)
         copies.append(pltpu.make_async_copy(part.at[sl], dy.at[sl], sems.at[j]))
         copies[-1].start()
+    for i in range(half // step):
+        cols = slice(half + i * step, half + (i + 1) * step)
+        dots = lax.dot_general(coeff[:, cols], ts[...], TN, preferred_element_type=F32)
+        dxo[pl.ds(i * step, step)] = dots.astype(BF)
     for copy in copies:
         copy.wait()
-
-
-def other_kernel(coeff, ts, dxo):
-    half = dxo.shape[0]
-    step = 256
-    for i in range(half // step):
-        cols = slice(half + i * step, half + (i + 1) * step)
-        part = lax.dot_general(coeff[:, cols], ts[...], TN, preferred_element_type=F32)
-        dxo[pl.ds(i * step, step)] = part.astype(BF)
 
 
 def image_kernel(coeff, ts, other, dxs):
@@ -105,31 +101,27 @@
 def local(kernel, outs, args, smem=0, scratch=(), flops=0, nbytes=2**20, trans=0):
     return pl.pallas_call(
         kernel,
-        out_shape=tuple(jax.ShapeDtypeStruct(shape, BF) for shape, _ in outs),
+        out_shape=tuple((pltpu.HBM if spec is HBM else jax.ShapeDtypeStruct)(shape, BF) for shape, spec in outs),
         in_specs=[SMEM] * smem + [VMEM] * (len(args) - smem),
         out_specs=tuple(spec for _, spec in outs),
         scratch_shapes=list(scratch),
-        compiler_params=pltpu.CompilerParams(vmem_limit_bytes=40 * 2**20),
+        compiler_params=pltpu.CompilerParams(vmem_limit_bytes=24 * 2**20),
         cost_estimate=pl.CostEstimate(flops=flops, bytes_accessed=nbytes, transcendentals=trans),
     )(*args)
 
 
-def ring_gather(block):
-    up = down = block
-    held = [block]
-    for _ in range(3):
-        up = shifted(up, "z", 1)
-        down = shifted(down, "z", -1)
-        held += [up, down]
-    return jnp.concatenate(held + [shifted(up, "z", 1)], 0)
+PLACES = (4, 3, 5, 2, 6, 1, 7)
 
 
-def ring_reduce(parts):
-    up, down = shifted(parts[7], "z", 1), shifted(parts[5], "z", -1)
-    up, down = shifted(add(parts[6], up), "z", 1), shifted(add(parts[3], down), "z", -1)
-    up, down = shifted(add(parts[4], up), "z", 1), shifted(add(parts[1], down), "z", -1)
-    up = shifted(add(parts[2], up), "z", 1)
-    return parts[0].astype(F32) + up.astype(F32) + down.astype(F32)
+def direct_gather(block):
+    return [block] + [shifted(block, "z", -k) for k in PLACES]
+
+
+def direct_reduce(parts):
+    total = parts[0].astype(F32)
+    for got in [shifted(parts[i + 1], "z", k) for i, k in enumerate(PLACES)]:
+        total = total + got.astype(F32)
+    return total
 
 
 def on_device(images, texts, log_temp, bias):
@@ -145,23 +137,23 @@
     spread, images = lax.optimization_barrier((spread, images))
     ts = lax.all_to_all(spread, PLANE, 0, 0, tiled=True).reshape(pooled, width)
     (x,) = local(unit_kernel, [((rows, width), VMEM)], [images])
-    xs = ring_gather(x)
+    (xs,) = local(pack_kernel, [((half, width), VMEM)], direct_gather(x))
     xo = shifted(xs, "core", 1)
     img_unit, img_norm = to_unit(images)
     txt_unit, txt_norm = to_unit(texts)
     place = lax.axis_index(PLANE).astype(jnp.int32).reshape(1)
     scal = jnp.stack([temp, bias[0]])
     unit_flops = 2 * half * pooled * width
-    coeff, dy = local(
-        text_kernel, [((pooled, 2 * half), VMEM), ((pooled, width), HBM)], [place, scal, xs, xo, ts], smem=2,
+    coeff, dxo, dy = local(
+        pair_kernel, [((pooled, 2 * half), VMEM), ((half, width), VMEM), ((pooled, width), HBM)],
+        [place, scal, xs, xo, ts], smem=2,
         scratch=[pltpu.VMEM((pooled, width), BF), pltpu.SemaphoreType.DMA((4,))],
-        flops=4 * unit_flops, nbytes=9 * 2**20, trans=4 * half * pooled,
+        flops=5 * unit_flops, nbytes=9 * 2**20, trans=4 * half * pooled,
     )
     dyr = lax.all_to_all(dy.reshape(n_plane, rows, width), PLANE, 0, 0, tiled=True)
-    (dxo,) = local(other_kernel, [((half, width), VMEM)], [coeff, ts], flops=unit_flops, nbytes=5 * 2**20)
     other = shifted(dxo, "core", 1)
     (mine,) = local(image_kernel, [((half, width), VMEM)], [coeff, ts, other], flops=unit_flops, nbytes=6 * 2**20)
-    image_sum = ring_reduce(mine.reshape(-1, rows, width))
+    image_sum = direct_reduce(mine.reshape(-1, rows, width))
     text_sum = jnp.sum(dyr.astype(F32), axis=0)
     grad_images = from_unit(temp * image_sum, img_unit, img_norm)
     grad_texts = from_unit(temp * text_sum, txt_unit, txt_norm)

time: 123 us -> 107 us (0.87)
  the two profiles are of different devices: /device:TPU:8 before, /device:TPU:66 now
where the time goes in v5:
time: 107 us; the launch traced here: 106 us
  starting transfers between devices  51.7 us (48%)
  waiting for transfers between devices  28.5 us (27%)
  Pallas kernels  15.7 us (15%)
  other arithmetic  4.5 us (4%)
  local copies, waits for them, and re-layouts  4.01 us (4%)
  between operations  2.08 us (2%)
    ppermute x16, starting transfers between devices, shifted(): lax.ppermute(block, axis, [(i, (i + distance) % n) for i in range(n)])  36.8 us
    ppermute x16, waiting for transfers between devices, shifted(): lax.ppermute(block, axis, [(i, (i + distance) % n) for i in range(n)])  28.5 us
    pallas_call x5, Pallas kernels, local(): pl.pallas_call(kernel, out_shape=tuple(((pltpu.HBM if spec is HBM else ja...  15.7 us
    all_to_all x1, starting transfers between devices, on_device(): ts = lax.all_to_all(spread, PLANE, 0, 0, tiled=True).reshape(pooled, width)  7.62 us
    all_to_all x1, starting transfers between devices, on_device(): lax.all_to_all(dy.reshape(n_plane, rows, width), PLANE, 0, 0, tiled=True)  7.24 us
    unnamed x10, local copies, waits for them, and re-layouts  3.93 us
  transfers between devices with their start and end apart: 18, of which 10 were waited for; matrix products, arithmetic and copies ran while one was open for 1% of the time, Pallas kernels for 4%

profile of v5, /device:TPU:66, one launch (start us, length us, event | category | flops | bytes accessed | tf_op | source)
XLA Modules:
  0.0 106.5 jit_solution(18276325514487478821)
XLA Ops:
  1.6 1.7 %shard_map.59 = bf16[16,64,1152]{2,1,0:T(8,128)(2,1)} custom-call(f32[64,1152]{1,0:T(8,128)S(1)} %copy-done.1), custom_call_target="tpu_custom_call" | custom-call | bytes 1048576 | tf_op jit(solution)/shard_map/pallas_call | solution.py:102
  3.3 7.6 %all-to-all-start = ((bf16[16,64,1152]{2,1,0:T(8,128)(2,1)}), bf16[16,64,1152]{2,1,0:T(8,128)(2,1)S(1)}, u32[]{:S(2)}, u32[]{:S(2)}) async-start(bf16[16,64,1152]{2,1,0:T(8,128)(2,1)} %shard_map.59), calls=%async_computation | async-start | bytes 4718592 | tf_op jit(solution)/shard_map/all_to_all | solution.py:138
  11.1 5.5 %collective-permute-start = (bf16[64,1152]{1,0:T(8,128)(2,1)S(1)}, bf16[64,1152]{1,0:T(8,128)(2,1)S(1)}, u32[]{:S(2)}, u32[]{:S(2)}) collective-permute-start(bf16[64,1152]{1,0:T(8,128)(2,1)S(1)} %shard_map.60.refs_0_), channel_id=1, source_target_pairs={{0,4},{1,5},{2,6},{3,7},{4,0},{5,1},{6,2},{7,3},{8,12},{9,13},{10,... | collective-permute-start | bytes 442376 | tf_op jit(solution)/shard_map/ppermute | solution.py:19
  17.5 4.0 %collective-permute-start.2 = (bf16[64,1152]{1,0:T(8,128)(2,1)S(1)}, bf16[64,1152]{1,0:T(8,128)(2,1)S(1)}, u32[]{:S(2)}, u32[]{:S(2)}) collective-permute-start(bf16[64,1152]{1,0:T(8,128)(2,1)S(1)} %shard_map.60.refs_0_), channel_id=1, source_target_pairs={{0,3},{1,4},{2,5},{3,6},{4,7},{5,0},{6,1},{7,2},{8,11},{9,12},{10,... | collective-permute-start | bytes 442376 | tf_op jit(solution)/shard_map/ppermute | solution.py:19
  21.8 3.9 %collective-permute-start.4 = (bf16[64,1152]{1,0:T(8,128)(2,1)S(1)}, bf16[64,1152]{1,0:T(8,128)(2,1)S(1)}, u32[]{:S(2)}, u32[]{:S(2)}) collective-permute-start(bf16[64,1152]{1,0:T(8,128)(2,1)S(1)} %shard_map.60.refs_0_), channel_id=1, source_target_pairs={{0,2},{1,3},{2,4},{3,5},{4,6},{5,7},{6,0},{7,1},{8,10},{9,11},{10,... | collective-permute-start | bytes 442376 | tf_op jit(solution)/shard_map/ppermute | solution.py:19
  25.7 1.4 %collective-permute-done.refs_1_ = bf16[64,1152]{1,0:T(8,128)(2,1)S(1)} collective-permute-done((bf16[64,1152]{1,0:T(8,128)(2,1)S(1)}, bf16[64,1152]{1,0:T(8,128)(2,1)S(1)}, u32[]{:S(2)}, u32[]{:S(2)}) %collective-permute-start) | collective-permute-done | bytes 147488 | tf_op jit(solution)/shard_map/ppermute | solution.py:19
  27.1 1.7 %collective-permute-start.5 = (bf16[64,1152]{1,0:T(8,128)(2,1)S(1)}, bf16[64,1152]{1,0:T(8,128)(2,1)S(1)}, u32[]{:S(2)}, u32[]{:S(2)}) collective-permute-start(bf16[64,1152]{1,0:T(8,128)(2,1)S(1)} %shard_map.60.refs_0_), channel_id=1, source_target_pairs={{0,7},{1,0},{2,1},{3,2},{4,3},{5,4},{6,5},{7,6},{8,15},{9,8},{10,9... | collective-permute-start | bytes 442376 | tf_op jit(solution)/shard_map/ppermute | solution.py:19
  28.8 1.8 %collective-permute-done.1.refs_2_ = bf16[64,1152]{1,0:T(8,128)(2,1)S(1)} collective-permute-done((bf16[64,1152]{1,0:T(8,128)(2,1)S(1)}, bf16[64,1152]{1,0:T(8,128)(2,1)S(1)}, u32[]{:S(2)}, u32[]{:S(2)}) %collective-permute-start.1) | collective-permute-done | bytes 147488 | tf_op jit(solution)/shard_map/ppermute | solution.py:19
  30.6 6.2 %collective-permute-start.6 = (bf16[64,1152]{1,0:T(8,128)(2,1)S(1)}, bf16[64,1152]{1,0:T(8,128)(2,1)S(1)}, u32[]{:S(2)}, u32[]{:S(2)}) collective-permute-start(bf16[64,1152]{1,0:T(8,128)(2,1)S(1)} %shard_map.60.refs_0_), channel_id=1, source_target_pairs={{0,1},{1,2},{2,3},{3,4},{4,5},{5,6},{6,7},{7,0},{8,9},{9,10},{10,1... | collective-permute-start | bytes 442376 | tf_op jit(solution)/shard_map/ppermute | solution.py:19
  36.8 2.2 %collective-permute-done.3.refs_4_ = bf16[64,1152]{1,0:T(8,128)(2,1)S(1)} collective-permute-done((bf16[64,1152]{1,0:T(8,128)(2,1)S(1)}, bf16[64,1152]{1,0:T(8,128)(2,1)S(1)}, u32[]{:S(2)}, u32[]{:S(2)}) %collective-permute-start.3) | collective-permute-done | bytes 147488 | tf_op jit(solution)/shard_map/ppermute | solution.py:19
  39.2 2.3 %collective-permute-done.5.refs_6_ = bf16[64,1152]{1,0:T(8,128)(2,1)S(1)} collective-permute-done((bf16[64,1152]{1,0:T(8,128)(2,1)S(1)}, bf16[64,1152]{1,0:T(8,128)(2,1)S(1)}, u32[]{:S(2)}, u32[]{:S(2)}) %collective-permute-start.5) | collective-permute-done | bytes 147488 | tf_op jit(solution)/shard_map/ppermute | solution.py:19
  45.1 1.8 %collective-permute-done.7.xo = bf16[512,1152]{1,0:T(8,128)(2,1)} collective-permute-done((bf16[512,1152]{1,0:T(8,128)(2,1)}, bf16[512,1152]{1,0:T(8,128)(2,1)}, u32[]{:S(2)}, u32[]{:S(2)}) %collective-permute-start.7) | collective-permute-done | bytes 1179680 | tf_op jit(solution)/shard_map/ppermute | solution.py:19
  46.8 9.9 %shard_map.62 = (bf16[1024,1024]{1,0:T(8,128)(2,1)S(1)}, bf16[512,1152]{1,0:T(8,128)(2,1)}, bf16[1024,1152]{1,0:T(8,128)(2,1)}) custom-call(s32[1]{0:T(128)} %bitcast.1.place, f32[2]{0:T(128)S(1)} %pad_maximum_fusion.scal, bf16[512,1152]{1,0:T(8,128)(2,1)} %shard_map.61.xs, bf16[512,1152]{1,0:T(8,128)(2,1)} %collective-permute-done.7.xo, ...), custom_call_target="tpu_custom_call" | custom-call | flops 6039797760 | bytes 9437184 | tf_op jit(solution)/shard_map/pallas_call | solution.py:102
  58.3 7.2 %all-to-all-start.1 = ((bf16[16,64,1152]{2,1,0:T(8,128)(2,1)}), bf16[16,64,1152]{2,1,0:T(8,128)(2,1)}, u32[]{:S(2)}, u32[]{:S(2)}) async-start(bf16[16,64,1152]{2,1,0:T(8,128)(2,1)} %bitcast.6), calls=%async_computation.1 | async-start | bytes 4718592 | tf_op jit(solution)/shard_map/all_to_all | solution.py:153
  65.7 1.6 %copy-done.4 = bf16[1024,1024]{1,0:T(8,128)(2,1)S(1)} copy-done((bf16[1024,1024]{1,0:T(8,128)(2,1)S(1)}, bf16[1024,1024]{1,0:T(8,128)(2,1)}, u32[]{:S(2)}) %copy-start.4) | copy-done | bytes 2097176
  67.2 2.8 %shard_map.63 = bf16[512,1152]{1,0:T(8,128)(2,1)S(1)} custom-call(bf16[1024,1024]{1,0:T(8,128)(2,1)S(1)} %copy-done.4, bf16[1024,1152]{1,0:T(8,128)(2,1)S(1)} %bitcast.5, bf16[512,1152]{1,0:T(8,128)(2,1)} %collective-permute-done.8.other), custom_call_target="tpu_custom_call" | custom-call | flops 1207959552 | bytes 6291456 | tf_op jit(solution)/shard_map/pallas_call | solution.py:102
  70.8 1.5 %collective-permute-start.14 = (bf16[64,1152]{1,0:T(8,128)(2,1)S(1)}, bf16[64,1152]{1,0:T(8,128)(2,1)S(1)}, u32[]{:S(2)}, u32[]{:S(2)}) collective-permute-start(bf16[64,1152]{1,0:T(8,128)(2,1)S(1)} %get-tuple-element.16), channel_id=1, source_target_pairs={{0,1},{1,2},{2,3},{3,4},{4,5},{5,6},{6,7},{7,0},{8,9},{9,10},{10,1... | collective-permute-start | bytes 442376 | tf_op jit(solution)/shard_map/ppermute | solution.py:19
  72.4 1.9 %collective-permute-start.13 = (bf16[64,1152]{1,0:T(8,128)(2,1)S(1)}, bf16[64,1152]{1,0:T(8,128)(2,1)S(1)}, u32[]{:S(2)}, u32[]{:S(2)}) collective-permute-start(bf16[64,1152]{1,0:T(8,128)(2,1)S(1)} %get-tuple-element.17), channel_id=1, source_target_pairs={{0,6},{1,7},{2,0},{3,1},{4,2},{5,3},{6,4},{7,5},{8,14},{9,15},{10,... | collective-permute-start | bytes 442376 | tf_op jit(solution)/shard_map/ppermute | solution.py:19
  74.3 2.3 %collective-permute-start.12 = (bf16[64,1152]{1,0:T(8,128)(2,1)S(1)}, bf16[64,1152]{1,0:T(8,128)(2,1)S(1)}, u32[]{:S(2)}, u32[]{:S(2)}) collective-permute-start(bf16[64,1152]{1,0:T(8,128)(2,1)S(1)} %get-tuple-element.18), channel_id=1, source_target_pairs={{0,2},{1,3},{2,4},{3,5},{4,6},{5,7},{6,0},{7,1},{8,10},{9,11},{10,... | collective-permute-start | bytes 442376 | tf_op jit(solution)/shard_map/ppermute | solution.py:19
  76.6 4.5 %collective-permute-start.11 = (bf16[64,1152]{1,0:T(8,128)(2,1)S(1)}, bf16[64,1152]{1,0:T(8,128)(2,1)S(1)}, u32[]{:S(2)}, u32[]{:S(2)}) collective-permute-start(bf16[64,1152]{1,0:T(8,128)(2,1)S(1)} %get-tuple-element.19), channel_id=1, source_target_pairs={{0,5},{1,6},{2,7},{3,0},{4,1},{5,2},{6,3},{7,4},{8,13},{9,14},{10,... | collective-permute-start | bytes 442376 | tf_op jit(solution)/shard_map/ppermute | solution.py:19
  81.7 2.8 %collective-permute-start.9 = (bf16[64,1152]{1,0:T(8,128)(2,1)S(1)}, bf16[64,1152]{1,0:T(8,128)(2,1)S(1)}, u32[]{:S(2)}, u32[]{:S(2)}) collective-permute-start(bf16[64,1152]{1,0:T(8,128)(2,1)S(1)} %get-tuple-element.14), channel_id=1, source_target_pairs={{0,4},{1,5},{2,6},{3,7},{4,0},{5,1},{6,2},{7,3},{8,12},{9,13},{10,... | collective-permute-start | bytes 442376 | tf_op jit(solution)/shard_map/ppermute | solution.py:19
  84.8 13.7 %collective-permute-done.11 = bf16[64,1152]{1,0:T(8,128)(2,1)S(1)} collective-permute-done((bf16[64,1152]{1,0:T(8,128)(2,1)S(1)}, bf16[64,1152]{1,0:T(8,128)(2,1)S(1)}, u32[]{:S(2)}, u32[]{:S(2)}) %collective-permute-start.11) | collective-permute-done | bytes 147488 | tf_op jit(solution)/shard_map/ppermute | solution.py:19
  98.4 3.8 %collective-permute-done.10 = bf16[64,1152]{1,0:T(8,128)(2,1)S(1)} collective-permute-done((bf16[64,1152]{1,0:T(8,128)(2,1)S(1)}, bf16[64,1152]{1,0:T(8,128)(2,1)S(1)}, u32[]{:S(2)}, u32[]{:S(2)}) %collective-permute-start.10) | collective-permute-done | bytes 147488 | tf_op jit(solution)/shard_map/ppermute | solution.py:19
  103.4 2.0 %convert_reduce_fusion = f32[64,1152]{1,0:T(8,128)S(1)} fusion(bf16[16,64,1152]{2,1,0:T(8,128)(2,1)} %all-to-all-done.1), kind=kLoop, calls=%fused_computation | loop fusion | flops 2285568 | bytes 2654208 | tf_op jit(solution)/shard_map/reduce_sum | solution.py:157
  (38 shorter events, 10.1 us)
Async XLA Ops:
  0.6 1.0 copy-start.1
  3.3 7.6 %copy-start = (f32[64,1152]{1,0:T(8,128)S(1)}, f32[64,1152]{1,0:T(8,128)}, u32[]{:S(2)}) copy-start(f32[64,1152]{1,0:T(8,128)} %raw.2) | copy-start | bytes 884740
  3.3 43.5 %all-to-all-start = ((bf16[16,64,1152]{2,1,0:T(8,128)(2,1)}), bf16[16,64,1152]{2,1,0:T(8,128)(2,1)S(1)}, u32[]{:S(2)}, u32[]{:S(2)}) async-start(bf16[16,64,1152]{2,1,0:T(8,128)(2,1)} %shard_map.59), calls=%async_computation | async-start | bytes 4718592 | tf_op jit(solution)/shard_map/all_to_all | solution.py:138
  11.1 16.0 %collective-permute-start = (bf16[64,1152]{1,0:T(8,128)(2,1)S(1)}, bf16[64,1152]{1,0:T(8,128)(2,1)S(1)}, u32[]{:S(2)}, u32[]{:S(2)}) collective-permute-start(bf16[64,1152]{1,0:T(8,128)(2,1)S(1)} %shard_map.60.refs_0_), channel_id=1, source_target_pairs={{0,4},{1,5},{2,6},{3,7},{4,0},{5,1},{6,2},{7,3},{8,12},{9,13},{10,... | collective-permute-start | bytes 442376 | tf_op jit(solution)/shard_map/ppermute | solution.py:19
  16.5 14.1 %collective-permute-start.1 = (bf16[64,1152]{1,0:T(8,128)(2,1)S(1)}, bf16[64,1152]{1,0:T(8,128)(2,1)S(1)}, u32[]{:S(2)}, u32[]{:S(2)}) collective-permute-start(bf16[64,1152]{1,0:T(8,128)(2,1)S(1)} %shard_map.60.refs_0_), channel_id=1, source_target_pairs={{0,5},{1,6},{2,7},{3,0},{4,1},{5,2},{6,3},{7,4},{8,13},{9,14},{10,... | collective-permute-start | bytes 442376 | tf_op jit(solution)/shard_map/ppermute | solution.py:19
  17.5 19.3 %collective-permute-start.2 = (bf16[64,1152]{1,0:T(8,128)(2,1)S(1)}, bf16[64,1152]{1,0:T(8,128)(2,1)S(1)}, u32[]{:S(2)}, u32[]{:S(2)}) collective-permute-start(bf16[64,1152]{1,0:T(8,128)(2,1)S(1)} %shard_map.60.refs_0_), channel_id=1, source_target_pairs={{0,3},{1,4},{2,5},{3,6},{4,7},{5,0},{6,1},{7,2},{8,11},{9,12},{10,... | collective-permute-start | bytes 442376 | tf_op jit(solution)/shard_map/ppermute | solution.py:19
  21.6 17.5 %collective-permute-start.3 = (bf16[64,1152]{1,0:T(8,128)(2,1)S(1)}, bf16[64,1152]{1,0:T(8,128)(2,1)S(1)}, u32[]{:S(2)}, u32[]{:S(2)}) collective-permute-start(bf16[64,1152]{1,0:T(8,128)(2,1)S(1)} %shard_map.60.refs_0_), channel_id=1, source_target_pairs={{0,6},{1,7},{2,0},{3,1},{4,2},{5,3},{6,4},{7,5},{8,14},{9,15},{10,... | collective-permute-start | bytes 442376 | tf_op jit(solution)/shard_map/ppermute | solution.py:19
  21.8 17.4 %collective-permute-start.4 = (bf16[64,1152]{1,0:T(8,128)(2,1)S(1)}, bf16[64,1152]{1,0:T(8,128)(2,1)S(1)}, u32[]{:S(2)}, u32[]{:S(2)}) collective-permute-start(bf16[64,1152]{1,0:T(8,128)(2,1)S(1)} %shard_map.60.refs_0_), channel_id=1, source_target_pairs={{0,2},{1,3},{2,4},{3,5},{4,6},{5,7},{6,0},{7,1},{8,10},{9,11},{10,... | collective-permute-start | bytes 442376 | tf_op jit(solution)/shard_map/ppermute | solution.py:19
  27.1 14.4 %collective-permute-start.5 = (bf16[64,1152]{1,0:T(8,128)(2,1)S(1)}, bf16[64,1152]{1,0:T(8,128)(2,1)S(1)}, u32[]{:S(2)}, u32[]{:S(2)}) collective-permute-start(bf16[64,1152]{1,0:T(8,128)(2,1)S(1)} %shard_map.60.refs_0_), channel_id=1, source_target_pairs={{0,7},{1,0},{2,1},{3,2},{4,3},{5,4},{6,5},{7,6},{8,15},{9,8},{10,9... | collective-permute-start | bytes 442376 | tf_op jit(solution)/shard_map/ppermute | solution.py:19
  30.6 11.9 %collective-permute-start.6 = (bf16[64,1152]{1,0:T(8,128)(2,1)S(1)}, bf16[64,1152]{1,0:T(8,128)(2,1)S(1)}, u32[]{:S(2)}, u32[]{:S(2)}) collective-permute-start(bf16[64,1152]{1,0:T(8,128)(2,1)S(1)} %shard_map.60.refs_0_), channel_id=1, source_target_pairs={{0,1},{1,2},{2,3},{3,4},{4,5},{5,6},{6,7},{7,0},{8,9},{9,10},{10,1... | collective-permute-start | bytes 442376 | tf_op jit(solution)/shard_map/ppermute | solution.py:19
  43.6 3.2 %collective-permute-start.7 = (bf16[512,1152]{1,0:T(8,128)(2,1)}, bf16[512,1152]{1,0:T(8,128)(2,1)}, u32[]{:S(2)}, u32[]{:S(2)}) collective-permute-start(bf16[512,1152]{1,0:T(8,128)(2,1)} %shard_map.61.xs), channel_id=1, source_target_pairs={{0,16},{16,0},{1,17},{17,1},{2,18},{18,2},{3,19},{19,3},{4,20},{20... | collective-permute-start | bytes 3538952 | tf_op jit(solution)/shard_map/ppermute | solution.py:19
  56.8 1.4 %copy-start.3 = (bf16[1024,1024]{1,0:T(8,128)(2,1)}, bf16[1024,1024]{1,0:T(8,128)(2,1)S(1)}, u32[]{:S(2)}) copy-start(bf16[1024,1024]{1,0:T(8,128)(2,1)S(1)} %get-tuple-element.9.coeff) | copy-start | bytes 6291460
  58.2 7.5 %collective-permute-start.8 = (bf16[512,1152]{1,0:T(8,128)(2,1)}, bf16[512,1152]{1,0:T(8,128)(2,1)}, u32[]{:S(2)}, u32[]{:S(2)}) collective-permute-start(bf16[512,1152]{1,0:T(8,128)(2,1)} %get-tuple-element.10), channel_id=1, source_target_pairs={{0,16},{16,0},{1,17},{17,1},{2,18},{18,2},{3,19},{19,3},{4,20},{20... | collective-permute-start | bytes 3538952 | tf_op jit(solution)/shard_map/ppermute | solution.py:19
  58.3 45.1 %all-to-all-start.1 = ((bf16[16,64,1152]{2,1,0:T(8,128)(2,1)}), bf16[16,64,1152]{2,1,0:T(8,128)(2,1)}, u32[]{:S(2)}, u32[]{:S(2)}) async-start(bf16[16,64,1152]{2,1,0:T(8,128)(2,1)} %bitcast.6), calls=%async_computation.1 | async-start | bytes 4718592 | tf_op jit(solution)/shard_map/all_to_all | solution.py:153
  65.7 1.6 %copy-start.4 = (bf16[1024,1024]{1,0:T(8,128)(2,1)S(1)}, bf16[1024,1024]{1,0:T(8,128)(2,1)}, u32[]{:S(2)}) copy-start(bf16[1024,1024]{1,0:T(8,128)(2,1)} %copy-done.3) | copy-start | bytes 6291460
  70.1 2.2 %copy-start.2 = (f32[64,1152]{1,0:T(8,128)S(1)}, f32[64,1152]{1,0:T(8,128)}, u32[]{:S(2)}) copy-start(f32[64,1152]{1,0:T(8,128)} %raw.1) | copy-start | bytes 884740
  70.2 10.9 %collective-permute-start.15 = (bf16[64,1152]{1,0:T(8,128)(2,1)S(1)}, bf16[64,1152]{1,0:T(8,128)(2,1)S(1)}, u32[]{:S(2)}, u32[]{:S(2)}) collective-permute-start(bf16[64,1152]{1,0:T(8,128)(2,1)S(1)} %get-tuple-element.15), channel_id=1, source_target_pairs={{0,7},{1,0},{2,1},{3,2},{4,3},{5,4},{6,5},{7,6},{8,15},{9,8},{10,9... | collective-permute-start | bytes 442376 | tf_op jit(solution)/shard_map/ppermute | solution.py:19
  70.8 10.9 %collective-permute-start.14 = (bf16[64,1152]{1,0:T(8,128)(2,1)S(1)}, bf16[64,1152]{1,0:T(8,128)(2,1)S(1)}, u32[]{:S(2)}, u32[]{:S(2)}) collective-permute-start(bf16[64,1152]{1,0:T(8,128)(2,1)S(1)} %get-tuple-element.16), channel_id=1, source_target_pairs={{0,1},{1,2},{2,3},{3,4},{4,5},{5,6},{6,7},{7,0},{8,9},{9,10},{10,1... | collective-permute-start | bytes 442376 | tf_op jit(solution)/shard_map/ppermute | solution.py:19
  72.4 12.3 %collective-permute-start.13 = (bf16[64,1152]{1,0:T(8,128)(2,1)S(1)}, bf16[64,1152]{1,0:T(8,128)(2,1)S(1)}, u32[]{:S(2)}, u32[]{:S(2)}) collective-permute-start(bf16[64,1152]{1,0:T(8,128)(2,1)S(1)} %get-tuple-element.17), channel_id=1, source_target_pairs={{0,6},{1,7},{2,0},{3,1},{4,2},{5,3},{6,4},{7,5},{8,14},{9,15},{10,... | collective-permute-start | bytes 442376 | tf_op jit(solution)/shard_map/ppermute | solution.py:19
  74.3 10.4 %collective-permute-start.12 = (bf16[64,1152]{1,0:T(8,128)(2,1)S(1)}, bf16[64,1152]{1,0:T(8,128)(2,1)S(1)}, u32[]{:S(2)}, u32[]{:S(2)}) collective-permute-start(bf16[64,1152]{1,0:T(8,128)(2,1)S(1)} %get-tuple-element.18), channel_id=1, source_target_pairs={{0,2},{1,3},{2,4},{3,5},{4,6},{5,7},{6,0},{7,1},{8,10},{9,11},{10,... | collective-permute-start | bytes 442376 | tf_op jit(solution)/shard_map/ppermute | solution.py:19
  76.6 21.8 %collective-permute-start.11 = (bf16[64,1152]{1,0:T(8,128)(2,1)S(1)}, bf16[64,1152]{1,0:T(8,128)(2,1)S(1)}, u32[]{:S(2)}, u32[]{:S(2)}) collective-permute-start(bf16[64,1152]{1,0:T(8,128)(2,1)S(1)} %get-tuple-element.19), channel_id=1, source_target_pairs={{0,5},{1,6},{2,7},{3,0},{4,1},{5,2},{6,3},{7,4},{8,13},{9,14},{10,... | collective-permute-start | bytes 442376 | tf_op jit(solution)/shard_map/ppermute | solution.py:19
  81.1 21.1 %collective-permute-start.10 = (bf16[64,1152]{1,0:T(8,128)(2,1)S(1)}, bf16[64,1152]{1,0:T(8,128)(2,1)S(1)}, u32[]{:S(2)}, u32[]{:S(2)}) collective-permute-start(bf16[64,1152]{1,0:T(8,128)(2,1)S(1)} %get-tuple-element.20), channel_id=1, source_target_pairs={{0,3},{1,4},{2,5},{3,6},{4,7},{5,0},{6,1},{7,2},{8,11},{9,12},{10,... | collective-permute-start | bytes 442376 | tf_op jit(solution)/shard_map/ppermute | solution.py:19
  81.7 20.6 %collective-permute-start.9 = (bf16[64,1152]{1,0:T(8,128)(2,1)S(1)}, bf16[64,1152]{1,0:T(8,128)(2,1)S(1)}, u32[]{:S(2)}, u32[]{:S(2)}) collective-permute-start(bf16[64,1152]{1,0:T(8,128)(2,1)S(1)} %get-tuple-element.14), channel_id=1, source_target_pairs={{0,4},{1,5},{2,6},{3,7},{4,0},{5,1},{6,2},{7,3},{8,12},{9,13},{10,... | collective-permute-start | bytes 442376 | tf_op jit(solution)/shard_map/ppermute | solution.py:19

commit v6 on v5

v6 whole, which is shorter than its diff:
```python
import jax
import jax.numpy as jnp
from jax import lax
from jax.experimental import pallas as pl
from jax.experimental.pallas import tpu as pltpu
from jax.sharding import Mesh, PartitionSpec as P

AXES = ("yh", "x", "core", "yl", "z")
PLANE = ("yh", "x", "yl")
BF = jnp.bfloat16
F32 = jnp.float32
LOG2E = 1.4426950408889634
ROWS = 64
NT = (((1,), (1,)), ((), ()))
TN = (((0,), (0,)), ((), ()))


def shifted(block, axis, distance):
    n = lax.axis_size(axis)
    return lax.ppermute(block, axis, [(i, (i + distance) % n) for i in range(n)])


def to_unit(raw):
    norm = jnp.sqrt(jnp.sum(raw * raw, axis=1, keepdims=True) + 1e-06)
    return (raw / norm, norm)


def from_unit(grad, unit, norm):
    return (grad - unit * jnp.sum(unit * grad, axis=1, keepdims=True)) / norm


def unit_rows(raw):
    norm = jnp.sqrt(jnp.sum(raw * raw, axis=1, keepdims=True) + 1e-06)
    return (raw / norm).astype(BF)


def spread_kernel(raw, out, unit, sems):
    unit[...] = unit_rows(raw[...])
    copies = [pltpu.make_async_copy(unit, out.at[k], sems.at[k]) for k in range(out.shape[0])]
    for copy in copies:
        copy.start()
    for copy in copies:
        copy.wait()


def unit_kernel(raw, out):
    out[...] = unit_rows(raw[...])


def pack_kernel(*refs):
    for k, block in enumerate(refs[:-1]):
        refs[-1][k * ROWS : (k + 1) * ROWS] = block[...]


def sigmoid(temp, offset, dots):
    return 1.0 / (1.0 + jnp.exp2(dots * (temp * -LOG2E) + offset * -LOG2E))


def pair_kernel(place, scal, xs, xo, ts, coeff, dxo, dy, x, held, part, sems):
    temp = scal[0]
    offset = scal[1]
    half = xs.shape[0]
    pooled = ts.shape[0]
    steps = 4
    step = pooled // steps
    loads = [
        pltpu.make_async_copy(xs, x.at[0:half], sems.at[0]),
        pltpu.make_async_copy(xo, x.at[half : 2 * half], sems.at[1]),
    ]
    for copy in loads:
        copy.start()
    for copy in loads:
        copy.wait()
    for j in range(steps):
        sl = pl.ds(j * step, step)
        dots = lax.dot_general(ts[sl], x[...], NT, preferred_element_type=F32)
        held[sl] = sigmoid(temp, offset, dots).astype(BF)
    at = pl.multiple_of(place[0] * ROWS, ROWS)
    dots = lax.dot_general(ts[pl.ds(at, ROWS)], x[0:ROWS], NT, preferred_element_type=F32)
    eye = lax.broadcasted_iota(jnp.int32, (ROWS, ROWS), 0) == lax.broadcasted_iota(
        jnp.int32, (ROWS, ROWS), 1
    )
    held[pl.ds(at, ROWS), 0:ROWS] = (sigmoid(temp, offset, dots) - eye.astype(F32)).astype(BF)
    copies = [pltpu.make_async_copy(held, coeff, sems.at[2])]
    copies[0].start()
    for j in range(steps):
        sl = pl.ds(j * step, step)
        part[sl] = jnp.dot(held[sl], x[...], preferred_element_type=F32).astype(BF)
        copies.append(pltpu.make_async_copy(part.at[sl], dy.at[sl], sems.at[3 + j]))
        copies[-1].start()
    wide = 256
    for i in range(half // wide):
        cols = slice(half + i * wide, half + (i + 1) * wide)
        dots = lax.dot_general(held[:, cols], ts[...], TN, preferred_element_type=F32)
        dxo[pl.ds(i * wide, wide)] = dots.astype(BF)
    for copy in copies:
        copy.wait()


def image_kernel(coeff, ts, other, *outs):
    wide = 256
    for i in range(other.shape[0] // wide):
        sl = pl.ds(i * wide, wide)
        part = lax.dot_general(coeff[:, i * wide : (i + 1) * wide], ts[...], TN, preferred_element_type=F32)
        part += other[sl].astype(F32)
        for k in range(wide // ROWS):
            out = outs[i * (wide // ROWS) + k]
            out[...] = part[k * ROWS : (k + 1) * ROWS].astype(out.dtype)


def text_kernel(scal, raw, got, out):
    total = got[0].astype(F32)
    for k in range(1, got.shape[0]):
        total += got[k].astype(F32)
    unit, norm = to_unit(raw[...])
    out[...] = from_unit(scal[0] * total, unit, norm)


VMEM = pl.BlockSpec(memory_space=pltpu.VMEM)
SMEM = pl.BlockSpec(memory_space=pltpu.SMEM)
HBM = pl.BlockSpec(memory_space=pltpu.HBM)


def local(kernel, outs, args, smem=0, hbm=0, scratch=(), flops=0, nbytes=2**20, trans=0, vmem=8):
    specs = [SMEM] * smem + [HBM] * hbm
    return pl.pallas_call(
        kernel,
        out_shape=tuple((pltpu.HBM if spec is HBM else jax.ShapeDtypeStruct)(shape, dtype) for shape, dtype, spec in outs),
        in_specs=specs + [VMEM] * (len(args) - len(specs)),
        out_specs=tuple(spec for _, _, spec in outs),
        scratch_shapes=list(scratch),
        compiler_params=pltpu.CompilerParams(vmem_limit_bytes=vmem * 2**20),
        cost_estimate=pl.CostEstimate(flops=flops, bytes_accessed=nbytes, transcendentals=trans),
    )(*args)


def add(a, b):
    return (a.astype(F32) + b.astype(F32)).astype(BF)


def ring_gather(block):
    far = shifted(block, "z", 4)
    up = [block]
    down = [block]
    for _ in range(3):
        up.append(shifted(up[-1], "z", -1))
        down.append(shifted(down[-1], "z", 1))
    return up + [far] + down[:0:-1]


def ring_reduce(parts):
    far = shifted(parts[4], "z", 4)
    up, down = parts[3], parts[5]
    for k in (2, 1, 0):
        up, down = shifted(up, "z", 1), shifted(down, "z", -1)
        if k:
            up, down = add(parts[k], up), add(parts[8 - k], down)
    return parts[0] + up.astype(F32) + down.astype(F32) + far.astype(F32)


def on_device(images, texts, log_temp, bias):
    temp = jnp.exp(log_temp[0])
    rows, width = images.shape
    n_plane = lax.axis_size(PLANE)
    half = ROWS * lax.axis_size("z")
    pooled = ROWS * n_plane
    (spread,) = local(
        spread_kernel, [((n_plane, rows, width), BF, HBM)], [texts],
        scratch=[pltpu.VMEM((rows, width), BF), pltpu.SemaphoreType.DMA((n_plane,))],
    )
    spread, images = lax.optimization_barrier((spread, images))
    ts = lax.all_to_all(spread, PLANE, 0, 0, tiled=True).reshape(pooled, width)
    (x,) = local(unit_kernel, [((rows, width), BF, VMEM)], [images])
    (xs,) = local(pack_kernel, [((half, width), BF, VMEM)], ring_gather(x))
    xo = shifted(xs, "core", 1)
    img_unit, img_norm = to_unit(images)
    place = lax.axis_index(PLANE).astype(jnp.int32).reshape(1)
    scal = jnp.stack([temp, bias[0]])
    unit_flops = 2 * half * pooled * width
    coeff, dxo, dy = local(
        pair_kernel,
        [((pooled, 2 * half), BF, HBM), ((half, width), BF, VMEM), ((pooled, width), BF, HBM)],
        [place, scal, xs, xo, ts], smem=2, hbm=2,
        scratch=[
            pltpu.VMEM((2 * half, width), BF),
            pltpu.VMEM((pooled, 2 * half), BF),
            pltpu.VMEM((pooled, width), BF),
            pltpu.SemaphoreType.DMA((7,)),
        ],
        flops=5 * unit_flops, nbytes=9 * 2**20, trans=4 * half * pooled, vmem=24,
    )
    dyr = lax.all_to_all(dy.reshape(n_plane, rows, width), PLANE, 0, 0, tiled=True)
    other = shifted(dxo, "core", 1)
    parts = local(
        image_kernel,
        [((rows, width), BF if k else F32, VMEM) for k in range(half // rows)],
        [coeff, ts, other], vmem=16,
    )
    image_sum = ring_reduce(parts)
    grad_images = from_unit(temp * image_sum, img_unit, img_norm)
    (grad_texts,) = local(text_kernel, [((rows, width), F32, VMEM)], [scal, texts, dyr], smem=1, vmem=8)
    return (grad_images, grad_texts)


def solution(mesh):
    fine = Mesh(mesh.devices.reshape(2, 4, 2, 2, 8), AXES)
    split = P(AXES, None)
    return jax.shard_map(
        on_device,
        mesh=fine,
        in_specs=(split, split, P(), P()),
        out_specs=(split, split),
        check_vma=False,
    )
```

time: 107 us -> 107 us (level)
  the two profiles are of different devices: /device:TPU:66 before, /device:TPU:8 now
where the time goes in v6:
time: 107 us; the launch traced here: 106 us
  starting transfers between devices  45 us (42%)
  waiting for transfers between devices  33.7 us (31%)
  Pallas kernels  16.5 us (15%)
  local copies, waits for them, and re-layouts  5.21 us (5%)
  other arithmetic  3.31 us (3%)
  between operations  2.08 us (2%)
    ppermute x16, starting transfers between devices, shifted(): lax.ppermute(block, axis, [(i, (i + distance) % n) for i in range(n)])  31.4 us
    ppermute x16, waiting for transfers between devices, shifted(): lax.ppermute(block, axis, [(i, (i + distance) % n) for i in range(n)])  24.5 us
    pallas_call x6, Pallas kernels, local(): pl.pallas_call(kernel, out_shape=tuple(((pltpu.HBM if spec is HBM else ja...  16.5 us
    all_to_all x1, waiting for transfers between devices, on_device(): lax.all_to_all(dy.reshape(n_plane, rows, width), PLANE, 0, 0, tiled=True)  9.28 us
    all_to_all x1, starting transfers between devices, on_device(): ts = lax.all_to_all(spread, PLANE, 0, 0, tiled=True).reshape(pooled, width)  7.54 us
    all_to_all x1, starting transfers between devices, on_device(): lax.all_to_all(dy.reshape(n_plane, rows, width), PLANE, 0, 0, tiled=True)  6.01 us
    unnamed x16, local copies, waits for them, and re-layouts  5.21 us
  transfers between devices with their start and end apart: 18, of which 11 were waited for; matrix products, arithmetic and copies ran while one was open for 3% of the time, Pallas kernels for 1%

profile of v6, /device:TPU:8, one launch (start us, length us, event | category | flops | bytes accessed | tf_op | source)
XLA Modules:
  0.0 105.8 jit_solution(14202218230697128591)
XLA Ops:
  1.6 1.7 %shard_map.59 = bf16[16,64,1152]{2,1,0:T(8,128)(2,1)} custom-call(f32[64,1152]{1,0:T(8,128)S(1)} %copy-done.2), custom_call_target="tpu_custom_call" | custom-call | bytes 1048576 | tf_op jit(solution)/shard_map/pallas_call | solution.py:126
  3.3 7.5 %all-to-all-start = ((bf16[16,64,1152]{2,1,0:T(8,128)(2,1)}), bf16[16,64,1152]{2,1,0:T(8,128)(2,1)S(1)}, u32[]{:S(2)}, u32[]{:S(2)}) async-start(bf16[16,64,1152]{2,1,0:T(8,128)(2,1)} %shard_map.59), calls=%async_computation | async-start | bytes 4718592 | tf_op jit(solution)/shard_map/all_to_all | solution.py:172
  11.0 5.9 %collective-permute-start = (bf16[64,1152]{1,0:T(8,128)(2,1)S(1)}, bf16[64,1152]{1,0:T(8,128)(2,1)S(1)}, u32[]{:S(2)}, u32[]{:S(2)}) collective-permute-start(bf16[64,1152]{1,0:T(8,128)(2,1)S(1)} %shard_map.60.refs_0_), channel_id=1, source_target_pairs={{0,7},{1,0},{2,1},{3,2},{4,3},{5,4},{6,5},{7,6},{8,15},{9,8},{10,9... | collective-permute-start | bytes 442376 | tf_op jit(solution)/shard_map/ppermute | solution.py:20
  16.9 2.7 %collective-permute-done.refs_1_ = bf16[64,1152]{1,0:T(8,128)(2,1)S(1)} collective-permute-done((bf16[64,1152]{1,0:T(8,128)(2,1)S(1)}, bf16[64,1152]{1,0:T(8,128)(2,1)S(1)}, u32[]{:S(2)}, u32[]{:S(2)}) %collective-permute-start) | collective-permute-done | bytes 147488 | tf_op jit(solution)/shard_map/ppermute | solution.py:20
  19.6 3.7 %collective-permute-start.1 = (bf16[64,1152]{1,0:T(8,128)(2,1)S(1)}, bf16[64,1152]{1,0:T(8,128)(2,1)S(1)}, u32[]{:S(2)}, u32[]{:S(2)}) collective-permute-start(bf16[64,1152]{1,0:T(8,128)(2,1)S(1)} %collective-permute-done.refs_1_), channel_id=1, source_target_pairs={{0,7},{1,0},{2,1},{3,2},{4,3},{5,4},{6,5},{7,6},{8,15},{9,8},{10,9... | collective-permute-start | bytes 442376 | tf_op jit(solution)/shard_map/ppermute | solution.py:20
  23.3 2.1 %collective-permute-start.3 = (bf16[64,1152]{1,0:T(8,128)(2,1)S(1)}, bf16[64,1152]{1,0:T(8,128)(2,1)S(1)}, u32[]{:S(2)}, u32[]{:S(2)}) collective-permute-start(bf16[64,1152]{1,0:T(8,128)(2,1)S(1)} %shard_map.60.refs_0_), channel_id=1, source_target_pairs={{0,4},{1,5},{2,6},{3,7},{4,0},{5,1},{6,2},{7,3},{8,12},{9,13},{10,... | collective-permute-start | bytes 442376 | tf_op jit(solution)/shard_map/ppermute | solution.py:20
  27.0 3.7 %collective-permute-start.2 = (bf16[64,1152]{1,0:T(8,128)(2,1)S(1)}, bf16[64,1152]{1,0:T(8,128)(2,1)S(1)}, u32[]{:S(2)}, u32[]{:S(2)}) collective-permute-start(bf16[64,1152]{1,0:T(8,128)(2,1)S(1)} %collective-permute-done.1.refs_2_), channel_id=1, source_target_pairs={{0,7},{1,0},{2,1},{3,2},{4,3},{5,4},{6,5},{7,6},{8,15},{9,8},{10,9... | collective-permute-start | bytes 442376 | tf_op jit(solution)/shard_map/ppermute | solution.py:20
  30.7 3.2 %collective-permute-done.5.refs_6_ = bf16[64,1152]{1,0:T(8,128)(2,1)S(1)} collective-permute-done((bf16[64,1152]{1,0:T(8,128)(2,1)S(1)}, bf16[64,1152]{1,0:T(8,128)(2,1)S(1)}, u32[]{:S(2)}, u32[]{:S(2)}) %collective-permute-start.5) | collective-permute-done | bytes 147488 | tf_op jit(solution)/shard_map/ppermute | solution.py:20
  33.9 2.2 %collective-permute-done.3.refs_4_ = bf16[64,1152]{1,0:T(8,128)(2,1)S(1)} collective-permute-done((bf16[64,1152]{1,0:T(8,128)(2,1)S(1)}, bf16[64,1152]{1,0:T(8,128)(2,1)S(1)}, u32[]{:S(2)}, u32[]{:S(2)}) %collective-permute-start.3) | collective-permute-done | bytes 147488 | tf_op jit(solution)/shard_map/ppermute | solution.py:20
  36.1 4.1 %collective-permute-done.6.refs_5_ = bf16[64,1152]{1,0:T(8,128)(2,1)S(1)} collective-permute-done((bf16[64,1152]{1,0:T(8,128)(2,1)S(1)}, bf16[64,1152]{1,0:T(8,128)(2,1)S(1)}, u32[]{:S(2)}, u32[]{:S(2)}) %collective-permute-start.6) | collective-permute-done | bytes 147488 | tf_op jit(solution)/shard_map/ppermute | solution.py:20
  42.8 1.8 %collective-permute-done.7.xo = bf16[512,1152]{1,0:T(8,128)(2,1)} collective-permute-done((bf16[512,1152]{1,0:T(8,128)(2,1)}, bf16[512,1152]{1,0:T(8,128)(2,1)}, u32[]{:S(2)}, u32[]{:S(2)}) %collective-permute-start.7) | collective-permute-done | bytes 1179680 | tf_op jit(solution)/shard_map/ppermute | solution.py:20
  44.6 9.6 %shard_map.62 = (bf16[1024,1024]{1,0:T(8,128)(2,1)}, bf16[512,1152]{1,0:T(8,128)(2,1)S(1)}, bf16[1024,1152]{1,0:T(8,128)(2,1)}) custom-call(s32[1]{0:T(128)} %bitcast.1.place, f32[2]{0:T(128)S(1)} %pad_maximum_fusion.scal, bf16[512,1152]{1,0:T(8,128)(2,1)} %shard_map.61.xs, bf16[512,1152]{1,0:T(8,128)(2,1)} %collective-permute-done.7.xo, ...), custom_call_target="tpu_custom_call" | custom-call | flops 6039797760 | bytes 9437184 | tf_op jit(solution)/shard_map/pallas_call | solution.py:126
  54.4 2.7 %collective-permute-done.8.other = bf16[512,1152]{1,0:T(8,128)(2,1)S(1)} collective-permute-done((bf16[512,1152]{1,0:T(8,128)(2,1)S(1)}, bf16[512,1152]{1,0:T(8,128)(2,1)S(1)}, u32[]{:S(2)}, u32[]{:S(2)}) %collective-permute-start.8) | collective-permute-done | bytes 1179680 | tf_op jit(solution)/shard_map/ppermute | solution.py:20
  57.1 1.6 %copy-done.1 = bf16[1024,1024]{1,0:T(8,128)(2,1)S(1)} copy-done((bf16[1024,1024]{1,0:T(8,128)(2,1)S(1)}, bf16[1024,1024]{1,0:T(8,128)(2,1)}, u32[]{:S(2)}) %copy-start.1) | copy-done | bytes 2097176
  58.7 2.2 %shard_map.63 = (f32[64,1152]{1,0:T(8,128)S(1)}, bf16[64,1152]{1,0:T(8,128)(2,1)S(1)}, bf16[64,1152]{1,0:T(8,128)(2,1)S(1)}, bf16[64,1152]{1,0:T(8,128)(2,1)}, b...) custom-call(bf16[1024,1024]{1,0:T(8,128)(2,1)S(1)} %copy-done.1, ...), custom_call_target="tpu_custom_call" | custom-call | bytes 1048576 | tf_op jit(solution)/shard_map/pallas_call | solution.py:126
  64.8 6.0 %all-to-all-start.1 = ((bf16[16,64,1152]{2,1,0:T(8,128)(2,1)}), bf16[16,64,1152]{2,1,0:T(8,128)(2,1)S(1)}, u32[]{:S(2)}, u32[]{:S(2)}) async-start(bf16[16,64,1152]{2,1,0:T(8,128)(2,1)} %bitcast.6), calls=%async_computation.1 | async-start | bytes 4718592 | tf_op jit(solution)/shard_map/all_to_all | solution.py:192
  70.8 3.3 %collective-permute-start.12 = (bf16[64,1152]{1,0:T(8,128)(2,1)}, bf16[64,1152]{1,0:T(8,128)(2,1)S(1)}, u32[]{:S(2)}, u32[]{:S(2)}) collective-permute-start(bf16[64,1152]{1,0:T(8,128)(2,1)} %copy-done.7), channel_id=1, source_target_pairs={{0,7},{1,0},{2,1},{3,2},{4,3},{5,4},{6,5},{7,6},{8,15},{9,8},{10,9... | collective-permute-start | bytes 442376 | tf_op jit(solution)/shard_map/ppermute | solution.py:20
  74.2 4.4 %collective-permute-start.15 = (bf16[64,1152]{1,0:T(8,128)(2,1)}, bf16[64,1152]{1,0:T(8,128)(2,1)S(1)}, u32[]{:S(2)}, u32[]{:S(2)}) collective-permute-start(bf16[64,1152]{1,0:T(8,128)(2,1)} %copy-done.6), channel_id=1, source_target_pairs={{0,4},{1,5},{2,6},{3,7},{4,0},{5,1},{6,2},{7,3},{8,12},{9,13},{10,... | collective-permute-start | bytes 442376 | tf_op jit(solution)/shard_map/ppermute | solution.py:20
  80.6 3.3 %collective-permute-start.13 = (bf16[64,1152]{1,0:T(8,128)(2,1)S(1)}, bf16[64,1152]{1,0:T(8,128)(2,1)S(1)}, u32[]{:S(2)}, u32[]{:S(2)}) collective-permute-start(bf16[64,1152]{1,0:T(8,128)(2,1)S(1)} %add_convert_fusion.1), channel_id=1, source_target_pairs={{0,7},{1,0},{2,1},{3,2},{4,3},{5,4},{6,5},{7,6},{8,15},{9,8},{10,9... | collective-permute-start | bytes 442376 | tf_op jit(solution)/shard_map/ppermute | solution.py:20
  83.9 3.2 %collective-permute-done.10 = bf16[64,1152]{1,0:T(8,128)(2,1)S(1)} collective-permute-done((bf16[64,1152]{1,0:T(8,128)(2,1)S(1)}, bf16[64,1152]{1,0:T(8,128)(2,1)S(1)}, u32[]{:S(2)}, u32[]{:S(2)}) %collective-permute-start.10) | collective-permute-done | bytes 147488 | tf_op jit(solution)/shard_map/ppermute | solution.py:20
  88.4 2.3 %collective-permute-start.14 = (bf16[64,1152]{1,0:T(8,128)(2,1)S(1)}, bf16[64,1152]{1,0:T(8,128)(2,1)S(1)}, u32[]{:S(2)}, u32[]{:S(2)}) collective-permute-start(bf16[64,1152]{1,0:T(8,128)(2,1)S(1)} %add_convert_fusion), channel_id=1, source_target_pairs={{0,7},{1,0},{2,1},{3,2},{4,3},{5,4},{6,5},{7,6},{8,15},{9,8},{10,9... | collective-permute-start | bytes 442376 | tf_op jit(solution)/shard_map/ppermute | solution.py:20
  90.7 2.9 %collective-permute-done.11 = bf16[64,1152]{1,0:T(8,128)(2,1)S(1)} collective-permute-done((bf16[64,1152]{1,0:T(8,128)(2,1)S(1)}, bf16[64,1152]{1,0:T(8,128)(2,1)S(1)}, u32[]{:S(2)}, u32[]{:S(2)}) %collective-permute-start.11) | collective-permute-done | bytes 147488 | tf_op jit(solution)/shard_map/ppermute | solution.py:20
  94.8 9.3 %all-to-all-done.1.got = bf16[16,64,1152]{2,1,0:T(8,128)(2,1)S(1)} async-done(((bf16[16,64,1152]{2,1,0:T(8,128)(2,1)}), bf16[16,64,1152]{2,1,0:T(8,128)(2,1)S(1)}, u32[]{:S(2)}, u32[]{:S(2)}) %all-to-all-start.1) | async-done | bytes 2359328 | tf_op jit(solution)/shard_map/all_to_all | solution.py:192
  104.1 1.7 %shard_map.64 = f32[64,1152]{1,0:T(8,128)} custom-call(f32[2]{0:T(128)S(1)} %pad_maximum_fusion.scal, f32[64,1152]{1,0:T(8,128)S(1)} %copy-done.3, bf16[16,64,1152]{2,1,0:T(8,128)(2,1)S(1)} %all-to-all-done.1.got), custom_call_target="tpu_custom_call" | custom-call | bytes 1048576 | tf_op jit(solution)/shard_map/pallas_call | solution.py:126
  (43 shorter events, 12.6 us)
Async XLA Ops:
  0.6 1.0 copy-start.2
  3.3 7.5 %copy-start = (f32[64,1152]{1,0:T(8,128)S(1)}, f32[64,1152]{1,0:T(8,128)}, u32[]{:S(2)}) copy-start(f32[64,1152]{1,0:T(8,128)} %raw.3) | copy-start | bytes 884740
  3.3 41.2 %all-to-all-start = ((bf16[16,64,1152]{2,1,0:T(8,128)(2,1)}), bf16[16,64,1152]{2,1,0:T(8,128)(2,1)S(1)}, u32[]{:S(2)}, u32[]{:S(2)}) async-start(bf16[16,64,1152]{2,1,0:T(8,128)(2,1)} %shard_map.59), calls=%async_computation | async-start | bytes 4718592 | tf_op jit(solution)/shard_map/all_to_all | solution.py:172
  11.0 8.6 %collective-permute-start = (bf16[64,1152]{1,0:T(8,128)(2,1)S(1)}, bf16[64,1152]{1,0:T(8,128)(2,1)S(1)}, u32[]{:S(2)}, u32[]{:S(2)}) collective-permute-start(bf16[64,1152]{1,0:T(8,128)(2,1)S(1)} %shard_map.60.refs_0_), channel_id=1, source_target_pairs={{0,7},{1,0},{2,1},{3,2},{4,3},{5,4},{6,5},{7,6},{8,15},{9,8},{10,9... | collective-permute-start | bytes 442376 | tf_op jit(solution)/shard_map/ppermute | solution.py:20
  16.9 6.4 %collective-permute-start.4 = (bf16[64,1152]{1,0:T(8,128)(2,1)S(1)}, bf16[64,1152]{1,0:T(8,128)(2,1)S(1)}, u32[]{:S(2)}, u32[]{:S(2)}) collective-permute-start(bf16[64,1152]{1,0:T(8,128)(2,1)S(1)} %shard_map.60.refs_0_), channel_id=1, source_target_pairs={{0,1},{1,2},{2,3},{3,4},{4,5},{5,6},{6,7},{7,0},{8,9},{9,10},{10,1... | collective-permute-start | bytes 442376 | tf_op jit(solution)/shard_map/ppermute | solution.py:20
  19.6 7.4 %collective-permute-start.1 = (bf16[64,1152]{1,0:T(8,128)(2,1)S(1)}, bf16[64,1152]{1,0:T(8,128)(2,1)S(1)}, u32[]{:S(2)}, u32[]{:S(2)}) collective-permute-start(bf16[64,1152]{1,0:T(8,128)(2,1)S(1)} %collective-permute-done.refs_1_), channel_id=1, source_target_pairs={{0,7},{1,0},{2,1},{3,2},{4,3},{5,4},{6,5},{7,6},{8,15},{9,8},{10,9... | collective-permute-start | bytes 442376 | tf_op jit(solution)/shard_map/ppermute | solution.py:20
  23.3 10.6 %collective-permute-start.5 = (bf16[64,1152]{1,0:T(8,128)(2,1)S(1)}, bf16[64,1152]{1,0:T(8,128)(2,1)S(1)}, u32[]{:S(2)}, u32[]{:S(2)}) collective-permute-start(bf16[64,1152]{1,0:T(8,128)(2,1)S(1)} %collective-permute-done.4.refs_7_), channel_id=1, source_target_pairs={{0,1},{1,2},{2,3},{3,4},{4,5},{5,6},{6,7},{7,0},{8,9},{9,10},{10,1... | collective-permute-start | bytes 442376 | tf_op jit(solution)/shard_map/ppermute | solution.py:20
  23.3 12.8 %collective-permute-start.3 = (bf16[64,1152]{1,0:T(8,128)(2,1)S(1)}, bf16[64,1152]{1,0:T(8,128)(2,1)S(1)}, u32[]{:S(2)}, u32[]{:S(2)}) collective-permute-start(bf16[64,1152]{1,0:T(8,128)(2,1)S(1)} %shard_map.60.refs_0_), channel_id=1, source_target_pairs={{0,4},{1,5},{2,6},{3,7},{4,0},{5,1},{6,2},{7,3},{8,12},{9,13},{10,... | collective-permute-start | bytes 442376 | tf_op jit(solution)/shard_map/ppermute | solution.py:20
  27.0 9.1 %collective-permute-start.2 = (bf16[64,1152]{1,0:T(8,128)(2,1)S(1)}, bf16[64,1152]{1,0:T(8,128)(2,1)S(1)}, u32[]{:S(2)}, u32[]{:S(2)}) collective-permute-start(bf16[64,1152]{1,0:T(8,128)(2,1)S(1)} %collective-permute-done.1.refs_2_), channel_id=1, source_target_pairs={{0,7},{1,0},{2,1},{3,2},{4,3},{5,4},{6,5},{7,6},{8,15},{9,8},{10,9... | collective-permute-start | bytes 442376 | tf_op jit(solution)/shard_map/ppermute | solution.py:20
  33.9 6.4 %collective-permute-start.6 = (bf16[64,1152]{1,0:T(8,128)(2,1)S(1)}, bf16[64,1152]{1,0:T(8,128)(2,1)S(1)}, u32[]{:S(2)}, u32[]{:S(2)}) collective-permute-start(bf16[64,1152]{1,0:T(8,128)(2,1)S(1)} %collective-permute-done.5.refs_6_), channel_id=1, source_target_pairs={{0,1},{1,2},{2,3},{3,4},{4,5},{5,6},{6,7},{7,0},{8,9},{9,10},{10,1... | collective-permute-start | bytes 442376 | tf_op jit(solution)/shard_map/ppermute | solution.py:20
  41.4 3.2 %collective-permute-start.7 = (bf16[512,1152]{1,0:T(8,128)(2,1)}, bf16[512,1152]{1,0:T(8,128)(2,1)}, u32[]{:S(2)}, u32[]{:S(2)}) collective-permute-start(bf16[512,1152]{1,0:T(8,128)(2,1)} %shard_map.61.xs), channel_id=1, source_target_pairs={{0,16},{16,0},{1,17},{17,1},{2,18},{18,2},{3,19},{19,3},{4,20},{20... | collective-permute-start | bytes 3538952 | tf_op jit(solution)/shard_map/ppermute | solution.py:20
  54.2 2.9 %collective-permute-start.8 = (bf16[512,1152]{1,0:T(8,128)(2,1)S(1)}, bf16[512,1152]{1,0:T(8,128)(2,1)S(1)}, u32[]{:S(2)}, u32[]{:S(2)}) collective-permute-start(bf16[512,1152]{1,0:T(8,128)(2,1)S(1)} %get-tuple-element.18), channel_id=1, source_target_pairs={{0,16},{16,0},{1,17},{17,1},{2,18},{18,2},{3,19},{19,3},{4,20},{20... | collective-permute-start | bytes 3538952 | tf_op jit(solution)/shard_map/ppermute | solution.py:20
  57.1 1.6 %copy-start.1 = (bf16[1024,1024]{1,0:T(8,128)(2,1)S(1)}, bf16[1024,1024]{1,0:T(8,128)(2,1)}, u32[]{:S(2)}) copy-start(bf16[1024,1024]{1,0:T(8,128)(2,1)} %get-tuple-element.17.coeff) | copy-start | bytes 6291460
  61.5 0.7 copy-start.5
  62.9 0.7 copy-start.7
  63.5 15.0 %collective-permute-start.9 = (bf16[64,1152]{1,0:T(8,128)(2,1)}, bf16[64,1152]{1,0:T(8,128)(2,1)}, u32[]{:S(2)}, u32[]{:S(2)}) collective-permute-start(bf16[64,1152]{1,0:T(8,128)(2,1)} %get-tuple-element.22), channel_id=1, source_target_pairs={{0,1},{1,2},{2,3},{3,4},{4,5},{5,6},{6,7},{7,0},{8,9},{9,10},{10,1... | collective-permute-start | bytes 442376 | tf_op jit(solution)/shard_map/ppermute | solution.py:20
  64.8 39.2 %all-to-all-start.1 = ((bf16[16,64,1152]{2,1,0:T(8,128)(2,1)}), bf16[16,64,1152]{2,1,0:T(8,128)(2,1)S(1)}, u32[]{:S(2)}, u32[]{:S(2)}) async-start(bf16[16,64,1152]{2,1,0:T(8,128)(2,1)} %bitcast.6), calls=%async_computation.1 | async-start | bytes 4718592 | tf_op jit(solution)/shard_map/all_to_all | solution.py:192
  70.8 33.2 %copy-start.3 = (f32[64,1152]{1,0:T(8,128)S(1)}, f32[64,1152]{1,0:T(8,128)}, u32[]{:S(2)}) copy-start(f32[64,1152]{1,0:T(8,128)} %raw.4) | copy-start | bytes 884740
  70.8 8.8 %collective-permute-start.12 = (bf16[64,1152]{1,0:T(8,128)(2,1)}, bf16[64,1152]{1,0:T(8,128)(2,1)S(1)}, u32[]{:S(2)}, u32[]{:S(2)}) collective-permute-start(bf16[64,1152]{1,0:T(8,128)(2,1)} %copy-done.7), channel_id=1, source_target_pairs={{0,7},{1,0},{2,1},{3,2},{4,3},{5,4},{6,5},{7,6},{8,15},{9,8},{10,9... | collective-permute-start | bytes 442376 | tf_op jit(solution)/shard_map/ppermute | solution.py:20
  74.2 16.5 %collective-permute-start.15 = (bf16[64,1152]{1,0:T(8,128)(2,1)}, bf16[64,1152]{1,0:T(8,128)(2,1)S(1)}, u32[]{:S(2)}, u32[]{:S(2)}) collective-permute-start(bf16[64,1152]{1,0:T(8,128)(2,1)} %copy-done.6), channel_id=1, source_target_pairs={{0,4},{1,5},{2,6},{3,7},{4,0},{5,1},{6,2},{7,3},{8,12},{9,13},{10,... | collective-permute-start | bytes 442376 | tf_op jit(solution)/shard_map/ppermute | solution.py:20
  79.6 7.5 %collective-permute-start.10 = (bf16[64,1152]{1,0:T(8,128)(2,1)S(1)}, bf16[64,1152]{1,0:T(8,128)(2,1)S(1)}, u32[]{:S(2)}, u32[]{:S(2)}) collective-permute-start(bf16[64,1152]{1,0:T(8,128)(2,1)S(1)} %add_convert_fusion.3), channel_id=1, source_target_pairs={{0,1},{1,2},{2,3},{3,4},{4,5},{5,6},{6,7},{7,0},{8,9},{9,10},{10,1... | collective-permute-start | bytes 442376 | tf_op jit(solution)/shard_map/ppermute | solution.py:20
  80.6 7.7 %collective-permute-start.13 = (bf16[64,1152]{1,0:T(8,128)(2,1)S(1)}, bf16[64,1152]{1,0:T(8,128)(2,1)S(1)}, u32[]{:S(2)}, u32[]{:S(2)}) collective-permute-start(bf16[64,1152]{1,0:T(8,128)(2,1)S(1)} %add_convert_fusion.1), channel_id=1, source_target_pairs={{0,7},{1,0},{2,1},{3,2},{4,3},{5,4},{6,5},{7,6},{8,15},{9,8},{10,9... | collective-permute-start | bytes 442376 | tf_op jit(solution)/shard_map/ppermute | solution.py:20
  87.2 6.4 %collective-permute-start.11 = (bf16[64,1152]{1,0:T(8,128)(2,1)S(1)}, bf16[64,1152]{1,0:T(8,128)(2,1)S(1)}, u32[]{:S(2)}, u32[]{:S(2)}) collective-permute-start(bf16[64,1152]{1,0:T(8,128)(2,1)S(1)} %add_convert_fusion.2), channel_id=1, source_target_pairs={{0,1},{1,2},{2,3},{3,4},{4,5},{5,6},{6,7},{7,0},{8,9},{9,10},{10,1... | collective-permute-start | bytes 442376 | tf_op jit(solution)/shard_map/ppermute | solution.py:20
  88.4 5.3 %collective-permute-start.14 = (bf16[64,1152]{1,0:T(8,128)(2,1)S(1)}, bf16[64,1152]{1,0:T(8,128)(2,1)S(1)}, u32[]{:S(2)}, u32[]{:S(2)}) collective-permute-start(bf16[64,1152]{1,0:T(8,128)(2,1)S(1)} %add_convert_fusion), channel_id=1, source_target_pairs={{0,7},{1,0},{2,1},{3,2},{4,3},{5,4},{6,5},{7,6},{8,15},{9,8},{10,9... | collective-permute-start | bytes 442376 | tf_op jit(solution)/shard_map/ppermute | solution.py:20
  (2 other events, 1.3 us)

commit v7 on v6

--- a/solution.py
+++ b/solution.py
@@ -97,15 +97,23 @@
         copy.wait()
 
 
-def image_kernel(coeff, ts, other, *outs):
+def image_kernel(coeff, ts, other, own, rest, held, sems):
     wide = 256
-    for i in range(other.shape[0] // wide):
-        sl = pl.ds(i * wide, wide)
-        part = lax.dot_general(coeff[:, i * wide : (i + 1) * wide], ts[...], TN, preferred_element_type=F32)
-        part += other[sl].astype(F32)
-        for k in range(wide // ROWS):
-            out = outs[i * (wide // ROWS) + k]
-            out[...] = part[k * ROWS : (k + 1) * ROWS].astype(out.dtype)
+    n = other.shape[0] // wide
+    loads = []
+    for i in range(n):
+        cols = slice(i * wide, (i + 1) * wide)
+        loads.append(pltpu.make_async_copy(coeff.at[:, cols], held.at[:, cols], sems.at[i]))
+        loads[-1].start()
+    for i in range(n):
+        loads[i].wait()
+        part = lax.dot_general(held[:, i * wide : (i + 1) * wide], ts[...], TN, preferred_element_type=F32)
+        part += other[pl.ds(i * wide, wide)].astype(F32)
+        if i == 0:
+            own[...] = part[0:ROWS]
+            rest[0 : wide - ROWS] = part[ROWS:].astype(BF)
+        else:
+            rest[pl.ds(i * wide - ROWS, wide)] = part.astype(BF)
 
 
 def text_kernel(scal, raw, got, out):
@@ -148,14 +156,13 @@
     return up + [far] + down[:0:-1]
 
 
-def ring_reduce(parts):
-    far = shifted(parts[4], "z", 4)
-    up, down = parts[3], parts[5]
-    for k in (2, 1, 0):
-        up, down = shifted(up, "z", 1), shifted(down, "z", -1)
-        if k:
-            up, down = add(parts[k], up), add(parts[8 - k], down)
-    return parts[0] + up.astype(F32) + down.astype(F32) + far.astype(F32)
+def near_reduce(own, rest):
+    direct = [shifted(rest[k - 1], "z", k) for k in (4, 3, 5)]
+    up, down = shifted(rest[1], "z", 1), shifted(rest[5], "z", -1)
+    up, down = shifted(add(rest[0], up), "z", 1), shifted(add(rest[6], down), "z", -1)
+    for got in direct + [up, down]:
+        own = own + got.astype(F32)
+    return own
 
 
 def on_device(images, texts, log_temp, bias):
@@ -191,12 +198,13 @@
     )
     dyr = lax.all_to_all(dy.reshape(n_plane, rows, width), PLANE, 0, 0, tiled=True)
     other = shifted(dxo, "core", 1)
-    parts = local(
+    own, rest = local(
         image_kernel,
-        [((rows, width), BF if k else F32, VMEM) for k in range(half // rows)],
-        [coeff, ts, other], vmem=16,
-    )
-    image_sum = ring_reduce(parts)
+        [((rows, width), F32, VMEM), ((half - rows, width), BF, VMEM)],
+        [coeff, ts, other], hbm=1, vmem=16, flops=unit_flops, nbytes=6 * 2**20,
+        scratch=[pltpu.VMEM((pooled, half), BF), pltpu.SemaphoreType.DMA((half // 256,))],
+    )
+    image_sum = near_reduce(own, rest.reshape(-1, rows, width))
     grad_images = from_unit(temp * image_sum, img_unit, img_norm)
     (grad_texts,) = local(text_kernel, [((rows, width), F32, VMEM)], [scal, texts, dyr], smem=1, vmem=8)
     return (grad_images, grad_texts)

time: 107 us -> 101 us (0.944)
  the two profiles are of different devices: /device:TPU:8 before, /device:TPU:36 now
where the time goes in v7:
time: 101 us
  starting transfers between devices  43.8 us (43%)
  waiting for transfers between devices  30.4 us (30%)
  Pallas kernels  18.8 us (19%)
  local copies, waits for them, and re-layouts  4.29 us (4%)
  between operations  2.09 us (2%)
  other arithmetic  1.36 us (1%)
    ppermute x16, waiting for transfers between devices, shifted(): lax.ppermute(block, axis, [(i, (i + distance) % n) for i in range(n)])  30.4 us
    ppermute x16, starting transfers between devices, shifted(): lax.ppermute(block, axis, [(i, (i + distance) % n) for i in range(n)])  28.8 us
    pallas_call x6, Pallas kernels, local(): pl.pallas_call(kernel, out_shape=tuple(((pltpu.HBM if spec is HBM else ja...  18.8 us
    all_to_all x1, starting transfers between devices, on_device(): ts = lax.all_to_all(spread, PLANE, 0, 0, tiled=True).reshape(pooled, width)  7.59 us
    all_to_all x1, starting transfers between devices, on_device(): lax.all_to_all(dy.reshape(n_plane, rows, width), PLANE, 0, 0, tiled=True)  7.35 us
    unnamed x12, local copies, waits for them, and re-layouts  4.22 us
  transfers between devices with their start and end apart: 18, of which 9 were waited for; matrix products, arithmetic and copies ran while one was open for 1% of the time, Pallas kernels for 4%

profile of v7, /device:TPU:36, one launch (start us, length us, event | category | flops | bytes accessed | tf_op | source)
XLA Modules:
  0.0 100.8 jit_solution(1105344119677482976)
XLA Ops:
  1.6 1.7 %shard_map.59 = bf16[16,64,1152]{2,1,0:T(8,128)(2,1)} custom-call(f32[64,1152]{1,0:T(8,128)S(1)} %copy-done.4), custom_call_target="tpu_custom_call" | custom-call | bytes 1048576 | tf_op jit(solution)/shard_map/pallas_call | solution.py:134
  3.3 7.6 %all-to-all-start = ((bf16[16,64,1152]{2,1,0:T(8,128)(2,1)}), bf16[16,64,1152]{2,1,0:T(8,128)(2,1)S(1)}, u32[]{:S(2)}, u32[]{:S(2)}) async-start(bf16[16,64,1152]{2,1,0:T(8,128)(2,1)} %shard_map.59), calls=%async_computation | async-start | bytes 4718592 | tf_op jit(solution)/shard_map/all_to_all | solution.py:179
  11.2 1.9 %collective-permute-start.4 = (bf16[64,1152]{1,0:T(8,128)(2,1)S(1)}, bf16[64,1152]{1,0:T(8,128)(2,1)S(1)}, u32[]{:S(2)}, u32[]{:S(2)}) collective-permute-start(bf16[64,1152]{1,0:T(8,128)(2,1)S(1)} %shard_map.60.refs_0_), channel_id=1, source_target_pairs={{0,1},{1,2},{2,3},{3,4},{4,5},{5,6},{6,7},{7,0},{8,9},{9,10},{10,1... | collective-permute-start | bytes 442376 | tf_op jit(solution)/shard_map/ppermute | solution.py:20
  13.2 3.2 %collective-permute-done.refs_1_ = bf16[64,1152]{1,0:T(8,128)(2,1)S(1)} collective-permute-done((bf16[64,1152]{1,0:T(8,128)(2,1)S(1)}, bf16[64,1152]{1,0:T(8,128)(2,1)S(1)}, u32[]{:S(2)}, u32[]{:S(2)}) %collective-permute-start) | collective-permute-done | bytes 147488 | tf_op jit(solution)/shard_map/ppermute | solution.py:20
  16.3 3.4 %collective-permute-start.1 = (bf16[64,1152]{1,0:T(8,128)(2,1)S(1)}, bf16[64,1152]{1,0:T(8,128)(2,1)S(1)}, u32[]{:S(2)}, u32[]{:S(2)}) collective-permute-start(bf16[64,1152]{1,0:T(8,128)(2,1)S(1)} %collective-permute-done.refs_1_), channel_id=1, source_target_pairs={{0,7},{1,0},{2,1},{3,2},{4,3},{5,4},{6,5},{7,6},{8,15},{9,8},{10,9... | collective-permute-start | bytes 442376 | tf_op jit(solution)/shard_map/ppermute | solution.py:20
  20.2 4.4 %collective-permute-start.3 = (bf16[64,1152]{1,0:T(8,128)(2,1)S(1)}, bf16[64,1152]{1,0:T(8,128)(2,1)S(1)}, u32[]{:S(2)}, u32[]{:S(2)}) collective-permute-start(bf16[64,1152]{1,0:T(8,128)(2,1)S(1)} %shard_map.60.refs_0_), channel_id=1, source_target_pairs={{0,4},{1,5},{2,6},{3,7},{4,0},{5,1},{6,2},{7,3},{8,12},{9,13},{10,... | collective-permute-start | bytes 442376 | tf_op jit(solution)/shard_map/ppermute | solution.py:20
  24.6 2.6 %collective-permute-start.2 = (bf16[64,1152]{1,0:T(8,128)(2,1)S(1)}, bf16[64,1152]{1,0:T(8,128)(2,1)S(1)}, u32[]{:S(2)}, u32[]{:S(2)}) collective-permute-start(bf16[64,1152]{1,0:T(8,128)(2,1)S(1)} %collective-permute-done.1.refs_2_), channel_id=1, source_target_pairs={{0,7},{1,0},{2,1},{3,2},{4,3},{5,4},{6,5},{7,6},{8,15},{9,8},{10,9... | collective-permute-start | bytes 442376 | tf_op jit(solution)/shard_map/ppermute | solution.py:20
  27.2 2.1 %collective-permute-done.5.refs_6_ = bf16[64,1152]{1,0:T(8,128)(2,1)S(1)} collective-permute-done((bf16[64,1152]{1,0:T(8,128)(2,1)S(1)}, bf16[64,1152]{1,0:T(8,128)(2,1)S(1)}, u32[]{:S(2)}, u32[]{:S(2)}) %collective-permute-start.5) | collective-permute-done | bytes 147488 | tf_op jit(solution)/shard_map/ppermute | solution.py:20
  29.3 4.6 %collective-permute-done.3.refs_4_ = bf16[64,1152]{1,0:T(8,128)(2,1)S(1)} collective-permute-done((bf16[64,1152]{1,0:T(8,128)(2,1)S(1)}, bf16[64,1152]{1,0:T(8,128)(2,1)S(1)}, u32[]{:S(2)}, u32[]{:S(2)}) %collective-permute-start.3) | collective-permute-done | bytes 147488 | tf_op jit(solution)/shard_map/ppermute | solution.py:20
  34.2 2.8 %collective-permute-done.6.refs_5_ = bf16[64,1152]{1,0:T(8,128)(2,1)S(1)} collective-permute-done((bf16[64,1152]{1,0:T(8,128)(2,1)S(1)}, bf16[64,1152]{1,0:T(8,128)(2,1)S(1)}, u32[]{:S(2)}, u32[]{:S(2)}) %collective-permute-start.6) | collective-permute-done | bytes 147488 | tf_op jit(solution)/shard_map/ppermute | solution.py:20
  39.6 1.8 %collective-permute-done.7.xo = bf16[512,1152]{1,0:T(8,128)(2,1)} collective-permute-done((bf16[512,1152]{1,0:T(8,128)(2,1)}, bf16[512,1152]{1,0:T(8,128)(2,1)}, u32[]{:S(2)}, u32[]{:S(2)}) %collective-permute-start.7) | collective-permute-done | bytes 1179680 | tf_op jit(solution)/shard_map/ppermute | solution.py:20
  41.4 10.9 %shard_map.62 = (bf16[1024,1024]{1,0:T(8,128)(2,1)}, bf16[512,1152]{1,0:T(8,128)(2,1)}, bf16[1024,1152]{1,0:T(8,128)(2,1)}) custom-call(s32[1]{0:T(128)} %bitcast.1.place, f32[2]{0:T(128)S(1)} %pad_maximum_fusion.scal, bf16[512,1152]{1,0:T(8,128)(2,1)} %shard_map.61.xs, bf16[512,1152]{1,0:T(8,128)(2,1)} %collective-permute-done.7.xo, ...), custom_call_target="tpu_custom_call" | custom-call | flops 6039797760 | bytes 9437184 | tf_op jit(solution)/shard_map/pallas_call | solution.py:134
  52.6 7.4 %all-to-all-start.1 = ((bf16[16,64,1152]{2,1,0:T(8,128)(2,1)}), bf16[16,64,1152]{2,1,0:T(8,128)(2,1)S(1)}, u32[]{:S(2)}, u32[]{:S(2)}) async-start(bf16[16,64,1152]{2,1,0:T(8,128)(2,1)} %bitcast.6), calls=%async_computation.1 | async-start | bytes 4718592 | tf_op jit(solution)/shard_map/all_to_all | solution.py:199
  59.9 1.7 %copy-done.1 = bf16[16,64,1152]{2,1,0:T(8,128)(2,1)S(1)} copy-done((bf16[16,64,1152]{2,1,0:T(8,128)(2,1)S(1)}, bf16[16,64,1152]{2,1,0:T(8,128)(2,1)}, u32[]{:S(2)}) %copy-start.1) | copy-done | bytes 2359320
  61.6 1.6 %copy-done.3 = bf16[1024,1024]{1,0:T(8,128)(2,1)S(1)} copy-done((bf16[1024,1024]{1,0:T(8,128)(2,1)S(1)}, bf16[1024,1024]{1,0:T(8,128)(2,1)}, u32[]{:S(2)}) %copy-start.3) | copy-done | bytes 2097176
  63.2 3.2 %shard_map.63 = (f32[64,1152]{1,0:T(8,128)S(1)}, bf16[448,1152]{1,0:T(8,128)(2,1)S(1)}) custom-call(bf16[1024,1024]{1,0:T(8,128)(2,1)S(1)} %copy-done.3, bf16[1024,1152]{1,0:T(8,128)(2,1)S(1)} %bitcast.5, bf16[512,1152]{1,0:T(8,128)(2,1)} %collective-permute-done.8.other), custom_call_target="tpu_custom_call" | custom-call | flops 1207959552 | bytes 6291456 | tf_op jit(solution)/shard_map/pallas_call | solution.py:134
  66.5 2.0 %collective-permute-start.12 = (bf16[64,1152]{1,0:T(8,128)(2,1)S(1)}, bf16[64,1152]{1,0:T(8,128)(2,1)S(1)}, u32[]{:S(2)}, u32[]{:S(2)}) collective-permute-start(bf16[64,1152]{1,0:T(8,128)(2,1)S(1)} %get-tuple-element.20), channel_id=1, source_target_pairs={{0,1},{1,2},{2,3},{3,4},{4,5},{5,6},{6,7},{7,0},{8,9},{9,10},{10,1... | collective-permute-start | bytes 442376 | tf_op jit(solution)/shard_map/ppermute | solution.py:20
  68.5 1.3 %collective-permute-start.14 = (bf16[64,1152]{1,0:T(8,128)(2,1)S(1)}, bf16[64,1152]{1,0:T(8,128)(2,1)S(1)}, u32[]{:S(2)}, u32[]{:S(2)}) collective-permute-start(bf16[64,1152]{1,0:T(8,128)(2,1)S(1)} %get-tuple-element.19), channel_id=1, source_target_pairs={{0,7},{1,0},{2,1},{3,2},{4,3},{5,4},{6,5},{7,6},{8,15},{9,8},{10,9... | collective-permute-start | bytes 442376 | tf_op jit(solution)/shard_map/ppermute | solution.py:20
  69.9 6.2 %collective-permute-start.10 = (bf16[64,1152]{1,0:T(8,128)(2,1)S(1)}, bf16[64,1152]{1,0:T(8,128)(2,1)S(1)}, u32[]{:S(2)}, u32[]{:S(2)}) collective-permute-start(bf16[64,1152]{1,0:T(8,128)(2,1)S(1)} %get-tuple-element.22), channel_id=1, source_target_pairs={{0,3},{1,4},{2,5},{3,6},{4,7},{5,0},{6,1},{7,2},{8,11},{9,12},{10,... | collective-permute-start | bytes 442376 | tf_op jit(solution)/shard_map/ppermute | solution.py:20
  76.1 4.0 %collective-permute-start.9 = (bf16[64,1152]{1,0:T(8,128)(2,1)S(1)}, bf16[64,1152]{1,0:T(8,128)(2,1)S(1)}, u32[]{:S(2)}, u32[]{:S(2)}) collective-permute-start(bf16[64,1152]{1,0:T(8,128)(2,1)S(1)} %get-tuple-element.18), channel_id=1, source_target_pairs={{0,4},{1,5},{2,6},{3,7},{4,0},{5,1},{6,2},{7,3},{8,12},{9,13},{10,... | collective-permute-start | bytes 442376 | tf_op jit(solution)/shard_map/ppermute | solution.py:20
  81.3 1.5 %collective-permute-start.15 = (bf16[64,1152]{1,0:T(8,128)(2,1)S(1)}, bf16[64,1152]{1,0:T(8,128)(2,1)S(1)}, u32[]{:S(2)}, u32[]{:S(2)}) collective-permute-start(bf16[64,1152]{1,0:T(8,128)(2,1)S(1)} %get-tuple-element.24), channel_id=1, source_target_pairs={{0,7},{1,0},{2,1},{3,2},{4,3},{5,4},{6,5},{7,6},{8,15},{9,8},{10,9... | collective-permute-start | bytes 442376 | tf_op jit(solution)/shard_map/ppermute | solution.py:20
  82.8 4.9 %collective-permute-done.10 = bf16[64,1152]{1,0:T(8,128)(2,1)S(1)} collective-permute-done((bf16[64,1152]{1,0:T(8,128)(2,1)S(1)}, bf16[64,1152]{1,0:T(8,128)(2,1)S(1)}, u32[]{:S(2)}, u32[]{:S(2)}) %collective-permute-start.10) | collective-permute-done | bytes 147488 | tf_op jit(solution)/shard_map/ppermute | solution.py:20
  87.7 10.3 %collective-permute-done.11 = bf16[64,1152]{1,0:T(8,128)(2,1)S(1)} collective-permute-done((bf16[64,1152]{1,0:T(8,128)(2,1)S(1)}, bf16[64,1152]{1,0:T(8,128)(2,1)S(1)}, u32[]{:S(2)}, u32[]{:S(2)}) %collective-permute-start.11) | collective-permute-done | bytes 147488 | tf_op jit(solution)/shard_map/ppermute | solution.py:20
  99.1 1.7 %shard_map.64 = f32[64,1152]{1,0:T(8,128)} custom-call(f32[2]{0:T(128)S(1)} %pad_maximum_fusion.scal, f32[64,1152]{1,0:T(8,128)S(1)} %copy-done.5, bf16[16,64,1152]{2,1,0:T(8,128)(2,1)S(1)} %all-to-all-done.1.got), custom_call_target="tpu_custom_call" | custom-call | bytes 1048576 | tf_op jit(solution)/shard_map/pallas_call | solution.py:134
  (37 shorter events, 6.0 us)
Async XLA Ops:
  0.6 1.0 copy-start.4
  3.3 7.6 %copy-start.2 = (f32[64,1152]{1,0:T(8,128)S(1)}, f32[64,1152]{1,0:T(8,128)}, u32[]{:S(2)}) copy-start(f32[64,1152]{1,0:T(8,128)} %raw.3) | copy-start | bytes 884740
  3.3 38.1 %all-to-all-start = ((bf16[16,64,1152]{2,1,0:T(8,128)(2,1)}), bf16[16,64,1152]{2,1,0:T(8,128)(2,1)S(1)}, u32[]{:S(2)}, u32[]{:S(2)}) async-start(bf16[16,64,1152]{2,1,0:T(8,128)(2,1)} %shard_map.59), calls=%async_computation | async-start | bytes 4718592 | tf_op jit(solution)/shard_map/all_to_all | solution.py:179
  11.0 5.3 %collective-permute-start = (bf16[64,1152]{1,0:T(8,128)(2,1)S(1)}, bf16[64,1152]{1,0:T(8,128)(2,1)S(1)}, u32[]{:S(2)}, u32[]{:S(2)}) collective-permute-start(bf16[64,1152]{1,0:T(8,128)(2,1)S(1)} %shard_map.60.refs_0_), channel_id=1, source_target_pairs={{0,7},{1,0},{2,1},{3,2},{4,3},{5,4},{6,5},{7,6},{8,15},{9,8},{10,9... | collective-permute-start | bytes 442376 | tf_op jit(solution)/shard_map/ppermute | solution.py:20
  11.2 9.0 %collective-permute-start.4 = (bf16[64,1152]{1,0:T(8,128)(2,1)S(1)}, bf16[64,1152]{1,0:T(8,128)(2,1)S(1)}, u32[]{:S(2)}, u32[]{:S(2)}) collective-permute-start(bf16[64,1152]{1,0:T(8,128)(2,1)S(1)} %shard_map.60.refs_0_), channel_id=1, source_target_pairs={{0,1},{1,2},{2,3},{3,4},{4,5},{5,6},{6,7},{7,0},{8,9},{9,10},{10,1... | collective-permute-start | bytes 442376 | tf_op jit(solution)/shard_map/ppermute | solution.py:20
  16.3 8.3 %collective-permute-start.1 = (bf16[64,1152]{1,0:T(8,128)(2,1)S(1)}, bf16[64,1152]{1,0:T(8,128)(2,1)S(1)}, u32[]{:S(2)}, u32[]{:S(2)}) collective-permute-start(bf16[64,1152]{1,0:T(8,128)(2,1)S(1)} %collective-permute-done.refs_1_), channel_id=1, source_target_pairs={{0,7},{1,0},{2,1},{3,2},{4,3},{5,4},{6,5},{7,6},{8,15},{9,8},{10,9... | collective-permute-start | bytes 442376 | tf_op jit(solution)/shard_map/ppermute | solution.py:20
  20.2 9.1 %collective-permute-start.5 = (bf16[64,1152]{1,0:T(8,128)(2,1)S(1)}, bf16[64,1152]{1,0:T(8,128)(2,1)S(1)}, u32[]{:S(2)}, u32[]{:S(2)}) collective-permute-start(bf16[64,1152]{1,0:T(8,128)(2,1)S(1)} %collective-permute-done.4.refs_7_), channel_id=1, source_target_pairs={{0,1},{1,2},{2,3},{3,4},{4,5},{5,6},{6,7},{7,0},{8,9},{9,10},{10,1... | collective-permute-start | bytes 442376 | tf_op jit(solution)/shard_map/ppermute | solution.py:20
  20.2 13.7 %collective-permute-start.3 = (bf16[64,1152]{1,0:T(8,128)(2,1)S(1)}, bf16[64,1152]{1,0:T(8,128)(2,1)S(1)}, u32[]{:S(2)}, u32[]{:S(2)}) collective-permute-start(bf16[64,1152]{1,0:T(8,128)(2,1)S(1)} %shard_map.60.refs_0_), channel_id=1, source_target_pairs={{0,4},{1,5},{2,6},{3,7},{4,0},{5,1},{6,2},{7,3},{8,12},{9,13},{10,... | collective-permute-start | bytes 442376 | tf_op jit(solution)/shard_map/ppermute | solution.py:20
  24.6 9.7 %collective-permute-start.2 = (bf16[64,1152]{1,0:T(8,128)(2,1)S(1)}, bf16[64,1152]{1,0:T(8,128)(2,1)S(1)}, u32[]{:S(2)}, u32[]{:S(2)}) collective-permute-start(bf16[64,1152]{1,0:T(8,128)(2,1)S(1)} %collective-permute-done.1.refs_2_), channel_id=1, source_target_pairs={{0,7},{1,0},{2,1},{3,2},{4,3},{5,4},{6,5},{7,6},{8,15},{9,8},{10,9... | collective-permute-start | bytes 442376 | tf_op jit(solution)/shard_map/ppermute | solution.py:20
  29.3 7.8 %collective-permute-start.6 = (bf16[64,1152]{1,0:T(8,128)(2,1)S(1)}, bf16[64,1152]{1,0:T(8,128)(2,1)S(1)}, u32[]{:S(2)}, u32[]{:S(2)}) collective-permute-start(bf16[64,1152]{1,0:T(8,128)(2,1)S(1)} %collective-permute-done.5.refs_6_), channel_id=1, source_target_pairs={{0,1},{1,2},{2,3},{3,4},{4,5},{5,6},{6,7},{7,0},{8,9},{9,10},{10,1... | collective-permute-start | bytes 442376 | tf_op jit(solution)/shard_map/ppermute | solution.py:20
  38.2 3.2 %collective-permute-start.7 = (bf16[512,1152]{1,0:T(8,128)(2,1)}, bf16[512,1152]{1,0:T(8,128)(2,1)}, u32[]{:S(2)}, u32[]{:S(2)}) collective-permute-start(bf16[512,1152]{1,0:T(8,128)(2,1)} %shard_map.61.xs), channel_id=1, source_target_pairs={{0,16},{16,0},{1,17},{17,1},{2,18},{18,2},{3,19},{19,3},{4,20},{20... | collective-permute-start | bytes 3538952 | tf_op jit(solution)/shard_map/ppermute | solution.py:20
  41.4 10.9 %copy-start = (bf16[16,64,1152]{2,1,0:T(8,128)(2,1)}, bf16[16,64,1152]{2,1,0:T(8,128)(2,1)S(1)}, u32[]{:S(2)}) copy-start(bf16[16,64,1152]{2,1,0:T(8,128)(2,1)S(1)} %all-to-all-done) | copy-start | bytes 7077892
  52.3 7.6 %collective-permute-start.8 = (bf16[512,1152]{1,0:T(8,128)(2,1)}, bf16[512,1152]{1,0:T(8,128)(2,1)}, u32[]{:S(2)}, u32[]{:S(2)}) collective-permute-start(bf16[512,1152]{1,0:T(8,128)(2,1)} %get-tuple-element.12), channel_id=1, source_target_pairs={{0,16},{16,0},{1,17},{17,1},{2,18},{18,2},{3,19},{19,3},{4,20},{20... | collective-permute-start | bytes 3538952 | tf_op jit(solution)/shard_map/ppermute | solution.py:20
  52.6 46.5 %all-to-all-start.1 = ((bf16[16,64,1152]{2,1,0:T(8,128)(2,1)}), bf16[16,64,1152]{2,1,0:T(8,128)(2,1)S(1)}, u32[]{:S(2)}, u32[]{:S(2)}) async-start(bf16[16,64,1152]{2,1,0:T(8,128)(2,1)} %bitcast.6), calls=%async_computation.1 | async-start | bytes 4718592 | tf_op jit(solution)/shard_map/all_to_all | solution.py:199
  59.9 1.7 %copy-start.1 = (bf16[16,64,1152]{2,1,0:T(8,128)(2,1)S(1)}, bf16[16,64,1152]{2,1,0:T(8,128)(2,1)}, u32[]{:S(2)}) copy-start(bf16[16,64,1152]{2,1,0:T(8,128)(2,1)} %copy-done) | copy-start | bytes 7077892
  61.6 1.6 %copy-start.3 = (bf16[1024,1024]{1,0:T(8,128)(2,1)S(1)}, bf16[1024,1024]{1,0:T(8,128)(2,1)}, u32[]{:S(2)}) copy-start(bf16[1024,1024]{1,0:T(8,128)(2,1)} %get-tuple-element.11.coeff) | copy-start | bytes 6291460
  66.5 32.6 %copy-start.5 = (f32[64,1152]{1,0:T(8,128)S(1)}, f32[64,1152]{1,0:T(8,128)}, u32[]{:S(2)}) copy-start(f32[64,1152]{1,0:T(8,128)} %raw.4) | copy-start | bytes 884740
  66.5 13.6 %collective-permute-start.12 = (bf16[64,1152]{1,0:T(8,128)(2,1)S(1)}, bf16[64,1152]{1,0:T(8,128)(2,1)S(1)}, u32[]{:S(2)}, u32[]{:S(2)}) collective-permute-start(bf16[64,1152]{1,0:T(8,128)(2,1)S(1)} %get-tuple-element.20), channel_id=1, source_target_pairs={{0,1},{1,2},{2,3},{3,4},{4,5},{5,6},{6,7},{7,0},{8,9},{9,10},{10,1... | collective-permute-start | bytes 442376 | tf_op jit(solution)/shard_map/ppermute | solution.py:20
  68.5 11.6 %collective-permute-start.14 = (bf16[64,1152]{1,0:T(8,128)(2,1)S(1)}, bf16[64,1152]{1,0:T(8,128)(2,1)S(1)}, u32[]{:S(2)}, u32[]{:S(2)}) collective-permute-start(bf16[64,1152]{1,0:T(8,128)(2,1)S(1)} %get-tuple-element.19), channel_id=1, source_target_pairs={{0,7},{1,0},{2,1},{3,2},{4,3},{5,4},{6,5},{7,6},{8,15},{9,8},{10,9... | collective-permute-start | bytes 442376 | tf_op jit(solution)/shard_map/ppermute | solution.py:20
  69.9 17.8 %collective-permute-start.10 = (bf16[64,1152]{1,0:T(8,128)(2,1)S(1)}, bf16[64,1152]{1,0:T(8,128)(2,1)S(1)}, u32[]{:S(2)}, u32[]{:S(2)}) collective-permute-start(bf16[64,1152]{1,0:T(8,128)(2,1)S(1)} %get-tuple-element.22), channel_id=1, source_target_pairs={{0,3},{1,4},{2,5},{3,6},{4,7},{5,0},{6,1},{7,2},{8,11},{9,12},{10,... | collective-permute-start | bytes 442376 | tf_op jit(solution)/shard_map/ppermute | solution.py:20
  76.1 21.9 %collective-permute-start.11 = (bf16[64,1152]{1,0:T(8,128)(2,1)S(1)}, bf16[64,1152]{1,0:T(8,128)(2,1)S(1)}, u32[]{:S(2)}, u32[]{:S(2)}) collective-permute-start(bf16[64,1152]{1,0:T(8,128)(2,1)S(1)} %get-tuple-element.21), channel_id=1, source_target_pairs={{0,5},{1,6},{2,7},{3,0},{4,1},{5,2},{6,3},{7,4},{8,13},{9,14},{10,... | collective-permute-start | bytes 442376 | tf_op jit(solution)/shard_map/ppermute | solution.py:20
  76.1 21.9 %collective-permute-start.9 = (bf16[64,1152]{1,0:T(8,128)(2,1)S(1)}, bf16[64,1152]{1,0:T(8,128)(2,1)S(1)}, u32[]{:S(2)}, u32[]{:S(2)}) collective-permute-start(bf16[64,1152]{1,0:T(8,128)(2,1)S(1)} %get-tuple-element.18), channel_id=1, source_target_pairs={{0,4},{1,5},{2,6},{3,7},{4,0},{5,1},{6,2},{7,3},{8,12},{9,13},{10,... | collective-permute-start | bytes 442376 | tf_op jit(solution)/shard_map/ppermute | solution.py:20
  80.2 17.8 %collective-permute-start.13 = (bf16[64,1152]{1,0:T(8,128)(2,1)S(1)}, bf16[64,1152]{1,0:T(8,128)(2,1)S(1)}, u32[]{:S(2)}, u32[]{:S(2)}) collective-permute-start(bf16[64,1152]{1,0:T(8,128)(2,1)S(1)} %get-tuple-element.23), channel_id=1, source_target_pairs={{0,1},{1,2},{2,3},{3,4},{4,5},{5,6},{6,7},{7,0},{8,9},{9,10},{10,1... | collective-permute-start | bytes 442376 | tf_op jit(solution)/shard_map/ppermute | solution.py:20
  81.3 16.7 %collective-permute-start.15 = (bf16[64,1152]{1,0:T(8,128)(2,1)S(1)}, bf16[64,1152]{1,0:T(8,128)(2,1)S(1)}, u32[]{:S(2)}, u32[]{:S(2)}) collective-permute-start(bf16[64,1152]{1,0:T(8,128)(2,1)S(1)} %get-tuple-element.24), channel_id=1, source_target_pairs={{0,7},{1,0},{2,1},{3,2},{4,3},{5,4},{6,5},{7,6},{8,15},{9,8},{10,9... | collective-permute-start | bytes 442376 | tf_op jit(solution)/shard_map/ppermute | solution.py:20

commit v8 on v7

--- a/solution.py
+++ b/solution.py
@@ -56,72 +56,68 @@
     return 1.0 / (1.0 + jnp.exp2(dots * (temp * -LOG2E) + offset * -LOG2E))
 
 
-def pair_kernel(place, scal, xs, xo, ts, coeff, dxo, dy, x, held, part, sems):
+def pair_kernel(place, scal, xs, xo, ts, dxs, dxo, dy, x, held, mine, theirs, part, sems):
     temp = scal[0]
     offset = scal[1]
     half = xs.shape[0]
     pooled = ts.shape[0]
-    steps = 4
-    step = pooled // steps
+    wide = 512
+    step = 256
     loads = [
         pltpu.make_async_copy(xs, x.at[0:half], sems.at[0]),
         pltpu.make_async_copy(xo, x.at[half : 2 * half], sems.at[1]),
     ]
     for copy in loads:
         copy.start()
-    for copy in loads:
+    for h, copy in enumerate(loads):
         copy.wait()
-    for j in range(steps):
-        sl = pl.ds(j * step, step)
-        dots = lax.dot_general(ts[sl], x[...], NT, preferred_element_type=F32)
-        held[sl] = sigmoid(temp, offset, dots).astype(BF)
+        cols = slice(h * half, (h + 1) * half)
+        for j in range(pooled // step):
+            sl = pl.ds(j * step, step)
+            dots = lax.dot_general(ts[sl], x[cols], NT, preferred_element_type=F32)
+            held[sl, cols] = sigmoid(temp, offset, dots).astype(BF)
     at = pl.multiple_of(place[0] * ROWS, ROWS)
     dots = lax.dot_general(ts[pl.ds(at, ROWS)], x[0:ROWS], NT, preferred_element_type=F32)
     eye = lax.broadcasted_iota(jnp.int32, (ROWS, ROWS), 0) == lax.broadcasted_iota(
         jnp.int32, (ROWS, ROWS), 1
     )
     held[pl.ds(at, ROWS), 0:ROWS] = (sigmoid(temp, offset, dots) - eye.astype(F32)).astype(BF)
-    copies = [pltpu.make_async_copy(held, coeff, sems.at[2])]
-    copies[0].start()
-    for j in range(steps):
-        sl = pl.ds(j * step, step)
-        part[sl] = jnp.dot(held[sl], x[...], preferred_element_type=F32).astype(BF)
-        copies.append(pltpu.make_async_copy(part.at[sl], dy.at[sl], sems.at[3 + j]))
+    copies = []
+
+    def send(src, dst):
+        copies.append(pltpu.make_async_copy(src, dst, sems.at[2 + len(copies)]))
         copies[-1].start()
-    wide = 256
-    for i in range(half // wide):
-        cols = slice(half + i * wide, half + (i + 1) * wide)
-        dots = lax.dot_general(held[:, cols], ts[...], TN, preferred_element_type=F32)
-        dxo[pl.ds(i * wide, wide)] = dots.astype(BF)
+
+    for h, (buf, out) in enumerate(((mine, dxs), (theirs, dxo))):
+        for i in range(0, half, wide):
+            cols = slice(h * half + i, h * half + i + wide)
+            dots = lax.dot_general(held[:, cols], ts[...], TN, preferred_element_type=F32)
+            buf[i : i + wide] = dots.astype(buf.dtype)
+            send(buf.at[i : i + wide], out.at[i : i + wide])
+    for j in range(0, pooled, step):
+        part[j : j + step] = jnp.dot(held[j : j + step], x[...], preferred_element_type=F32).astype(BF)
+        send(part.at[j : j + step], dy.at[j : j + step])
     for copy in copies:
         copy.wait()
 
 
-def image_kernel(coeff, ts, other, own, rest, held, sems):
-    wide = 256
-    n = other.shape[0] // wide
-    loads = []
-    for i in range(n):
-        cols = slice(i * wide, (i + 1) * wide)
-        loads.append(pltpu.make_async_copy(coeff.at[:, cols], held.at[:, cols], sems.at[i]))
-        loads[-1].start()
-    for i in range(n):
-        loads[i].wait()
-        part = lax.dot_general(held[:, i * wide : (i + 1) * wide], ts[...], TN, preferred_element_type=F32)
-        part += other[pl.ds(i * wide, wide)].astype(F32)
-        if i == 0:
-            own[...] = part[0:ROWS]
-            rest[0 : wide - ROWS] = part[ROWS:].astype(BF)
-        else:
-            rest[pl.ds(i * wide - ROWS, wide)] = part.astype(BF)
-
-
-def text_kernel(scal, raw, got, out):
-    total = got[0].astype(F32)
-    for k in range(1, got.shape[0]):
-        total += got[k].astype(F32)
-    unit, norm = to_unit(raw[...])
-    out[...] = from_unit(scal[0] * total, unit, norm)
+def join_kernel(dxs, other, own, rest):
+    own[...] = dxs[0:ROWS] + other[0:ROWS].astype(F32)
+    rest[...] = (dxs[ROWS:] + other[ROWS:].astype(F32)).astype(BF)
+
+
+def finish_kernel(scal, images, texts, dyr, own, *refs):
+    got, (out_images, out_texts) = refs[:-2], refs[-2:]
+    total = dyr[0].astype(F32)
+    for k in range(1, dyr.shape[0]):
+        total += dyr[k].astype(F32)
+    unit, norm = to_unit(texts[...])
+    out_texts[...] = from_unit(scal[0] * total, unit, norm)
+    total = own[...]
+    for part in got:
+        total += part[...].astype(F32)
+    unit, norm = to_unit(images[...])
+    out_images[...] = from_unit(scal[0] * total, unit, norm)
 
 
 VMEM = pl.BlockSpec(memory_space=pltpu.VMEM)
@@ -156,13 +152,11 @@
     return up + [far] + down[:0:-1]
 
 
-def near_reduce(own, rest):
+def near_reduce(rest):
     direct = [shifted(rest[k - 1], "z", k) for k in (4, 3, 5)]
     up, down = shifted(rest[1], "z", 1), shifted(rest[5], "z", -1)
     up, down = shifted(add(rest[0], up), "z", 1), shifted(add(rest[6], down), "z", -1)
-    for got in direct + [up, down]:
-        own = own + got.astype(F32)
-    return own
+    return direct + [up, down]
 
 
 def on_device(images, texts, log_temp, bias):
@@ -180,33 +174,33 @@
     (x,) = local(unit_kernel, [((rows, width), BF, VMEM)], [images])
     (xs,) = local(pack_kernel, [((half, width), BF, VMEM)], ring_gather(x))
     xo = shifted(xs, "core", 1)
-    img_unit, img_norm = to_unit(images)
     place = lax.axis_index(PLANE).astype(jnp.int32).reshape(1)
     scal = jnp.stack([temp, bias[0]])
     unit_flops = 2 * half * pooled * width
-    coeff, dxo, dy = local(
+    dxs, dxo, dy = local(
         pair_kernel,
-        [((pooled, 2 * half), BF, HBM), ((half, width), BF, VMEM), ((pooled, width), BF, HBM)],
+        [((half, width), F32, HBM), ((half, width), BF, HBM), ((pooled, width), BF, HBM)],
         [place, scal, xs, xo, ts], smem=2, hbm=2,
         scratch=[
             pltpu.VMEM((2 * half, width), BF),
             pltpu.VMEM((pooled, 2 * half), BF),
+            pltpu.VMEM((half, width), F32),
+            pltpu.VMEM((half, width), BF),
             pltpu.VMEM((pooled, width), BF),
-            pltpu.SemaphoreType.DMA((7,)),
+            pltpu.SemaphoreType.DMA((8,)),
         ],
-        flops=5 * unit_flops, nbytes=9 * 2**20, trans=4 * half * pooled, vmem=24,
+        flops=6 * unit_flops, nbytes=9 * 2**20, trans=4 * half * pooled, vmem=24,
     )
     dyr = lax.all_to_all(dy.reshape(n_plane, rows, width), PLANE, 0, 0, tiled=True)
     other = shifted(dxo, "core", 1)
     own, rest = local(
-        image_kernel,
-        [((rows, width), F32, VMEM), ((half - rows, width), BF, VMEM)],
-        [coeff, ts, other], hbm=1, vmem=16, flops=unit_flops, nbytes=6 * 2**20,
-        scratch=[pltpu.VMEM((pooled, half), BF), pltpu.SemaphoreType.DMA((half // 256,))],
-    )
-    image_sum = near_reduce(own, rest.reshape(-1, rows, width))
-    grad_images = from_unit(temp * image_sum, img_unit, img_norm)
-    (grad_texts,) = local(text_kernel, [((rows, width), F32, VMEM)], [scal, texts, dyr], smem=1, vmem=8)
+        join_kernel, [((rows, width), F32, VMEM), ((half - rows, width), BF, VMEM)], [dxs, other],
+        nbytes=5 * 2**20, vmem=16,
+    )
+    got = near_reduce(rest.reshape(-1, rows, width))
+    grad_images, grad_texts = local(
+        finish_kernel, [((rows, width), F32, VMEM)] * 2, [scal, images, texts, dyr, own] + got, smem=1, vmem=16
+    )
     return (grad_images, grad_texts)
 
 

time: 101 us -> 103 us (1.020)
  the two profiles are of different devices: /device:TPU:36 before, /device:TPU:8 now
where the time goes in v8:
time: 103 us; the launch traced here: 102 us
  starting transfers between devices  46.2 us (45%)
  waiting for transfers between devices  28.3 us (27%)
  Pallas kernels  18.2 us (18%)
  local copies, waits for them, and re-layouts  7.4 us (7%)
  between operations  2.07 us (2%)
    ppermute x16, starting transfers between devices, shifted(): lax.ppermute(block, axis, [(i, (i + distance) % n) for i in range(n)])  31.4 us
    ppermute x16, waiting for transfers between devices, shifted(): lax.ppermute(block, axis, [(i, (i + distance) % n) for i in range(n)])  28.2 us
    pallas_call x6, Pallas kernels, local(): pl.pallas_call(kernel, out_shape=tuple(((pltpu.HBM if spec is HBM else ja...  18.2 us
    all_to_all x1, starting transfers between devices, on_device(): ts = lax.all_to_all(spread, PLANE, 0, 0, tiled=True).reshape(pooled, width)  7.54 us
    unnamed x20, local copies, waits for them, and re-layouts  7.34 us
    all_to_all x1, starting transfers between devices, on_device(): lax.all_to_all(dy.reshape(n_plane, rows, width), PLANE, 0, 0, tiled=True)  7.3 us
  transfers between devices with their start and end apart: 18, of which 9 were waited for; matrix products, arithmetic and copies ran while one was open for 0% of the time, Pallas kernels for 3%

profile of v8, /device:TPU:8, one launch (start us, length us, event | category | flops | bytes accessed | tf_op | source)
XLA Modules:
  0.0 102.3 jit_solution(15062702395583912033)
XLA Ops:
  1.6 1.7 %shard_map.59 = bf16[16,64,1152]{2,1,0:T(8,128)(2,1)} custom-call(f32[64,1152]{1,0:T(8,128)S(1)} %copy-done.2), custom_call_target="tpu_custom_call" | custom-call | bytes 1048576 | tf_op jit(solution)/shard_map/pallas_call | solution.py:130
  3.3 7.5 %all-to-all-start = ((bf16[16,64,1152]{2,1,0:T(8,128)(2,1)}), bf16[16,64,1152]{2,1,0:T(8,128)(2,1)S(1)}, u32[]{:S(2)}, u32[]{:S(2)}) async-start(bf16[16,64,1152]{2,1,0:T(8,128)(2,1)} %shard_map.59), calls=%async_computation | async-start | bytes 4718592 | tf_op jit(solution)/shard_map/all_to_all | solution.py:173
  11.0 2.0 %collective-permute-start.4 = (bf16[64,1152]{1,0:T(8,128)(2,1)S(1)}, bf16[64,1152]{1,0:T(8,128)(2,1)S(1)}, u32[]{:S(2)}, u32[]{:S(2)}) collective-permute-start(bf16[64,1152]{1,0:T(8,128)(2,1)S(1)} %shard_map.60.refs_0_), channel_id=1, source_target_pairs={{0,1},{1,2},{2,3},{3,4},{4,5},{5,6},{6,7},{7,0},{8,9},{9,10},{10,1... | collective-permute-start | bytes 442376 | tf_op jit(solution)/shard_map/ppermute | solution.py:20
  13.0 4.0 %collective-permute-start = (bf16[64,1152]{1,0:T(8,128)(2,1)S(1)}, bf16[64,1152]{1,0:T(8,128)(2,1)S(1)}, u32[]{:S(2)}, u32[]{:S(2)}) collective-permute-start(bf16[64,1152]{1,0:T(8,128)(2,1)S(1)} %shard_map.60.refs_0_), channel_id=1, source_target_pairs={{0,7},{1,0},{2,1},{3,2},{4,3},{5,4},{6,5},{7,6},{8,15},{9,8},{10,9... | collective-permute-start | bytes 442376 | tf_op jit(solution)/shard_map/ppermute | solution.py:20
  17.0 3.2 %collective-permute-done.4.refs_7_ = bf16[64,1152]{1,0:T(8,128)(2,1)S(1)} collective-permute-done((bf16[64,1152]{1,0:T(8,128)(2,1)S(1)}, bf16[64,1152]{1,0:T(8,128)(2,1)S(1)}, u32[]{:S(2)}, u32[]{:S(2)}) %collective-permute-start.4) | collective-permute-done | bytes 147488 | tf_op jit(solution)/shard_map/ppermute | solution.py:20
  20.2 3.2 %collective-permute-start.1 = (bf16[64,1152]{1,0:T(8,128)(2,1)S(1)}, bf16[64,1152]{1,0:T(8,128)(2,1)S(1)}, u32[]{:S(2)}, u32[]{:S(2)}) collective-permute-start(bf16[64,1152]{1,0:T(8,128)(2,1)S(1)} %collective-permute-done.refs_1_), channel_id=1, source_target_pairs={{0,7},{1,0},{2,1},{3,2},{4,3},{5,4},{6,5},{7,6},{8,15},{9,8},{10,9... | collective-permute-start | bytes 442376 | tf_op jit(solution)/shard_map/ppermute | solution.py:20
  23.4 4.4 %collective-permute-start.3 = (bf16[64,1152]{1,0:T(8,128)(2,1)S(1)}, bf16[64,1152]{1,0:T(8,128)(2,1)S(1)}, u32[]{:S(2)}, u32[]{:S(2)}) collective-permute-start(bf16[64,1152]{1,0:T(8,128)(2,1)S(1)} %shard_map.60.refs_0_), channel_id=1, source_target_pairs={{0,4},{1,5},{2,6},{3,7},{4,0},{5,1},{6,2},{7,3},{8,12},{9,13},{10,... | collective-permute-start | bytes 442376 | tf_op jit(solution)/shard_map/ppermute | solution.py:20
  28.0 4.9 %collective-permute-done.1.refs_2_ = bf16[64,1152]{1,0:T(8,128)(2,1)S(1)} collective-permute-done((bf16[64,1152]{1,0:T(8,128)(2,1)S(1)}, bf16[64,1152]{1,0:T(8,128)(2,1)S(1)}, u32[]{:S(2)}, u32[]{:S(2)}) %collective-permute-start.1) | collective-permute-done | bytes 147488 | tf_op jit(solution)/shard_map/ppermute | solution.py:20
  32.9 3.8 %collective-permute-start.2 = (bf16[64,1152]{1,0:T(8,128)(2,1)S(1)}, bf16[64,1152]{1,0:T(8,128)(2,1)S(1)}, u32[]{:S(2)}, u32[]{:S(2)}) collective-permute-start(bf16[64,1152]{1,0:T(8,128)(2,1)S(1)} %collective-permute-done.1.refs_2_), channel_id=1, source_target_pairs={{0,7},{1,0},{2,1},{3,2},{4,3},{5,4},{6,5},{7,6},{8,15},{9,8},{10,9... | collective-permute-start | bytes 442376 | tf_op jit(solution)/shard_map/ppermute | solution.py:20
  36.8 2.7 %collective-permute-done.2.refs_3_ = bf16[64,1152]{1,0:T(8,128)(2,1)S(1)} collective-permute-done((bf16[64,1152]{1,0:T(8,128)(2,1)S(1)}, bf16[64,1152]{1,0:T(8,128)(2,1)S(1)}, u32[]{:S(2)}, u32[]{:S(2)}) %collective-permute-start.2) | collective-permute-done | bytes 147488 | tf_op jit(solution)/shard_map/ppermute | solution.py:20
  39.4 1.1 %shard_map.61.xs = bf16[512,1152]{1,0:T(8,128)(2,1)} custom-call(bf16[64,1152]{1,0:T(8,128)(2,1)S(1)} %shard_map.60.refs_0_, bf16[64,1152]{1,0:T(8,128)(2,1)S(1)} %collective-permute-done.refs_1_, bf16[64,1152]{1,0:T(8,128)(2,1)S(1)} %collective-permute-done.1.refs_2_, bf16[64,1152]{1,0:T(8,128)(2,1)S(1)} %collective-permute-done.2.refs_3_, ...), custom_call_target="tpu_custom_call" | custom-call | bytes 1048576 | tf_op jit(solution)/shard_map/pallas_call | solution.py:130
  42.0 1.8 %collective-permute-done.7.xo = bf16[512,1152]{1,0:T(8,128)(2,1)} collective-permute-done((bf16[512,1152]{1,0:T(8,128)(2,1)}, bf16[512,1152]{1,0:T(8,128)(2,1)}, u32[]{:S(2)}, u32[]{:S(2)}) %collective-permute-start.7) | collective-permute-done | bytes 1179680 | tf_op jit(solution)/shard_map/ppermute | solution.py:20
  43.8 11.8 %shard_map.62 = (f32[512,1152]{1,0:T(8,128)}, bf16[512,1152]{1,0:T(8,128)(2,1)}, bf16[1024,1152]{1,0:T(8,128)(2,1)}) custom-call(s32[1]{0:T(128)} %bitcast.place, f32[2]{0:T(128)S(1)} %pad_maximum_fusion.scal, bf16[512,1152]{1,0:T(8,128)(2,1)} %shard_map.61.xs, bf16[512,1152]{1,0:T(8,128)(2,1)} %collective-permute-done.7.xo, bf16[1024,1152]{1,0:T(8,128)(2,1)S(1)} %bitcast.3), custom_call_target="tpu_custom_call" | custom-call | flops 7247757312 | bytes 9437184 | tf_op jit(solution)/shard_map/pallas_call | solution.py:130
  55.8 7.3 %all-to-all-start.1 = ((bf16[16,64,1152]{2,1,0:T(8,128)(2,1)}), bf16[16,64,1152]{2,1,0:T(8,128)(2,1)S(1)}, u32[]{:S(2)}, u32[]{:S(2)}) async-start(bf16[16,64,1152]{2,1,0:T(8,128)(2,1)} %bitcast.4), calls=%async_computation.1 | async-start | bytes 4718592 | tf_op jit(solution)/shard_map/all_to_all | solution.py:194
  63.1 1.7 %copy-done = f32[512,1152]{1,0:T(8,128)S(1)} copy-done((f32[512,1152]{1,0:T(8,128)S(1)}, f32[512,1152]{1,0:T(8,128)}, u32[]{:S(2)}) %copy-start) | copy-done | bytes 2359320
  64.8 1.5 %shard_map.63 = (f32[64,1152]{1,0:T(8,128)S(1)}, bf16[448,1152]{1,0:T(8,128)(2,1)S(1)}) custom-call(f32[512,1152]{1,0:T(8,128)S(1)} %copy-done, bf16[512,1152]{1,0:T(8,128)(2,1)} %collective-permute-done.8.other), custom_call_target="tpu_custom_call" | custom-call | bytes 5242880 | tf_op jit(solution)/shard_map/pallas_call | solution.py:130
  66.3 3.7 %collective-permute-start.14 = (bf16[64,1152]{1,0:T(8,128)(2,1)S(1)}, bf16[64,1152]{1,0:T(8,128)(2,1)S(1)}, u32[]{:S(2)}, u32[]{:S(2)}) collective-permute-start(bf16[64,1152]{1,0:T(8,128)(2,1)S(1)} %get-tuple-element.18), channel_id=1, source_target_pairs={{0,7},{1,0},{2,1},{3,2},{4,3},{5,4},{6,5},{7,6},{8,15},{9,8},{10,9... | collective-permute-start | bytes 442376 | tf_op jit(solution)/shard_map/ppermute | solution.py:20
  70.1 2.7 %collective-permute-start.11 = (bf16[64,1152]{1,0:T(8,128)(2,1)S(1)}, bf16[64,1152]{1,0:T(8,128)(2,1)S(1)}, u32[]{:S(2)}, u32[]{:S(2)}) collective-permute-start(bf16[64,1152]{1,0:T(8,128)(2,1)S(1)} %get-tuple-element.20), channel_id=1, source_target_pairs={{0,5},{1,6},{2,7},{3,0},{4,1},{5,2},{6,3},{7,4},{8,13},{9,14},{10,... | collective-permute-start | bytes 442376 | tf_op jit(solution)/shard_map/ppermute | solution.py:20
  73.9 3.2 %collective-permute-start.9 = (bf16[64,1152]{1,0:T(8,128)(2,1)S(1)}, bf16[64,1152]{1,0:T(8,128)(2,1)S(1)}, u32[]{:S(2)}, u32[]{:S(2)}) collective-permute-start(bf16[64,1152]{1,0:T(8,128)(2,1)S(1)} %get-tuple-element.22), channel_id=1, source_target_pairs={{0,4},{1,5},{2,6},{3,7},{4,0},{5,1},{6,2},{7,3},{8,12},{9,13},{10,... | collective-permute-start | bytes 442376 | tf_op jit(solution)/shard_map/ppermute | solution.py:20
  77.2 3.0 %collective-permute-start.15 = (bf16[64,1152]{1,0:T(8,128)(2,1)S(1)}, bf16[64,1152]{1,0:T(8,128)(2,1)S(1)}, u32[]{:S(2)}, u32[]{:S(2)}) collective-permute-start(bf16[64,1152]{1,0:T(8,128)(2,1)S(1)} %get-tuple-element.16), channel_id=1, source_target_pairs={{0,7},{1,0},{2,1},{3,2},{4,3},{5,4},{6,5},{7,6},{8,15},{9,8},{10,9... | collective-permute-start | bytes 442376 | tf_op jit(solution)/shard_map/ppermute | solution.py:20
  80.1 9.6 %collective-permute-done.11.refs_2_ = bf16[64,1152]{1,0:T(8,128)(2,1)S(1)} collective-permute-done((bf16[64,1152]{1,0:T(8,128)(2,1)S(1)}, bf16[64,1152]{1,0:T(8,128)(2,1)S(1)}, u32[]{:S(2)}, u32[]{:S(2)}) %collective-permute-start.11) | collective-permute-done | bytes 147488 | tf_op jit(solution)/shard_map/ppermute | solution.py:20
  91.2 1.8 %collective-permute-done.15.refs_4_ = bf16[64,1152]{1,0:T(8,128)(2,1)S(1)} collective-permute-done((bf16[64,1152]{1,0:T(8,128)(2,1)S(1)}, bf16[64,1152]{1,0:T(8,128)(2,1)S(1)}, u32[]{:S(2)}, u32[]{:S(2)}) %collective-permute-start.15) | collective-permute-done | bytes 147488 | tf_op jit(solution)/shard_map/ppermute | solution.py:20
  93.7 3.3 %collective-permute-done.13.refs_3_ = bf16[64,1152]{1,0:T(8,128)(2,1)S(1)} collective-permute-done((bf16[64,1152]{1,0:T(8,128)(2,1)S(1)}, bf16[64,1152]{1,0:T(8,128)(2,1)S(1)}, u32[]{:S(2)}, u32[]{:S(2)}) %collective-permute-start.13) | collective-permute-done | bytes 147488 | tf_op jit(solution)/shard_map/ppermute | solution.py:20
  100.4 1.9 %shard_map.64 = (f32[64,1152]{1,0:T(8,128)}, f32[64,1152]{1,0:T(8,128)}) custom-call(f32[2]{0:T(128)S(1)} %pad_maximum_fusion.scal, f32[64,1152]{1,0:T(8,128)S(1)} %copy-done.1, f32[64,1152]{1,0:T(8,128)S(1)} %copy-done.3, bf16[16,64,1152]{2,1,0:T(8,128)(2,1)S(1)} %all-to-all-done.1.dyr, f32[64,1152]{1,0:T(8,128)S(1)} %get-tuple-element.14.own, ...), custom_call_target="tpu_custom_call" | custom-call | bytes 1048576 | tf_op jit(solution)/shard_map/pallas_call | solution.py:130
  (41 shorter events, 8.4 us)
Async XLA Ops:
  0.6 1.0 copy-start.2
  3.3 7.5 %copy-start.1 = (f32[64,1152]{1,0:T(8,128)S(1)}, f32[64,1152]{1,0:T(8,128)}, u32[]{:S(2)}) copy-start(f32[64,1152]{1,0:T(8,128)} %images) | copy-start | bytes 884740
  3.3 40.5 %all-to-all-start = ((bf16[16,64,1152]{2,1,0:T(8,128)(2,1)}), bf16[16,64,1152]{2,1,0:T(8,128)(2,1)S(1)}, u32[]{:S(2)}, u32[]{:S(2)}) async-start(bf16[16,64,1152]{2,1,0:T(8,128)(2,1)} %shard_map.59), calls=%async_computation | async-start | bytes 4718592 | tf_op jit(solution)/shard_map/all_to_all | solution.py:173
  11.0 9.2 %collective-permute-start.4 = (bf16[64,1152]{1,0:T(8,128)(2,1)S(1)}, bf16[64,1152]{1,0:T(8,128)(2,1)S(1)}, u32[]{:S(2)}, u32[]{:S(2)}) collective-permute-start(bf16[64,1152]{1,0:T(8,128)(2,1)S(1)} %shard_map.60.refs_0_), channel_id=1, source_target_pairs={{0,1},{1,2},{2,3},{3,4},{4,5},{5,6},{6,7},{7,0},{8,9},{9,10},{10,1... | collective-permute-start | bytes 442376 | tf_op jit(solution)/shard_map/ppermute | solution.py:20
  13.0 7.2 %collective-permute-start = (bf16[64,1152]{1,0:T(8,128)(2,1)S(1)}, bf16[64,1152]{1,0:T(8,128)(2,1)S(1)}, u32[]{:S(2)}, u32[]{:S(2)}) collective-permute-start(bf16[64,1152]{1,0:T(8,128)(2,1)S(1)} %shard_map.60.refs_0_), channel_id=1, source_target_pairs={{0,7},{1,0},{2,1},{3,2},{4,3},{5,4},{6,5},{7,6},{8,15},{9,8},{10,9... | collective-permute-start | bytes 442376 | tf_op jit(solution)/shard_map/ppermute | solution.py:20
  20.2 7.9 %collective-permute-start.5 = (bf16[64,1152]{1,0:T(8,128)(2,1)S(1)}, bf16[64,1152]{1,0:T(8,128)(2,1)S(1)}, u32[]{:S(2)}, u32[]{:S(2)}) collective-permute-start(bf16[64,1152]{1,0:T(8,128)(2,1)S(1)} %collective-permute-done.4.refs_7_), channel_id=1, source_target_pairs={{0,1},{1,2},{2,3},{3,4},{4,5},{5,6},{6,7},{7,0},{8,9},{9,10},{10,1... | collective-permute-start | bytes 442376 | tf_op jit(solution)/shard_map/ppermute | solution.py:20
  20.2 12.7 %collective-permute-start.1 = (bf16[64,1152]{1,0:T(8,128)(2,1)S(1)}, bf16[64,1152]{1,0:T(8,128)(2,1)S(1)}, u32[]{:S(2)}, u32[]{:S(2)}) collective-permute-start(bf16[64,1152]{1,0:T(8,128)(2,1)S(1)} %collective-permute-done.refs_1_), channel_id=1, source_target_pairs={{0,7},{1,0},{2,1},{3,2},{4,3},{5,4},{6,5},{7,6},{8,15},{9,8},{10,9... | collective-permute-start | bytes 442376 | tf_op jit(solution)/shard_map/ppermute | solution.py:20
  23.4 13.3 %collective-permute-start.3 = (bf16[64,1152]{1,0:T(8,128)(2,1)S(1)}, bf16[64,1152]{1,0:T(8,128)(2,1)S(1)}, u32[]{:S(2)}, u32[]{:S(2)}) collective-permute-start(bf16[64,1152]{1,0:T(8,128)(2,1)S(1)} %shard_map.60.refs_0_), channel_id=1, source_target_pairs={{0,4},{1,5},{2,6},{3,7},{4,0},{5,1},{6,2},{7,3},{8,12},{9,13},{10,... | collective-permute-start | bytes 442376 | tf_op jit(solution)/shard_map/ppermute | solution.py:20
  28.0 8.7 %collective-permute-start.6 = (bf16[64,1152]{1,0:T(8,128)(2,1)S(1)}, bf16[64,1152]{1,0:T(8,128)(2,1)S(1)}, u32[]{:S(2)}, u32[]{:S(2)}) collective-permute-start(bf16[64,1152]{1,0:T(8,128)(2,1)S(1)} %collective-permute-done.5.refs_6_), channel_id=1, source_target_pairs={{0,1},{1,2},{2,3},{3,4},{4,5},{5,6},{6,7},{7,0},{8,9},{9,10},{10,1... | collective-permute-start | bytes 442376 | tf_op jit(solution)/shard_map/ppermute | solution.py:20
  32.9 6.5 %collective-permute-start.2 = (bf16[64,1152]{1,0:T(8,128)(2,1)S(1)}, bf16[64,1152]{1,0:T(8,128)(2,1)S(1)}, u32[]{:S(2)}, u32[]{:S(2)}) collective-permute-start(bf16[64,1152]{1,0:T(8,128)(2,1)S(1)} %collective-permute-done.1.refs_2_), channel_id=1, source_target_pairs={{0,7},{1,0},{2,1},{3,2},{4,3},{5,4},{6,5},{7,6},{8,15},{9,8},{10,9... | collective-permute-start | bytes 442376 | tf_op jit(solution)/shard_map/ppermute | solution.py:20
  40.5 3.2 %collective-permute-start.7 = (bf16[512,1152]{1,0:T(8,128)(2,1)}, bf16[512,1152]{1,0:T(8,128)(2,1)}, u32[]{:S(2)}, u32[]{:S(2)}) collective-permute-start(bf16[512,1152]{1,0:T(8,128)(2,1)} %shard_map.61.xs), channel_id=1, source_target_pairs={{0,16},{16,0},{1,17},{17,1},{2,18},{18,2},{3,19},{19,3},{4,20},{20... | collective-permute-start | bytes 3538952 | tf_op jit(solution)/shard_map/ppermute | solution.py:20
  55.6 7.5 %collective-permute-start.8 = (bf16[512,1152]{1,0:T(8,128)(2,1)}, bf16[512,1152]{1,0:T(8,128)(2,1)}, u32[]{:S(2)}, u32[]{:S(2)}) collective-permute-start(bf16[512,1152]{1,0:T(8,128)(2,1)} %get-tuple-element.13), channel_id=1, source_target_pairs={{0,16},{16,0},{1,17},{17,1},{2,18},{18,2},{3,19},{19,3},{4,20},{20... | collective-permute-start | bytes 3538952 | tf_op jit(solution)/shard_map/ppermute | solution.py:20
  55.8 41.8 %all-to-all-start.1 = ((bf16[16,64,1152]{2,1,0:T(8,128)(2,1)}), bf16[16,64,1152]{2,1,0:T(8,128)(2,1)S(1)}, u32[]{:S(2)}, u32[]{:S(2)}) async-start(bf16[16,64,1152]{2,1,0:T(8,128)(2,1)} %bitcast.4), calls=%async_computation.1 | async-start | bytes 4718592 | tf_op jit(solution)/shard_map/all_to_all | solution.py:194
  63.1 1.7 %copy-start = (f32[512,1152]{1,0:T(8,128)S(1)}, f32[512,1152]{1,0:T(8,128)}, u32[]{:S(2)}) copy-start(f32[512,1152]{1,0:T(8,128)} %get-tuple-element.12.dxs) | copy-start | bytes 7077892
  64.8 32.9 %copy-start.3 = (f32[64,1152]{1,0:T(8,128)S(1)}, f32[64,1152]{1,0:T(8,128)}, u32[]{:S(2)}) copy-start(f32[64,1152]{1,0:T(8,128)} %texts.1) | copy-start | bytes 884740
  66.3 10.7 %collective-permute-start.14 = (bf16[64,1152]{1,0:T(8,128)(2,1)S(1)}, bf16[64,1152]{1,0:T(8,128)(2,1)S(1)}, u32[]{:S(2)}, u32[]{:S(2)}) collective-permute-start(bf16[64,1152]{1,0:T(8,128)(2,1)S(1)} %get-tuple-element.18), channel_id=1, source_target_pairs={{0,7},{1,0},{2,1},{3,2},{4,3},{5,4},{6,5},{7,6},{8,15},{9,8},{10,9... | collective-permute-start | bytes 442376 | tf_op jit(solution)/shard_map/ppermute | solution.py:20
  70.1 7.0 %collective-permute-start.12 = (bf16[64,1152]{1,0:T(8,128)(2,1)S(1)}, bf16[64,1152]{1,0:T(8,128)(2,1)S(1)}, u32[]{:S(2)}, u32[]{:S(2)}) collective-permute-start(bf16[64,1152]{1,0:T(8,128)(2,1)S(1)} %get-tuple-element.19), channel_id=1, source_target_pairs={{0,1},{1,2},{2,3},{3,4},{4,5},{5,6},{6,7},{7,0},{8,9},{9,10},{10,1... | collective-permute-start | bytes 442376 | tf_op jit(solution)/shard_map/ppermute | solution.py:20
  70.1 19.7 %collective-permute-start.11 = (bf16[64,1152]{1,0:T(8,128)(2,1)S(1)}, bf16[64,1152]{1,0:T(8,128)(2,1)S(1)}, u32[]{:S(2)}, u32[]{:S(2)}) collective-permute-start(bf16[64,1152]{1,0:T(8,128)(2,1)S(1)} %get-tuple-element.20), channel_id=1, source_target_pairs={{0,5},{1,6},{2,7},{3,0},{4,1},{5,2},{6,3},{7,4},{8,13},{9,14},{10,... | collective-permute-start | bytes 442376 | tf_op jit(solution)/shard_map/ppermute | solution.py:20
  72.8 17.0 %collective-permute-start.10 = (bf16[64,1152]{1,0:T(8,128)(2,1)S(1)}, bf16[64,1152]{1,0:T(8,128)(2,1)S(1)}, u32[]{:S(2)}, u32[]{:S(2)}) collective-permute-start(bf16[64,1152]{1,0:T(8,128)(2,1)S(1)} %get-tuple-element.21), channel_id=1, source_target_pairs={{0,3},{1,4},{2,5},{3,6},{4,7},{5,0},{6,1},{7,2},{8,11},{9,12},{10,... | collective-permute-start | bytes 442376 | tf_op jit(solution)/shard_map/ppermute | solution.py:20
  73.9 16.6 %collective-permute-start.9 = (bf16[64,1152]{1,0:T(8,128)(2,1)S(1)}, bf16[64,1152]{1,0:T(8,128)(2,1)S(1)}, u32[]{:S(2)}, u32[]{:S(2)}) collective-permute-start(bf16[64,1152]{1,0:T(8,128)(2,1)S(1)} %get-tuple-element.22), channel_id=1, source_target_pairs={{0,4},{1,5},{2,6},{3,7},{4,0},{5,1},{6,2},{7,3},{8,12},{9,13},{10,... | collective-permute-start | bytes 442376 | tf_op jit(solution)/shard_map/ppermute | solution.py:20
  77.2 15.8 %collective-permute-start.15 = (bf16[64,1152]{1,0:T(8,128)(2,1)S(1)}, bf16[64,1152]{1,0:T(8,128)(2,1)S(1)}, u32[]{:S(2)}, u32[]{:S(2)}) collective-permute-start(bf16[64,1152]{1,0:T(8,128)(2,1)S(1)} %get-tuple-element.16), channel_id=1, source_target_pairs={{0,7},{1,0},{2,1},{3,2},{4,3},{5,4},{6,5},{7,6},{8,15},{9,8},{10,9... | collective-permute-start | bytes 442376 | tf_op jit(solution)/shard_map/ppermute | solution.py:20
  80.1 16.8 %collective-permute-start.13 = (bf16[64,1152]{1,0:T(8,128)(2,1)S(1)}, bf16[64,1152]{1,0:T(8,128)(2,1)S(1)}, u32[]{:S(2)}, u32[]{:S(2)}) collective-permute-start(bf16[64,1152]{1,0:T(8,128)(2,1)S(1)} %get-tuple-element.17), channel_id=1, source_target_pairs={{0,1},{1,2},{2,3},{3,4},{4,5},{5,6},{6,7},{7,0},{8,9},{9,10},{10,1... | collective-permute-start | bytes 442376 | tf_op jit(solution)/shard_map/ppermute | solution.py:20
  97.6 0.9 copy-start.5
  98.5 0.9 copy-start.7
  (4 other events, 2.9 us)

commit v9 on v8

--- a/solution.py
+++ b/solution.py
@@ -1,5 +1,6 @@
 import jax
 import jax.numpy as jnp
+import numpy as np
 from jax import lax
 from jax.experimental import pallas as pl
 from jax.experimental.pallas import tpu as pltpu
@@ -13,6 +14,26 @@
 ROWS = 64
 NT = (((1,), (1,)), ((), ()))
 TN = (((0,), (0,)), ((), ()))
+
+
+def plane_groups():
+    at = np.arange(256).reshape(2, 4, 2, 2, 8)
+    along_x, along_y = [], []
+    for core in range(2):
+        along_x.append(at[:, :, core].transpose(0, 2, 3, 1).reshape(-1, 4).tolist())
+        along_y.append(at[:, :, core].transpose(1, 3, 0, 2).reshape(-1, 4).tolist())
+    whole = at[:, :, 0].transpose(3, 0, 2, 1).reshape(-1, 16).tolist()
+    whole += at[:, :, 1].transpose(3, 1, 0, 2).reshape(-1, 16).tolist()
+    outer = along_y[0] + along_x[1]
+    inner = along_x[0] + along_y[1]
+    return whole, outer, inner
+
+
+WHOLE, OUTER, INNER = plane_groups()
+
+
+def swapped(blocks, groups):
+    return lax.all_to_all(blocks, AXES, 0, 0, axis_index_groups=groups, tiled=True)
 
 
 def shifted(block, axis, distance):
@@ -106,18 +127,20 @@
     rest[...] = (dxs[ROWS:] + other[ROWS:].astype(F32)).astype(BF)
 
 
-def finish_kernel(scal, images, texts, dyr, own, *refs):
-    got, (out_images, out_texts) = refs[:-2], refs[-2:]
-    total = dyr[0].astype(F32)
-    for k in range(1, dyr.shape[0]):
-        total += dyr[k].astype(F32)
-    unit, norm = to_unit(texts[...])
-    out_texts[...] = from_unit(scal[0] * total, unit, norm)
-    total = own[...]
-    for part in got:
+def finish_kernel(scal, raw, *refs):
+    total = refs[0][...].astype(F32)
+    for part in refs[1:-1]:
         total += part[...].astype(F32)
-    unit, norm = to_unit(images[...])
-    out_images[...] = from_unit(scal[0] * total, unit, norm)
+    unit, norm = to_unit(raw[...])
+    refs[-1][...] = from_unit(scal[0] * total, unit, norm)
+
+
+def finish_texts_kernel(scal, raw, got, out):
+    total = got[0].astype(F32)
+    for k in range(1, got.shape[0]):
+        total += got[k].astype(F32)
+    unit, norm = to_unit(raw[...])
+    out[...] = from_unit(scal[0] * total, unit, norm)
 
 
 VMEM = pl.BlockSpec(memory_space=pltpu.VMEM)
@@ -170,11 +193,12 @@
         scratch=[pltpu.VMEM((rows, width), BF), pltpu.SemaphoreType.DMA((n_plane,))],
     )
     spread, images = lax.optimization_barrier((spread, images))
-    ts = lax.all_to_all(spread, PLANE, 0, 0, tiled=True).reshape(pooled, width)
+    ts = swapped(spread, WHOLE).reshape(pooled, width)
     (x,) = local(unit_kernel, [((rows, width), BF, VMEM)], [images])
     (xs,) = local(pack_kernel, [((half, width), BF, VMEM)], ring_gather(x))
     xo = shifted(xs, "core", 1)
-    place = lax.axis_index(PLANE).astype(jnp.int32).reshape(1)
+    at_x, at_y = lax.axis_index("x"), lax.axis_index(("yh", "yl"))
+    place = jnp.where(lax.axis_index("core") == 0, 4 * at_y + at_x, 4 * at_x + at_y).astype(jnp.int32).reshape(1)
     scal = jnp.stack([temp, bias[0]])
     unit_flops = 2 * half * pooled * width
     dxs, dxo, dy = local(
@@ -191,16 +215,17 @@
         ],
         flops=6 * unit_flops, nbytes=9 * 2**20, trans=4 * half * pooled, vmem=24,
     )
-    dyr = lax.all_to_all(dy.reshape(n_plane, rows, width), PLANE, 0, 0, tiled=True)
+    half_way = swapped(dy.reshape(4, 4 * rows, width), OUTER)
+    half_way = jnp.sum(half_way.astype(F32), axis=0).astype(BF)
+    dyr = swapped(half_way.reshape(4, rows, width), INNER)
     other = shifted(dxo, "core", 1)
     own, rest = local(
         join_kernel, [((rows, width), F32, VMEM), ((half - rows, width), BF, VMEM)], [dxs, other],
         nbytes=5 * 2**20, vmem=16,
     )
     got = near_reduce(rest.reshape(-1, rows, width))
-    grad_images, grad_texts = local(
-        finish_kernel, [((rows, width), F32, VMEM)] * 2, [scal, images, texts, dyr, own] + got, smem=1, vmem=16
-    )
+    (grad_images,) = local(finish_kernel, [((rows, width), F32, VMEM)], [scal, images, own] + got, smem=1)
+    (grad_texts,) = local(finish_texts_kernel, [((rows, width), F32, VMEM)], [scal, texts, dyr], smem=1)
     return (grad_images, grad_texts)
 
 

time: 103 us -> 103 us (level)
  starting transfers between devices: 46.2 us -> 55.4 us
  local copies, waits for them, and re-layouts: 7.4 us -> 1.05 us
  waiting for transfers between devices: 28.3 us -> 23.1 us
  other arithmetic: 0.15 us -> 4.12 us
  Pallas kernels: 18.2 us -> 15.9 us
    ppermute x16, waiting for transfers between devices: 28.2 us -> 20 us  [shifted(): lax.ppermute(block, axis, [(i, (i + distance) % n) for i in range(n)])]
    unnamed x20 -> x16, local copies, waits for them, and re-layouts: 7.34 us -> 0.99 us
    ppermute x16, starting transfers between devices: 31.4 us -> 37.1 us  [shifted(): lax.ppermute(block, axis, [(i, (i + distance) % n) for i in range(n)])]
    all_to_all x2 -> x3, starting transfers between devices: 14.8 us -> 18.4 us  [swapped(): lax.all_to_all(blocks, AXES, 0, 0, axis_index_groups=groups, tiled=True)]
    all_to_all x2 -> x3, waiting for transfers between devices: 0.05 us -> 3.15 us  [swapped(): lax.all_to_all(blocks, AXES, 0, 0, axis_index_groups=groups, tiled=True)]
    reduce_sum x0 -> x1, other arithmetic: none -> 2.99 us  [on_device(): half_way = jnp.sum(half_way.astype(F32), axis=0).astype(BF)]
    pallas_call x6 -> x7, Pallas kernels: 18.2 us -> 15.9 us  [local(): pl.pallas_call(kernel, out_shape=tuple(((pltpu.HBM if spec is HBM else ja...]
  transfers between devices with their start and end apart: 18 -> 19, of which waited for: 9 -> 8; matrix products, arithmetic and copies ran while one was open for 0% -> 4% of each run, Pallas kernels for 3% -> 2%
where the time goes in v9:
time: 103 us; the launch traced here: 102 us
  starting transfers between devices  55.4 us (54%)
  waiting for transfers between devices  23.1 us (22%)
  Pallas kernels  15.9 us (15%)
  other arithmetic  4.12 us (4%)
  between operations  2.12 us (2%)
  local copies, waits for them, and re-layouts  1.05 us (1%)
    ppermute x16, starting transfers between devices, shifted(): lax.ppermute(block, axis, [(i, (i + distance) % n) for i in range(n)])  37.1 us
    ppermute x16, waiting for transfers between devices, shifted(): lax.ppermute(block, axis, [(i, (i + distance) % n) for i in range(n)])  20 us
    all_to_all x3, starting transfers between devices, swapped(): lax.all_to_all(blocks, AXES, 0, 0, axis_index_groups=groups, tiled=True)  18.4 us
    pallas_call x7, Pallas kernels, local(): pl.pallas_call(kernel, out_shape=tuple(((pltpu.HBM if spec is HBM else ja...  15.9 us
    all_to_all x3, waiting for transfers between devices, swapped(): lax.all_to_all(blocks, AXES, 0, 0, axis_index_groups=groups, tiled=True)  3.15 us
    reduce_sum x1, other arithmetic, on_device(): half_way = jnp.sum(half_way.astype(F32), axis=0).astype(BF)  2.99 us
  transfers between devices with their start and end apart: 19, of which 8 were waited for; matrix products, arithmetic and copies ran while one was open for 4% of the time, Pallas kernels for 2%

profile of v9, /device:TPU:8, one launch (start us, length us, event | category | flops | bytes accessed | tf_op | source)
XLA Modules:
  0.0 101.7 jit_solution(907839916395612582)
XLA Ops:
  1.6 1.6 %shard_map.59 = bf16[16,64,1152]{2,1,0:T(8,128)(2,1)} custom-call(f32[64,1152]{1,0:T(8,128)S(1)} %copy-done.3), custom_call_target="tpu_custom_call" | custom-call | bytes 1048576 | tf_op jit(solution)/shard_map/pallas_call | solution.py:153
  3.3 7.5 %all-to-all-start = ((bf16[16,64,1152]{2,1,0:T(8,128)(2,1)}), bf16[16,64,1152]{2,1,0:T(8,128)(2,1)S(1)}, u32[]{:S(2)}, u32[]{:S(2)}) async-start(bf16[16,64,1152]{2,1,0:T(8,128)(2,1)} %shard_map.59), calls=%async_computation | async-start | bytes 4718592 | tf_op jit(solution)/shard_map/all_to_all | solution.py:36
  10.9 2.0 %collective-permute-start.4 = (bf16[64,1152]{1,0:T(8,128)(2,1)S(1)}, bf16[64,1152]{1,0:T(8,128)(2,1)S(1)}, u32[]{:S(2)}, u32[]{:S(2)}) collective-permute-start(bf16[64,1152]{1,0:T(8,128)(2,1)S(1)} %shard_map.60.refs_0_), channel_id=1, source_target_pairs={{0,1},{1,2},{2,3},{3,4},{4,5},{5,6},{6,7},{7,0},{8,9},{9,10},{10,1... | collective-permute-start | bytes 442376 | tf_op jit(solution)/shard_map/ppermute | solution.py:41
  12.9 4.0 %collective-permute-start = (bf16[64,1152]{1,0:T(8,128)(2,1)S(1)}, bf16[64,1152]{1,0:T(8,128)(2,1)S(1)}, u32[]{:S(2)}, u32[]{:S(2)}) collective-permute-start(bf16[64,1152]{1,0:T(8,128)(2,1)S(1)} %shard_map.60.refs_0_), channel_id=1, source_target_pairs={{0,7},{1,0},{2,1},{3,2},{4,3},{5,4},{6,5},{7,6},{8,15},{9,8},{10,9... | collective-permute-start | bytes 442376 | tf_op jit(solution)/shard_map/ppermute | solution.py:41
  17.0 3.2 %collective-permute-done.4.refs_7_ = bf16[64,1152]{1,0:T(8,128)(2,1)S(1)} collective-permute-done((bf16[64,1152]{1,0:T(8,128)(2,1)S(1)}, bf16[64,1152]{1,0:T(8,128)(2,1)S(1)}, u32[]{:S(2)}, u32[]{:S(2)}) %collective-permute-start.4) | collective-permute-done | bytes 147488 | tf_op jit(solution)/shard_map/ppermute | solution.py:41
  20.2 3.2 %collective-permute-start.1 = (bf16[64,1152]{1,0:T(8,128)(2,1)S(1)}, bf16[64,1152]{1,0:T(8,128)(2,1)S(1)}, u32[]{:S(2)}, u32[]{:S(2)}) collective-permute-start(bf16[64,1152]{1,0:T(8,128)(2,1)S(1)} %collective-permute-done.refs_1_), channel_id=1, source_target_pairs={{0,7},{1,0},{2,1},{3,2},{4,3},{5,4},{6,5},{7,6},{8,15},{9,8},{10,9... | collective-permute-start | bytes 442376 | tf_op jit(solution)/shard_map/ppermute | solution.py:41
  23.4 4.4 %collective-permute-start.3 = (bf16[64,1152]{1,0:T(8,128)(2,1)S(1)}, bf16[64,1152]{1,0:T(8,128)(2,1)S(1)}, u32[]{:S(2)}, u32[]{:S(2)}) collective-permute-start(bf16[64,1152]{1,0:T(8,128)(2,1)S(1)} %shard_map.60.refs_0_), channel_id=1, source_target_pairs={{0,4},{1,5},{2,6},{3,7},{4,0},{5,1},{6,2},{7,3},{8,12},{9,13},{10,... | collective-permute-start | bytes 442376 | tf_op jit(solution)/shard_map/ppermute | solution.py:41
  28.0 4.9 %collective-permute-done.1.refs_2_ = bf16[64,1152]{1,0:T(8,128)(2,1)S(1)} collective-permute-done((bf16[64,1152]{1,0:T(8,128)(2,1)S(1)}, bf16[64,1152]{1,0:T(8,128)(2,1)S(1)}, u32[]{:S(2)}, u32[]{:S(2)}) %collective-permute-start.1) | collective-permute-done | bytes 147488 | tf_op jit(solution)/shard_map/ppermute | solution.py:41
  32.9 3.8 %collective-permute-start.2 = (bf16[64,1152]{1,0:T(8,128)(2,1)S(1)}, bf16[64,1152]{1,0:T(8,128)(2,1)S(1)}, u32[]{:S(2)}, u32[]{:S(2)}) collective-permute-start(bf16[64,1152]{1,0:T(8,128)(2,1)S(1)} %collective-permute-done.1.refs_2_), channel_id=1, source_target_pairs={{0,7},{1,0},{2,1},{3,2},{4,3},{5,4},{6,5},{7,6},{8,15},{9,8},{10,9... | collective-permute-start | bytes 442376 | tf_op jit(solution)/shard_map/ppermute | solution.py:41
  36.8 2.7 %collective-permute-done.2.refs_3_ = bf16[64,1152]{1,0:T(8,128)(2,1)S(1)} collective-permute-done((bf16[64,1152]{1,0:T(8,128)(2,1)S(1)}, bf16[64,1152]{1,0:T(8,128)(2,1)S(1)}, u32[]{:S(2)}, u32[]{:S(2)}) %collective-permute-start.2) | collective-permute-done | bytes 147488 | tf_op jit(solution)/shard_map/ppermute | solution.py:41
  41.2 1.5 %collective-permute-done.7.xo = bf16[512,1152]{1,0:T(8,128)(2,1)} collective-permute-done((bf16[512,1152]{1,0:T(8,128)(2,1)S(1)}, bf16[512,1152]{1,0:T(8,128)(2,1)}, u32[]{:S(2)}, u32[]{:S(2)}) %collective-permute-start.7) | collective-permute-done | bytes 1179680 | tf_op jit(solution)/shard_map/ppermute | solution.py:41
  42.8 10.8 %shard_map.62 = (f32[512,1152]{1,0:T(8,128)}, bf16[512,1152]{1,0:T(8,128)(2,1)}, bf16[1024,1152]{1,0:T(8,128)(2,1)}) custom-call(s32[1]{0:T(128)} %bitcast.place, f32[2]{0:T(128)S(1)} %pad_maximum_fusion.scal, bf16[512,1152]{1,0:T(8,128)(2,1)S(1)} %shard_map.61.xs, bf16[512,1152]{1,0:T(8,128)(2,1)} %collective-permute-done.7.xo, bf16[1024,1152]{1,0:T(8,128)(2,1)S(1)} %bitcast.4), custom_call_target="tpu_custom_call" | custom-call | flops 7247757312 | bytes 9437184 | tf_op jit(solution)/shard_map/pallas_call | solution.py:153
  53.8 7.2 %all-to-all-start.1 = ((bf16[4,256,1152]{2,1,0:T(8,128)(2,1)}), bf16[4,256,1152]{2,1,0:T(8,128)(2,1)}, u32[]{:S(2)}, u32[]{:S(2)}) async-start(bf16[4,256,1152]{2,1,0:T(8,128)(2,1)} %bitcast.5), calls=%async_computation.1 | async-start | bytes 4718592 | tf_op jit(solution)/shard_map/all_to_all | solution.py:36
  61.3 5.9 %collective-permute-start.14 = (bf16[64,1152]{1,0:T(8,128)(2,1)S(1)}, bf16[64,1152]{1,0:T(8,128)(2,1)S(1)}, u32[]{:S(2)}, u32[]{:S(2)}) collective-permute-start(bf16[64,1152]{1,0:T(8,128)(2,1)S(1)} %get-tuple-element.18), channel_id=1, source_target_pairs={{0,7},{1,0},{2,1},{3,2},{4,3},{5,4},{6,5},{7,6},{8,15},{9,8},{10,9... | collective-permute-start | bytes 442376 | tf_op jit(solution)/shard_map/ppermute | solution.py:41
  67.3 2.9 %collective-permute-start.11 = (bf16[64,1152]{1,0:T(8,128)(2,1)S(1)}, bf16[64,1152]{1,0:T(8,128)(2,1)S(1)}, u32[]{:S(2)}, u32[]{:S(2)}) collective-permute-start(bf16[64,1152]{1,0:T(8,128)(2,1)S(1)} %get-tuple-element.20), channel_id=1, source_target_pairs={{0,5},{1,6},{2,7},{3,0},{4,1},{5,2},{6,3},{7,4},{8,13},{9,14},{10,... | collective-permute-start | bytes 442376 | tf_op jit(solution)/shard_map/ppermute | solution.py:41
  71.1 3.4 %collective-permute-start.9 = (bf16[64,1152]{1,0:T(8,128)(2,1)S(1)}, bf16[64,1152]{1,0:T(8,128)(2,1)S(1)}, u32[]{:S(2)}, u32[]{:S(2)}) collective-permute-start(bf16[64,1152]{1,0:T(8,128)(2,1)S(1)} %get-tuple-element.22), channel_id=1, source_target_pairs={{0,4},{1,5},{2,6},{3,7},{4,0},{5,1},{6,2},{7,3},{8,12},{9,13},{10,... | collective-permute-start | bytes 442376 | tf_op jit(solution)/shard_map/ppermute | solution.py:41
  74.5 3.1 %all-to-all-done.1 = bf16[4,256,1152]{2,1,0:T(8,128)(2,1)} async-done(((bf16[4,256,1152]{2,1,0:T(8,128)(2,1)}), bf16[4,256,1152]{2,1,0:T(8,128)(2,1)}, u32[]{:S(2)}, u32[]{:S(2)}) %all-to-all-start.1) | async-done | bytes 2359328 | tf_op jit(solution)/shard_map/all_to_all | solution.py:36
  77.6 3.0 %reduce_sum.12 = bf16[256,1152]{1,0:T(8,128)(2,1)} reduce(bf16[4,256,1152]{2,1,0:T(8,128)(2,1)} %all-to-all-done.1, bf16[]{:T(256)} %constant.27.clone.1), dimensions={0}, to_apply=%region_0.1 | reduce | flops 884736 | bytes 2949122 | tf_op jit(solution)/shard_map/reduce_sum | solution.py:219
  80.6 3.6 %all-to-all-start.2 = ((bf16[4,64,1152]{2,1,0:T(8,128)(2,1)}), bf16[4,64,1152]{2,1,0:T(8,128)(2,1)S(1)}, u32[]{:S(2)}, u32[]{:S(2)}) async-start(bf16[4,64,1152]{2,1,0:T(8,128)(2,1)} %bitcast.3), calls=%async_computation.2 | async-start | bytes 1179648 | tf_op jit(solution)/shard_map/all_to_all | solution.py:36
  85.3 5.9 %collective-permute-start.15 = (bf16[64,1152]{1,0:T(8,128)(2,1)S(1)}, bf16[64,1152]{1,0:T(8,128)(2,1)S(1)}, u32[]{:S(2)}, u32[]{:S(2)}) collective-permute-start(bf16[64,1152]{1,0:T(8,128)(2,1)S(1)} %get-tuple-element.16), channel_id=1, source_target_pairs={{0,7},{1,0},{2,1},{3,2},{4,3},{5,4},{6,5},{7,6},{8,15},{9,8},{10,9... | collective-permute-start | bytes 442376 | tf_op jit(solution)/shard_map/ppermute | solution.py:41
  91.2 4.0 %collective-permute-done.15.refs_5_ = bf16[64,1152]{1,0:T(8,128)(2,1)S(1)} collective-permute-done((bf16[64,1152]{1,0:T(8,128)(2,1)S(1)}, bf16[64,1152]{1,0:T(8,128)(2,1)S(1)}, u32[]{:S(2)}, u32[]{:S(2)}) %collective-permute-start.15) | collective-permute-done | bytes 147488 | tf_op jit(solution)/shard_map/ppermute | solution.py:41
  95.2 3.4 %collective-permute-done.13.refs_4_ = bf16[64,1152]{1,0:T(8,128)(2,1)S(1)} collective-permute-done((bf16[64,1152]{1,0:T(8,128)(2,1)S(1)}, bf16[64,1152]{1,0:T(8,128)(2,1)S(1)}, u32[]{:S(2)}, u32[]{:S(2)}) %collective-permute-start.13) | collective-permute-done | bytes 147488 | tf_op jit(solution)/shard_map/ppermute | solution.py:41
  98.7 1.5 %shard_map.64 = f32[64,1152]{1,0:T(8,128)} custom-call(f32[2]{0:T(128)S(1)} %pad_maximum_fusion.scal, f32[64,1152]{1,0:T(8,128)S(1)} %copy-done.2, f32[64,1152]{1,0:T(8,128)S(1)} %copy-done.7, bf16[64,1152]{1,0:T(8,128)(2,1)S(1)} %collective-permute-done.9.refs_1_, bf16[64,1152]{1,0:T(8,128)(2,1)S(1)} %collective-permute-done.10.refs_2_, ...), custom_call_target="tpu_custom_call" | custom-call | bytes 1048576 | tf_op jit(solution)/shard_map/pallas_call | solution.py:153
  100.2 1.5 %shard_map.65 = f32[64,1152]{1,0:T(8,128)} custom-call(f32[2]{0:T(128)S(1)} %pad_maximum_fusion.scal, f32[64,1152]{1,0:T(8,128)S(1)} %copy-done.4, bf16[4,64,1152]{2,1,0:T(8,128)(2,1)S(1)} %all-to-all-done.2.got), custom_call_target="tpu_custom_call" | custom-call | bytes 1048576 | tf_op jit(solution)/shard_map/pallas_call | solution.py:153
  (41 shorter events, 4.3 us)
Async XLA Ops:
  3.3 39.5 %all-to-all-start = ((bf16[16,64,1152]{2,1,0:T(8,128)(2,1)}), bf16[16,64,1152]{2,1,0:T(8,128)(2,1)S(1)}, u32[]{:S(2)}, u32[]{:S(2)}) async-start(bf16[16,64,1152]{2,1,0:T(8,128)(2,1)} %shard_map.59), calls=%async_computation | async-start | bytes 4718592 | tf_op jit(solution)/shard_map/all_to_all | solution.py:36
  10.9 9.2 %collective-permute-start.4 = (bf16[64,1152]{1,0:T(8,128)(2,1)S(1)}, bf16[64,1152]{1,0:T(8,128)(2,1)S(1)}, u32[]{:S(2)}, u32[]{:S(2)}) collective-permute-start(bf16[64,1152]{1,0:T(8,128)(2,1)S(1)} %shard_map.60.refs_0_), channel_id=1, source_target_pairs={{0,1},{1,2},{2,3},{3,4},{4,5},{5,6},{6,7},{7,0},{8,9},{9,10},{10,1... | collective-permute-start | bytes 442376 | tf_op jit(solution)/shard_map/ppermute | solution.py:41
  12.9 7.2 %collective-permute-start = (bf16[64,1152]{1,0:T(8,128)(2,1)S(1)}, bf16[64,1152]{1,0:T(8,128)(2,1)S(1)}, u32[]{:S(2)}, u32[]{:S(2)}) collective-permute-start(bf16[64,1152]{1,0:T(8,128)(2,1)S(1)} %shard_map.60.refs_0_), channel_id=1, source_target_pairs={{0,7},{1,0},{2,1},{3,2},{4,3},{5,4},{6,5},{7,6},{8,15},{9,8},{10,9... | collective-permute-start | bytes 442376 | tf_op jit(solution)/shard_map/ppermute | solution.py:41
  20.2 7.8 %collective-permute-start.5 = (bf16[64,1152]{1,0:T(8,128)(2,1)S(1)}, bf16[64,1152]{1,0:T(8,128)(2,1)S(1)}, u32[]{:S(2)}, u32[]{:S(2)}) collective-permute-start(bf16[64,1152]{1,0:T(8,128)(2,1)S(1)} %collective-permute-done.4.refs_7_), channel_id=1, source_target_pairs={{0,1},{1,2},{2,3},{3,4},{4,5},{5,6},{6,7},{7,0},{8,9},{9,10},{10,1... | collective-permute-start | bytes 442376 | tf_op jit(solution)/shard_map/ppermute | solution.py:41
  20.2 12.8 %collective-permute-start.1 = (bf16[64,1152]{1,0:T(8,128)(2,1)S(1)}, bf16[64,1152]{1,0:T(8,128)(2,1)S(1)}, u32[]{:S(2)}, u32[]{:S(2)}) collective-permute-start(bf16[64,1152]{1,0:T(8,128)(2,1)S(1)} %collective-permute-done.refs_1_), channel_id=1, source_target_pairs={{0,7},{1,0},{2,1},{3,2},{4,3},{5,4},{6,5},{7,6},{8,15},{9,8},{10,9... | collective-permute-start | bytes 442376 | tf_op jit(solution)/shard_map/ppermute | solution.py:41
  23.4 13.4 %collective-permute-start.3 = (bf16[64,1152]{1,0:T(8,128)(2,1)S(1)}, bf16[64,1152]{1,0:T(8,128)(2,1)S(1)}, u32[]{:S(2)}, u32[]{:S(2)}) collective-permute-start(bf16[64,1152]{1,0:T(8,128)(2,1)S(1)} %shard_map.60.refs_0_), channel_id=1, source_target_pairs={{0,4},{1,5},{2,6},{3,7},{4,0},{5,1},{6,2},{7,3},{8,12},{9,13},{10,... | collective-permute-start | bytes 442376 | tf_op jit(solution)/shard_map/ppermute | solution.py:41
  28.0 8.8 %collective-permute-start.6 = (bf16[64,1152]{1,0:T(8,128)(2,1)S(1)}, bf16[64,1152]{1,0:T(8,128)(2,1)S(1)}, u32[]{:S(2)}, u32[]{:S(2)}) collective-permute-start(bf16[64,1152]{1,0:T(8,128)(2,1)S(1)} %collective-permute-done.5.refs_6_), channel_id=1, source_target_pairs={{0,1},{1,2},{2,3},{3,4},{4,5},{5,6},{6,7},{7,0},{8,9},{9,10},{10,1... | collective-permute-start | bytes 442376 | tf_op jit(solution)/shard_map/ppermute | solution.py:41
  32.9 6.5 %collective-permute-start.2 = (bf16[64,1152]{1,0:T(8,128)(2,1)S(1)}, bf16[64,1152]{1,0:T(8,128)(2,1)S(1)}, u32[]{:S(2)}, u32[]{:S(2)}) collective-permute-start(bf16[64,1152]{1,0:T(8,128)(2,1)S(1)} %collective-permute-done.1.refs_2_), channel_id=1, source_target_pairs={{0,7},{1,0},{2,1},{3,2},{4,3},{5,4},{6,5},{7,6},{8,15},{9,8},{10,9... | collective-permute-start | bytes 442376 | tf_op jit(solution)/shard_map/ppermute | solution.py:41
  39.5 3.2 %collective-permute-start.7 = (bf16[512,1152]{1,0:T(8,128)(2,1)S(1)}, bf16[512,1152]{1,0:T(8,128)(2,1)}, u32[]{:S(2)}, u32[]{:S(2)}) collective-permute-start(bf16[512,1152]{1,0:T(8,128)(2,1)S(1)} %shard_map.61.xs), channel_id=1, source_target_pairs={{0,16},{16,0},{1,17},{17,1},{2,18},{18,2},{3,19},{19,3},{4,20},{20... | collective-permute-start | bytes 3538952 | tf_op jit(solution)/shard_map/ppermute | solution.py:41
  53.6 7.4 %collective-permute-start.8 = (bf16[512,1152]{1,0:T(8,128)(2,1)}, bf16[512,1152]{1,0:T(8,128)(2,1)S(1)}, u32[]{:S(2)}, u32[]{:S(2)}) collective-permute-start(bf16[512,1152]{1,0:T(8,128)(2,1)} %get-tuple-element.12), channel_id=1, source_target_pairs={{0,16},{16,0},{1,17},{17,1},{2,18},{18,2},{3,19},{19,3},{4,20},{20... | collective-permute-start | bytes 3538952 | tf_op jit(solution)/shard_map/ppermute | solution.py:41
  53.8 23.8 %all-to-all-start.1 = ((bf16[4,256,1152]{2,1,0:T(8,128)(2,1)}), bf16[4,256,1152]{2,1,0:T(8,128)(2,1)}, u32[]{:S(2)}, u32[]{:S(2)}) async-start(bf16[4,256,1152]{2,1,0:T(8,128)(2,1)} %bitcast.5), calls=%async_computation.1 | async-start | bytes 4718592 | tf_op jit(solution)/shard_map/all_to_all | solution.py:36
  61.2 9.9 %copy-start.5 = (bf16[448,1152]{1,0:T(8,128)(2,1)}, bf16[448,1152]{1,0:T(8,128)(2,1)S(1)}, u32[]{:S(2)}) copy-start(bf16[448,1152]{1,0:T(8,128)(2,1)S(1)} %get-tuple-element.14) | copy-start | bytes 3096580
  61.2 9.9 %copy-start.6 = (f32[64,1152]{1,0:T(8,128)}, f32[64,1152]{1,0:T(8,128)S(1)}, u32[]{:S(2)}) copy-start(f32[64,1152]{1,0:T(8,128)S(1)} %get-tuple-element.13.refs_0_) | copy-start | bytes 884740
  61.3 22.9 %collective-permute-start.14 = (bf16[64,1152]{1,0:T(8,128)(2,1)S(1)}, bf16[64,1152]{1,0:T(8,128)(2,1)S(1)}, u32[]{:S(2)}, u32[]{:S(2)}) collective-permute-start(bf16[64,1152]{1,0:T(8,128)(2,1)S(1)} %get-tuple-element.18), channel_id=1, source_target_pairs={{0,7},{1,0},{2,1},{3,2},{4,3},{5,4},{6,5},{7,6},{8,15},{9,8},{10,9... | collective-permute-start | bytes 442376 | tf_op jit(solution)/shard_map/ppermute | solution.py:41
  67.3 16.9 %collective-permute-start.12 = (bf16[64,1152]{1,0:T(8,128)(2,1)S(1)}, bf16[64,1152]{1,0:T(8,128)(2,1)S(1)}, u32[]{:S(2)}, u32[]{:S(2)}) collective-permute-start(bf16[64,1152]{1,0:T(8,128)(2,1)S(1)} %get-tuple-element.19), channel_id=1, source_target_pairs={{0,1},{1,2},{2,3},{3,4},{4,5},{5,6},{6,7},{7,0},{8,9},{9,10},{10,1... | collective-permute-start | bytes 442376 | tf_op jit(solution)/shard_map/ppermute | solution.py:41
  67.3 24.0 %collective-permute-start.11 = (bf16[64,1152]{1,0:T(8,128)(2,1)S(1)}, bf16[64,1152]{1,0:T(8,128)(2,1)S(1)}, u32[]{:S(2)}, u32[]{:S(2)}) collective-permute-start(bf16[64,1152]{1,0:T(8,128)(2,1)S(1)} %get-tuple-element.20), channel_id=1, source_target_pairs={{0,5},{1,6},{2,7},{3,0},{4,1},{5,2},{6,3},{7,4},{8,13},{9,14},{10,... | collective-permute-start | bytes 442376 | tf_op jit(solution)/shard_map/ppermute | solution.py:41
  70.2 21.1 %collective-permute-start.10 = (bf16[64,1152]{1,0:T(8,128)(2,1)S(1)}, bf16[64,1152]{1,0:T(8,128)(2,1)S(1)}, u32[]{:S(2)}, u32[]{:S(2)}) collective-permute-start(bf16[64,1152]{1,0:T(8,128)(2,1)S(1)} %get-tuple-element.21), channel_id=1, source_target_pairs={{0,3},{1,4},{2,5},{3,6},{4,7},{5,0},{6,1},{7,2},{8,11},{9,12},{10,... | collective-permute-start | bytes 442376 | tf_op jit(solution)/shard_map/ppermute | solution.py:41
  71.1 27.6 %copy-start.2 = (f32[64,1152]{1,0:T(8,128)S(1)}, f32[64,1152]{1,0:T(8,128)}, u32[]{:S(2)}) copy-start(f32[64,1152]{1,0:T(8,128)} %raw.4) | copy-start | bytes 884740
  71.1 20.1 %collective-permute-start.9 = (bf16[64,1152]{1,0:T(8,128)(2,1)S(1)}, bf16[64,1152]{1,0:T(8,128)(2,1)S(1)}, u32[]{:S(2)}, u32[]{:S(2)}) collective-permute-start(bf16[64,1152]{1,0:T(8,128)(2,1)S(1)} %get-tuple-element.22), channel_id=1, source_target_pairs={{0,4},{1,5},{2,6},{3,7},{4,0},{5,1},{6,2},{7,3},{8,12},{9,13},{10,... | collective-permute-start | bytes 442376 | tf_op jit(solution)/shard_map/ppermute | solution.py:41
  74.4 24.2 %copy-start.7 = (f32[64,1152]{1,0:T(8,128)S(1)}, f32[64,1152]{1,0:T(8,128)}, u32[]{:S(2)}) copy-start(f32[64,1152]{1,0:T(8,128)} %copy-done.6) | copy-start | bytes 884740
  80.6 19.6 %copy-start.4 = (f32[64,1152]{1,0:T(8,128)S(1)}, f32[64,1152]{1,0:T(8,128)}, u32[]{:S(2)}) copy-start(f32[64,1152]{1,0:T(8,128)} %raw.5) | copy-start | bytes 884740
  80.6 19.6 %all-to-all-start.2 = ((bf16[4,64,1152]{2,1,0:T(8,128)(2,1)}), bf16[4,64,1152]{2,1,0:T(8,128)(2,1)S(1)}, u32[]{:S(2)}, u32[]{:S(2)}) async-start(bf16[4,64,1152]{2,1,0:T(8,128)(2,1)} %bitcast.3), calls=%async_computation.2 | async-start | bytes 1179648 | tf_op jit(solution)/shard_map/all_to_all | solution.py:36
  85.3 10.0 %collective-permute-start.15 = (bf16[64,1152]{1,0:T(8,128)(2,1)S(1)}, bf16[64,1152]{1,0:T(8,128)(2,1)S(1)}, u32[]{:S(2)}, u32[]{:S(2)}) collective-permute-start(bf16[64,1152]{1,0:T(8,128)(2,1)S(1)} %get-tuple-element.16), channel_id=1, source_target_pairs={{0,7},{1,0},{2,1},{3,2},{4,3},{5,4},{6,5},{7,6},{8,15},{9,8},{10,9... | collective-permute-start | bytes 442376 | tf_op jit(solution)/shard_map/ppermute | solution.py:41
  91.2 7.4 %collective-permute-start.13 = (bf16[64,1152]{1,0:T(8,128)(2,1)S(1)}, bf16[64,1152]{1,0:T(8,128)(2,1)S(1)}, u32[]{:S(2)}, u32[]{:S(2)}) collective-permute-start(bf16[64,1152]{1,0:T(8,128)(2,1)S(1)} %get-tuple-element.17), channel_id=1, source_target_pairs={{0,1},{1,2},{2,3},{3,4},{4,5},{5,6},{6,7},{7,0},{8,9},{9,10},{10,1... | collective-permute-start | bytes 442376 | tf_op jit(solution)/shard_map/ppermute | solution.py:41
  (3 other events, 15.7 us)

commit v10 on v9

--- a/solution.py
+++ b/solution.py
@@ -135,6 +135,19 @@
     refs[-1][...] = from_unit(scal[0] * total, unit, norm)
 
 
+def sum_kernel(got, out, part, sems):
+    copies = []
+    for j in range(out.shape[0]):
+        total = got[0, j].astype(F32)
+        for k in range(1, got.shape[0]):
+            total += got[k, j].astype(F32)
+        part[j] = total.astype(BF)
+        copies.append(pltpu.make_async_copy(part.at[j], out.at[j], sems.at[j]))
+        copies[-1].start()
+    for copy in copies:
+        copy.wait()
+
+
 def finish_texts_kernel(scal, raw, got, out):
     total = got[0].astype(F32)
     for k in range(1, got.shape[0]):
@@ -165,21 +178,20 @@
     return (a.astype(F32) + b.astype(F32)).astype(BF)
 
 
-def ring_gather(block):
+def ring_gather(block, scalars):
     far = shifted(block, "z", 4)
     up = [block]
     down = [block]
-    for _ in range(3):
+    for k in range(3):
         up.append(shifted(up[-1], "z", -1))
         down.append(shifted(down[-1], "z", 1))
-    return up + [far] + down[:0:-1]
-
-
-def near_reduce(rest):
-    direct = [shifted(rest[k - 1], "z", k) for k in (4, 3, 5)]
-    up, down = shifted(rest[1], "z", 1), shifted(rest[5], "z", -1)
-    up, down = shifted(add(rest[0], up), "z", 1), shifted(add(rest[6], down), "z", -1)
-    return direct + [up, down]
+        if k == 0:
+            up[-1], scalars = lax.optimization_barrier((up[-1], scalars))
+    return up + [far] + down[:0:-1], scalars
+
+
+def direct_reduce(rest):
+    return [shifted(rest[k - 1], "z", k) for k in (4, 3, 5, 2, 6, 1, 7)]
 
 
 def on_device(images, texts, log_temp, bias):
@@ -195,11 +207,12 @@
     spread, images = lax.optimization_barrier((spread, images))
     ts = swapped(spread, WHOLE).reshape(pooled, width)
     (x,) = local(unit_kernel, [((rows, width), BF, VMEM)], [images])
-    (xs,) = local(pack_kernel, [((half, width), BF, VMEM)], ring_gather(x))
-    xo = shifted(xs, "core", 1)
     at_x, at_y = lax.axis_index("x"), lax.axis_index(("yh", "yl"))
     place = jnp.where(lax.axis_index("core") == 0, 4 * at_y + at_x, 4 * at_x + at_y).astype(jnp.int32).reshape(1)
     scal = jnp.stack([temp, bias[0]])
+    blocks, (place, scal) = ring_gather(x, (place, scal))
+    (xs,) = local(pack_kernel, [((half, width), BF, VMEM)], blocks)
+    xo = shifted(xs, "core", 1)
     unit_flops = 2 * half * pooled * width
     dxs, dxo, dy = local(
         pair_kernel,
@@ -216,14 +229,17 @@
         flops=6 * unit_flops, nbytes=9 * 2**20, trans=4 * half * pooled, vmem=24,
     )
     half_way = swapped(dy.reshape(4, 4 * rows, width), OUTER)
-    half_way = jnp.sum(half_way.astype(F32), axis=0).astype(BF)
-    dyr = swapped(half_way.reshape(4, rows, width), INNER)
+    (half_way,) = local(
+        sum_kernel, [((4, rows, width), BF, HBM)], [half_way.reshape(4, 4, rows, width)], nbytes=3 * 2**20, vmem=16,
+        scratch=[pltpu.VMEM((4, rows, width), BF), pltpu.SemaphoreType.DMA((4,))],
+    )
+    dyr = swapped(half_way, INNER)
     other = shifted(dxo, "core", 1)
     own, rest = local(
         join_kernel, [((rows, width), F32, VMEM), ((half - rows, width), BF, VMEM)], [dxs, other],
         nbytes=5 * 2**20, vmem=16,
     )
-    got = near_reduce(rest.reshape(-1, rows, width))
+    got = direct_reduce(rest.reshape(-1, rows, width))
     (grad_images,) = local(finish_kernel, [((rows, width), F32, VMEM)], [scal, images, own] + got, smem=1)
     (grad_texts,) = local(finish_texts_kernel, [((rows, width), F32, VMEM)], [scal, texts, dyr], smem=1)
     return (grad_images, grad_texts)

time: 103 us -> 121 us (1.17)
  the two profiles are of different devices: /device:TPU:8 before, /device:TPU:49 now
where the time goes in v10:
time: 121 us
  waiting for transfers between devices  48 us (40%)
  starting transfers between devices  43.1 us (36%)
  Pallas kernels  17.1 us (14%)
  local copies, waits for them, and re-layouts  10.5 us (9%)
  between operations  2.11 us (2%)
    ppermute x16, waiting for transfers between devices, shifted(): lax.ppermute(block, axis, [(i, (i + distance) % n) for i in range(n)])  37.5 us
    ppermute x16, starting transfers between devices, shifted(): lax.ppermute(block, axis, [(i, (i + distance) % n) for i in range(n)])  27.8 us
    pallas_call x8, Pallas kernels, local(): pl.pallas_call(kernel, out_shape=tuple(((pltpu.HBM if spec is HBM else ja...  17.1 us
    all_to_all x3, starting transfers between devices, swapped(): lax.all_to_all(blocks, AXES, 0, 0, axis_index_groups=groups, tiled=True)  15.3 us
    all_to_all x3, waiting for transfers between devices, swapped(): lax.all_to_all(blocks, AXES, 0, 0, axis_index_groups=groups, tiled=True)  10.5 us
    unnamed x32, local copies, waits for them, and re-layouts  10.4 us
  transfers between devices with their start and end apart: 19, of which 12 were waited for; matrix products, arithmetic and copies ran while one was open for 0% of the time, Pallas kernels for 2%

profile of v10, /device:TPU:49, one launch (start us, length us, event | category | flops | bytes accessed | tf_op | source)
XLA Modules:
  0.0 120.8 jit_solution(1291944029536792600)
XLA Ops:
  1.6 1.7 %shard_map.59 = bf16[16,64,1152]{2,1,0:T(8,128)(2,1)} custom-call(f32[64,1152]{1,0:T(8,128)S(1)} %copy-done.3), custom_call_target="tpu_custom_call" | custom-call | bytes 1048576 | tf_op jit(solution)/shard_map/pallas_call | solution.py:166
  3.3 6.9 %all-to-all-start = ((bf16[16,64,1152]{2,1,0:T(8,128)(2,1)}), bf16[16,64,1152]{2,1,0:T(8,128)(2,1)S(1)}, u32[]{:S(2)}, u32[]{:S(2)}) async-start(bf16[16,64,1152]{2,1,0:T(8,128)(2,1)} %shard_map.59), calls=%async_computation | async-start | bytes 4718592 | tf_op jit(solution)/shard_map/all_to_all | solution.py:36
  10.4 1.7 %collective-permute-start.4 = (bf16[64,1152]{1,0:T(8,128)(2,1)S(1)}, bf16[64,1152]{1,0:T(8,128)(2,1)S(1)}, u32[]{:S(2)}, u32[]{:S(2)}) collective-permute-start(bf16[64,1152]{1,0:T(8,128)(2,1)S(1)} %shard_map.60.refs_0_), channel_id=1, source_target_pairs={{0,1},{1,2},{2,3},{3,4},{4,5},{5,6},{6,7},{7,0},{8,9},{9,10},{10,1... | collective-permute-start | bytes 442376 | tf_op jit(solution)/shard_map/ppermute | solution.py:41
  14.9 3.8 %collective-permute-done.4.refs_7_ = bf16[64,1152]{1,0:T(8,128)(2,1)S(1)} collective-permute-done((bf16[64,1152]{1,0:T(8,128)(2,1)S(1)}, bf16[64,1152]{1,0:T(8,128)(2,1)S(1)}, u32[]{:S(2)}, u32[]{:S(2)}) %collective-permute-start.4) | collective-permute-done | bytes 147488 | tf_op jit(solution)/shard_map/ppermute | solution.py:41
  19.3 2.7 %collective-permute-start.1 = (bf16[64,1152]{1,0:T(8,128)(2,1)S(1)}, bf16[64,1152]{1,0:T(8,128)(2,1)S(1)}, u32[]{:S(2)}, u32[]{:S(2)}) collective-permute-start(bf16[64,1152]{1,0:T(8,128)(2,1)S(1)} %collective-permute-done.refs_1_), channel_id=1, source_target_pairs={{0,7},{1,0},{2,1},{3,2},{4,3},{5,4},{6,5},{7,6},{8,15},{9,8},{10,9... | collective-permute-start | bytes 442376 | tf_op jit(solution)/shard_map/ppermute | solution.py:41
  22.6 1.6 %collective-permute-start.3 = (bf16[64,1152]{1,0:T(8,128)(2,1)S(1)}, bf16[64,1152]{1,0:T(8,128)(2,1)S(1)}, u32[]{:S(2)}, u32[]{:S(2)}) collective-permute-start(bf16[64,1152]{1,0:T(8,128)(2,1)S(1)} %shard_map.60.refs_0_), channel_id=1, source_target_pairs={{0,4},{1,5},{2,6},{3,7},{4,0},{5,1},{6,2},{7,3},{8,12},{9,13},{10,... | collective-permute-start | bytes 442376 | tf_op jit(solution)/shard_map/ppermute | solution.py:41
  25.6 2.3 %collective-permute-start.2 = (bf16[64,1152]{1,0:T(8,128)(2,1)S(1)}, bf16[64,1152]{1,0:T(8,128)(2,1)S(1)}, u32[]{:S(2)}, u32[]{:S(2)}) collective-permute-start(bf16[64,1152]{1,0:T(8,128)(2,1)S(1)} %collective-permute-done.1.refs_2_), channel_id=1, source_target_pairs={{0,7},{1,0},{2,1},{3,2},{4,3},{5,4},{6,5},{7,6},{8,15},{9,8},{10,9... | collective-permute-start | bytes 442376 | tf_op jit(solution)/shard_map/ppermute | solution.py:41
  27.9 4.1 %collective-permute-done.3.refs_4_ = bf16[64,1152]{1,0:T(8,128)(2,1)S(1)} collective-permute-done((bf16[64,1152]{1,0:T(8,128)(2,1)S(1)}, bf16[64,1152]{1,0:T(8,128)(2,1)S(1)}, u32[]{:S(2)}, u32[]{:S(2)}) %collective-permute-start.3) | collective-permute-done | bytes 147488 | tf_op jit(solution)/shard_map/ppermute | solution.py:41
  32.0 3.4 %collective-permute-done.6.refs_5_ = bf16[64,1152]{1,0:T(8,128)(2,1)S(1)} collective-permute-done((bf16[64,1152]{1,0:T(8,128)(2,1)S(1)}, bf16[64,1152]{1,0:T(8,128)(2,1)S(1)}, u32[]{:S(2)}, u32[]{:S(2)}) %collective-permute-start.6) | collective-permute-done | bytes 147488 | tf_op jit(solution)/shard_map/ppermute | solution.py:41
  39.7 1.6 %collective-permute-start.7 = (bf16[512,1152]{1,0:T(8,128)(2,1)S(1)}, bf16[512,1152]{1,0:T(8,128)(2,1)S(1)}, u32[]{:S(2)}, u32[]{:S(2)}) collective-permute-start(bf16[512,1152]{1,0:T(8,128)(2,1)S(1)} %shard_map.61.xs), channel_id=1, source_target_pairs={{0,16},{16,0},{1,17},{17,1},{2,18},{18,2},{3,19},{19,3},{4,20},{20... | collective-permute-start | bytes 3538952 | tf_op jit(solution)/shard_map/ppermute | solution.py:41
  41.3 2.5 %collective-permute-done.7.xo = bf16[512,1152]{1,0:T(8,128)(2,1)S(1)} collective-permute-done((bf16[512,1152]{1,0:T(8,128)(2,1)S(1)}, bf16[512,1152]{1,0:T(8,128)(2,1)S(1)}, u32[]{:S(2)}, u32[]{:S(2)}) %collective-permute-start.7) | collective-permute-done | bytes 1179680 | tf_op jit(solution)/shard_map/ppermute | solution.py:41
  46.1 10.9 %shard_map.62 = (f32[512,1152]{1,0:T(8,128)}, bf16[512,1152]{1,0:T(8,128)(2,1)}, bf16[1024,1152]{1,0:T(8,128)(2,1)}) custom-call(s32[1]{0:T(128)} %bitcast.place, f32[2]{0:T(128)S(1)} %pad_maximum_fusion.scal, bf16[512,1152]{1,0:T(8,128)(2,1)S(1)} %shard_map.61.xs, bf16[512,1152]{1,0:T(8,128)(2,1)S(1)} %copy-done.14, bf16[1024,1152]{1,0:T(8,128)(2,1)S(1)} %bitcast.5), custom_call_target="tpu_custom_call" | custom-call | flops 7247757312 | bytes 9437184 | tf_op jit(solution)/shard_map/pallas_call | solution.py:166
  57.0 4.1 %all-to-all-start.1 = ((bf16[4,256,1152]{2,1,0:T(8,128)(2,1)}), bf16[4,256,1152]{2,1,0:T(8,128)(2,1)S(1)}, u32[]{:S(2)}, u32[]{:S(2)}) async-start(bf16[4,256,1152]{2,1,0:T(8,128)(2,1)} %bitcast.6), calls=%async_computation.1 | async-start | bytes 4718592 | tf_op jit(solution)/shard_map/all_to_all | solution.py:36
  62.4 2.5 %collective-permute-done.8.other = bf16[512,1152]{1,0:T(8,128)(2,1)S(1)} collective-permute-done((bf16[512,1152]{1,0:T(8,128)(2,1)S(1)}, bf16[512,1152]{1,0:T(8,128)(2,1)S(1)}, u32[]{:S(2)}, u32[]{:S(2)}) %collective-permute-start.8) | collective-permute-done | bytes 1179680 | tf_op jit(solution)/shard_map/ppermute | solution.py:41
  64.8 1.7 %copy-done = f32[512,1152]{1,0:T(8,128)S(1)} copy-done((f32[512,1152]{1,0:T(8,128)S(1)}, f32[512,1152]{1,0:T(8,128)}, u32[]{:S(2)}) %copy-start) | copy-done | bytes 2359320
  67.4 10.5 %all-to-all-done.1 = bf16[4,256,1152]{2,1,0:T(8,128)(2,1)S(1)} async-done(((bf16[4,256,1152]{2,1,0:T(8,128)(2,1)}), bf16[4,256,1152]{2,1,0:T(8,128)(2,1)S(1)}, u32[]{:S(2)}, u32[]{:S(2)}) %all-to-all-start.1) | async-done | bytes 2359328 | tf_op jit(solution)/shard_map/all_to_all | solution.py:36
  78.9 4.4 %all-to-all-start.2 = ((bf16[4,64,1152]{2,1,0:T(8,128)(2,1)}), bf16[4,64,1152]{2,1,0:T(8,128)(2,1)S(1)}, u32[]{:S(2)}, u32[]{:S(2)}) async-start(bf16[4,64,1152]{2,1,0:T(8,128)(2,1)} %shard_map.65), calls=%async_computation.2 | async-start | bytes 1179648 | tf_op jit(solution)/shard_map/all_to_all | solution.py:36
  86.2 4.0 %collective-permute-start.13 = (bf16[64,1152]{1,0:T(8,128)(2,1)S(1)}, bf16[64,1152]{1,0:T(8,128)(2,1)S(1)}, u32[]{:S(2)}, u32[]{:S(2)}) collective-permute-start(bf16[64,1152]{1,0:T(8,128)(2,1)S(1)} %get-tuple-element.24), channel_id=1, source_target_pairs={{0,6},{1,7},{2,0},{3,1},{4,2},{5,3},{6,4},{7,5},{8,14},{9,15},{10,... | collective-permute-start | bytes 442376 | tf_op jit(solution)/shard_map/ppermute | solution.py:41
  92.4 3.5 %collective-permute-start.10 = (bf16[64,1152]{1,0:T(8,128)(2,1)S(1)}, bf16[64,1152]{1,0:T(8,128)(2,1)S(1)}, u32[]{:S(2)}, u32[]{:S(2)}) collective-permute-start(bf16[64,1152]{1,0:T(8,128)(2,1)S(1)} %get-tuple-element.27), channel_id=1, source_target_pairs={{0,3},{1,4},{2,5},{3,6},{4,7},{5,0},{6,1},{7,2},{8,11},{9,12},{10,... | collective-permute-start | bytes 442376 | tf_op jit(solution)/shard_map/ppermute | solution.py:41
  96.0 3.3 %collective-permute-start.9 = (bf16[64,1152]{1,0:T(8,128)(2,1)S(1)}, bf16[64,1152]{1,0:T(8,128)(2,1)S(1)}, u32[]{:S(2)}, u32[]{:S(2)}) collective-permute-start(bf16[64,1152]{1,0:T(8,128)(2,1)S(1)} %get-tuple-element.28), channel_id=1, source_target_pairs={{0,4},{1,5},{2,6},{3,7},{4,0},{5,1},{6,2},{7,3},{8,12},{9,13},{10,... | collective-permute-start | bytes 442376 | tf_op jit(solution)/shard_map/ppermute | solution.py:41
  99.3 1.6 %collective-permute-done.12.refs_4_ = bf16[64,1152]{1,0:T(8,128)(2,1)S(1)} collective-permute-done((bf16[64,1152]{1,0:T(8,128)(2,1)S(1)}, bf16[64,1152]{1,0:T(8,128)(2,1)S(1)}, u32[]{:S(2)}, u32[]{:S(2)}) %collective-permute-start.12) | collective-permute-done | bytes 147488 | tf_op jit(solution)/shard_map/ppermute | solution.py:41
  100.9 1.8 %collective-permute-done.11.refs_3_ = bf16[64,1152]{1,0:T(8,128)(2,1)S(1)} collective-permute-done((bf16[64,1152]{1,0:T(8,128)(2,1)S(1)}, bf16[64,1152]{1,0:T(8,128)(2,1)S(1)}, u32[]{:S(2)}, u32[]{:S(2)}) %collective-permute-start.11) | collective-permute-done | bytes 147488 | tf_op jit(solution)/shard_map/ppermute | solution.py:41
  102.7 12.1 %collective-permute-done.10.refs_2_ = bf16[64,1152]{1,0:T(8,128)(2,1)S(1)} collective-permute-done((bf16[64,1152]{1,0:T(8,128)(2,1)S(1)}, bf16[64,1152]{1,0:T(8,128)(2,1)S(1)}, u32[]{:S(2)}, u32[]{:S(2)}) %collective-permute-start.10) | collective-permute-done | bytes 147488 | tf_op jit(solution)/shard_map/ppermute | solution.py:41
  114.8 2.9 %collective-permute-done.9.refs_1_ = bf16[64,1152]{1,0:T(8,128)(2,1)S(1)} collective-permute-done((bf16[64,1152]{1,0:T(8,128)(2,1)S(1)}, bf16[64,1152]{1,0:T(8,128)(2,1)S(1)}, u32[]{:S(2)}, u32[]{:S(2)}) %collective-permute-start.9) | collective-permute-done | bytes 147488 | tf_op jit(solution)/shard_map/ppermute | solution.py:41
  (56 shorter events, 23.0 us)
Async XLA Ops:
  3.3 6.9 %copy-start.1 = (f32[64,1152]{1,0:T(8,128)S(1)}, f32[64,1152]{1,0:T(8,128)}, u32[]{:S(2)}) copy-start(f32[64,1152]{1,0:T(8,128)} %raw.4) | copy-start | bytes 884740
  3.3 41.5 %all-to-all-start = ((bf16[16,64,1152]{2,1,0:T(8,128)(2,1)}), bf16[16,64,1152]{2,1,0:T(8,128)(2,1)S(1)}, u32[]{:S(2)}, u32[]{:S(2)}) async-start(bf16[16,64,1152]{2,1,0:T(8,128)(2,1)} %shard_map.59), calls=%async_computation | async-start | bytes 4718592 | tf_op jit(solution)/shard_map/all_to_all | solution.py:36
  10.3 4.5 %collective-permute-start = (bf16[64,1152]{1,0:T(8,128)(2,1)S(1)}, bf16[64,1152]{1,0:T(8,128)(2,1)S(1)}, u32[]{:S(2)}, u32[]{:S(2)}) collective-permute-start(bf16[64,1152]{1,0:T(8,128)(2,1)S(1)} %shard_map.60.refs_0_), channel_id=1, source_target_pairs={{0,7},{1,0},{2,1},{3,2},{4,3},{5,4},{6,5},{7,6},{8,15},{9,8},{10,9... | collective-permute-start | bytes 442376 | tf_op jit(solution)/shard_map/ppermute | solution.py:41
  10.4 8.2 %collective-permute-start.4 = (bf16[64,1152]{1,0:T(8,128)(2,1)S(1)}, bf16[64,1152]{1,0:T(8,128)(2,1)S(1)}, u32[]{:S(2)}, u32[]{:S(2)}) collective-permute-start(bf16[64,1152]{1,0:T(8,128)(2,1)S(1)} %shard_map.60.refs_0_), channel_id=1, source_target_pairs={{0,1},{1,2},{2,3},{3,4},{4,5},{5,6},{6,7},{7,0},{8,9},{9,10},{10,1... | collective-permute-start | bytes 442376 | tf_op jit(solution)/shard_map/ppermute | solution.py:41
  18.6 6.3 %collective-permute-start.5 = (bf16[64,1152]{1,0:T(8,128)(2,1)S(1)}, bf16[64,1152]{1,0:T(8,128)(2,1)S(1)}, u32[]{:S(2)}, u32[]{:S(2)}) collective-permute-start(bf16[64,1152]{1,0:T(8,128)(2,1)S(1)} %collective-permute-done.4.refs_7_), channel_id=1, source_target_pairs={{0,1},{1,2},{2,3},{3,4},{4,5},{5,6},{6,7},{7,0},{8,9},{9,10},{10,1... | collective-permute-start | bytes 442376 | tf_op jit(solution)/shard_map/ppermute | solution.py:41
  19.3 6.3 %collective-permute-start.1 = (bf16[64,1152]{1,0:T(8,128)(2,1)S(1)}, bf16[64,1152]{1,0:T(8,128)(2,1)S(1)}, u32[]{:S(2)}, u32[]{:S(2)}) collective-permute-start(bf16[64,1152]{1,0:T(8,128)(2,1)S(1)} %collective-permute-done.refs_1_), channel_id=1, source_target_pairs={{0,7},{1,0},{2,1},{3,2},{4,3},{5,4},{6,5},{7,6},{8,15},{9,8},{10,9... | collective-permute-start | bytes 442376 | tf_op jit(solution)/shard_map/ppermute | solution.py:41
  22.6 9.4 %collective-permute-start.3 = (bf16[64,1152]{1,0:T(8,128)(2,1)S(1)}, bf16[64,1152]{1,0:T(8,128)(2,1)S(1)}, u32[]{:S(2)}, u32[]{:S(2)}) collective-permute-start(bf16[64,1152]{1,0:T(8,128)(2,1)S(1)} %shard_map.60.refs_0_), channel_id=1, source_target_pairs={{0,4},{1,5},{2,6},{3,7},{4,0},{5,1},{6,2},{7,3},{8,12},{9,13},{10,... | collective-permute-start | bytes 442376 | tf_op jit(solution)/shard_map/ppermute | solution.py:41
  24.9 10.6 %collective-permute-start.6 = (bf16[64,1152]{1,0:T(8,128)(2,1)S(1)}, bf16[64,1152]{1,0:T(8,128)(2,1)S(1)}, u32[]{:S(2)}, u32[]{:S(2)}) collective-permute-start(bf16[64,1152]{1,0:T(8,128)(2,1)S(1)} %collective-permute-done.5.refs_6_), channel_id=1, source_target_pairs={{0,1},{1,2},{2,3},{3,4},{4,5},{5,6},{6,7},{7,0},{8,9},{9,10},{10,1... | collective-permute-start | bytes 442376 | tf_op jit(solution)/shard_map/ppermute | solution.py:41
  25.6 11.2 %collective-permute-start.2 = (bf16[64,1152]{1,0:T(8,128)(2,1)S(1)}, bf16[64,1152]{1,0:T(8,128)(2,1)S(1)}, u32[]{:S(2)}, u32[]{:S(2)}) collective-permute-start(bf16[64,1152]{1,0:T(8,128)(2,1)S(1)} %collective-permute-done.1.refs_2_), channel_id=1, source_target_pairs={{0,7},{1,0},{2,1},{3,2},{4,3},{5,4},{6,5},{7,6},{8,15},{9,8},{10,9... | collective-permute-start | bytes 442376 | tf_op jit(solution)/shard_map/ppermute | solution.py:41
  39.7 4.1 %collective-permute-start.7 = (bf16[512,1152]{1,0:T(8,128)(2,1)S(1)}, bf16[512,1152]{1,0:T(8,128)(2,1)S(1)}, u32[]{:S(2)}, u32[]{:S(2)}) collective-permute-start(bf16[512,1152]{1,0:T(8,128)(2,1)S(1)} %shard_map.61.xs), channel_id=1, source_target_pairs={{0,16},{16,0},{1,17},{17,1},{2,18},{18,2},{3,19},{19,3},{4,20},{20... | collective-permute-start | bytes 3538952 | tf_op jit(solution)/shard_map/ppermute | solution.py:41
  57.0 4.1 %copy-start.15 = (bf16[512,1152]{1,0:T(8,128)(2,1)S(1)}, bf16[512,1152]{1,0:T(8,128)(2,1)}, u32[]{:S(2)}) copy-start(bf16[512,1152]{1,0:T(8,128)(2,1)} %get-tuple-element.18) | copy-start | bytes 3538948
  57.0 20.9 %all-to-all-start.1 = ((bf16[4,256,1152]{2,1,0:T(8,128)(2,1)}), bf16[4,256,1152]{2,1,0:T(8,128)(2,1)S(1)}, u32[]{:S(2)}, u32[]{:S(2)}) async-start(bf16[4,256,1152]{2,1,0:T(8,128)(2,1)} %bitcast.6), calls=%async_computation.1 | async-start | bytes 4718592 | tf_op jit(solution)/shard_map/all_to_all | solution.py:36
  61.1 3.7 %collective-permute-start.8 = (bf16[512,1152]{1,0:T(8,128)(2,1)S(1)}, bf16[512,1152]{1,0:T(8,128)(2,1)S(1)}, u32[]{:S(2)}, u32[]{:S(2)}) collective-permute-start(bf16[512,1152]{1,0:T(8,128)(2,1)S(1)} %copy-done.15), channel_id=1, source_target_pairs={{0,16},{16,0},{1,17},{17,1},{2,18},{18,2},{3,19},{19,3},{4,20},{20... | collective-permute-start | bytes 3538952 | tf_op jit(solution)/shard_map/ppermute | solution.py:41
  78.9 38.9 %copy-start.2 = (f32[64,1152]{1,0:T(8,128)S(1)}, f32[64,1152]{1,0:T(8,128)}, u32[]{:S(2)}) copy-start(f32[64,1152]{1,0:T(8,128)} %raw.4) | copy-start | bytes 884740
  78.9 38.8 %copy-start.8 = (f32[64,1152]{1,0:T(8,128)S(1)}, f32[64,1152]{1,0:T(8,128)}, u32[]{:S(2)}) copy-start(f32[64,1152]{1,0:T(8,128)} %copy-done.7) | copy-start | bytes 884740
  78.9 40.4 %copy-start.4 = (f32[64,1152]{1,0:T(8,128)S(1)}, f32[64,1152]{1,0:T(8,128)}, u32[]{:S(2)}) copy-start(f32[64,1152]{1,0:T(8,128)} %raw.5) | copy-start | bytes 884740
  78.9 40.4 %all-to-all-start.2 = ((bf16[4,64,1152]{2,1,0:T(8,128)(2,1)}), bf16[4,64,1152]{2,1,0:T(8,128)(2,1)S(1)}, u32[]{:S(2)}, u32[]{:S(2)}) async-start(bf16[4,64,1152]{2,1,0:T(8,128)(2,1)} %shard_map.65), calls=%async_computation.2 | async-start | bytes 1179648 | tf_op jit(solution)/shard_map/all_to_all | solution.py:36
  83.4 9.0 %collective-permute-start.15 = (bf16[64,1152]{1,0:T(8,128)(2,1)S(1)}, bf16[64,1152]{1,0:T(8,128)(2,1)S(1)}, u32[]{:S(2)}, u32[]{:S(2)}) collective-permute-start(bf16[64,1152]{1,0:T(8,128)(2,1)S(1)} %get-tuple-element.22), channel_id=1, source_target_pairs={{0,7},{1,0},{2,1},{3,2},{4,3},{5,4},{6,5},{7,6},{8,15},{9,8},{10,9... | collective-permute-start | bytes 442376 | tf_op jit(solution)/shard_map/ppermute | solution.py:41
  84.8 11.2 %collective-permute-start.14 = (bf16[64,1152]{1,0:T(8,128)(2,1)S(1)}, bf16[64,1152]{1,0:T(8,128)(2,1)S(1)}, u32[]{:S(2)}, u32[]{:S(2)}) collective-permute-start(bf16[64,1152]{1,0:T(8,128)(2,1)S(1)} %get-tuple-element.23), channel_id=1, source_target_pairs={{0,1},{1,2},{2,3},{3,4},{4,5},{5,6},{6,7},{7,0},{8,9},{9,10},{10,1... | collective-permute-start | bytes 442376 | tf_op jit(solution)/shard_map/ppermute | solution.py:41
  86.2 13.0 %collective-permute-start.13 = (bf16[64,1152]{1,0:T(8,128)(2,1)S(1)}, bf16[64,1152]{1,0:T(8,128)(2,1)S(1)}, u32[]{:S(2)}, u32[]{:S(2)}) collective-permute-start(bf16[64,1152]{1,0:T(8,128)(2,1)S(1)} %get-tuple-element.24), channel_id=1, source_target_pairs={{0,6},{1,7},{2,0},{3,1},{4,2},{5,3},{6,4},{7,5},{8,14},{9,15},{10,... | collective-permute-start | bytes 442376 | tf_op jit(solution)/shard_map/ppermute | solution.py:41
  90.2 10.7 %collective-permute-start.12 = (bf16[64,1152]{1,0:T(8,128)(2,1)S(1)}, bf16[64,1152]{1,0:T(8,128)(2,1)S(1)}, u32[]{:S(2)}, u32[]{:S(2)}) collective-permute-start(bf16[64,1152]{1,0:T(8,128)(2,1)S(1)} %get-tuple-element.25), channel_id=1, source_target_pairs={{0,2},{1,3},{2,4},{3,5},{4,6},{5,7},{6,0},{7,1},{8,10},{9,11},{10,... | collective-permute-start | bytes 442376 | tf_op jit(solution)/shard_map/ppermute | solution.py:41
  91.5 11.2 %collective-permute-start.11 = (bf16[64,1152]{1,0:T(8,128)(2,1)S(1)}, bf16[64,1152]{1,0:T(8,128)(2,1)S(1)}, u32[]{:S(2)}, u32[]{:S(2)}) collective-permute-start(bf16[64,1152]{1,0:T(8,128)(2,1)S(1)} %get-tuple-element.26), channel_id=1, source_target_pairs={{0,5},{1,6},{2,7},{3,0},{4,1},{5,2},{6,3},{7,4},{8,13},{9,14},{10,... | collective-permute-start | bytes 442376 | tf_op jit(solution)/shard_map/ppermute | solution.py:41
  92.4 22.4 %collective-permute-start.10 = (bf16[64,1152]{1,0:T(8,128)(2,1)S(1)}, bf16[64,1152]{1,0:T(8,128)(2,1)S(1)}, u32[]{:S(2)}, u32[]{:S(2)}) collective-permute-start(bf16[64,1152]{1,0:T(8,128)(2,1)S(1)} %get-tuple-element.27), channel_id=1, source_target_pairs={{0,3},{1,4},{2,5},{3,6},{4,7},{5,0},{6,1},{7,2},{8,11},{9,12},{10,... | collective-permute-start | bytes 442376 | tf_op jit(solution)/shard_map/ppermute | solution.py:41
  96.0 21.8 %collective-permute-start.9 = (bf16[64,1152]{1,0:T(8,128)(2,1)S(1)}, bf16[64,1152]{1,0:T(8,128)(2,1)S(1)}, u32[]{:S(2)}, u32[]{:S(2)}) collective-permute-start(bf16[64,1152]{1,0:T(8,128)(2,1)S(1)} %get-tuple-element.28), channel_id=1, source_target_pairs={{0,4},{1,5},{2,6},{3,7},{4,0},{5,1},{6,2},{7,3},{8,12},{9,13},{10,... | collective-permute-start | bytes 442376 | tf_op jit(solution)/shard_map/ppermute | solution.py:41
  (11 other events, 10.4 us)

commit v11 on v9

--- a/solution.py
+++ b/solution.py
@@ -133,6 +133,19 @@
         total += part[...].astype(F32)
     unit, norm = to_unit(raw[...])
     refs[-1][...] = from_unit(scal[0] * total, unit, norm)
+
+
+def sum_kernel(got, out, part, sems):
+    copies = []
+    for j in range(out.shape[0]):
+        total = got[0, j].astype(F32)
+        for k in range(1, got.shape[0]):
+            total += got[k, j].astype(F32)
+        part[j] = total.astype(BF)
+        copies.append(pltpu.make_async_copy(part.at[j], out.at[j], sems.at[j]))
+        copies[-1].start()
+    for copy in copies:
+        copy.wait()
 
 
 def finish_texts_kernel(scal, raw, got, out):
@@ -216,14 +229,18 @@
         flops=6 * unit_flops, nbytes=9 * 2**20, trans=4 * half * pooled, vmem=24,
     )
     half_way = swapped(dy.reshape(4, 4 * rows, width), OUTER)
-    half_way = jnp.sum(half_way.astype(F32), axis=0).astype(BF)
-    dyr = swapped(half_way.reshape(4, rows, width), INNER)
     other = shifted(dxo, "core", 1)
     own, rest = local(
         join_kernel, [((rows, width), F32, VMEM), ((half - rows, width), BF, VMEM)], [dxs, other],
         nbytes=5 * 2**20, vmem=16,
     )
     got = near_reduce(rest.reshape(-1, rows, width))
+    half_way, *got[3:] = lax.optimization_barrier((half_way, *got[3:]))
+    (half_way,) = local(
+        sum_kernel, [((4, rows, width), BF, HBM)], [half_way.reshape(4, 4, rows, width)], nbytes=3 * 2**20, vmem=16,
+        scratch=[pltpu.VMEM((4, rows, width), BF), pltpu.SemaphoreType.DMA((4,))],
+    )
+    dyr = swapped(half_way, INNER)
     (grad_images,) = local(finish_kernel, [((rows, width), F32, VMEM)], [scal, images, own] + got, smem=1)
     (grad_texts,) = local(finish_texts_kernel, [((rows, width), F32, VMEM)], [scal, texts, dyr], smem=1)
     return (grad_images, grad_texts)

time: 103 us -> 112 us (1.087)
  waiting for transfers between devices: 23.1 us -> 40.5 us
  starting transfers between devices: 55.4 us -> 48.5 us
  other arithmetic: 4.12 us -> 0.15 us
  local copies, waits for them, and re-layouts: 1.05 us -> 3.51 us
    ppermute x16, waiting for transfers between devices: 20 us -> 40.5 us  [shifted(): lax.ppermute(block, axis, [(i, (i + distance) % n) for i in range(n)])]
    ppermute x16, starting transfers between devices: 37.1 us -> 31.2 us  [shifted(): lax.ppermute(block, axis, [(i, (i + distance) % n) for i in range(n)])]
    all_to_all x3, waiting for transfers between devices: 3.15 us -> 0.01 us  [swapped(): lax.all_to_all(blocks, AXES, 0, 0, axis_index_groups=groups, tiled=True)]
    reduce_sum x1 -> x0, other arithmetic: 2.99 us -> none  [on_device(): half_way = jnp.sum(half_way.astype(F32), axis=0).astype(BF)]
    unnamed x16 -> x14, local copies, waits for them, and re-layouts: 0.99 us -> 2.65 us
    pallas_call x7 -> x8, Pallas kernels: 15.9 us -> 16.8 us  [local(): pl.pallas_call(kernel, out_shape=tuple(((pltpu.HBM if spec is HBM else ja...]
  transfers between devices with their start and end apart: 19 -> 19, of which waited for: 8 -> 11; matrix products, arithmetic and copies ran while one was open for 4% -> 1% of each run, Pallas kernels for 2% -> 2%
where the time goes in v11:
time: 112 us
  starting transfers between devices  48.5 us (43%)
  waiting for transfers between devices  40.5 us (36%)
  Pallas kernels  16.8 us (15%)
  local copies, waits for them, and re-layouts  3.51 us (3%)
  between operations  2.09 us (2%)
    ppermute x16, waiting for transfers between devices, shifted(): lax.ppermute(block, axis, [(i, (i + distance) % n) for i in range(n)])  40.5 us
    ppermute x16, starting transfers between devices, shifted(): lax.ppermute(block, axis, [(i, (i + distance) % n) for i in range(n)])  31.2 us
    all_to_all x3, starting transfers between devices, swapped(): lax.all_to_all(blocks, AXES, 0, 0, axis_index_groups=groups, tiled=True)  17.3 us
    pallas_call x8, Pallas kernels, local(): pl.pallas_call(kernel, out_shape=tuple(((pltpu.HBM if spec is HBM else ja...  16.8 us
    unnamed x14, local copies, waits for them, and re-layouts  2.65 us
  transfers between devices with their start and end apart: 19, of which 11 were waited for; matrix products, arithmetic and copies ran while one was open for 1% of the time, Pallas kernels for 2%

profile of v11, /device:TPU:8, one launch (start us, length us, event | category | flops | bytes accessed | tf_op | source)
XLA Modules:
  0.0 111.5 jit_solution(2009486863428311790)
XLA Ops:
  1.6 1.7 %shard_map.59 = bf16[16,64,1152]{2,1,0:T(8,128)(2,1)} custom-call(f32[64,1152]{1,0:T(8,128)S(1)} %copy-done.3), custom_call_target="tpu_custom_call" | custom-call | bytes 1048576 | tf_op jit(solution)/shard_map/pallas_call | solution.py:166
  3.3 7.5 %all-to-all-start = ((bf16[16,64,1152]{2,1,0:T(8,128)(2,1)}), bf16[16,64,1152]{2,1,0:T(8,128)(2,1)S(1)}, u32[]{:S(2)}, u32[]{:S(2)}) async-start(bf16[16,64,1152]{2,1,0:T(8,128)(2,1)} %shard_map.59), calls=%async_computation | async-start | bytes 4718592 | tf_op jit(solution)/shard_map/all_to_all | solution.py:36
  11.0 2.0 %collective-permute-start.4 = (bf16[64,1152]{1,0:T(8,128)(2,1)S(1)}, bf16[64,1152]{1,0:T(8,128)(2,1)S(1)}, u32[]{:S(2)}, u32[]{:S(2)}) collective-permute-start(bf16[64,1152]{1,0:T(8,128)(2,1)S(1)} %shard_map.60.refs_0_), channel_id=1, source_target_pairs={{0,1},{1,2},{2,3},{3,4},{4,5},{5,6},{6,7},{7,0},{8,9},{9,10},{10,1... | collective-permute-start | bytes 442376 | tf_op jit(solution)/shard_map/ppermute | solution.py:41
  13.0 4.0 %collective-permute-start = (bf16[64,1152]{1,0:T(8,128)(2,1)S(1)}, bf16[64,1152]{1,0:T(8,128)(2,1)S(1)}, u32[]{:S(2)}, u32[]{:S(2)}) collective-permute-start(bf16[64,1152]{1,0:T(8,128)(2,1)S(1)} %shard_map.60.refs_0_), channel_id=1, source_target_pairs={{0,7},{1,0},{2,1},{3,2},{4,3},{5,4},{6,5},{7,6},{8,15},{9,8},{10,9... | collective-permute-start | bytes 442376 | tf_op jit(solution)/shard_map/ppermute | solution.py:41
  17.0 3.2 %collective-permute-done.4.refs_7_ = bf16[64,1152]{1,0:T(8,128)(2,1)S(1)} collective-permute-done((bf16[64,1152]{1,0:T(8,128)(2,1)S(1)}, bf16[64,1152]{1,0:T(8,128)(2,1)S(1)}, u32[]{:S(2)}, u32[]{:S(2)}) %collective-permute-start.4) | collective-permute-done | bytes 147488 | tf_op jit(solution)/shard_map/ppermute | solution.py:41
  20.2 3.2 %collective-permute-start.1 = (bf16[64,1152]{1,0:T(8,128)(2,1)S(1)}, bf16[64,1152]{1,0:T(8,128)(2,1)S(1)}, u32[]{:S(2)}, u32[]{:S(2)}) collective-permute-start(bf16[64,1152]{1,0:T(8,128)(2,1)S(1)} %collective-permute-done.refs_1_), channel_id=1, source_target_pairs={{0,7},{1,0},{2,1},{3,2},{4,3},{5,4},{6,5},{7,6},{8,15},{9,8},{10,9... | collective-permute-start | bytes 442376 | tf_op jit(solution)/shard_map/ppermute | solution.py:41
  23.4 4.4 %collective-permute-start.3 = (bf16[64,1152]{1,0:T(8,128)(2,1)S(1)}, bf16[64,1152]{1,0:T(8,128)(2,1)S(1)}, u32[]{:S(2)}, u32[]{:S(2)}) collective-permute-start(bf16[64,1152]{1,0:T(8,128)(2,1)S(1)} %shard_map.60.refs_0_), channel_id=1, source_target_pairs={{0,4},{1,5},{2,6},{3,7},{4,0},{5,1},{6,2},{7,3},{8,12},{9,13},{10,... | collective-permute-start | bytes 442376 | tf_op jit(solution)/shard_map/ppermute | solution.py:41
  28.0 4.9 %collective-permute-done.1.refs_2_ = bf16[64,1152]{1,0:T(8,128)(2,1)S(1)} collective-permute-done((bf16[64,1152]{1,0:T(8,128)(2,1)S(1)}, bf16[64,1152]{1,0:T(8,128)(2,1)S(1)}, u32[]{:S(2)}, u32[]{:S(2)}) %collective-permute-start.1) | collective-permute-done | bytes 147488 | tf_op jit(solution)/shard_map/ppermute | solution.py:41
  33.0 3.8 %collective-permute-start.2 = (bf16[64,1152]{1,0:T(8,128)(2,1)S(1)}, bf16[64,1152]{1,0:T(8,128)(2,1)S(1)}, u32[]{:S(2)}, u32[]{:S(2)}) collective-permute-start(bf16[64,1152]{1,0:T(8,128)(2,1)S(1)} %collective-permute-done.1.refs_2_), channel_id=1, source_target_pairs={{0,7},{1,0},{2,1},{3,2},{4,3},{5,4},{6,5},{7,6},{8,15},{9,8},{10,9... | collective-permute-start | bytes 442376 | tf_op jit(solution)/shard_map/ppermute | solution.py:41
  36.8 2.7 %collective-permute-done.2.refs_3_ = bf16[64,1152]{1,0:T(8,128)(2,1)S(1)} collective-permute-done((bf16[64,1152]{1,0:T(8,128)(2,1)S(1)}, bf16[64,1152]{1,0:T(8,128)(2,1)S(1)}, u32[]{:S(2)}, u32[]{:S(2)}) %collective-permute-start.2) | collective-permute-done | bytes 147488 | tf_op jit(solution)/shard_map/ppermute | solution.py:41
  41.3 1.5 %collective-permute-done.7.xo = bf16[512,1152]{1,0:T(8,128)(2,1)} collective-permute-done((bf16[512,1152]{1,0:T(8,128)(2,1)S(1)}, bf16[512,1152]{1,0:T(8,128)(2,1)}, u32[]{:S(2)}, u32[]{:S(2)}) %collective-permute-start.7) | collective-permute-done | bytes 1179680 | tf_op jit(solution)/shard_map/ppermute | solution.py:41
  42.8 10.7 %shard_map.62 = (f32[512,1152]{1,0:T(8,128)}, bf16[512,1152]{1,0:T(8,128)(2,1)}, bf16[1024,1152]{1,0:T(8,128)(2,1)}) custom-call(s32[1]{0:T(128)} %bitcast.place, f32[2]{0:T(128)S(1)} %pad_maximum_fusion.scal, bf16[512,1152]{1,0:T(8,128)(2,1)S(1)} %shard_map.61.xs, bf16[512,1152]{1,0:T(8,128)(2,1)} %collective-permute-done.7.xo, bf16[1024,1152]{1,0:T(8,128)(2,1)S(1)} %bitcast.5), custom_call_target="tpu_custom_call" | custom-call | flops 7247757312 | bytes 9437184 | tf_op jit(solution)/shard_map/pallas_call | solution.py:166
  53.7 6.2 %all-to-all-start.1 = ((bf16[4,256,1152]{2,1,0:T(8,128)(2,1)}), bf16[4,256,1152]{2,1,0:T(8,128)(2,1)S(1)}, u32[]{:S(2)}, u32[]{:S(2)}) async-start(bf16[4,256,1152]{2,1,0:T(8,128)(2,1)} %bitcast.6), calls=%async_computation.1 | async-start | bytes 4718592 | tf_op jit(solution)/shard_map/all_to_all | solution.py:36
  59.9 1.7 %copy-done = f32[512,1152]{1,0:T(8,128)S(1)} copy-done((f32[512,1152]{1,0:T(8,128)S(1)}, f32[512,1152]{1,0:T(8,128)}, u32[]{:S(2)}) %copy-start) | copy-done | bytes 2359320
  62.7 5.9 %collective-permute-start.14 = (bf16[64,1152]{1,0:T(8,128)(2,1)S(1)}, bf16[64,1152]{1,0:T(8,128)(2,1)S(1)}, u32[]{:S(2)}, u32[]{:S(2)}) collective-permute-start(bf16[64,1152]{1,0:T(8,128)(2,1)S(1)} %get-tuple-element.24), channel_id=1, source_target_pairs={{0,7},{1,0},{2,1},{3,2},{4,3},{5,4},{6,5},{7,6},{8,15},{9,8},{10,9... | collective-permute-start | bytes 442376 | tf_op jit(solution)/shard_map/ppermute | solution.py:41
  68.6 3.6 %collective-permute-done.14 = bf16[64,1152]{1,0:T(8,128)(2,1)S(1)} collective-permute-done((bf16[64,1152]{1,0:T(8,128)(2,1)S(1)}, bf16[64,1152]{1,0:T(8,128)(2,1)S(1)}, u32[]{:S(2)}, u32[]{:S(2)}) %collective-permute-start.14) | collective-permute-done | bytes 147488 | tf_op jit(solution)/shard_map/ppermute | solution.py:41
  72.1 3.9 %collective-permute-done.12 = bf16[64,1152]{1,0:T(8,128)(2,1)S(1)} collective-permute-done((bf16[64,1152]{1,0:T(8,128)(2,1)S(1)}, bf16[64,1152]{1,0:T(8,128)(2,1)S(1)}, u32[]{:S(2)}, u32[]{:S(2)}) %collective-permute-start.12) | collective-permute-done | bytes 147488 | tf_op jit(solution)/shard_map/ppermute | solution.py:41
  76.2 2.0 %collective-permute-start.13 = (bf16[64,1152]{1,0:T(8,128)(2,1)S(1)}, bf16[64,1152]{1,0:T(8,128)(2,1)S(1)}, u32[]{:S(2)}, u32[]{:S(2)}) collective-permute-start(bf16[64,1152]{1,0:T(8,128)(2,1)S(1)} %get-tuple-element.23), channel_id=1, source_target_pairs={{0,1},{1,2},{2,3},{3,4},{4,5},{5,6},{6,7},{7,0},{8,9},{9,10},{10,1... | collective-permute-start | bytes 442376 | tf_op jit(solution)/shard_map/ppermute | solution.py:41
  78.2 3.1 %collective-permute-done.15.refs_5_ = bf16[64,1152]{1,0:T(8,128)(2,1)S(1)} collective-permute-done((bf16[64,1152]{1,0:T(8,128)(2,1)S(1)}, bf16[64,1152]{1,0:T(8,128)(2,1)S(1)}, u32[]{:S(2)}, u32[]{:S(2)}) %collective-permute-start.15) | collective-permute-done | bytes 147488 | tf_op jit(solution)/shard_map/ppermute | solution.py:41
  83.6 3.5 %all-to-all-start.2 = ((bf16[4,64,1152]{2,1,0:T(8,128)(2,1)}), bf16[4,64,1152]{2,1,0:T(8,128)(2,1)S(1)}, u32[]{:S(2)}, u32[]{:S(2)}) async-start(bf16[4,64,1152]{2,1,0:T(8,128)(2,1)} %shard_map.65), calls=%async_computation.2 | async-start | bytes 1179648 | tf_op jit(solution)/shard_map/all_to_all | solution.py:36
  87.7 3.3 %collective-permute-start.10 = (bf16[64,1152]{1,0:T(8,128)(2,1)}, bf16[64,1152]{1,0:T(8,128)(2,1)S(1)}, u32[]{:S(2)}, u32[]{:S(2)}) collective-permute-start(bf16[64,1152]{1,0:T(8,128)(2,1)} %get-tuple-element.27), channel_id=1, source_target_pairs={{0,3},{1,4},{2,5},{3,6},{4,7},{5,0},{6,1},{7,2},{8,11},{9,12},{10,... | collective-permute-start | bytes 442376 | tf_op jit(solution)/shard_map/ppermute | solution.py:41
  92.4 8.1 %collective-permute-done.11.refs_3_ = bf16[64,1152]{1,0:T(8,128)(2,1)S(1)} collective-permute-done((bf16[64,1152]{1,0:T(8,128)(2,1)}, bf16[64,1152]{1,0:T(8,128)(2,1)S(1)}, u32[]{:S(2)}, u32[]{:S(2)}) %collective-permute-start.11) | collective-permute-done | bytes 147488 | tf_op jit(solution)/shard_map/ppermute | solution.py:41
  100.5 8.0 %collective-permute-done.10.refs_2_ = bf16[64,1152]{1,0:T(8,128)(2,1)S(1)} collective-permute-done((bf16[64,1152]{1,0:T(8,128)(2,1)}, bf16[64,1152]{1,0:T(8,128)(2,1)S(1)}, u32[]{:S(2)}, u32[]{:S(2)}) %collective-permute-start.10) | collective-permute-done | bytes 147488 | tf_op jit(solution)/shard_map/ppermute | solution.py:41
  108.5 1.5 %shard_map.64 = f32[64,1152]{1,0:T(8,128)} custom-call(f32[2]{0:T(128)S(1)} %pad_maximum_fusion.scal, f32[64,1152]{1,0:T(8,128)S(1)} %copy-done.2, f32[64,1152]{1,0:T(8,128)S(1)} %copy-done.6, bf16[64,1152]{1,0:T(8,128)(2,1)S(1)} %collective-permute-done.9.refs_1_, bf16[64,1152]{1,0:T(8,128)(2,1)S(1)} %collective-permute-done.10.refs_2_, ...), custom_call_target="tpu_custom_call" | custom-call | bytes 1048576 | tf_op jit(solution)/shard_map/pallas_call | solution.py:166
  (39 shorter events, 9.0 us)
Async XLA Ops:
  3.3 7.6 %copy-start.1 = (f32[64,1152]{1,0:T(8,128)S(1)}, f32[64,1152]{1,0:T(8,128)}, u32[]{:S(2)}) copy-start(f32[64,1152]{1,0:T(8,128)} %raw.4) | copy-start | bytes 884740
  3.3 39.5 %all-to-all-start = ((bf16[16,64,1152]{2,1,0:T(8,128)(2,1)}), bf16[16,64,1152]{2,1,0:T(8,128)(2,1)S(1)}, u32[]{:S(2)}, u32[]{:S(2)}) async-start(bf16[16,64,1152]{2,1,0:T(8,128)(2,1)} %shard_map.59), calls=%async_computation | async-start | bytes 4718592 | tf_op jit(solution)/shard_map/all_to_all | solution.py:36
  11.0 9.2 %collective-permute-start.4 = (bf16[64,1152]{1,0:T(8,128)(2,1)S(1)}, bf16[64,1152]{1,0:T(8,128)(2,1)S(1)}, u32[]{:S(2)}, u32[]{:S(2)}) collective-permute-start(bf16[64,1152]{1,0:T(8,128)(2,1)S(1)} %shard_map.60.refs_0_), channel_id=1, source_target_pairs={{0,1},{1,2},{2,3},{3,4},{4,5},{5,6},{6,7},{7,0},{8,9},{9,10},{10,1... | collective-permute-start | bytes 442376 | tf_op jit(solution)/shard_map/ppermute | solution.py:41
  13.0 7.2 %collective-permute-start = (bf16[64,1152]{1,0:T(8,128)(2,1)S(1)}, bf16[64,1152]{1,0:T(8,128)(2,1)S(1)}, u32[]{:S(2)}, u32[]{:S(2)}) collective-permute-start(bf16[64,1152]{1,0:T(8,128)(2,1)S(1)} %shard_map.60.refs_0_), channel_id=1, source_target_pairs={{0,7},{1,0},{2,1},{3,2},{4,3},{5,4},{6,5},{7,6},{8,15},{9,8},{10,9... | collective-permute-start | bytes 442376 | tf_op jit(solution)/shard_map/ppermute | solution.py:41
  20.2 7.8 %collective-permute-start.5 = (bf16[64,1152]{1,0:T(8,128)(2,1)S(1)}, bf16[64,1152]{1,0:T(8,128)(2,1)S(1)}, u32[]{:S(2)}, u32[]{:S(2)}) collective-permute-start(bf16[64,1152]{1,0:T(8,128)(2,1)S(1)} %collective-permute-done.4.refs_7_), channel_id=1, source_target_pairs={{0,1},{1,2},{2,3},{3,4},{4,5},{5,6},{6,7},{7,0},{8,9},{9,10},{10,1... | collective-permute-start | bytes 442376 | tf_op jit(solution)/shard_map/ppermute | solution.py:41
  20.2 12.8 %collective-permute-start.1 = (bf16[64,1152]{1,0:T(8,128)(2,1)S(1)}, bf16[64,1152]{1,0:T(8,128)(2,1)S(1)}, u32[]{:S(2)}, u32[]{:S(2)}) collective-permute-start(bf16[64,1152]{1,0:T(8,128)(2,1)S(1)} %collective-permute-done.refs_1_), channel_id=1, source_target_pairs={{0,7},{1,0},{2,1},{3,2},{4,3},{5,4},{6,5},{7,6},{8,15},{9,8},{10,9... | collective-permute-start | bytes 442376 | tf_op jit(solution)/shard_map/ppermute | solution.py:41
  23.4 13.4 %collective-permute-start.3 = (bf16[64,1152]{1,0:T(8,128)(2,1)S(1)}, bf16[64,1152]{1,0:T(8,128)(2,1)S(1)}, u32[]{:S(2)}, u32[]{:S(2)}) collective-permute-start(bf16[64,1152]{1,0:T(8,128)(2,1)S(1)} %shard_map.60.refs_0_), channel_id=1, source_target_pairs={{0,4},{1,5},{2,6},{3,7},{4,0},{5,1},{6,2},{7,3},{8,12},{9,13},{10,... | collective-permute-start | bytes 442376 | tf_op jit(solution)/shard_map/ppermute | solution.py:41
  28.0 8.8 %collective-permute-start.6 = (bf16[64,1152]{1,0:T(8,128)(2,1)S(1)}, bf16[64,1152]{1,0:T(8,128)(2,1)S(1)}, u32[]{:S(2)}, u32[]{:S(2)}) collective-permute-start(bf16[64,1152]{1,0:T(8,128)(2,1)S(1)} %collective-permute-done.5.refs_6_), channel_id=1, source_target_pairs={{0,1},{1,2},{2,3},{3,4},{4,5},{5,6},{6,7},{7,0},{8,9},{9,10},{10,1... | collective-permute-start | bytes 442376 | tf_op jit(solution)/shard_map/ppermute | solution.py:41
  33.0 6.5 %collective-permute-start.2 = (bf16[64,1152]{1,0:T(8,128)(2,1)S(1)}, bf16[64,1152]{1,0:T(8,128)(2,1)S(1)}, u32[]{:S(2)}, u32[]{:S(2)}) collective-permute-start(bf16[64,1152]{1,0:T(8,128)(2,1)S(1)} %collective-permute-done.1.refs_2_), channel_id=1, source_target_pairs={{0,7},{1,0},{2,1},{3,2},{4,3},{5,4},{6,5},{7,6},{8,15},{9,8},{10,9... | collective-permute-start | bytes 442376 | tf_op jit(solution)/shard_map/ppermute | solution.py:41
  39.6 3.2 %collective-permute-start.7 = (bf16[512,1152]{1,0:T(8,128)(2,1)S(1)}, bf16[512,1152]{1,0:T(8,128)(2,1)}, u32[]{:S(2)}, u32[]{:S(2)}) collective-permute-start(bf16[512,1152]{1,0:T(8,128)(2,1)S(1)} %shard_map.61.xs), channel_id=1, source_target_pairs={{0,16},{16,0},{1,17},{17,1},{2,18},{18,2},{3,19},{19,3},{4,20},{20... | collective-permute-start | bytes 3538952 | tf_op jit(solution)/shard_map/ppermute | solution.py:41
  53.5 6.5 %collective-permute-start.8 = (bf16[512,1152]{1,0:T(8,128)(2,1)}, bf16[512,1152]{1,0:T(8,128)(2,1)S(1)}, u32[]{:S(2)}, u32[]{:S(2)}) collective-permute-start(bf16[512,1152]{1,0:T(8,128)(2,1)} %get-tuple-element.15), channel_id=1, source_target_pairs={{0,16},{16,0},{1,17},{17,1},{2,18},{18,2},{3,19},{19,3},{4,20},{20... | collective-permute-start | bytes 3538952 | tf_op jit(solution)/shard_map/ppermute | solution.py:41
  53.7 28.9 %all-to-all-start.1 = ((bf16[4,256,1152]{2,1,0:T(8,128)(2,1)}), bf16[4,256,1152]{2,1,0:T(8,128)(2,1)S(1)}, u32[]{:S(2)}, u32[]{:S(2)}) async-start(bf16[4,256,1152]{2,1,0:T(8,128)(2,1)} %bitcast.6), calls=%async_computation.1 | async-start | bytes 4718592 | tf_op jit(solution)/shard_map/all_to_all | solution.py:36
  61.8 19.5 %copy-start.5 = (f32[64,1152]{1,0:T(8,128)}, f32[64,1152]{1,0:T(8,128)S(1)}, u32[]{:S(2)}) copy-start(f32[64,1152]{1,0:T(8,128)S(1)} %get-tuple-element.16.refs_0_) | copy-start | bytes 884740
  62.7 9.4 %collective-permute-start.14 = (bf16[64,1152]{1,0:T(8,128)(2,1)S(1)}, bf16[64,1152]{1,0:T(8,128)(2,1)S(1)}, u32[]{:S(2)}, u32[]{:S(2)}) collective-permute-start(bf16[64,1152]{1,0:T(8,128)(2,1)S(1)} %get-tuple-element.24), channel_id=1, source_target_pairs={{0,7},{1,0},{2,1},{3,2},{4,3},{5,4},{6,5},{7,6},{8,15},{9,8},{10,9... | collective-permute-start | bytes 442376 | tf_op jit(solution)/shard_map/ppermute | solution.py:41
  68.5 39.9 %copy-start.2 = (f32[64,1152]{1,0:T(8,128)S(1)}, f32[64,1152]{1,0:T(8,128)}, u32[]{:S(2)}) copy-start(f32[64,1152]{1,0:T(8,128)} %raw.4) | copy-start | bytes 884740
  68.6 7.5 %collective-permute-start.12 = (bf16[64,1152]{1,0:T(8,128)(2,1)S(1)}, bf16[64,1152]{1,0:T(8,128)(2,1)S(1)}, u32[]{:S(2)}, u32[]{:S(2)}) collective-permute-start(bf16[64,1152]{1,0:T(8,128)(2,1)S(1)} %get-tuple-element.25), channel_id=1, source_target_pairs={{0,1},{1,2},{2,3},{3,4},{4,5},{5,6},{6,7},{7,0},{8,9},{9,10},{10,1... | collective-permute-start | bytes 442376 | tf_op jit(solution)/shard_map/ppermute | solution.py:41
  76.1 5.2 %collective-permute-start.15 = (bf16[64,1152]{1,0:T(8,128)(2,1)S(1)}, bf16[64,1152]{1,0:T(8,128)(2,1)S(1)}, u32[]{:S(2)}, u32[]{:S(2)}) collective-permute-start(bf16[64,1152]{1,0:T(8,128)(2,1)S(1)} %get-tuple-element.22), channel_id=1, source_target_pairs={{0,7},{1,0},{2,1},{3,2},{4,3},{5,4},{6,5},{7,6},{8,15},{9,8},{10,9... | collective-permute-start | bytes 442376 | tf_op jit(solution)/shard_map/ppermute | solution.py:41
  76.2 6.4 %collective-permute-start.13 = (bf16[64,1152]{1,0:T(8,128)(2,1)S(1)}, bf16[64,1152]{1,0:T(8,128)(2,1)S(1)}, u32[]{:S(2)}, u32[]{:S(2)}) collective-permute-start(bf16[64,1152]{1,0:T(8,128)(2,1)S(1)} %get-tuple-element.23), channel_id=1, source_target_pairs={{0,1},{1,2},{2,3},{3,4},{4,5},{5,6},{6,7},{7,0},{8,9},{9,10},{10,1... | collective-permute-start | bytes 442376 | tf_op jit(solution)/shard_map/ppermute | solution.py:41
  82.6 25.9 %copy-start.6 = (f32[64,1152]{1,0:T(8,128)S(1)}, f32[64,1152]{1,0:T(8,128)}, u32[]{:S(2)}) copy-start(f32[64,1152]{1,0:T(8,128)} %copy-done.5) | copy-start | bytes 884740
  82.6 27.4 %copy-start.4 = (f32[64,1152]{1,0:T(8,128)S(1)}, f32[64,1152]{1,0:T(8,128)}, u32[]{:S(2)}) copy-start(f32[64,1152]{1,0:T(8,128)} %raw.5) | copy-start | bytes 884740
  83.6 26.4 %all-to-all-start.2 = ((bf16[4,64,1152]{2,1,0:T(8,128)(2,1)}), bf16[4,64,1152]{2,1,0:T(8,128)(2,1)S(1)}, u32[]{:S(2)}, u32[]{:S(2)}) async-start(bf16[4,64,1152]{2,1,0:T(8,128)(2,1)} %shard_map.65), calls=%async_computation.2 | async-start | bytes 1179648 | tf_op jit(solution)/shard_map/all_to_all | solution.py:36
  87.1 13.4 %collective-permute-start.11 = (bf16[64,1152]{1,0:T(8,128)(2,1)}, bf16[64,1152]{1,0:T(8,128)(2,1)S(1)}, u32[]{:S(2)}, u32[]{:S(2)}) collective-permute-start(bf16[64,1152]{1,0:T(8,128)(2,1)} %get-tuple-element.26), channel_id=1, source_target_pairs={{0,5},{1,6},{2,7},{3,0},{4,1},{5,2},{6,3},{7,4},{8,13},{9,14},{10,... | collective-permute-start | bytes 442376 | tf_op jit(solution)/shard_map/ppermute | solution.py:41
  87.7 20.8 %collective-permute-start.10 = (bf16[64,1152]{1,0:T(8,128)(2,1)}, bf16[64,1152]{1,0:T(8,128)(2,1)S(1)}, u32[]{:S(2)}, u32[]{:S(2)}) collective-permute-start(bf16[64,1152]{1,0:T(8,128)(2,1)} %get-tuple-element.27), channel_id=1, source_target_pairs={{0,3},{1,4},{2,5},{3,6},{4,7},{5,0},{6,1},{7,2},{8,11},{9,12},{10,... | collective-permute-start | bytes 442376 | tf_op jit(solution)/shard_map/ppermute | solution.py:41
  91.0 17.5 %collective-permute-start.9 = (bf16[64,1152]{1,0:T(8,128)(2,1)}, bf16[64,1152]{1,0:T(8,128)(2,1)S(1)}, u32[]{:S(2)}, u32[]{:S(2)}) collective-permute-start(bf16[64,1152]{1,0:T(8,128)(2,1)} %get-tuple-element.28), channel_id=1, source_target_pairs={{0,4},{1,5},{2,6},{3,7},{4,0},{5,1},{6,2},{7,3},{8,12},{9,13},{10,... | collective-permute-start | bytes 442376 | tf_op jit(solution)/shard_map/ppermute | solution.py:41
  (2 other events, 2.6 us)

commit v12 on v11

--- a/solution.py
+++ b/solution.py
@@ -122,9 +122,10 @@
         copy.wait()
 
 
-def join_kernel(dxs, other, own, rest):
-    own[...] = dxs[0:ROWS] + other[0:ROWS].astype(F32)
-    rest[...] = (dxs[ROWS:] + other[ROWS:].astype(F32)).astype(BF)
+def join_kernel(dxs, other, *outs):
+    for k, out in enumerate(outs):
+        sl = slice(k * ROWS, (k + 1) * ROWS)
+        out[...] = (dxs[sl] + other[sl].astype(F32)).astype(out.dtype)
 
 
 def finish_kernel(scal, raw, *refs):
@@ -188,11 +189,8 @@
     return up + [far] + down[:0:-1]
 
 
-def near_reduce(rest):
-    direct = [shifted(rest[k - 1], "z", k) for k in (4, 3, 5)]
-    up, down = shifted(rest[1], "z", 1), shifted(rest[5], "z", -1)
-    up, down = shifted(add(rest[0], up), "z", 1), shifted(add(rest[6], down), "z", -1)
-    return direct + [up, down]
+def ring_step(up, down):
+    return shifted(up, "z", 1), shifted(down, "z", -1)
 
 
 def on_device(images, texts, log_temp, bias):
@@ -230,18 +228,22 @@
     )
     half_way = swapped(dy.reshape(4, 4 * rows, width), OUTER)
     other = shifted(dxo, "core", 1)
-    own, rest = local(
-        join_kernel, [((rows, width), F32, VMEM), ((half - rows, width), BF, VMEM)], [dxs, other],
+    parts = local(
+        join_kernel, [((rows, width), BF if k else F32, VMEM) for k in range(half // rows)], [dxs, other],
         nbytes=5 * 2**20, vmem=16,
     )
-    got = near_reduce(rest.reshape(-1, rows, width))
-    half_way, *got[3:] = lax.optimization_barrier((half_way, *got[3:]))
+    far = shifted(parts[4], "z", 4)
+    up, down = ring_step(parts[3], parts[5])
+    up, down = ring_step(add(parts[2], up), add(parts[6], down))
+    up, down = add(parts[1], up), add(parts[7], down)
+    half_way, far, up, down = lax.optimization_barrier((half_way, far, up, down))
     (half_way,) = local(
         sum_kernel, [((4, rows, width), BF, HBM)], [half_way.reshape(4, 4, rows, width)], nbytes=3 * 2**20, vmem=16,
         scratch=[pltpu.VMEM((4, rows, width), BF), pltpu.SemaphoreType.DMA((4,))],
     )
+    up, down = ring_step(up, down)
     dyr = swapped(half_way, INNER)
-    (grad_images,) = local(finish_kernel, [((rows, width), F32, VMEM)], [scal, images, own] + got, smem=1)
+    (grad_images,) = local(finish_kernel, [((rows, width), F32, VMEM)], [scal, images, parts[0], far, up, down], smem=1)
     (grad_texts,) = local(finish_texts_kernel, [((rows, width), F32, VMEM)], [scal, texts, dyr], smem=1)
     return (grad_images, grad_texts)
 

time: 112 us -> 107 us (0.955)
  the two profiles are of different devices: /device:TPU:8 before, /device:TPU:2 now
where the time goes in v12:
time: 107 us
  starting transfers between devices  52.6 us (49%)
  waiting for transfers between devices  29.5 us (28%)
  Pallas kernels  17.5 us (16%)
  local copies, waits for them, and re-layouts  3.3 us (3%)
  between operations  2.09 us (2%)
  other arithmetic  1.8 us (2%)
    ppermute x16, starting transfers between devices, shifted(): lax.ppermute(block, axis, [(i, (i + distance) % n) for i in range(n)])  34.7 us
    ppermute x16, waiting for transfers between devices, shifted(): lax.ppermute(block, axis, [(i, (i + distance) % n) for i in range(n)])  29.5 us
    all_to_all x3, starting transfers between devices, swapped(): lax.all_to_all(blocks, AXES, 0, 0, axis_index_groups=groups, tiled=True)  17.8 us
    pallas_call x8, Pallas kernels, local(): pl.pallas_call(kernel, out_shape=tuple(((pltpu.HBM if spec is HBM else ja...  17.5 us
    unnamed x12, local copies, waits for them, and re-layouts  3.3 us
  transfers between devices with their start and end apart: 19, of which 9 were waited for; matrix products, arithmetic and copies ran while one was open for 2% of the time, Pallas kernels for 2%

profile of v12, /device:TPU:2, one launch (start us, length us, event | category | flops | bytes accessed | tf_op | source)
XLA Modules:
  0.0 106.8 jit_solution(13308582437901799633)
XLA Ops:
  1.6 1.7 %shard_map.59 = bf16[16,64,1152]{2,1,0:T(8,128)(2,1)} custom-call(f32[64,1152]{1,0:T(8,128)S(1)} %copy-done.3), custom_call_target="tpu_custom_call" | custom-call | bytes 1048576 | tf_op jit(solution)/shard_map/pallas_call | solution.py:167
  3.3 7.6 %all-to-all-start = ((bf16[16,64,1152]{2,1,0:T(8,128)(2,1)}), bf16[16,64,1152]{2,1,0:T(8,128)(2,1)S(1)}, u32[]{:S(2)}, u32[]{:S(2)}) async-start(bf16[16,64,1152]{2,1,0:T(8,128)(2,1)} %shard_map.59), calls=%async_computation | async-start | bytes 4718592 | tf_op jit(solution)/shard_map/all_to_all | solution.py:36
  11.1 2.0 %collective-permute-start.4 = (bf16[64,1152]{1,0:T(8,128)(2,1)S(1)}, bf16[64,1152]{1,0:T(8,128)(2,1)S(1)}, u32[]{:S(2)}, u32[]{:S(2)}) collective-permute-start(bf16[64,1152]{1,0:T(8,128)(2,1)S(1)} %shard_map.60.refs_0_), channel_id=1, source_target_pairs={{0,1},{1,2},{2,3},{3,4},{4,5},{5,6},{6,7},{7,0},{8,9},{9,10},{10,1... | collective-permute-start | bytes 442376 | tf_op jit(solution)/shard_map/ppermute | solution.py:41
  13.1 4.0 %collective-permute-start = (bf16[64,1152]{1,0:T(8,128)(2,1)S(1)}, bf16[64,1152]{1,0:T(8,128)(2,1)S(1)}, u32[]{:S(2)}, u32[]{:S(2)}) collective-permute-start(bf16[64,1152]{1,0:T(8,128)(2,1)S(1)} %shard_map.60.refs_0_), channel_id=1, source_target_pairs={{0,7},{1,0},{2,1},{3,2},{4,3},{5,4},{6,5},{7,6},{8,15},{9,8},{10,9... | collective-permute-start | bytes 442376 | tf_op jit(solution)/shard_map/ppermute | solution.py:41
  17.1 3.2 %collective-permute-done.4.refs_7_ = bf16[64,1152]{1,0:T(8,128)(2,1)S(1)} collective-permute-done((bf16[64,1152]{1,0:T(8,128)(2,1)S(1)}, bf16[64,1152]{1,0:T(8,128)(2,1)S(1)}, u32[]{:S(2)}, u32[]{:S(2)}) %collective-permute-start.4) | collective-permute-done | bytes 147488 | tf_op jit(solution)/shard_map/ppermute | solution.py:41
  20.3 3.2 %collective-permute-start.1 = (bf16[64,1152]{1,0:T(8,128)(2,1)S(1)}, bf16[64,1152]{1,0:T(8,128)(2,1)S(1)}, u32[]{:S(2)}, u32[]{:S(2)}) collective-permute-start(bf16[64,1152]{1,0:T(8,128)(2,1)S(1)} %collective-permute-done.refs_1_), channel_id=1, source_target_pairs={{0,7},{1,0},{2,1},{3,2},{4,3},{5,4},{6,5},{7,6},{8,15},{9,8},{10,9... | collective-permute-start | bytes 442376 | tf_op jit(solution)/shard_map/ppermute | solution.py:41
  23.5 4.4 %collective-permute-start.3 = (bf16[64,1152]{1,0:T(8,128)(2,1)S(1)}, bf16[64,1152]{1,0:T(8,128)(2,1)S(1)}, u32[]{:S(2)}, u32[]{:S(2)}) collective-permute-start(bf16[64,1152]{1,0:T(8,128)(2,1)S(1)} %shard_map.60.refs_0_), channel_id=1, source_target_pairs={{0,4},{1,5},{2,6},{3,7},{4,0},{5,1},{6,2},{7,3},{8,12},{9,13},{10,... | collective-permute-start | bytes 442376 | tf_op jit(solution)/shard_map/ppermute | solution.py:41
  28.2 4.8 %collective-permute-done.1.refs_2_ = bf16[64,1152]{1,0:T(8,128)(2,1)S(1)} collective-permute-done((bf16[64,1152]{1,0:T(8,128)(2,1)S(1)}, bf16[64,1152]{1,0:T(8,128)(2,1)S(1)}, u32[]{:S(2)}, u32[]{:S(2)}) %collective-permute-start.1) | collective-permute-done | bytes 147488 | tf_op jit(solution)/shard_map/ppermute | solution.py:41
  32.9 3.8 %collective-permute-start.2 = (bf16[64,1152]{1,0:T(8,128)(2,1)S(1)}, bf16[64,1152]{1,0:T(8,128)(2,1)S(1)}, u32[]{:S(2)}, u32[]{:S(2)}) collective-permute-start(bf16[64,1152]{1,0:T(8,128)(2,1)S(1)} %collective-permute-done.1.refs_2_), channel_id=1, source_target_pairs={{0,7},{1,0},{2,1},{3,2},{4,3},{5,4},{6,5},{7,6},{8,15},{9,8},{10,9... | collective-permute-start | bytes 442376 | tf_op jit(solution)/shard_map/ppermute | solution.py:41
  36.8 2.7 %collective-permute-done.2.refs_3_ = bf16[64,1152]{1,0:T(8,128)(2,1)S(1)} collective-permute-done((bf16[64,1152]{1,0:T(8,128)(2,1)S(1)}, bf16[64,1152]{1,0:T(8,128)(2,1)S(1)}, u32[]{:S(2)}, u32[]{:S(2)}) %collective-permute-start.2) | collective-permute-done | bytes 147488 | tf_op jit(solution)/shard_map/ppermute | solution.py:41
  41.2 1.5 %collective-permute-done.7.xo = bf16[512,1152]{1,0:T(8,128)(2,1)} collective-permute-done((bf16[512,1152]{1,0:T(8,128)(2,1)S(1)}, bf16[512,1152]{1,0:T(8,128)(2,1)}, u32[]{:S(2)}, u32[]{:S(2)}) %collective-permute-start.7) | collective-permute-done | bytes 1179680 | tf_op jit(solution)/shard_map/ppermute | solution.py:41
  42.8 10.8 %shard_map.62 = (f32[512,1152]{1,0:T(8,128)}, bf16[512,1152]{1,0:T(8,128)(2,1)}, bf16[1024,1152]{1,0:T(8,128)(2,1)}) custom-call(s32[1]{0:T(128)} %bitcast.place, f32[2]{0:T(128)S(1)} %pad_maximum_fusion.scal, bf16[512,1152]{1,0:T(8,128)(2,1)S(1)} %shard_map.61.xs, bf16[512,1152]{1,0:T(8,128)(2,1)} %collective-permute-done.7.xo, bf16[1024,1152]{1,0:T(8,128)(2,1)S(1)} %bitcast.5), custom_call_target="tpu_custom_call" | custom-call | flops 7247757312 | bytes 9437184 | tf_op jit(solution)/shard_map/pallas_call | solution.py:167
  53.8 2.9 %collective-permute-done.8.other = bf16[512,1152]{1,0:T(8,128)(2,1)S(1)} collective-permute-done((bf16[512,1152]{1,0:T(8,128)(2,1)}, bf16[512,1152]{1,0:T(8,128)(2,1)S(1)}, u32[]{:S(2)}, u32[]{:S(2)}) %collective-permute-start.8) | collective-permute-done | bytes 1179680 | tf_op jit(solution)/shard_map/ppermute | solution.py:41
  56.7 1.7 %copy-done = f32[512,1152]{1,0:T(8,128)S(1)} copy-done((f32[512,1152]{1,0:T(8,128)S(1)}, f32[512,1152]{1,0:T(8,128)}, u32[]{:S(2)}) %copy-start) | copy-done | bytes 2359320
  60.3 5.0 %all-to-all-start.1 = ((bf16[4,256,1152]{2,1,0:T(8,128)(2,1)}), bf16[4,256,1152]{2,1,0:T(8,128)(2,1)S(1)}, u32[]{:S(2)}, u32[]{:S(2)}) async-start(bf16[4,256,1152]{2,1,0:T(8,128)(2,1)} %bitcast.6), calls=%async_computation.1 | async-start | bytes 4718592 | tf_op jit(solution)/shard_map/all_to_all | solution.py:36
  65.3 6.3 %collective-permute-start.9 = (bf16[64,1152]{1,0:T(8,128)(2,1)S(1)}, bf16[64,1152]{1,0:T(8,128)(2,1)S(1)}, u32[]{:S(2)}, u32[]{:S(2)}) collective-permute-start(bf16[64,1152]{1,0:T(8,128)(2,1)S(1)} %get-tuple-element.25), channel_id=1, source_target_pairs={{0,4},{1,5},{2,6},{3,7},{4,0},{5,1},{6,2},{7,3},{8,12},{9,13},{10,... | collective-permute-start | bytes 442376 | tf_op jit(solution)/shard_map/ppermute | solution.py:41
  71.6 2.2 %collective-permute-start.12 = (bf16[64,1152]{1,0:T(8,128)(2,1)}, bf16[64,1152]{1,0:T(8,128)(2,1)S(1)}, u32[]{:S(2)}, u32[]{:S(2)}) collective-permute-start(bf16[64,1152]{1,0:T(8,128)(2,1)} %copy-done.5), channel_id=1, source_target_pairs={{0,7},{1,0},{2,1},{3,2},{4,3},{5,4},{6,5},{7,6},{8,15},{9,8},{10,9... | collective-permute-start | bytes 442376 | tf_op jit(solution)/shard_map/ppermute | solution.py:41
  74.9 7.4 %collective-permute-done.12 = bf16[64,1152]{1,0:T(8,128)(2,1)S(1)} collective-permute-done((bf16[64,1152]{1,0:T(8,128)(2,1)}, bf16[64,1152]{1,0:T(8,128)(2,1)S(1)}, u32[]{:S(2)}, u32[]{:S(2)}) %collective-permute-start.12) | collective-permute-done | bytes 147488 | tf_op jit(solution)/shard_map/ppermute | solution.py:41
  82.3 4.0 %collective-permute-start.13 = (bf16[64,1152]{1,0:T(8,128)(2,1)S(1)}, bf16[64,1152]{1,0:T(8,128)(2,1)S(1)}, u32[]{:S(2)}, u32[]{:S(2)}) collective-permute-start(bf16[64,1152]{1,0:T(8,128)(2,1)S(1)} %add_convert_fusion.1), channel_id=1, source_target_pairs={{0,7},{1,0},{2,1},{3,2},{4,3},{5,4},{6,5},{7,6},{8,15},{9,8},{10,9... | collective-permute-start | bytes 442376 | tf_op jit(solution)/shard_map/ppermute | solution.py:41
  86.4 3.7 %collective-permute-done.13 = bf16[64,1152]{1,0:T(8,128)(2,1)S(1)} collective-permute-done((bf16[64,1152]{1,0:T(8,128)(2,1)S(1)}, bf16[64,1152]{1,0:T(8,128)(2,1)S(1)}, u32[]{:S(2)}, u32[]{:S(2)}) %collective-permute-start.13) | collective-permute-done | bytes 147488 | tf_op jit(solution)/shard_map/ppermute | solution.py:41
  91.7 5.2 %all-to-all-start.2 = ((bf16[4,64,1152]{2,1,0:T(8,128)(2,1)}), bf16[4,64,1152]{2,1,0:T(8,128)(2,1)S(1)}, u32[]{:S(2)}, u32[]{:S(2)}) async-start(bf16[4,64,1152]{2,1,0:T(8,128)(2,1)} %shard_map.65), calls=%async_computation.2 | async-start | bytes 1179648 | tf_op jit(solution)/shard_map/all_to_all | solution.py:36
  97.5 3.2 %collective-permute-start.15 = (bf16[64,1152]{1,0:T(8,128)(2,1)}, bf16[64,1152]{1,0:T(8,128)(2,1)S(1)}, u32[]{:S(2)}, u32[]{:S(2)}) collective-permute-start(bf16[64,1152]{1,0:T(8,128)(2,1)} %add_convert_fusion), channel_id=1, source_target_pairs={{0,7},{1,0},{2,1},{3,2},{4,3},{5,4},{6,5},{7,6},{8,15},{9,8},{10,9... | collective-permute-start | bytes 442376 | tf_op jit(solution)/shard_map/ppermute | solution.py:41
  100.7 3.1 %collective-permute-done.14.refs_2_ = bf16[64,1152]{1,0:T(8,128)(2,1)S(1)} collective-permute-done((bf16[64,1152]{1,0:T(8,128)(2,1)S(1)}, bf16[64,1152]{1,0:T(8,128)(2,1)S(1)}, u32[]{:S(2)}, u32[]{:S(2)}) %collective-permute-start.14) | collective-permute-done | bytes 147488 | tf_op jit(solution)/shard_map/ppermute | solution.py:41
  105.3 1.5 %shard_map.66 = f32[64,1152]{1,0:T(8,128)} custom-call(f32[2]{0:T(128)S(1)} %pad_maximum_fusion.scal, f32[64,1152]{1,0:T(8,128)S(1)} %copy-done.4, bf16[4,64,1152]{2,1,0:T(8,128)(2,1)S(1)} %all-to-all-done.2.got), custom_call_target="tpu_custom_call" | custom-call | bytes 1048576 | tf_op jit(solution)/shard_map/pallas_call | solution.py:167
  (39 shorter events, 8.7 us)
Async XLA Ops:
  0.6 1.0 copy-start.3
  3.3 7.6 %copy-start.1 = (f32[64,1152]{1,0:T(8,128)S(1)}, f32[64,1152]{1,0:T(8,128)}, u32[]{:S(2)}) copy-start(f32[64,1152]{1,0:T(8,128)} %raw.4) | copy-start | bytes 884740
  3.3 39.5 %all-to-all-start = ((bf16[16,64,1152]{2,1,0:T(8,128)(2,1)}), bf16[16,64,1152]{2,1,0:T(8,128)(2,1)S(1)}, u32[]{:S(2)}, u32[]{:S(2)}) async-start(bf16[16,64,1152]{2,1,0:T(8,128)(2,1)} %shard_map.59), calls=%async_computation | async-start | bytes 4718592 | tf_op jit(solution)/shard_map/all_to_all | solution.py:36
  11.1 9.2 %collective-permute-start.4 = (bf16[64,1152]{1,0:T(8,128)(2,1)S(1)}, bf16[64,1152]{1,0:T(8,128)(2,1)S(1)}, u32[]{:S(2)}, u32[]{:S(2)}) collective-permute-start(bf16[64,1152]{1,0:T(8,128)(2,1)S(1)} %shard_map.60.refs_0_), channel_id=1, source_target_pairs={{0,1},{1,2},{2,3},{3,4},{4,5},{5,6},{6,7},{7,0},{8,9},{9,10},{10,1... | collective-permute-start | bytes 442376 | tf_op jit(solution)/shard_map/ppermute | solution.py:41
  13.1 7.2 %collective-permute-start = (bf16[64,1152]{1,0:T(8,128)(2,1)S(1)}, bf16[64,1152]{1,0:T(8,128)(2,1)S(1)}, u32[]{:S(2)}, u32[]{:S(2)}) collective-permute-start(bf16[64,1152]{1,0:T(8,128)(2,1)S(1)} %shard_map.60.refs_0_), channel_id=1, source_target_pairs={{0,7},{1,0},{2,1},{3,2},{4,3},{5,4},{6,5},{7,6},{8,15},{9,8},{10,9... | collective-permute-start | bytes 442376 | tf_op jit(solution)/shard_map/ppermute | solution.py:41
  20.3 7.9 %collective-permute-start.5 = (bf16[64,1152]{1,0:T(8,128)(2,1)S(1)}, bf16[64,1152]{1,0:T(8,128)(2,1)S(1)}, u32[]{:S(2)}, u32[]{:S(2)}) collective-permute-start(bf16[64,1152]{1,0:T(8,128)(2,1)S(1)} %collective-permute-done.4.refs_7_), channel_id=1, source_target_pairs={{0,1},{1,2},{2,3},{3,4},{4,5},{5,6},{6,7},{7,0},{8,9},{9,10},{10,1... | collective-permute-start | bytes 442376 | tf_op jit(solution)/shard_map/ppermute | solution.py:41
  20.3 12.6 %collective-permute-start.1 = (bf16[64,1152]{1,0:T(8,128)(2,1)S(1)}, bf16[64,1152]{1,0:T(8,128)(2,1)S(1)}, u32[]{:S(2)}, u32[]{:S(2)}) collective-permute-start(bf16[64,1152]{1,0:T(8,128)(2,1)S(1)} %collective-permute-done.refs_1_), channel_id=1, source_target_pairs={{0,7},{1,0},{2,1},{3,2},{4,3},{5,4},{6,5},{7,6},{8,15},{9,8},{10,9... | collective-permute-start | bytes 442376 | tf_op jit(solution)/shard_map/ppermute | solution.py:41
  23.5 13.2 %collective-permute-start.3 = (bf16[64,1152]{1,0:T(8,128)(2,1)S(1)}, bf16[64,1152]{1,0:T(8,128)(2,1)S(1)}, u32[]{:S(2)}, u32[]{:S(2)}) collective-permute-start(bf16[64,1152]{1,0:T(8,128)(2,1)S(1)} %shard_map.60.refs_0_), channel_id=1, source_target_pairs={{0,4},{1,5},{2,6},{3,7},{4,0},{5,1},{6,2},{7,3},{8,12},{9,13},{10,... | collective-permute-start | bytes 442376 | tf_op jit(solution)/shard_map/ppermute | solution.py:41
  28.1 8.6 %collective-permute-start.6 = (bf16[64,1152]{1,0:T(8,128)(2,1)S(1)}, bf16[64,1152]{1,0:T(8,128)(2,1)S(1)}, u32[]{:S(2)}, u32[]{:S(2)}) collective-permute-start(bf16[64,1152]{1,0:T(8,128)(2,1)S(1)} %collective-permute-done.5.refs_6_), channel_id=1, source_target_pairs={{0,1},{1,2},{2,3},{3,4},{4,5},{5,6},{6,7},{7,0},{8,9},{9,10},{10,1... | collective-permute-start | bytes 442376 | tf_op jit(solution)/shard_map/ppermute | solution.py:41
  32.9 6.5 %collective-permute-start.2 = (bf16[64,1152]{1,0:T(8,128)(2,1)S(1)}, bf16[64,1152]{1,0:T(8,128)(2,1)S(1)}, u32[]{:S(2)}, u32[]{:S(2)}) collective-permute-start(bf16[64,1152]{1,0:T(8,128)(2,1)S(1)} %collective-permute-done.1.refs_2_), channel_id=1, source_target_pairs={{0,7},{1,0},{2,1},{3,2},{4,3},{5,4},{6,5},{7,6},{8,15},{9,8},{10,9... | collective-permute-start | bytes 442376 | tf_op jit(solution)/shard_map/ppermute | solution.py:41
  39.5 3.2 %collective-permute-start.7 = (bf16[512,1152]{1,0:T(8,128)(2,1)S(1)}, bf16[512,1152]{1,0:T(8,128)(2,1)}, u32[]{:S(2)}, u32[]{:S(2)}) collective-permute-start(bf16[512,1152]{1,0:T(8,128)(2,1)S(1)} %shard_map.61.xs), channel_id=1, source_target_pairs={{0,16},{16,0},{1,17},{17,1},{2,18},{18,2},{3,19},{19,3},{4,20},{20... | collective-permute-start | bytes 3538952 | tf_op jit(solution)/shard_map/ppermute | solution.py:41
  53.6 3.1 %collective-permute-start.8 = (bf16[512,1152]{1,0:T(8,128)(2,1)}, bf16[512,1152]{1,0:T(8,128)(2,1)S(1)}, u32[]{:S(2)}, u32[]{:S(2)}) collective-permute-start(bf16[512,1152]{1,0:T(8,128)(2,1)} %get-tuple-element.22), channel_id=1, source_target_pairs={{0,16},{16,0},{1,17},{17,1},{2,18},{18,2},{3,19},{19,3},{4,20},{20... | collective-permute-start | bytes 3538952 | tf_op jit(solution)/shard_map/ppermute | solution.py:41
  56.7 1.7 %copy-start = (f32[512,1152]{1,0:T(8,128)S(1)}, f32[512,1152]{1,0:T(8,128)}, u32[]{:S(2)}) copy-start(f32[512,1152]{1,0:T(8,128)} %get-tuple-element.21.dxs) | copy-start | bytes 7077892
  59.9 13.9 %collective-permute-start.10 = (bf16[64,1152]{1,0:T(8,128)(2,1)}, bf16[64,1152]{1,0:T(8,128)(2,1)}, u32[]{:S(2)}, u32[]{:S(2)}) collective-permute-start(bf16[64,1152]{1,0:T(8,128)(2,1)} %get-tuple-element.28), channel_id=1, source_target_pairs={{0,1},{1,2},{2,3},{3,4},{4,5},{5,6},{6,7},{7,0},{8,9},{9,10},{10,1... | collective-permute-start | bytes 442376 | tf_op jit(solution)/shard_map/ppermute | solution.py:41
  60.3 30.4 %all-to-all-start.1 = ((bf16[4,256,1152]{2,1,0:T(8,128)(2,1)}), bf16[4,256,1152]{2,1,0:T(8,128)(2,1)S(1)}, u32[]{:S(2)}, u32[]{:S(2)}) async-start(bf16[4,256,1152]{2,1,0:T(8,128)(2,1)} %bitcast.6), calls=%async_computation.1 | async-start | bytes 4718592 | tf_op jit(solution)/shard_map/all_to_all | solution.py:36
  65.3 25.4 %collective-permute-start.9 = (bf16[64,1152]{1,0:T(8,128)(2,1)S(1)}, bf16[64,1152]{1,0:T(8,128)(2,1)S(1)}, u32[]{:S(2)}, u32[]{:S(2)}) collective-permute-start(bf16[64,1152]{1,0:T(8,128)(2,1)S(1)} %get-tuple-element.25), channel_id=1, source_target_pairs={{0,4},{1,5},{2,6},{3,7},{4,0},{5,1},{6,2},{7,3},{8,12},{9,13},{10,... | collective-permute-start | bytes 442376 | tf_op jit(solution)/shard_map/ppermute | solution.py:41
  71.6 10.6 %collective-permute-start.12 = (bf16[64,1152]{1,0:T(8,128)(2,1)}, bf16[64,1152]{1,0:T(8,128)(2,1)S(1)}, u32[]{:S(2)}, u32[]{:S(2)}) collective-permute-start(bf16[64,1152]{1,0:T(8,128)(2,1)} %copy-done.5), channel_id=1, source_target_pairs={{0,7},{1,0},{2,1},{3,2},{4,3},{5,4},{6,5},{7,6},{8,15},{9,8},{10,9... | collective-permute-start | bytes 442376 | tf_op jit(solution)/shard_map/ppermute | solution.py:41
  74.8 11.5 %collective-permute-start.11 = (bf16[64,1152]{1,0:T(8,128)(2,1)S(1)}, bf16[64,1152]{1,0:T(8,128)(2,1)S(1)}, u32[]{:S(2)}, u32[]{:S(2)}) collective-permute-start(bf16[64,1152]{1,0:T(8,128)(2,1)S(1)} %add_convert_fusion.3), channel_id=1, source_target_pairs={{0,1},{1,2},{2,3},{3,4},{4,5},{5,6},{6,7},{7,0},{8,9},{9,10},{10,1... | collective-permute-start | bytes 442376 | tf_op jit(solution)/shard_map/ppermute | solution.py:41
  82.3 7.8 %collective-permute-start.13 = (bf16[64,1152]{1,0:T(8,128)(2,1)S(1)}, bf16[64,1152]{1,0:T(8,128)(2,1)S(1)}, u32[]{:S(2)}, u32[]{:S(2)}) collective-permute-start(bf16[64,1152]{1,0:T(8,128)(2,1)S(1)} %add_convert_fusion.1), channel_id=1, source_target_pairs={{0,7},{1,0},{2,1},{3,2},{4,3},{5,4},{6,5},{7,6},{8,15},{9,8},{10,9... | collective-permute-start | bytes 442376 | tf_op jit(solution)/shard_map/ppermute | solution.py:41
  86.4 17.4 %copy-start.2 = (f32[64,1152]{1,0:T(8,128)S(1)}, f32[64,1152]{1,0:T(8,128)}, u32[]{:S(2)}) copy-start(f32[64,1152]{1,0:T(8,128)} %raw.4) | copy-start | bytes 884740
  90.7 14.5 %copy-start.4 = (f32[64,1152]{1,0:T(8,128)S(1)}, f32[64,1152]{1,0:T(8,128)}, u32[]{:S(2)}) copy-start(f32[64,1152]{1,0:T(8,128)} %raw.5) | copy-start | bytes 884740
  91.7 13.5 %all-to-all-start.2 = ((bf16[4,64,1152]{2,1,0:T(8,128)(2,1)}), bf16[4,64,1152]{2,1,0:T(8,128)(2,1)S(1)}, u32[]{:S(2)}, u32[]{:S(2)}) async-start(bf16[4,64,1152]{2,1,0:T(8,128)(2,1)} %shard_map.65), calls=%async_computation.2 | async-start | bytes 1179648 | tf_op jit(solution)/shard_map/all_to_all | solution.py:36
  97.0 6.8 %collective-permute-start.14 = (bf16[64,1152]{1,0:T(8,128)(2,1)S(1)}, bf16[64,1152]{1,0:T(8,128)(2,1)S(1)}, u32[]{:S(2)}, u32[]{:S(2)}) collective-permute-start(bf16[64,1152]{1,0:T(8,128)(2,1)S(1)} %add_convert_fusion.2), channel_id=1, source_target_pairs={{0,1},{1,2},{2,3},{3,4},{4,5},{5,6},{6,7},{7,0},{8,9},{9,10},{10,1... | collective-permute-start | bytes 442376 | tf_op jit(solution)/shard_map/ppermute | solution.py:41
  97.5 6.3 %collective-permute-start.15 = (bf16[64,1152]{1,0:T(8,128)(2,1)}, bf16[64,1152]{1,0:T(8,128)(2,1)S(1)}, u32[]{:S(2)}, u32[]{:S(2)}) collective-permute-start(bf16[64,1152]{1,0:T(8,128)(2,1)} %add_convert_fusion), channel_id=1, source_target_pairs={{0,7},{1,0},{2,1},{3,2},{4,3},{5,4},{6,5},{7,6},{8,15},{9,8},{10,9... | collective-permute-start | bytes 442376 | tf_op jit(solution)/shard_map/ppermute | solution.py:41
  (1 other events, 0.7 us)

commit v13 on v11

--- a/solution.py
+++ b/solution.py
@@ -188,11 +188,10 @@
     return up + [far] + down[:0:-1]
 
 
-def near_reduce(rest):
+def near_step(rest):
     direct = [shifted(rest[k - 1], "z", k) for k in (4, 3, 5)]
     up, down = shifted(rest[1], "z", 1), shifted(rest[5], "z", -1)
-    up, down = shifted(add(rest[0], up), "z", 1), shifted(add(rest[6], down), "z", -1)
-    return direct + [up, down]
+    return direct, add(rest[0], up), add(rest[6], down)
 
 
 def on_device(images, texts, log_temp, bias):
@@ -234,13 +233,14 @@
         join_kernel, [((rows, width), F32, VMEM), ((half - rows, width), BF, VMEM)], [dxs, other],
         nbytes=5 * 2**20, vmem=16,
     )
-    got = near_reduce(rest.reshape(-1, rows, width))
-    half_way, *got[3:] = lax.optimization_barrier((half_way, *got[3:]))
+    direct, up, down = near_step(rest.reshape(-1, rows, width))
+    half_way, up, down = lax.optimization_barrier((half_way, up, down))
     (half_way,) = local(
         sum_kernel, [((4, rows, width), BF, HBM)], [half_way.reshape(4, 4, rows, width)], nbytes=3 * 2**20, vmem=16,
         scratch=[pltpu.VMEM((4, rows, width), BF), pltpu.SemaphoreType.DMA((4,))],
     )
     dyr = swapped(half_way, INNER)
+    got = direct + [shifted(up, "z", 1), shifted(down, "z", -1)]
     (grad_images,) = local(finish_kernel, [((rows, width), F32, VMEM)], [scal, images, own] + got, smem=1)
     (grad_texts,) = local(finish_texts_kernel, [((rows, width), F32, VMEM)], [scal, texts, dyr], smem=1)
     return (grad_images, grad_texts)

time: 112 us -> 115 us (1.027)
  starting transfers between devices: 48.5 us -> 55.4 us
  waiting for transfers between devices: 40.5 us -> 36.3 us
    ppermute x16, starting transfers between devices: 31.2 us -> 38.2 us  [shifted(): lax.ppermute(block, axis, [(i, (i + distance) % n) for i in range(n)])]
    ppermute x16, waiting for transfers between devices: 40.5 us -> 35.5 us  [shifted(): lax.ppermute(block, axis, [(i, (i + distance) % n) for i in range(n)])]
where the time goes in v13:
time: 115 us
  starting transfers between devices  55.4 us (48%)
  waiting for transfers between devices  36.3 us (32%)
  Pallas kernels  16.8 us (15%)
  local copies, waits for them, and re-layouts  3.39 us (3%)
  between operations  2.08 us (2%)
    ppermute x16, starting transfers between devices, shifted(): lax.ppermute(block, axis, [(i, (i + distance) % n) for i in range(n)])  38.2 us
    ppermute x16, waiting for transfers between devices, shifted(): lax.ppermute(block, axis, [(i, (i + distance) % n) for i in range(n)])  35.5 us
    all_to_all x3, starting transfers between devices, swapped(): lax.all_to_all(blocks, AXES, 0, 0, axis_index_groups=groups, tiled=True)  17.3 us
    pallas_call x8, Pallas kernels, local(): pl.pallas_call(kernel, out_shape=tuple(((pltpu.HBM if spec is HBM else ja...  16.8 us
    unnamed x14, local copies, waits for them, and re-layouts  2.65 us
  transfers between devices with their start and end apart: 19, of which 11 were waited for; matrix products, arithmetic and copies ran while one was open for 1% of the time, Pallas kernels for 2%

profile of v13, /device:TPU:8, one launch (start us, length us, event | category | flops | bytes accessed | tf_op | source)
XLA Modules:
  0.0 114.9 jit_solution(16362576081404093017)
XLA Ops:
  1.6 1.7 %shard_map.59 = bf16[16,64,1152]{2,1,0:T(8,128)(2,1)} custom-call(f32[64,1152]{1,0:T(8,128)S(1)} %copy-done.3), custom_call_target="tpu_custom_call" | custom-call | bytes 1048576 | tf_op jit(solution)/shard_map/pallas_call | solution.py:166
  3.3 7.5 %all-to-all-start = ((bf16[16,64,1152]{2,1,0:T(8,128)(2,1)}), bf16[16,64,1152]{2,1,0:T(8,128)(2,1)S(1)}, u32[]{:S(2)}, u32[]{:S(2)}) async-start(bf16[16,64,1152]{2,1,0:T(8,128)(2,1)} %shard_map.59), calls=%async_computation | async-start | bytes 4718592 | tf_op jit(solution)/shard_map/all_to_all | solution.py:36
  11.0 2.0 %collective-permute-start.4 = (bf16[64,1152]{1,0:T(8,128)(2,1)S(1)}, bf16[64,1152]{1,0:T(8,128)(2,1)S(1)}, u32[]{:S(2)}, u32[]{:S(2)}) collective-permute-start(bf16[64,1152]{1,0:T(8,128)(2,1)S(1)} %shard_map.60.refs_0_), channel_id=1, source_target_pairs={{0,1},{1,2},{2,3},{3,4},{4,5},{5,6},{6,7},{7,0},{8,9},{9,10},{10,1... | collective-permute-start | bytes 442376 | tf_op jit(solution)/shard_map/ppermute | solution.py:41
  13.0 4.0 %collective-permute-start = (bf16[64,1152]{1,0:T(8,128)(2,1)S(1)}, bf16[64,1152]{1,0:T(8,128)(2,1)S(1)}, u32[]{:S(2)}, u32[]{:S(2)}) collective-permute-start(bf16[64,1152]{1,0:T(8,128)(2,1)S(1)} %shard_map.60.refs_0_), channel_id=1, source_target_pairs={{0,7},{1,0},{2,1},{3,2},{4,3},{5,4},{6,5},{7,6},{8,15},{9,8},{10,9... | collective-permute-start | bytes 442376 | tf_op jit(solution)/shard_map/ppermute | solution.py:41
  17.0 3.2 %collective-permute-done.4.refs_7_ = bf16[64,1152]{1,0:T(8,128)(2,1)S(1)} collective-permute-done((bf16[64,1152]{1,0:T(8,128)(2,1)S(1)}, bf16[64,1152]{1,0:T(8,128)(2,1)S(1)}, u32[]{:S(2)}, u32[]{:S(2)}) %collective-permute-start.4) | collective-permute-done | bytes 147488 | tf_op jit(solution)/shard_map/ppermute | solution.py:41
  20.2 3.2 %collective-permute-start.1 = (bf16[64,1152]{1,0:T(8,128)(2,1)S(1)}, bf16[64,1152]{1,0:T(8,128)(2,1)S(1)}, u32[]{:S(2)}, u32[]{:S(2)}) collective-permute-start(bf16[64,1152]{1,0:T(8,128)(2,1)S(1)} %collective-permute-done.refs_1_), channel_id=1, source_target_pairs={{0,7},{1,0},{2,1},{3,2},{4,3},{5,4},{6,5},{7,6},{8,15},{9,8},{10,9... | collective-permute-start | bytes 442376 | tf_op jit(solution)/shard_map/ppermute | solution.py:41
  23.4 4.4 %collective-permute-start.3 = (bf16[64,1152]{1,0:T(8,128)(2,1)S(1)}, bf16[64,1152]{1,0:T(8,128)(2,1)S(1)}, u32[]{:S(2)}, u32[]{:S(2)}) collective-permute-start(bf16[64,1152]{1,0:T(8,128)(2,1)S(1)} %shard_map.60.refs_0_), channel_id=1, source_target_pairs={{0,4},{1,5},{2,6},{3,7},{4,0},{5,1},{6,2},{7,3},{8,12},{9,13},{10,... | collective-permute-start | bytes 442376 | tf_op jit(solution)/shard_map/ppermute | solution.py:41
  28.0 4.9 %collective-permute-done.1.refs_2_ = bf16[64,1152]{1,0:T(8,128)(2,1)S(1)} collective-permute-done((bf16[64,1152]{1,0:T(8,128)(2,1)S(1)}, bf16[64,1152]{1,0:T(8,128)(2,1)S(1)}, u32[]{:S(2)}, u32[]{:S(2)}) %collective-permute-start.1) | collective-permute-done | bytes 147488 | tf_op jit(solution)/shard_map/ppermute | solution.py:41
  33.0 3.8 %collective-permute-start.2 = (bf16[64,1152]{1,0:T(8,128)(2,1)S(1)}, bf16[64,1152]{1,0:T(8,128)(2,1)S(1)}, u32[]{:S(2)}, u32[]{:S(2)}) collective-permute-start(bf16[64,1152]{1,0:T(8,128)(2,1)S(1)} %collective-permute-done.1.refs_2_), channel_id=1, source_target_pairs={{0,7},{1,0},{2,1},{3,2},{4,3},{5,4},{6,5},{7,6},{8,15},{9,8},{10,9... | collective-permute-start | bytes 442376 | tf_op jit(solution)/shard_map/ppermute | solution.py:41
  36.8 2.7 %collective-permute-done.2.refs_3_ = bf16[64,1152]{1,0:T(8,128)(2,1)S(1)} collective-permute-done((bf16[64,1152]{1,0:T(8,128)(2,1)S(1)}, bf16[64,1152]{1,0:T(8,128)(2,1)S(1)}, u32[]{:S(2)}, u32[]{:S(2)}) %collective-permute-start.2) | collective-permute-done | bytes 147488 | tf_op jit(solution)/shard_map/ppermute | solution.py:41
  41.3 1.5 %collective-permute-done.7.xo = bf16[512,1152]{1,0:T(8,128)(2,1)} collective-permute-done((bf16[512,1152]{1,0:T(8,128)(2,1)S(1)}, bf16[512,1152]{1,0:T(8,128)(2,1)}, u32[]{:S(2)}, u32[]{:S(2)}) %collective-permute-start.7) | collective-permute-done | bytes 1179680 | tf_op jit(solution)/shard_map/ppermute | solution.py:41
  42.8 10.7 %shard_map.62 = (f32[512,1152]{1,0:T(8,128)}, bf16[512,1152]{1,0:T(8,128)(2,1)}, bf16[1024,1152]{1,0:T(8,128)(2,1)}) custom-call(s32[1]{0:T(128)} %bitcast.place, f32[2]{0:T(128)S(1)} %pad_maximum_fusion.scal, bf16[512,1152]{1,0:T(8,128)(2,1)S(1)} %shard_map.61.xs, bf16[512,1152]{1,0:T(8,128)(2,1)} %collective-permute-done.7.xo, bf16[1024,1152]{1,0:T(8,128)(2,1)S(1)} %bitcast.5), custom_call_target="tpu_custom_call" | custom-call | flops 7247757312 | bytes 9437184 | tf_op jit(solution)/shard_map/pallas_call | solution.py:166
  53.7 6.2 %all-to-all-start.1 = ((bf16[4,256,1152]{2,1,0:T(8,128)(2,1)}), bf16[4,256,1152]{2,1,0:T(8,128)(2,1)S(1)}, u32[]{:S(2)}, u32[]{:S(2)}) async-start(bf16[4,256,1152]{2,1,0:T(8,128)(2,1)} %bitcast.6), calls=%async_computation.1 | async-start | bytes 4718592 | tf_op jit(solution)/shard_map/all_to_all | solution.py:36
  59.9 1.7 %copy-done = f32[512,1152]{1,0:T(8,128)S(1)} copy-done((f32[512,1152]{1,0:T(8,128)S(1)}, f32[512,1152]{1,0:T(8,128)}, u32[]{:S(2)}) %copy-start) | copy-done | bytes 2359320
  62.6 5.9 %collective-permute-start.13 = (bf16[64,1152]{1,0:T(8,128)(2,1)S(1)}, bf16[64,1152]{1,0:T(8,128)(2,1)S(1)}, u32[]{:S(2)}, u32[]{:S(2)}) collective-permute-start(bf16[64,1152]{1,0:T(8,128)(2,1)S(1)} %get-tuple-element.24), channel_id=1, source_target_pairs={{0,7},{1,0},{2,1},{3,2},{4,3},{5,4},{6,5},{7,6},{8,15},{9,8},{10,9... | collective-permute-start | bytes 442376 | tf_op jit(solution)/shard_map/ppermute | solution.py:41
  68.4 2.7 %collective-permute-done.13 = bf16[64,1152]{1,0:T(8,128)(2,1)S(1)} collective-permute-done((bf16[64,1152]{1,0:T(8,128)(2,1)S(1)}, bf16[64,1152]{1,0:T(8,128)(2,1)S(1)}, u32[]{:S(2)}, u32[]{:S(2)}) %collective-permute-start.13) | collective-permute-done | bytes 147488 | tf_op jit(solution)/shard_map/ppermute | solution.py:41
  71.1 3.7 %collective-permute-done.12 = bf16[64,1152]{1,0:T(8,128)(2,1)S(1)} collective-permute-done((bf16[64,1152]{1,0:T(8,128)(2,1)S(1)}, bf16[64,1152]{1,0:T(8,128)(2,1)S(1)}, u32[]{:S(2)}, u32[]{:S(2)}) %collective-permute-start.12) | collective-permute-done | bytes 147488 | tf_op jit(solution)/shard_map/ppermute | solution.py:41
  77.4 3.5 %all-to-all-start.2 = ((bf16[4,64,1152]{2,1,0:T(8,128)(2,1)}), bf16[4,64,1152]{2,1,0:T(8,128)(2,1)S(1)}, u32[]{:S(2)}, u32[]{:S(2)}) async-start(bf16[4,64,1152]{2,1,0:T(8,128)(2,1)} %shard_map.65), calls=%async_computation.2 | async-start | bytes 1179648 | tf_op jit(solution)/shard_map/all_to_all | solution.py:36
  80.9 6.8 %collective-permute-start.11 = (bf16[64,1152]{1,0:T(8,128)(2,1)}, bf16[64,1152]{1,0:T(8,128)(2,1)S(1)}, u32[]{:S(2)}, u32[]{:S(2)}) collective-permute-start(bf16[64,1152]{1,0:T(8,128)(2,1)} %get-tuple-element.26), channel_id=1, source_target_pairs={{0,5},{1,6},{2,7},{3,0},{4,1},{5,2},{6,3},{7,4},{8,13},{9,14},{10,... | collective-permute-start | bytes 442376 | tf_op jit(solution)/shard_map/ppermute | solution.py:41
  87.7 4.3 %collective-permute-start.9 = (bf16[64,1152]{1,0:T(8,128)(2,1)S(1)}, bf16[64,1152]{1,0:T(8,128)(2,1)S(1)}, u32[]{:S(2)}, u32[]{:S(2)}) collective-permute-start(bf16[64,1152]{1,0:T(8,128)(2,1)S(1)} %get-tuple-element.28), channel_id=1, source_target_pairs={{0,4},{1,5},{2,6},{3,7},{4,0},{5,1},{6,2},{7,3},{8,12},{9,13},{10,... | collective-permute-start | bytes 442376 | tf_op jit(solution)/shard_map/ppermute | solution.py:41
  92.0 2.2 %collective-permute-start.14 = (bf16[64,1152]{1,0:T(8,128)(2,1)}, bf16[64,1152]{1,0:T(8,128)(2,1)S(1)}, u32[]{:S(2)}, u32[]{:S(2)}) collective-permute-start(bf16[64,1152]{1,0:T(8,128)(2,1)} %get-tuple-element.19), channel_id=1, source_target_pairs={{0,1},{1,2},{2,3},{3,4},{4,5},{5,6},{6,7},{7,0},{8,9},{9,10},{10,1... | collective-permute-start | bytes 442376 | tf_op jit(solution)/shard_map/ppermute | solution.py:41
  95.2 9.7 %collective-permute-done.11.refs_3_ = bf16[64,1152]{1,0:T(8,128)(2,1)S(1)} collective-permute-done((bf16[64,1152]{1,0:T(8,128)(2,1)}, bf16[64,1152]{1,0:T(8,128)(2,1)S(1)}, u32[]{:S(2)}, u32[]{:S(2)}) %collective-permute-start.11) | collective-permute-done | bytes 147488 | tf_op jit(solution)/shard_map/ppermute | solution.py:41
  104.9 2.7 %collective-permute-done.10.refs_2_ = bf16[64,1152]{1,0:T(8,128)(2,1)S(1)} collective-permute-done((bf16[64,1152]{1,0:T(8,128)(2,1)S(1)}, bf16[64,1152]{1,0:T(8,128)(2,1)S(1)}, u32[]{:S(2)}, u32[]{:S(2)}) %collective-permute-start.10) | collective-permute-done | bytes 147488 | tf_op jit(solution)/shard_map/ppermute | solution.py:41
  107.6 4.2 %collective-permute-done.14.refs_4_ = bf16[64,1152]{1,0:T(8,128)(2,1)S(1)} collective-permute-done((bf16[64,1152]{1,0:T(8,128)(2,1)}, bf16[64,1152]{1,0:T(8,128)(2,1)S(1)}, u32[]{:S(2)}, u32[]{:S(2)}) %collective-permute-start.14) | collective-permute-done | bytes 147488 | tf_op jit(solution)/shard_map/ppermute | solution.py:41
  (39 shorter events, 9.6 us)
Async XLA Ops:
  3.3 7.6 %copy-start.1 = (f32[64,1152]{1,0:T(8,128)S(1)}, f32[64,1152]{1,0:T(8,128)}, u32[]{:S(2)}) copy-start(f32[64,1152]{1,0:T(8,128)} %raw.4) | copy-start | bytes 884740
  3.3 39.5 %all-to-all-start = ((bf16[16,64,1152]{2,1,0:T(8,128)(2,1)}), bf16[16,64,1152]{2,1,0:T(8,128)(2,1)S(1)}, u32[]{:S(2)}, u32[]{:S(2)}) async-start(bf16[16,64,1152]{2,1,0:T(8,128)(2,1)} %shard_map.59), calls=%async_computation | async-start | bytes 4718592 | tf_op jit(solution)/shard_map/all_to_all | solution.py:36
  11.0 9.2 %collective-permute-start.4 = (bf16[64,1152]{1,0:T(8,128)(2,1)S(1)}, bf16[64,1152]{1,0:T(8,128)(2,1)S(1)}, u32[]{:S(2)}, u32[]{:S(2)}) collective-permute-start(bf16[64,1152]{1,0:T(8,128)(2,1)S(1)} %shard_map.60.refs_0_), channel_id=1, source_target_pairs={{0,1},{1,2},{2,3},{3,4},{4,5},{5,6},{6,7},{7,0},{8,9},{9,10},{10,1... | collective-permute-start | bytes 442376 | tf_op jit(solution)/shard_map/ppermute | solution.py:41
  13.0 7.2 %collective-permute-start = (bf16[64,1152]{1,0:T(8,128)(2,1)S(1)}, bf16[64,1152]{1,0:T(8,128)(2,1)S(1)}, u32[]{:S(2)}, u32[]{:S(2)}) collective-permute-start(bf16[64,1152]{1,0:T(8,128)(2,1)S(1)} %shard_map.60.refs_0_), channel_id=1, source_target_pairs={{0,7},{1,0},{2,1},{3,2},{4,3},{5,4},{6,5},{7,6},{8,15},{9,8},{10,9... | collective-permute-start | bytes 442376 | tf_op jit(solution)/shard_map/ppermute | solution.py:41
  20.2 7.8 %collective-permute-start.5 = (bf16[64,1152]{1,0:T(8,128)(2,1)S(1)}, bf16[64,1152]{1,0:T(8,128)(2,1)S(1)}, u32[]{:S(2)}, u32[]{:S(2)}) collective-permute-start(bf16[64,1152]{1,0:T(8,128)(2,1)S(1)} %collective-permute-done.4.refs_7_), channel_id=1, source_target_pairs={{0,1},{1,2},{2,3},{3,4},{4,5},{5,6},{6,7},{7,0},{8,9},{9,10},{10,1... | collective-permute-start | bytes 442376 | tf_op jit(solution)/shard_map/ppermute | solution.py:41
  20.2 12.8 %collective-permute-start.1 = (bf16[64,1152]{1,0:T(8,128)(2,1)S(1)}, bf16[64,1152]{1,0:T(8,128)(2,1)S(1)}, u32[]{:S(2)}, u32[]{:S(2)}) collective-permute-start(bf16[64,1152]{1,0:T(8,128)(2,1)S(1)} %collective-permute-done.refs_1_), channel_id=1, source_target_pairs={{0,7},{1,0},{2,1},{3,2},{4,3},{5,4},{6,5},{7,6},{8,15},{9,8},{10,9... | collective-permute-start | bytes 442376 | tf_op jit(solution)/shard_map/ppermute | solution.py:41
  23.4 13.4 %collective-permute-start.3 = (bf16[64,1152]{1,0:T(8,128)(2,1)S(1)}, bf16[64,1152]{1,0:T(8,128)(2,1)S(1)}, u32[]{:S(2)}, u32[]{:S(2)}) collective-permute-start(bf16[64,1152]{1,0:T(8,128)(2,1)S(1)} %shard_map.60.refs_0_), channel_id=1, source_target_pairs={{0,4},{1,5},{2,6},{3,7},{4,0},{5,1},{6,2},{7,3},{8,12},{9,13},{10,... | collective-permute-start | bytes 442376 | tf_op jit(solution)/shard_map/ppermute | solution.py:41
  28.0 8.8 %collective-permute-start.6 = (bf16[64,1152]{1,0:T(8,128)(2,1)S(1)}, bf16[64,1152]{1,0:T(8,128)(2,1)S(1)}, u32[]{:S(2)}, u32[]{:S(2)}) collective-permute-start(bf16[64,1152]{1,0:T(8,128)(2,1)S(1)} %collective-permute-done.5.refs_6_), channel_id=1, source_target_pairs={{0,1},{1,2},{2,3},{3,4},{4,5},{5,6},{6,7},{7,0},{8,9},{9,10},{10,1... | collective-permute-start | bytes 442376 | tf_op jit(solution)/shard_map/ppermute | solution.py:41
  33.0 6.5 %collective-permute-start.2 = (bf16[64,1152]{1,0:T(8,128)(2,1)S(1)}, bf16[64,1152]{1,0:T(8,128)(2,1)S(1)}, u32[]{:S(2)}, u32[]{:S(2)}) collective-permute-start(bf16[64,1152]{1,0:T(8,128)(2,1)S(1)} %collective-permute-done.1.refs_2_), channel_id=1, source_target_pairs={{0,7},{1,0},{2,1},{3,2},{4,3},{5,4},{6,5},{7,6},{8,15},{9,8},{10,9... | collective-permute-start | bytes 442376 | tf_op jit(solution)/shard_map/ppermute | solution.py:41
  39.6 3.2 %collective-permute-start.7 = (bf16[512,1152]{1,0:T(8,128)(2,1)S(1)}, bf16[512,1152]{1,0:T(8,128)(2,1)}, u32[]{:S(2)}, u32[]{:S(2)}) collective-permute-start(bf16[512,1152]{1,0:T(8,128)(2,1)S(1)} %shard_map.61.xs), channel_id=1, source_target_pairs={{0,16},{16,0},{1,17},{17,1},{2,18},{18,2},{3,19},{19,3},{4,20},{20... | collective-permute-start | bytes 3538952 | tf_op jit(solution)/shard_map/ppermute | solution.py:41
  53.5 6.5 %collective-permute-start.8 = (bf16[512,1152]{1,0:T(8,128)(2,1)}, bf16[512,1152]{1,0:T(8,128)(2,1)S(1)}, u32[]{:S(2)}, u32[]{:S(2)}) collective-permute-start(bf16[512,1152]{1,0:T(8,128)(2,1)} %get-tuple-element.15), channel_id=1, source_target_pairs={{0,16},{16,0},{1,17},{17,1},{2,18},{18,2},{3,19},{19,3},{4,20},{20... | collective-permute-start | bytes 3538952 | tf_op jit(solution)/shard_map/ppermute | solution.py:41
  53.7 22.7 %all-to-all-start.1 = ((bf16[4,256,1152]{2,1,0:T(8,128)(2,1)}), bf16[4,256,1152]{2,1,0:T(8,128)(2,1)S(1)}, u32[]{:S(2)}, u32[]{:S(2)}) async-start(bf16[4,256,1152]{2,1,0:T(8,128)(2,1)} %bitcast.6), calls=%async_computation.1 | async-start | bytes 4718592 | tf_op jit(solution)/shard_map/all_to_all | solution.py:36
  61.8 13.0 %copy-start.5 = (f32[64,1152]{1,0:T(8,128)}, f32[64,1152]{1,0:T(8,128)S(1)}, u32[]{:S(2)}) copy-start(f32[64,1152]{1,0:T(8,128)S(1)} %get-tuple-element.16.refs_0_) | copy-start | bytes 884740
  62.6 8.5 %collective-permute-start.13 = (bf16[64,1152]{1,0:T(8,128)(2,1)S(1)}, bf16[64,1152]{1,0:T(8,128)(2,1)S(1)}, u32[]{:S(2)}, u32[]{:S(2)}) collective-permute-start(bf16[64,1152]{1,0:T(8,128)(2,1)S(1)} %get-tuple-element.24), channel_id=1, source_target_pairs={{0,7},{1,0},{2,1},{3,2},{4,3},{5,4},{6,5},{7,6},{8,15},{9,8},{10,9... | collective-permute-start | bytes 442376 | tf_op jit(solution)/shard_map/ppermute | solution.py:41
  68.4 43.4 %copy-start.2 = (f32[64,1152]{1,0:T(8,128)S(1)}, f32[64,1152]{1,0:T(8,128)}, u32[]{:S(2)}) copy-start(f32[64,1152]{1,0:T(8,128)} %raw.4) | copy-start | bytes 884740
  68.4 6.4 %collective-permute-start.12 = (bf16[64,1152]{1,0:T(8,128)(2,1)S(1)}, bf16[64,1152]{1,0:T(8,128)(2,1)S(1)}, u32[]{:S(2)}, u32[]{:S(2)}) collective-permute-start(bf16[64,1152]{1,0:T(8,128)(2,1)S(1)} %get-tuple-element.25), channel_id=1, source_target_pairs={{0,1},{1,2},{2,3},{3,4},{4,5},{5,6},{6,7},{7,0},{8,9},{9,10},{10,1... | collective-permute-start | bytes 442376 | tf_op jit(solution)/shard_map/ppermute | solution.py:41
  75.6 36.2 %copy-start.6 = (f32[64,1152]{1,0:T(8,128)S(1)}, f32[64,1152]{1,0:T(8,128)}, u32[]{:S(2)}) copy-start(f32[64,1152]{1,0:T(8,128)} %copy-done.5) | copy-start | bytes 884740
  76.4 37.0 %copy-start.4 = (f32[64,1152]{1,0:T(8,128)S(1)}, f32[64,1152]{1,0:T(8,128)}, u32[]{:S(2)}) copy-start(f32[64,1152]{1,0:T(8,128)} %raw.5) | copy-start | bytes 884740
  77.4 36.0 %all-to-all-start.2 = ((bf16[4,64,1152]{2,1,0:T(8,128)(2,1)}), bf16[4,64,1152]{2,1,0:T(8,128)(2,1)S(1)}, u32[]{:S(2)}, u32[]{:S(2)}) async-start(bf16[4,64,1152]{2,1,0:T(8,128)(2,1)} %shard_map.65), calls=%async_computation.2 | async-start | bytes 1179648 | tf_op jit(solution)/shard_map/all_to_all | solution.py:36
  80.9 24.0 %collective-permute-start.11 = (bf16[64,1152]{1,0:T(8,128)(2,1)}, bf16[64,1152]{1,0:T(8,128)(2,1)S(1)}, u32[]{:S(2)}, u32[]{:S(2)}) collective-permute-start(bf16[64,1152]{1,0:T(8,128)(2,1)} %get-tuple-element.26), channel_id=1, source_target_pairs={{0,5},{1,6},{2,7},{3,0},{4,1},{5,2},{6,3},{7,4},{8,13},{9,14},{10,... | collective-permute-start | bytes 442376 | tf_op jit(solution)/shard_map/ppermute | solution.py:41
  87.7 19.9 %collective-permute-start.10 = (bf16[64,1152]{1,0:T(8,128)(2,1)S(1)}, bf16[64,1152]{1,0:T(8,128)(2,1)S(1)}, u32[]{:S(2)}, u32[]{:S(2)}) collective-permute-start(bf16[64,1152]{1,0:T(8,128)(2,1)S(1)} %get-tuple-element.27), channel_id=1, source_target_pairs={{0,3},{1,4},{2,5},{3,6},{4,7},{5,0},{6,1},{7,2},{8,11},{9,12},{10,... | collective-permute-start | bytes 442376 | tf_op jit(solution)/shard_map/ppermute | solution.py:41
  87.7 19.9 %collective-permute-start.9 = (bf16[64,1152]{1,0:T(8,128)(2,1)S(1)}, bf16[64,1152]{1,0:T(8,128)(2,1)S(1)}, u32[]{:S(2)}, u32[]{:S(2)}) collective-permute-start(bf16[64,1152]{1,0:T(8,128)(2,1)S(1)} %get-tuple-element.28), channel_id=1, source_target_pairs={{0,4},{1,5},{2,6},{3,7},{4,0},{5,1},{6,2},{7,3},{8,12},{9,13},{10,... | collective-permute-start | bytes 442376 | tf_op jit(solution)/shard_map/ppermute | solution.py:41
  92.0 19.8 %collective-permute-start.14 = (bf16[64,1152]{1,0:T(8,128)(2,1)}, bf16[64,1152]{1,0:T(8,128)(2,1)S(1)}, u32[]{:S(2)}, u32[]{:S(2)}) collective-permute-start(bf16[64,1152]{1,0:T(8,128)(2,1)} %get-tuple-element.19), channel_id=1, source_target_pairs={{0,1},{1,2},{2,3},{3,4},{4,5},{5,6},{6,7},{7,0},{8,9},{9,10},{10,1... | collective-permute-start | bytes 442376 | tf_op jit(solution)/shard_map/ppermute | solution.py:41
  94.2 17.6 %collective-permute-start.15 = (bf16[64,1152]{1,0:T(8,128)(2,1)}, bf16[64,1152]{1,0:T(8,128)(2,1)S(1)}, u32[]{:S(2)}, u32[]{:S(2)}) collective-permute-start(bf16[64,1152]{1,0:T(8,128)(2,1)} %get-tuple-element.20), channel_id=1, source_target_pairs={{0,7},{1,0},{2,1},{3,2},{4,3},{5,4},{6,5},{7,6},{8,15},{9,8},{10,9... | collective-permute-start | bytes 442376 | tf_op jit(solution)/shard_map/ppermute | solution.py:41
  (2 other events, 2.6 us)

commit v14 on v9

--- a/solution.py
+++ b/solution.py
@@ -1,6 +1,5 @@
 import jax
 import jax.numpy as jnp
-import numpy as np
 from jax import lax
 from jax.experimental import pallas as pl
 from jax.experimental.pallas import tpu as pltpu
@@ -14,26 +13,6 @@
 ROWS = 64
 NT = (((1,), (1,)), ((), ()))
 TN = (((0,), (0,)), ((), ()))
-
-
-def plane_groups():
-    at = np.arange(256).reshape(2, 4, 2, 2, 8)
-    along_x, along_y = [], []
-    for core in range(2):
-        along_x.append(at[:, :, core].transpose(0, 2, 3, 1).reshape(-1, 4).tolist())
-        along_y.append(at[:, :, core].transpose(1, 3, 0, 2).reshape(-1, 4).tolist())
-    whole = at[:, :, 0].transpose(3, 0, 2, 1).reshape(-1, 16).tolist()
-    whole += at[:, :, 1].transpose(3, 1, 0, 2).reshape(-1, 16).tolist()
-    outer = along_y[0] + along_x[1]
-    inner = along_x[0] + along_y[1]
-    return whole, outer, inner
-
-
-WHOLE, OUTER, INNER = plane_groups()
-
-
-def swapped(blocks, groups):
-    return lax.all_to_all(blocks, AXES, 0, 0, axis_index_groups=groups, tiled=True)
 
 
 def shifted(block, axis, distance):
@@ -193,12 +172,11 @@
         scratch=[pltpu.VMEM((rows, width), BF), pltpu.SemaphoreType.DMA((n_plane,))],
     )
     spread, images = lax.optimization_barrier((spread, images))
-    ts = swapped(spread, WHOLE).reshape(pooled, width)
+    ts = lax.all_to_all(spread, PLANE, 0, 0, tiled=True).reshape(pooled, width)
     (x,) = local(unit_kernel, [((rows, width), BF, VMEM)], [images])
     (xs,) = local(pack_kernel, [((half, width), BF, VMEM)], ring_gather(x))
     xo = shifted(xs, "core", 1)
-    at_x, at_y = lax.axis_index("x"), lax.axis_index(("yh", "yl"))
-    place = jnp.where(lax.axis_index("core") == 0, 4 * at_y + at_x, 4 * at_x + at_y).astype(jnp.int32).reshape(1)
+    place = lax.axis_index(PLANE).astype(jnp.int32).reshape(1)
     scal = jnp.stack([temp, bias[0]])
     unit_flops = 2 * half * pooled * width
     dxs, dxo, dy = local(
@@ -215,9 +193,7 @@
         ],
         flops=6 * unit_flops, nbytes=9 * 2**20, trans=4 * half * pooled, vmem=24,
     )
-    half_way = swapped(dy.reshape(4, 4 * rows, width), OUTER)
-    half_way = jnp.sum(half_way.astype(F32), axis=0).astype(BF)
-    dyr = swapped(half_way.reshape(4, rows, width), INNER)
+    dyr = lax.all_to_all(dy.reshape(n_plane, rows, width), PLANE, 0, 0, tiled=True)
     other = shifted(dxo, "core", 1)
     own, rest = local(
         join_kernel, [((rows, width), F32, VMEM), ((half - rows, width), BF, VMEM)], [dxs, other],

time: 103 us -> 98.3 us (0.954)
  starting transfers between devices: 55.4 us -> 46.1 us
  waiting for transfers between devices: 23.1 us -> 30.7 us
  other arithmetic: 4.12 us -> 0.15 us
  local copies, waits for them, and re-layouts: 1.05 us -> 2.69 us
    ppermute x16, waiting for transfers between devices: 20 us -> 29.7 us  [shifted(): lax.ppermute(block, axis, [(i, (i + distance) % n) for i in range(n)])]
    ppermute x16, starting transfers between devices: 37.1 us -> 32.2 us  [shifted(): lax.ppermute(block, axis, [(i, (i + distance) % n) for i in range(n)])]
    all_to_all x3 -> x2, starting transfers between devices: 18.4 us -> 13.9 us  [the longest x1 7.54 us: on_device(): ts = lax.all_to_all(spread, PLANE, 0, 0, tiled=True).reshape(pooled, width)]
    reduce_sum x1 -> x0, other arithmetic: 2.99 us -> none  [on_device(): half_way = jnp.sum(half_way.astype(F32), axis=0).astype(BF)]
    all_to_all x3 -> x2, waiting for transfers between devices: 3.15 us -> 1.03 us  [the longest x1 1.03 us: on_device(): ts = lax.all_to_all(spread, PLANE, 0, 0, tiled=True).reshape(pooled, width)]
    unnamed x16 -> x10, local copies, waits for them, and re-layouts: 0.99 us -> 2.63 us
  transfers between devices with their start and end apart: 19 -> 18, of which waited for: 8 -> 10; matrix products, arithmetic and copies ran while one was open for 4% -> 0% of each run, Pallas kernels for 2% -> 2%
where the time goes in v14:
time: 98.3 us; the launch traced here: 97.9 us
  starting transfers between devices  46.1 us (47%)
  waiting for transfers between devices  30.7 us (31%)
  Pallas kernels  16.2 us (16%)
  local copies, waits for them, and re-layouts  2.69 us (3%)
  between operations  2.09 us (2%)
    ppermute x16, starting transfers between devices, shifted(): lax.ppermute(block, axis, [(i, (i + distance) % n) for i in range(n)])  32.2 us
    ppermute x16, waiting for transfers between devices, shifted(): lax.ppermute(block, axis, [(i, (i + distance) % n) for i in range(n)])  29.7 us
    pallas_call x7, Pallas kernels, local(): pl.pallas_call(kernel, out_shape=tuple(((pltpu.HBM if spec is HBM else ja...  16.2 us
    all_to_all x1, starting transfers between devices, on_device(): ts = lax.all_to_all(spread, PLANE, 0, 0, tiled=True).reshape(pooled, width)  7.54 us
    all_to_all x1, starting transfers between devices, on_device(): lax.all_to_all(dy.reshape(n_plane, rows, width), PLANE, 0, 0, tiled=True)  6.39 us
    unnamed x10, local copies, waits for them, and re-layouts  2.63 us
  transfers between devices with their start and end apart: 18, of which 10 were waited for; matrix products, arithmetic and copies ran while one was open for 0% of the time, Pallas kernels for 2%

profile of v14, /device:TPU:8, one launch (start us, length us, event | category | flops | bytes accessed | tf_op | source)
XLA Modules:
  0.0 97.9 jit_solution(11227512109837528338)
XLA Ops:
  1.6 1.7 %shard_map.59 = bf16[16,64,1152]{2,1,0:T(8,128)(2,1)} custom-call(f32[64,1152]{1,0:T(8,128)S(1)} %copy-done.1), custom_call_target="tpu_custom_call" | custom-call | bytes 1048576 | tf_op jit(solution)/shard_map/pallas_call | solution.py:132
  3.3 7.5 %all-to-all-start = ((bf16[16,64,1152]{2,1,0:T(8,128)(2,1)}), bf16[16,64,1152]{2,1,0:T(8,128)(2,1)S(1)}, u32[]{:S(2)}, u32[]{:S(2)}) async-start(bf16[16,64,1152]{2,1,0:T(8,128)(2,1)} %shard_map.59), calls=%async_computation | async-start | bytes 4718592 | tf_op jit(solution)/shard_map/all_to_all | solution.py:175
  11.0 2.0 %collective-permute-start.4 = (bf16[64,1152]{1,0:T(8,128)(2,1)S(1)}, bf16[64,1152]{1,0:T(8,128)(2,1)S(1)}, u32[]{:S(2)}, u32[]{:S(2)}) collective-permute-start(bf16[64,1152]{1,0:T(8,128)(2,1)S(1)} %shard_map.60.refs_0_), channel_id=1, source_target_pairs={{0,1},{1,2},{2,3},{3,4},{4,5},{5,6},{6,7},{7,0},{8,9},{9,10},{10,1... | collective-permute-start | bytes 442376 | tf_op jit(solution)/shard_map/ppermute | solution.py:20
  13.0 4.0 %collective-permute-start = (bf16[64,1152]{1,0:T(8,128)(2,1)S(1)}, bf16[64,1152]{1,0:T(8,128)(2,1)S(1)}, u32[]{:S(2)}, u32[]{:S(2)}) collective-permute-start(bf16[64,1152]{1,0:T(8,128)(2,1)S(1)} %shard_map.60.refs_0_), channel_id=1, source_target_pairs={{0,7},{1,0},{2,1},{3,2},{4,3},{5,4},{6,5},{7,6},{8,15},{9,8},{10,9... | collective-permute-start | bytes 442376 | tf_op jit(solution)/shard_map/ppermute | solution.py:20
  17.0 3.2 %collective-permute-done.4.refs_7_ = bf16[64,1152]{1,0:T(8,128)(2,1)S(1)} collective-permute-done((bf16[64,1152]{1,0:T(8,128)(2,1)S(1)}, bf16[64,1152]{1,0:T(8,128)(2,1)S(1)}, u32[]{:S(2)}, u32[]{:S(2)}) %collective-permute-start.4) | collective-permute-done | bytes 147488 | tf_op jit(solution)/shard_map/ppermute | solution.py:20
  20.2 3.2 %collective-permute-start.1 = (bf16[64,1152]{1,0:T(8,128)(2,1)S(1)}, bf16[64,1152]{1,0:T(8,128)(2,1)S(1)}, u32[]{:S(2)}, u32[]{:S(2)}) collective-permute-start(bf16[64,1152]{1,0:T(8,128)(2,1)S(1)} %collective-permute-done.refs_1_), channel_id=1, source_target_pairs={{0,7},{1,0},{2,1},{3,2},{4,3},{5,4},{6,5},{7,6},{8,15},{9,8},{10,9... | collective-permute-start | bytes 442376 | tf_op jit(solution)/shard_map/ppermute | solution.py:20
  23.5 4.4 %collective-permute-start.3 = (bf16[64,1152]{1,0:T(8,128)(2,1)S(1)}, bf16[64,1152]{1,0:T(8,128)(2,1)S(1)}, u32[]{:S(2)}, u32[]{:S(2)}) collective-permute-start(bf16[64,1152]{1,0:T(8,128)(2,1)S(1)} %shard_map.60.refs_0_), channel_id=1, source_target_pairs={{0,4},{1,5},{2,6},{3,7},{4,0},{5,1},{6,2},{7,3},{8,12},{9,13},{10,... | collective-permute-start | bytes 442376 | tf_op jit(solution)/shard_map/ppermute | solution.py:20
  28.1 4.9 %collective-permute-done.1.refs_2_ = bf16[64,1152]{1,0:T(8,128)(2,1)S(1)} collective-permute-done((bf16[64,1152]{1,0:T(8,128)(2,1)S(1)}, bf16[64,1152]{1,0:T(8,128)(2,1)S(1)}, u32[]{:S(2)}, u32[]{:S(2)}) %collective-permute-start.1) | collective-permute-done | bytes 147488 | tf_op jit(solution)/shard_map/ppermute | solution.py:20
  32.9 3.8 %collective-permute-start.2 = (bf16[64,1152]{1,0:T(8,128)(2,1)S(1)}, bf16[64,1152]{1,0:T(8,128)(2,1)S(1)}, u32[]{:S(2)}, u32[]{:S(2)}) collective-permute-start(bf16[64,1152]{1,0:T(8,128)(2,1)S(1)} %collective-permute-done.1.refs_2_), channel_id=1, source_target_pairs={{0,7},{1,0},{2,1},{3,2},{4,3},{5,4},{6,5},{7,6},{8,15},{9,8},{10,9... | collective-permute-start | bytes 442376 | tf_op jit(solution)/shard_map/ppermute | solution.py:20
  36.8 2.7 %collective-permute-done.2.refs_3_ = bf16[64,1152]{1,0:T(8,128)(2,1)S(1)} collective-permute-done((bf16[64,1152]{1,0:T(8,128)(2,1)S(1)}, bf16[64,1152]{1,0:T(8,128)(2,1)S(1)}, u32[]{:S(2)}, u32[]{:S(2)}) %collective-permute-start.2) | collective-permute-done | bytes 147488 | tf_op jit(solution)/shard_map/ppermute | solution.py:20
  41.2 1.5 %collective-permute-done.7.xo = bf16[512,1152]{1,0:T(8,128)(2,1)} collective-permute-done((bf16[512,1152]{1,0:T(8,128)(2,1)S(1)}, bf16[512,1152]{1,0:T(8,128)(2,1)}, u32[]{:S(2)}, u32[]{:S(2)}) %collective-permute-start.7) | collective-permute-done | bytes 1179680 | tf_op jit(solution)/shard_map/ppermute | solution.py:20
  42.8 1.0 %all-to-all-done = bf16[16,64,1152]{2,1,0:T(8,128)(2,1)S(1)} async-done(((bf16[16,64,1152]{2,1,0:T(8,128)(2,1)}), bf16[16,64,1152]{2,1,0:T(8,128)(2,1)S(1)}, u32[]{:S(2)}, u32[]{:S(2)}) %all-to-all-start) | async-done | bytes 2359328 | tf_op jit(solution)/shard_map/all_to_all | solution.py:175
  43.8 10.8 %shard_map.62 = (f32[512,1152]{1,0:T(8,128)}, bf16[512,1152]{1,0:T(8,128)(2,1)}, bf16[1024,1152]{1,0:T(8,128)(2,1)}) custom-call(s32[1]{0:T(128)} %bitcast.place, f32[2]{0:T(128)S(1)} %pad_maximum_fusion.scal, bf16[512,1152]{1,0:T(8,128)(2,1)S(1)} %shard_map.61.xs, bf16[512,1152]{1,0:T(8,128)(2,1)} %collective-permute-done.7.xo, bf16[1024,1152]{1,0:T(8,128)(2,1)S(1)} %bitcast.3), custom_call_target="tpu_custom_call" | custom-call | flops 7247757312 | bytes 9437184 | tf_op jit(solution)/shard_map/pallas_call | solution.py:132
  54.7 6.4 %all-to-all-start.1 = ((bf16[16,64,1152]{2,1,0:T(8,128)(2,1)}), bf16[16,64,1152]{2,1,0:T(8,128)(2,1)S(1)}, u32[]{:S(2)}, u32[]{:S(2)}) async-start(bf16[16,64,1152]{2,1,0:T(8,128)(2,1)} %bitcast.4), calls=%async_computation.1 | async-start | bytes 4718592 | tf_op jit(solution)/shard_map/all_to_all | solution.py:196
  61.1 1.7 %copy-done = f32[512,1152]{1,0:T(8,128)S(1)} copy-done((f32[512,1152]{1,0:T(8,128)S(1)}, f32[512,1152]{1,0:T(8,128)}, u32[]{:S(2)}) %copy-start) | copy-done | bytes 2359320
  63.1 4.5 %collective-permute-start.14 = (bf16[64,1152]{1,0:T(8,128)(2,1)S(1)}, bf16[64,1152]{1,0:T(8,128)(2,1)S(1)}, u32[]{:S(2)}, u32[]{:S(2)}) collective-permute-start(bf16[64,1152]{1,0:T(8,128)(2,1)S(1)} %get-tuple-element.18), channel_id=1, source_target_pairs={{0,7},{1,0},{2,1},{3,2},{4,3},{5,4},{6,5},{7,6},{8,15},{9,8},{10,9... | collective-permute-start | bytes 442376 | tf_op jit(solution)/shard_map/ppermute | solution.py:20
  67.6 2.9 %collective-permute-start.11 = (bf16[64,1152]{1,0:T(8,128)(2,1)S(1)}, bf16[64,1152]{1,0:T(8,128)(2,1)S(1)}, u32[]{:S(2)}, u32[]{:S(2)}) collective-permute-start(bf16[64,1152]{1,0:T(8,128)(2,1)S(1)} %get-tuple-element.20), channel_id=1, source_target_pairs={{0,5},{1,6},{2,7},{3,0},{4,1},{5,2},{6,3},{7,4},{8,13},{9,14},{10,... | collective-permute-start | bytes 442376 | tf_op jit(solution)/shard_map/ppermute | solution.py:20
  71.5 3.4 %collective-permute-start.9 = (bf16[64,1152]{1,0:T(8,128)(2,1)S(1)}, bf16[64,1152]{1,0:T(8,128)(2,1)S(1)}, u32[]{:S(2)}, u32[]{:S(2)}) collective-permute-start(bf16[64,1152]{1,0:T(8,128)(2,1)S(1)} %get-tuple-element.22), channel_id=1, source_target_pairs={{0,4},{1,5},{2,6},{3,7},{4,0},{5,1},{6,2},{7,3},{8,12},{9,13},{10,... | collective-permute-start | bytes 442376 | tf_op jit(solution)/shard_map/ppermute | solution.py:20
  74.9 2.6 %collective-permute-start.15 = (bf16[64,1152]{1,0:T(8,128)(2,1)S(1)}, bf16[64,1152]{1,0:T(8,128)(2,1)S(1)}, u32[]{:S(2)}, u32[]{:S(2)}) collective-permute-start(bf16[64,1152]{1,0:T(8,128)(2,1)S(1)} %get-tuple-element.16), channel_id=1, source_target_pairs={{0,7},{1,0},{2,1},{3,2},{4,3},{5,4},{6,5},{7,6},{8,15},{9,8},{10,9... | collective-permute-start | bytes 442376 | tf_op jit(solution)/shard_map/ppermute | solution.py:20
  77.5 10.0 %collective-permute-done.11.refs_3_ = bf16[64,1152]{1,0:T(8,128)(2,1)S(1)} collective-permute-done((bf16[64,1152]{1,0:T(8,128)(2,1)S(1)}, bf16[64,1152]{1,0:T(8,128)(2,1)S(1)}, u32[]{:S(2)}, u32[]{:S(2)}) %collective-permute-start.11) | collective-permute-done | bytes 147488 | tf_op jit(solution)/shard_map/ppermute | solution.py:20
  88.4 2.4 %collective-permute-done.15.refs_5_ = bf16[64,1152]{1,0:T(8,128)(2,1)S(1)} collective-permute-done((bf16[64,1152]{1,0:T(8,128)(2,1)S(1)}, bf16[64,1152]{1,0:T(8,128)(2,1)S(1)}, u32[]{:S(2)}, u32[]{:S(2)}) %collective-permute-start.15) | collective-permute-done | bytes 147488 | tf_op jit(solution)/shard_map/ppermute | solution.py:20
  90.7 4.0 %collective-permute-done.13.refs_4_ = bf16[64,1152]{1,0:T(8,128)(2,1)S(1)} collective-permute-done((bf16[64,1152]{1,0:T(8,128)(2,1)S(1)}, bf16[64,1152]{1,0:T(8,128)(2,1)S(1)}, u32[]{:S(2)}, u32[]{:S(2)}) %collective-permute-start.13) | collective-permute-done | bytes 147488 | tf_op jit(solution)/shard_map/ppermute | solution.py:20
  94.7 1.5 %shard_map.64 = f32[64,1152]{1,0:T(8,128)} custom-call(f32[2]{0:T(128)S(1)} %pad_maximum_fusion.scal, f32[64,1152]{1,0:T(8,128)S(1)} %copy-done.4, f32[64,1152]{1,0:T(8,128)S(1)} %get-tuple-element.13.refs_0_, bf16[64,1152]{1,0:T(8,128)(2,1)S(1)} %collective-permute-done.9.refs_1_, bf16[64,1152]{1,0:T(8,128)(2,1)S(1)} %collective-permute-done.10.refs_2_, ...), custom_call_target="tpu_custom_call" | custom-call | bytes 1048576 | tf_op jit(solution)/shard_map/pallas_call | solution.py:132
  96.2 1.7 %shard_map.65 = f32[64,1152]{1,0:T(8,128)} custom-call(f32[2]{0:T(128)S(1)} %pad_maximum_fusion.scal, f32[64,1152]{1,0:T(8,128)S(1)} %copy-done.2, bf16[16,64,1152]{2,1,0:T(8,128)(2,1)S(1)} %all-to-all-done.1.got), custom_call_target="tpu_custom_call" | custom-call | bytes 1048576 | tf_op jit(solution)/shard_map/pallas_call | solution.py:132
  (32 shorter events, 4.1 us)
Async XLA Ops:
  0.6 1.0 copy-start.1
  3.3 7.5 %copy-start.3 = (f32[64,1152]{1,0:T(8,128)S(1)}, f32[64,1152]{1,0:T(8,128)}, u32[]{:S(2)}) copy-start(f32[64,1152]{1,0:T(8,128)} %raw.4) | copy-start | bytes 884740
  3.3 40.5 %all-to-all-start = ((bf16[16,64,1152]{2,1,0:T(8,128)(2,1)}), bf16[16,64,1152]{2,1,0:T(8,128)(2,1)S(1)}, u32[]{:S(2)}, u32[]{:S(2)}) async-start(bf16[16,64,1152]{2,1,0:T(8,128)(2,1)} %shard_map.59), calls=%async_computation | async-start | bytes 4718592 | tf_op jit(solution)/shard_map/all_to_all | solution.py:175
  11.0 9.2 %collective-permute-start.4 = (bf16[64,1152]{1,0:T(8,128)(2,1)S(1)}, bf16[64,1152]{1,0:T(8,128)(2,1)S(1)}, u32[]{:S(2)}, u32[]{:S(2)}) collective-permute-start(bf16[64,1152]{1,0:T(8,128)(2,1)S(1)} %shard_map.60.refs_0_), channel_id=1, source_target_pairs={{0,1},{1,2},{2,3},{3,4},{4,5},{5,6},{6,7},{7,0},{8,9},{9,10},{10,1... | collective-permute-start | bytes 442376 | tf_op jit(solution)/shard_map/ppermute | solution.py:20
  13.0 7.2 %collective-permute-start = (bf16[64,1152]{1,0:T(8,128)(2,1)S(1)}, bf16[64,1152]{1,0:T(8,128)(2,1)S(1)}, u32[]{:S(2)}, u32[]{:S(2)}) collective-permute-start(bf16[64,1152]{1,0:T(8,128)(2,1)S(1)} %shard_map.60.refs_0_), channel_id=1, source_target_pairs={{0,7},{1,0},{2,1},{3,2},{4,3},{5,4},{6,5},{7,6},{8,15},{9,8},{10,9... | collective-permute-start | bytes 442376 | tf_op jit(solution)/shard_map/ppermute | solution.py:20
  20.2 7.9 %collective-permute-start.5 = (bf16[64,1152]{1,0:T(8,128)(2,1)S(1)}, bf16[64,1152]{1,0:T(8,128)(2,1)S(1)}, u32[]{:S(2)}, u32[]{:S(2)}) collective-permute-start(bf16[64,1152]{1,0:T(8,128)(2,1)S(1)} %collective-permute-done.4.refs_7_), channel_id=1, source_target_pairs={{0,1},{1,2},{2,3},{3,4},{4,5},{5,6},{6,7},{7,0},{8,9},{9,10},{10,1... | collective-permute-start | bytes 442376 | tf_op jit(solution)/shard_map/ppermute | solution.py:20
  20.2 12.7 %collective-permute-start.1 = (bf16[64,1152]{1,0:T(8,128)(2,1)S(1)}, bf16[64,1152]{1,0:T(8,128)(2,1)S(1)}, u32[]{:S(2)}, u32[]{:S(2)}) collective-permute-start(bf16[64,1152]{1,0:T(8,128)(2,1)S(1)} %collective-permute-done.refs_1_), channel_id=1, source_target_pairs={{0,7},{1,0},{2,1},{3,2},{4,3},{5,4},{6,5},{7,6},{8,15},{9,8},{10,9... | collective-permute-start | bytes 442376 | tf_op jit(solution)/shard_map/ppermute | solution.py:20
  23.5 13.3 %collective-permute-start.3 = (bf16[64,1152]{1,0:T(8,128)(2,1)S(1)}, bf16[64,1152]{1,0:T(8,128)(2,1)S(1)}, u32[]{:S(2)}, u32[]{:S(2)}) collective-permute-start(bf16[64,1152]{1,0:T(8,128)(2,1)S(1)} %shard_map.60.refs_0_), channel_id=1, source_target_pairs={{0,4},{1,5},{2,6},{3,7},{4,0},{5,1},{6,2},{7,3},{8,12},{9,13},{10,... | collective-permute-start | bytes 442376 | tf_op jit(solution)/shard_map/ppermute | solution.py:20
  28.1 8.7 %collective-permute-start.6 = (bf16[64,1152]{1,0:T(8,128)(2,1)S(1)}, bf16[64,1152]{1,0:T(8,128)(2,1)S(1)}, u32[]{:S(2)}, u32[]{:S(2)}) collective-permute-start(bf16[64,1152]{1,0:T(8,128)(2,1)S(1)} %collective-permute-done.5.refs_6_), channel_id=1, source_target_pairs={{0,1},{1,2},{2,3},{3,4},{4,5},{5,6},{6,7},{7,0},{8,9},{9,10},{10,1... | collective-permute-start | bytes 442376 | tf_op jit(solution)/shard_map/ppermute | solution.py:20
  32.9 6.5 %collective-permute-start.2 = (bf16[64,1152]{1,0:T(8,128)(2,1)S(1)}, bf16[64,1152]{1,0:T(8,128)(2,1)S(1)}, u32[]{:S(2)}, u32[]{:S(2)}) collective-permute-start(bf16[64,1152]{1,0:T(8,128)(2,1)S(1)} %collective-permute-done.1.refs_2_), channel_id=1, source_target_pairs={{0,7},{1,0},{2,1},{3,2},{4,3},{5,4},{6,5},{7,6},{8,15},{9,8},{10,9... | collective-permute-start | bytes 442376 | tf_op jit(solution)/shard_map/ppermute | solution.py:20
  39.5 3.2 %collective-permute-start.7 = (bf16[512,1152]{1,0:T(8,128)(2,1)S(1)}, bf16[512,1152]{1,0:T(8,128)(2,1)}, u32[]{:S(2)}, u32[]{:S(2)}) collective-permute-start(bf16[512,1152]{1,0:T(8,128)(2,1)S(1)} %shard_map.61.xs), channel_id=1, source_target_pairs={{0,16},{16,0},{1,17},{17,1},{2,18},{18,2},{3,19},{19,3},{4,20},{20... | collective-permute-start | bytes 3538952 | tf_op jit(solution)/shard_map/ppermute | solution.py:20
  54.6 6.5 %collective-permute-start.8 = (bf16[512,1152]{1,0:T(8,128)(2,1)}, bf16[512,1152]{1,0:T(8,128)(2,1)S(1)}, u32[]{:S(2)}, u32[]{:S(2)}) collective-permute-start(bf16[512,1152]{1,0:T(8,128)(2,1)} %get-tuple-element.12), channel_id=1, source_target_pairs={{0,16},{16,0},{1,17},{17,1},{2,18},{18,2},{3,19},{19,3},{4,20},{20... | collective-permute-start | bytes 3538952 | tf_op jit(solution)/shard_map/ppermute | solution.py:20
  54.7 41.5 %all-to-all-start.1 = ((bf16[16,64,1152]{2,1,0:T(8,128)(2,1)}), bf16[16,64,1152]{2,1,0:T(8,128)(2,1)S(1)}, u32[]{:S(2)}, u32[]{:S(2)}) async-start(bf16[16,64,1152]{2,1,0:T(8,128)(2,1)} %bitcast.4), calls=%async_computation.1 | async-start | bytes 4718592 | tf_op jit(solution)/shard_map/all_to_all | solution.py:196
  61.1 1.7 %copy-start = (f32[512,1152]{1,0:T(8,128)S(1)}, f32[512,1152]{1,0:T(8,128)}, u32[]{:S(2)}) copy-start(f32[512,1152]{1,0:T(8,128)} %get-tuple-element.11.dxs) | copy-start | bytes 7077892
  62.8 31.9 %copy-start.4 = (f32[64,1152]{1,0:T(8,128)S(1)}, f32[64,1152]{1,0:T(8,128)}, u32[]{:S(2)}) copy-start(f32[64,1152]{1,0:T(8,128)} %raw.4) | copy-start | bytes 884740
  63.0 33.2 %copy-start.2 = (f32[64,1152]{1,0:T(8,128)S(1)}, f32[64,1152]{1,0:T(8,128)}, u32[]{:S(2)}) copy-start(f32[64,1152]{1,0:T(8,128)} %raw.5) | copy-start | bytes 884740
  63.1 11.7 %collective-permute-start.14 = (bf16[64,1152]{1,0:T(8,128)(2,1)S(1)}, bf16[64,1152]{1,0:T(8,128)(2,1)S(1)}, u32[]{:S(2)}, u32[]{:S(2)}) collective-permute-start(bf16[64,1152]{1,0:T(8,128)(2,1)S(1)} %get-tuple-element.18), channel_id=1, source_target_pairs={{0,7},{1,0},{2,1},{3,2},{4,3},{5,4},{6,5},{7,6},{8,15},{9,8},{10,9... | collective-permute-start | bytes 442376 | tf_op jit(solution)/shard_map/ppermute | solution.py:20
  67.6 7.2 %collective-permute-start.12 = (bf16[64,1152]{1,0:T(8,128)(2,1)S(1)}, bf16[64,1152]{1,0:T(8,128)(2,1)S(1)}, u32[]{:S(2)}, u32[]{:S(2)}) collective-permute-start(bf16[64,1152]{1,0:T(8,128)(2,1)S(1)} %get-tuple-element.19), channel_id=1, source_target_pairs={{0,1},{1,2},{2,3},{3,4},{4,5},{5,6},{6,7},{7,0},{8,9},{9,10},{10,1... | collective-permute-start | bytes 442376 | tf_op jit(solution)/shard_map/ppermute | solution.py:20
  67.6 19.9 %collective-permute-start.11 = (bf16[64,1152]{1,0:T(8,128)(2,1)S(1)}, bf16[64,1152]{1,0:T(8,128)(2,1)S(1)}, u32[]{:S(2)}, u32[]{:S(2)}) collective-permute-start(bf16[64,1152]{1,0:T(8,128)(2,1)S(1)} %get-tuple-element.20), channel_id=1, source_target_pairs={{0,5},{1,6},{2,7},{3,0},{4,1},{5,2},{6,3},{7,4},{8,13},{9,14},{10,... | collective-permute-start | bytes 442376 | tf_op jit(solution)/shard_map/ppermute | solution.py:20
  70.5 16.9 %collective-permute-start.10 = (bf16[64,1152]{1,0:T(8,128)(2,1)S(1)}, bf16[64,1152]{1,0:T(8,128)(2,1)S(1)}, u32[]{:S(2)}, u32[]{:S(2)}) collective-permute-start(bf16[64,1152]{1,0:T(8,128)(2,1)S(1)} %get-tuple-element.21), channel_id=1, source_target_pairs={{0,3},{1,4},{2,5},{3,6},{4,7},{5,0},{6,1},{7,2},{8,11},{9,12},{10,... | collective-permute-start | bytes 442376 | tf_op jit(solution)/shard_map/ppermute | solution.py:20
  71.5 16.9 %collective-permute-start.9 = (bf16[64,1152]{1,0:T(8,128)(2,1)S(1)}, bf16[64,1152]{1,0:T(8,128)(2,1)S(1)}, u32[]{:S(2)}, u32[]{:S(2)}) collective-permute-start(bf16[64,1152]{1,0:T(8,128)(2,1)S(1)} %get-tuple-element.22), channel_id=1, source_target_pairs={{0,4},{1,5},{2,6},{3,7},{4,0},{5,1},{6,2},{7,3},{8,12},{9,13},{10,... | collective-permute-start | bytes 442376 | tf_op jit(solution)/shard_map/ppermute | solution.py:20
  74.9 15.8 %collective-permute-start.15 = (bf16[64,1152]{1,0:T(8,128)(2,1)S(1)}, bf16[64,1152]{1,0:T(8,128)(2,1)S(1)}, u32[]{:S(2)}, u32[]{:S(2)}) collective-permute-start(bf16[64,1152]{1,0:T(8,128)(2,1)S(1)} %get-tuple-element.16), channel_id=1, source_target_pairs={{0,7},{1,0},{2,1},{3,2},{4,3},{5,4},{6,5},{7,6},{8,15},{9,8},{10,9... | collective-permute-start | bytes 442376 | tf_op jit(solution)/shard_map/ppermute | solution.py:20
  77.5 17.2 %collective-permute-start.13 = (bf16[64,1152]{1,0:T(8,128)(2,1)S(1)}, bf16[64,1152]{1,0:T(8,128)(2,1)S(1)}, u32[]{:S(2)}, u32[]{:S(2)}) collective-permute-start(bf16[64,1152]{1,0:T(8,128)(2,1)S(1)} %get-tuple-element.17), channel_id=1, source_target_pairs={{0,1},{1,2},{2,3},{3,4},{4,5},{5,6},{6,7},{7,0},{8,9},{9,10},{10,1... | collective-permute-start | bytes 442376 | tf_op jit(solution)/shard_map/ppermute | solution.py:20

commit v15 on v14

--- a/solution.py
+++ b/solution.py
@@ -34,9 +34,13 @@
     return (raw / norm).astype(BF)
 
 
-def spread_kernel(raw, out, unit, sems):
+def spread_kernel(texts, out, raw, unit, sems):
+    n = out.shape[0]
+    load = pltpu.make_async_copy(texts, raw, sems.at[n])
+    load.start()
+    load.wait()
     unit[...] = unit_rows(raw[...])
-    copies = [pltpu.make_async_copy(unit, out.at[k], sems.at[k]) for k in range(out.shape[0])]
+    copies = [pltpu.make_async_copy(unit, out.at[k], sems.at[k]) for k in range(n)]
     for copy in copies:
         copy.start()
     for copy in copies:
@@ -63,15 +67,14 @@
     pooled = ts.shape[0]
     wide = 512
     step = 256
-    loads = [
-        pltpu.make_async_copy(xs, x.at[0:half], sems.at[0]),
-        pltpu.make_async_copy(xo, x.at[half : 2 * half], sems.at[1]),
-    ]
-    for copy in loads:
-        copy.start()
-    for h, copy in enumerate(loads):
-        copy.wait()
-        cols = slice(h * half, (h + 1) * half)
+    loads = []
+    for c in range(0, 2 * half, step):
+        src = (xs if c < half else xo).at[c % half : c % half + step]
+        loads.append(pltpu.make_async_copy(src, x.at[c : c + step], sems.at[len(loads)]))
+        loads[-1].start()
+    for c, load in enumerate(loads):
+        load.wait()
+        cols = slice(c * step, (c + 1) * step)
         for j in range(pooled // step):
             sl = pl.ds(j * step, step)
             dots = lax.dot_general(ts[sl], x[cols], NT, preferred_element_type=F32)
@@ -85,7 +88,7 @@
     copies = []
 
     def send(src, dst):
-        copies.append(pltpu.make_async_copy(src, dst, sems.at[2 + len(copies)]))
+        copies.append(pltpu.make_async_copy(src, dst, sems.at[len(loads) + len(copies)]))
         copies[-1].start()
 
     for h, (buf, out) in enumerate(((mine, dxs), (theirs, dxo))):
@@ -94,9 +97,9 @@
             dots = lax.dot_general(held[:, cols], ts[...], TN, preferred_element_type=F32)
             buf[i : i + wide] = dots.astype(buf.dtype)
             send(buf.at[i : i + wide], out.at[i : i + wide])
-    for j in range(0, pooled, step):
-        part[j : j + step] = jnp.dot(held[j : j + step], x[...], preferred_element_type=F32).astype(BF)
-        send(part.at[j : j + step], dy.at[j : j + step])
+    for j, n in ((0, 256), (256, 256), (512, 256), (768, 128), (896, 128)):
+        part[j : j + n] = jnp.dot(held[j : j + n], x[...], preferred_element_type=F32).astype(BF)
+        send(part.at[j : j + n], dy.at[j : j + n])
     for copy in copies:
         copy.wait()
 
@@ -168,8 +171,12 @@
     half = ROWS * lax.axis_size("z")
     pooled = ROWS * n_plane
     (spread,) = local(
-        spread_kernel, [((n_plane, rows, width), BF, HBM)], [texts],
-        scratch=[pltpu.VMEM((rows, width), BF), pltpu.SemaphoreType.DMA((n_plane,))],
+        spread_kernel, [((n_plane, rows, width), BF, HBM)], [texts], hbm=1,
+        scratch=[
+            pltpu.VMEM((rows, width), F32),
+            pltpu.VMEM((rows, width), BF),
+            pltpu.SemaphoreType.DMA((n_plane + 1,)),
+        ],
     )
     spread, images = lax.optimization_barrier((spread, images))
     ts = lax.all_to_all(spread, PLANE, 0, 0, tiled=True).reshape(pooled, width)
@@ -189,7 +196,7 @@
             pltpu.VMEM((half, width), F32),
             pltpu.VMEM((half, width), BF),
             pltpu.VMEM((pooled, width), BF),
-            pltpu.SemaphoreType.DMA((8,)),
+            pltpu.SemaphoreType.DMA((11,)),
         ],
         flops=6 * unit_flops, nbytes=9 * 2**20, trans=4 * half * pooled, vmem=24,
     )

time: 98.3 us -> 98.9 us (level)
  no operation moved by 1% of the time
where the time goes in v15:
time: 98.9 us; the launch traced here: 98.5 us
  starting transfers between devices  46.1 us (47%)
  waiting for transfers between devices  30.7 us (31%)
  Pallas kernels  16.7 us (17%)
  local copies, waits for them, and re-layouts  2.69 us (3%)
  between operations  2.09 us (2%)
    ppermute x16, starting transfers between devices, shifted(): lax.ppermute(block, axis, [(i, (i + distance) % n) for i in range(n)])  32.2 us
    ppermute x16, waiting for transfers between devices, shifted(): lax.ppermute(block, axis, [(i, (i + distance) % n) for i in range(n)])  29.7 us
    pallas_call x7, Pallas kernels, local(): pl.pallas_call(kernel, out_shape=tuple(((pltpu.HBM if spec is HBM else ja...  16.7 us
    all_to_all x1, starting transfers between devices, on_device(): ts = lax.all_to_all(spread, PLANE, 0, 0, tiled=True).reshape(pooled, width)  7.54 us
    all_to_all x1, starting transfers between devices, on_device(): lax.all_to_all(dy.reshape(n_plane, rows, width), PLANE, 0, 0, tiled=True)  6.39 us
    unnamed x10, local copies, waits for them, and re-layouts  2.63 us
  transfers between devices with their start and end apart: 18, of which 10 were waited for; matrix products, arithmetic and copies ran while one was open for 0% of the time, Pallas kernels for 2%

profile of v15, /device:TPU:8, one launch (start us, length us, event | category | flops | bytes accessed | tf_op | source)
XLA Modules:
  0.0 98.5 jit_solution(16620758869682994411)
XLA Ops:
  1.6 1.8 %shard_map.59 = bf16[16,64,1152]{2,1,0:T(8,128)(2,1)} custom-call(f32[64,1152]{1,0:T(8,128)S(1)} %copy-done.1), custom_call_target="tpu_custom_call" | custom-call | bytes 1048576 | tf_op jit(solution)/shard_map/pallas_call | solution.py:135
  3.4 7.5 %all-to-all-start = ((bf16[16,64,1152]{2,1,0:T(8,128)(2,1)}), bf16[16,64,1152]{2,1,0:T(8,128)(2,1)S(1)}, u32[]{:S(2)}, u32[]{:S(2)}) async-start(bf16[16,64,1152]{2,1,0:T(8,128)(2,1)} %shard_map.59), calls=%async_computation | async-start | bytes 4718592 | tf_op jit(solution)/shard_map/all_to_all | solution.py:182
  11.1 2.0 %collective-permute-start.4 = (bf16[64,1152]{1,0:T(8,128)(2,1)S(1)}, bf16[64,1152]{1,0:T(8,128)(2,1)S(1)}, u32[]{:S(2)}, u32[]{:S(2)}) collective-permute-start(bf16[64,1152]{1,0:T(8,128)(2,1)S(1)} %shard_map.60.refs_0_), channel_id=1, source_target_pairs={{0,1},{1,2},{2,3},{3,4},{4,5},{5,6},{6,7},{7,0},{8,9},{9,10},{10,1... | collective-permute-start | bytes 442376 | tf_op jit(solution)/shard_map/ppermute | solution.py:20
  13.1 4.0 %collective-permute-start = (bf16[64,1152]{1,0:T(8,128)(2,1)S(1)}, bf16[64,1152]{1,0:T(8,128)(2,1)S(1)}, u32[]{:S(2)}, u32[]{:S(2)}) collective-permute-start(bf16[64,1152]{1,0:T(8,128)(2,1)S(1)} %shard_map.60.refs_0_), channel_id=1, source_target_pairs={{0,7},{1,0},{2,1},{3,2},{4,3},{5,4},{6,5},{7,6},{8,15},{9,8},{10,9... | collective-permute-start | bytes 442376 | tf_op jit(solution)/shard_map/ppermute | solution.py:20
  17.1 3.2 %collective-permute-done.4.refs_7_ = bf16[64,1152]{1,0:T(8,128)(2,1)S(1)} collective-permute-done((bf16[64,1152]{1,0:T(8,128)(2,1)S(1)}, bf16[64,1152]{1,0:T(8,128)(2,1)S(1)}, u32[]{:S(2)}, u32[]{:S(2)}) %collective-permute-start.4) | collective-permute-done | bytes 147488 | tf_op jit(solution)/shard_map/ppermute | solution.py:20
  20.3 3.2 %collective-permute-start.1 = (bf16[64,1152]{1,0:T(8,128)(2,1)S(1)}, bf16[64,1152]{1,0:T(8,128)(2,1)S(1)}, u32[]{:S(2)}, u32[]{:S(2)}) collective-permute-start(bf16[64,1152]{1,0:T(8,128)(2,1)S(1)} %collective-permute-done.refs_1_), channel_id=1, source_target_pairs={{0,7},{1,0},{2,1},{3,2},{4,3},{5,4},{6,5},{7,6},{8,15},{9,8},{10,9... | collective-permute-start | bytes 442376 | tf_op jit(solution)/shard_map/ppermute | solution.py:20
  23.5 4.4 %collective-permute-start.3 = (bf16[64,1152]{1,0:T(8,128)(2,1)S(1)}, bf16[64,1152]{1,0:T(8,128)(2,1)S(1)}, u32[]{:S(2)}, u32[]{:S(2)}) collective-permute-start(bf16[64,1152]{1,0:T(8,128)(2,1)S(1)} %shard_map.60.refs_0_), channel_id=1, source_target_pairs={{0,4},{1,5},{2,6},{3,7},{4,0},{5,1},{6,2},{7,3},{8,12},{9,13},{10,... | collective-permute-start | bytes 442376 | tf_op jit(solution)/shard_map/ppermute | solution.py:20
  28.1 4.9 %collective-permute-done.1.refs_2_ = bf16[64,1152]{1,0:T(8,128)(2,1)S(1)} collective-permute-done((bf16[64,1152]{1,0:T(8,128)(2,1)S(1)}, bf16[64,1152]{1,0:T(8,128)(2,1)S(1)}, u32[]{:S(2)}, u32[]{:S(2)}) %collective-permute-start.1) | collective-permute-done | bytes 147488 | tf_op jit(solution)/shard_map/ppermute | solution.py:20
  33.0 3.8 %collective-permute-start.2 = (bf16[64,1152]{1,0:T(8,128)(2,1)S(1)}, bf16[64,1152]{1,0:T(8,128)(2,1)S(1)}, u32[]{:S(2)}, u32[]{:S(2)}) collective-permute-start(bf16[64,1152]{1,0:T(8,128)(2,1)S(1)} %collective-permute-done.1.refs_2_), channel_id=1, source_target_pairs={{0,7},{1,0},{2,1},{3,2},{4,3},{5,4},{6,5},{7,6},{8,15},{9,8},{10,9... | collective-permute-start | bytes 442376 | tf_op jit(solution)/shard_map/ppermute | solution.py:20
  36.8 2.7 %collective-permute-done.2.refs_3_ = bf16[64,1152]{1,0:T(8,128)(2,1)S(1)} collective-permute-done((bf16[64,1152]{1,0:T(8,128)(2,1)S(1)}, bf16[64,1152]{1,0:T(8,128)(2,1)S(1)}, u32[]{:S(2)}, u32[]{:S(2)}) %collective-permute-start.2) | collective-permute-done | bytes 147488 | tf_op jit(solution)/shard_map/ppermute | solution.py:20
  41.3 1.5 %collective-permute-done.7.xo = bf16[512,1152]{1,0:T(8,128)(2,1)} collective-permute-done((bf16[512,1152]{1,0:T(8,128)(2,1)S(1)}, bf16[512,1152]{1,0:T(8,128)(2,1)}, u32[]{:S(2)}, u32[]{:S(2)}) %collective-permute-start.7) | collective-permute-done | bytes 1179680 | tf_op jit(solution)/shard_map/ppermute | solution.py:20
  42.8 1.0 %all-to-all-done = bf16[16,64,1152]{2,1,0:T(8,128)(2,1)S(1)} async-done(((bf16[16,64,1152]{2,1,0:T(8,128)(2,1)}), bf16[16,64,1152]{2,1,0:T(8,128)(2,1)S(1)}, u32[]{:S(2)}, u32[]{:S(2)}) %all-to-all-start) | async-done | bytes 2359328 | tf_op jit(solution)/shard_map/all_to_all | solution.py:182
  43.9 11.3 %shard_map.62 = (f32[512,1152]{1,0:T(8,128)}, bf16[512,1152]{1,0:T(8,128)(2,1)}, bf16[1024,1152]{1,0:T(8,128)(2,1)}) custom-call(s32[1]{0:T(128)} %bitcast.place, f32[2]{0:T(128)S(1)} %pad_maximum_fusion.scal, bf16[512,1152]{1,0:T(8,128)(2,1)S(1)} %shard_map.61.xs, bf16[512,1152]{1,0:T(8,128)(2,1)} %collective-permute-done.7.xo, bf16[1024,1152]{1,0:T(8,128)(2,1)S(1)} %bitcast.3), custom_call_target="tpu_custom_call" | custom-call | flops 7247757312 | bytes 9437184 | tf_op jit(solution)/shard_map/pallas_call | solution.py:135
  55.2 6.4 %all-to-all-start.1 = ((bf16[16,64,1152]{2,1,0:T(8,128)(2,1)}), bf16[16,64,1152]{2,1,0:T(8,128)(2,1)S(1)}, u32[]{:S(2)}, u32[]{:S(2)}) async-start(bf16[16,64,1152]{2,1,0:T(8,128)(2,1)} %bitcast.4), calls=%async_computation.1 | async-start | bytes 4718592 | tf_op jit(solution)/shard_map/all_to_all | solution.py:203
  61.6 1.7 %copy-done = f32[512,1152]{1,0:T(8,128)S(1)} copy-done((f32[512,1152]{1,0:T(8,128)S(1)}, f32[512,1152]{1,0:T(8,128)}, u32[]{:S(2)}) %copy-start) | copy-done | bytes 2359320
  63.6 4.5 %collective-permute-start.14 = (bf16[64,1152]{1,0:T(8,128)(2,1)S(1)}, bf16[64,1152]{1,0:T(8,128)(2,1)S(1)}, u32[]{:S(2)}, u32[]{:S(2)}) collective-permute-start(bf16[64,1152]{1,0:T(8,128)(2,1)S(1)} %get-tuple-element.18), channel_id=1, source_target_pairs={{0,7},{1,0},{2,1},{3,2},{4,3},{5,4},{6,5},{7,6},{8,15},{9,8},{10,9... | collective-permute-start | bytes 442376 | tf_op jit(solution)/shard_map/ppermute | solution.py:20
  68.2 2.9 %collective-permute-start.11 = (bf16[64,1152]{1,0:T(8,128)(2,1)S(1)}, bf16[64,1152]{1,0:T(8,128)(2,1)S(1)}, u32[]{:S(2)}, u32[]{:S(2)}) collective-permute-start(bf16[64,1152]{1,0:T(8,128)(2,1)S(1)} %get-tuple-element.20), channel_id=1, source_target_pairs={{0,5},{1,6},{2,7},{3,0},{4,1},{5,2},{6,3},{7,4},{8,13},{9,14},{10,... | collective-permute-start | bytes 442376 | tf_op jit(solution)/shard_map/ppermute | solution.py:20
  72.0 3.4 %collective-permute-start.9 = (bf16[64,1152]{1,0:T(8,128)(2,1)S(1)}, bf16[64,1152]{1,0:T(8,128)(2,1)S(1)}, u32[]{:S(2)}, u32[]{:S(2)}) collective-permute-start(bf16[64,1152]{1,0:T(8,128)(2,1)S(1)} %get-tuple-element.22), channel_id=1, source_target_pairs={{0,4},{1,5},{2,6},{3,7},{4,0},{5,1},{6,2},{7,3},{8,12},{9,13},{10,... | collective-permute-start | bytes 442376 | tf_op jit(solution)/shard_map/ppermute | solution.py:20
  75.4 2.6 %collective-permute-start.15 = (bf16[64,1152]{1,0:T(8,128)(2,1)S(1)}, bf16[64,1152]{1,0:T(8,128)(2,1)S(1)}, u32[]{:S(2)}, u32[]{:S(2)}) collective-permute-start(bf16[64,1152]{1,0:T(8,128)(2,1)S(1)} %get-tuple-element.16), channel_id=1, source_target_pairs={{0,7},{1,0},{2,1},{3,2},{4,3},{5,4},{6,5},{7,6},{8,15},{9,8},{10,9... | collective-permute-start | bytes 442376 | tf_op jit(solution)/shard_map/ppermute | solution.py:20
  78.1 10.0 %collective-permute-done.11.refs_3_ = bf16[64,1152]{1,0:T(8,128)(2,1)S(1)} collective-permute-done((bf16[64,1152]{1,0:T(8,128)(2,1)S(1)}, bf16[64,1152]{1,0:T(8,128)(2,1)S(1)}, u32[]{:S(2)}, u32[]{:S(2)}) %collective-permute-start.11) | collective-permute-done | bytes 147488 | tf_op jit(solution)/shard_map/ppermute | solution.py:20
  88.8 2.4 %collective-permute-done.15.refs_5_ = bf16[64,1152]{1,0:T(8,128)(2,1)S(1)} collective-permute-done((bf16[64,1152]{1,0:T(8,128)(2,1)S(1)}, bf16[64,1152]{1,0:T(8,128)(2,1)S(1)}, u32[]{:S(2)}, u32[]{:S(2)}) %collective-permute-start.15) | collective-permute-done | bytes 147488 | tf_op jit(solution)/shard_map/ppermute | solution.py:20
  91.3 4.0 %collective-permute-done.13.refs_4_ = bf16[64,1152]{1,0:T(8,128)(2,1)S(1)} collective-permute-done((bf16[64,1152]{1,0:T(8,128)(2,1)S(1)}, bf16[64,1152]{1,0:T(8,128)(2,1)S(1)}, u32[]{:S(2)}, u32[]{:S(2)}) %collective-permute-start.13) | collective-permute-done | bytes 147488 | tf_op jit(solution)/shard_map/ppermute | solution.py:20
  95.2 1.5 %shard_map.64 = f32[64,1152]{1,0:T(8,128)} custom-call(f32[2]{0:T(128)S(1)} %pad_maximum_fusion.scal, f32[64,1152]{1,0:T(8,128)S(1)} %copy-done.4, f32[64,1152]{1,0:T(8,128)S(1)} %get-tuple-element.13.refs_0_, bf16[64,1152]{1,0:T(8,128)(2,1)S(1)} %collective-permute-done.9.refs_1_, bf16[64,1152]{1,0:T(8,128)(2,1)S(1)} %collective-permute-done.10.refs_2_, ...), custom_call_target="tpu_custom_call" | custom-call | bytes 1048576 | tf_op jit(solution)/shard_map/pallas_call | solution.py:135
  96.8 1.7 %shard_map.65 = f32[64,1152]{1,0:T(8,128)} custom-call(f32[2]{0:T(128)S(1)} %pad_maximum_fusion.scal, f32[64,1152]{1,0:T(8,128)S(1)} %copy-done.2, bf16[16,64,1152]{2,1,0:T(8,128)(2,1)S(1)} %all-to-all-done.1.got), custom_call_target="tpu_custom_call" | custom-call | bytes 1048576 | tf_op jit(solution)/shard_map/pallas_call | solution.py:135
  (32 shorter events, 4.0 us)
Async XLA Ops:
  0.6 1.0 copy-start.1
  3.4 7.5 %copy-start.3 = (f32[64,1152]{1,0:T(8,128)S(1)}, f32[64,1152]{1,0:T(8,128)}, u32[]{:S(2)}) copy-start(f32[64,1152]{1,0:T(8,128)} %raw.2) | copy-start | bytes 884740
  3.4 40.5 %all-to-all-start = ((bf16[16,64,1152]{2,1,0:T(8,128)(2,1)}), bf16[16,64,1152]{2,1,0:T(8,128)(2,1)S(1)}, u32[]{:S(2)}, u32[]{:S(2)}) async-start(bf16[16,64,1152]{2,1,0:T(8,128)(2,1)} %shard_map.59), calls=%async_computation | async-start | bytes 4718592 | tf_op jit(solution)/shard_map/all_to_all | solution.py:182
  11.1 9.2 %collective-permute-start.4 = (bf16[64,1152]{1,0:T(8,128)(2,1)S(1)}, bf16[64,1152]{1,0:T(8,128)(2,1)S(1)}, u32[]{:S(2)}, u32[]{:S(2)}) collective-permute-start(bf16[64,1152]{1,0:T(8,128)(2,1)S(1)} %shard_map.60.refs_0_), channel_id=1, source_target_pairs={{0,1},{1,2},{2,3},{3,4},{4,5},{5,6},{6,7},{7,0},{8,9},{9,10},{10,1... | collective-permute-start | bytes 442376 | tf_op jit(solution)/shard_map/ppermute | solution.py:20
  13.1 7.2 %collective-permute-start = (bf16[64,1152]{1,0:T(8,128)(2,1)S(1)}, bf16[64,1152]{1,0:T(8,128)(2,1)S(1)}, u32[]{:S(2)}, u32[]{:S(2)}) collective-permute-start(bf16[64,1152]{1,0:T(8,128)(2,1)S(1)} %shard_map.60.refs_0_), channel_id=1, source_target_pairs={{0,7},{1,0},{2,1},{3,2},{4,3},{5,4},{6,5},{7,6},{8,15},{9,8},{10,9... | collective-permute-start | bytes 442376 | tf_op jit(solution)/shard_map/ppermute | solution.py:20
  20.3 7.9 %collective-permute-start.5 = (bf16[64,1152]{1,0:T(8,128)(2,1)S(1)}, bf16[64,1152]{1,0:T(8,128)(2,1)S(1)}, u32[]{:S(2)}, u32[]{:S(2)}) collective-permute-start(bf16[64,1152]{1,0:T(8,128)(2,1)S(1)} %collective-permute-done.4.refs_7_), channel_id=1, source_target_pairs={{0,1},{1,2},{2,3},{3,4},{4,5},{5,6},{6,7},{7,0},{8,9},{9,10},{10,1... | collective-permute-start | bytes 442376 | tf_op jit(solution)/shard_map/ppermute | solution.py:20
  20.3 12.7 %collective-permute-start.1 = (bf16[64,1152]{1,0:T(8,128)(2,1)S(1)}, bf16[64,1152]{1,0:T(8,128)(2,1)S(1)}, u32[]{:S(2)}, u32[]{:S(2)}) collective-permute-start(bf16[64,1152]{1,0:T(8,128)(2,1)S(1)} %collective-permute-done.refs_1_), channel_id=1, source_target_pairs={{0,7},{1,0},{2,1},{3,2},{4,3},{5,4},{6,5},{7,6},{8,15},{9,8},{10,9... | collective-permute-start | bytes 442376 | tf_op jit(solution)/shard_map/ppermute | solution.py:20
  23.5 13.3 %collective-permute-start.3 = (bf16[64,1152]{1,0:T(8,128)(2,1)S(1)}, bf16[64,1152]{1,0:T(8,128)(2,1)S(1)}, u32[]{:S(2)}, u32[]{:S(2)}) collective-permute-start(bf16[64,1152]{1,0:T(8,128)(2,1)S(1)} %shard_map.60.refs_0_), channel_id=1, source_target_pairs={{0,4},{1,5},{2,6},{3,7},{4,0},{5,1},{6,2},{7,3},{8,12},{9,13},{10,... | collective-permute-start | bytes 442376 | tf_op jit(solution)/shard_map/ppermute | solution.py:20
  28.1 8.7 %collective-permute-start.6 = (bf16[64,1152]{1,0:T(8,128)(2,1)S(1)}, bf16[64,1152]{1,0:T(8,128)(2,1)S(1)}, u32[]{:S(2)}, u32[]{:S(2)}) collective-permute-start(bf16[64,1152]{1,0:T(8,128)(2,1)S(1)} %collective-permute-done.5.refs_6_), channel_id=1, source_target_pairs={{0,1},{1,2},{2,3},{3,4},{4,5},{5,6},{6,7},{7,0},{8,9},{9,10},{10,1... | collective-permute-start | bytes 442376 | tf_op jit(solution)/shard_map/ppermute | solution.py:20
  33.0 6.5 %collective-permute-start.2 = (bf16[64,1152]{1,0:T(8,128)(2,1)S(1)}, bf16[64,1152]{1,0:T(8,128)(2,1)S(1)}, u32[]{:S(2)}, u32[]{:S(2)}) collective-permute-start(bf16[64,1152]{1,0:T(8,128)(2,1)S(1)} %collective-permute-done.1.refs_2_), channel_id=1, source_target_pairs={{0,7},{1,0},{2,1},{3,2},{4,3},{5,4},{6,5},{7,6},{8,15},{9,8},{10,9... | collective-permute-start | bytes 442376 | tf_op jit(solution)/shard_map/ppermute | solution.py:20
  39.6 3.2 %collective-permute-start.7 = (bf16[512,1152]{1,0:T(8,128)(2,1)S(1)}, bf16[512,1152]{1,0:T(8,128)(2,1)}, u32[]{:S(2)}, u32[]{:S(2)}) collective-permute-start(bf16[512,1152]{1,0:T(8,128)(2,1)S(1)} %shard_map.61.xs), channel_id=1, source_target_pairs={{0,16},{16,0},{1,17},{17,1},{2,18},{18,2},{3,19},{19,3},{4,20},{20... | collective-permute-start | bytes 3538952 | tf_op jit(solution)/shard_map/ppermute | solution.py:20
  55.1 6.5 %collective-permute-start.8 = (bf16[512,1152]{1,0:T(8,128)(2,1)}, bf16[512,1152]{1,0:T(8,128)(2,1)S(1)}, u32[]{:S(2)}, u32[]{:S(2)}) collective-permute-start(bf16[512,1152]{1,0:T(8,128)(2,1)} %get-tuple-element.12), channel_id=1, source_target_pairs={{0,16},{16,0},{1,17},{17,1},{2,18},{18,2},{3,19},{19,3},{4,20},{20... | collective-permute-start | bytes 3538952 | tf_op jit(solution)/shard_map/ppermute | solution.py:20
  55.2 41.5 %all-to-all-start.1 = ((bf16[16,64,1152]{2,1,0:T(8,128)(2,1)}), bf16[16,64,1152]{2,1,0:T(8,128)(2,1)S(1)}, u32[]{:S(2)}, u32[]{:S(2)}) async-start(bf16[16,64,1152]{2,1,0:T(8,128)(2,1)} %bitcast.4), calls=%async_computation.1 | async-start | bytes 4718592 | tf_op jit(solution)/shard_map/all_to_all | solution.py:203
  61.6 1.7 %copy-start = (f32[512,1152]{1,0:T(8,128)S(1)}, f32[512,1152]{1,0:T(8,128)}, u32[]{:S(2)}) copy-start(f32[512,1152]{1,0:T(8,128)} %get-tuple-element.11.dxs) | copy-start | bytes 7077892
  63.3 31.9 %copy-start.4 = (f32[64,1152]{1,0:T(8,128)S(1)}, f32[64,1152]{1,0:T(8,128)}, u32[]{:S(2)}) copy-start(f32[64,1152]{1,0:T(8,128)} %raw.2) | copy-start | bytes 884740
  63.6 33.2 %copy-start.2 = (f32[64,1152]{1,0:T(8,128)S(1)}, f32[64,1152]{1,0:T(8,128)}, u32[]{:S(2)}) copy-start(f32[64,1152]{1,0:T(8,128)} %raw.3) | copy-start | bytes 884740
  63.6 11.7 %collective-permute-start.14 = (bf16[64,1152]{1,0:T(8,128)(2,1)S(1)}, bf16[64,1152]{1,0:T(8,128)(2,1)S(1)}, u32[]{:S(2)}, u32[]{:S(2)}) collective-permute-start(bf16[64,1152]{1,0:T(8,128)(2,1)S(1)} %get-tuple-element.18), channel_id=1, source_target_pairs={{0,7},{1,0},{2,1},{3,2},{4,3},{5,4},{6,5},{7,6},{8,15},{9,8},{10,9... | collective-permute-start | bytes 442376 | tf_op jit(solution)/shard_map/ppermute | solution.py:20
  68.2 7.2 %collective-permute-start.12 = (bf16[64,1152]{1,0:T(8,128)(2,1)S(1)}, bf16[64,1152]{1,0:T(8,128)(2,1)S(1)}, u32[]{:S(2)}, u32[]{:S(2)}) collective-permute-start(bf16[64,1152]{1,0:T(8,128)(2,1)S(1)} %get-tuple-element.19), channel_id=1, source_target_pairs={{0,1},{1,2},{2,3},{3,4},{4,5},{5,6},{6,7},{7,0},{8,9},{9,10},{10,1... | collective-permute-start | bytes 442376 | tf_op jit(solution)/shard_map/ppermute | solution.py:20
  68.2 19.9 %collective-permute-start.11 = (bf16[64,1152]{1,0:T(8,128)(2,1)S(1)}, bf16[64,1152]{1,0:T(8,128)(2,1)S(1)}, u32[]{:S(2)}, u32[]{:S(2)}) collective-permute-start(bf16[64,1152]{1,0:T(8,128)(2,1)S(1)} %get-tuple-element.20), channel_id=1, source_target_pairs={{0,5},{1,6},{2,7},{3,0},{4,1},{5,2},{6,3},{7,4},{8,13},{9,14},{10,... | collective-permute-start | bytes 442376 | tf_op jit(solution)/shard_map/ppermute | solution.py:20
  71.1 17.0 %collective-permute-start.10 = (bf16[64,1152]{1,0:T(8,128)(2,1)S(1)}, bf16[64,1152]{1,0:T(8,128)(2,1)S(1)}, u32[]{:S(2)}, u32[]{:S(2)}) collective-permute-start(bf16[64,1152]{1,0:T(8,128)(2,1)S(1)} %get-tuple-element.21), channel_id=1, source_target_pairs={{0,3},{1,4},{2,5},{3,6},{4,7},{5,0},{6,1},{7,2},{8,11},{9,12},{10,... | collective-permute-start | bytes 442376 | tf_op jit(solution)/shard_map/ppermute | solution.py:20
  72.0 16.8 %collective-permute-start.9 = (bf16[64,1152]{1,0:T(8,128)(2,1)S(1)}, bf16[64,1152]{1,0:T(8,128)(2,1)S(1)}, u32[]{:S(2)}, u32[]{:S(2)}) collective-permute-start(bf16[64,1152]{1,0:T(8,128)(2,1)S(1)} %get-tuple-element.22), channel_id=1, source_target_pairs={{0,4},{1,5},{2,6},{3,7},{4,0},{5,1},{6,2},{7,3},{8,12},{9,13},{10,... | collective-permute-start | bytes 442376 | tf_op jit(solution)/shard_map/ppermute | solution.py:20
  75.4 15.8 %collective-permute-start.15 = (bf16[64,1152]{1,0:T(8,128)(2,1)S(1)}, bf16[64,1152]{1,0:T(8,128)(2,1)S(1)}, u32[]{:S(2)}, u32[]{:S(2)}) collective-permute-start(bf16[64,1152]{1,0:T(8,128)(2,1)S(1)} %get-tuple-element.16), channel_id=1, source_target_pairs={{0,7},{1,0},{2,1},{3,2},{4,3},{5,4},{6,5},{7,6},{8,15},{9,8},{10,9... | collective-permute-start | bytes 442376 | tf_op jit(solution)/shard_map/ppermute | solution.py:20
  78.1 17.2 %collective-permute-start.13 = (bf16[64,1152]{1,0:T(8,128)(2,1)S(1)}, bf16[64,1152]{1,0:T(8,128)(2,1)S(1)}, u32[]{:S(2)}, u32[]{:S(2)}) collective-permute-start(bf16[64,1152]{1,0:T(8,128)(2,1)S(1)} %get-tuple-element.17), channel_id=1, source_target_pairs={{0,1},{1,2},{2,3},{3,4},{4,5},{5,6},{6,7},{7,0},{8,9},{9,10},{10,1... | collective-permute-start | bytes 442376 | tf_op jit(solution)/shard_map/ppermute | solution.py:20

commit v16 on v14

--- a/solution.py
+++ b/solution.py
@@ -34,16 +34,23 @@
     return (raw / norm).astype(BF)
 
 
-def spread_kernel(raw, out, unit, sems):
+def spread_kernel(texts, out, raw, unit, sems):
+    n = out.shape[0]
+    load = pltpu.make_async_copy(texts, raw, sems.at[n])
+    load.start()
+    load.wait()
     unit[...] = unit_rows(raw[...])
-    copies = [pltpu.make_async_copy(unit, out.at[k], sems.at[k]) for k in range(out.shape[0])]
+    copies = [pltpu.make_async_copy(unit, out.at[k], sems.at[k]) for k in range(n)]
     for copy in copies:
         copy.start()
     for copy in copies:
         copy.wait()
 
 
-def unit_kernel(raw, out):
+def unit_kernel(images, out, raw, sem):
+    load = pltpu.make_async_copy(images, raw, sem)
+    load.start()
+    load.wait()
     out[...] = unit_rows(raw[...])
 
 
@@ -114,12 +121,20 @@
     refs[-1][...] = from_unit(scal[0] * total, unit, norm)
 
 
-def finish_texts_kernel(scal, raw, got, out):
-    total = got[0].astype(F32)
-    for k in range(1, got.shape[0]):
-        total += got[k].astype(F32)
-    unit, norm = to_unit(raw[...])
-    out[...] = from_unit(scal[0] * total, unit, norm)
+def finish_texts_kernel(scal, raw, got, out, part, sems):
+    copies = []
+    step = 16
+    for i in range(0, ROWS, step):
+        sl = slice(i, i + step)
+        total = got[0, sl].astype(F32)
+        for k in range(1, got.shape[0]):
+            total += got[k, sl].astype(F32)
+        unit, norm = to_unit(raw[sl])
+        part[sl] = from_unit(scal[0] * total, unit, norm)
+        copies.append(pltpu.make_async_copy(part.at[sl], out.at[sl], sems.at[len(copies)]))
+        copies[-1].start()
+    for copy in copies:
+        copy.wait()
 
 
 VMEM = pl.BlockSpec(memory_space=pltpu.VMEM)
@@ -168,12 +183,19 @@
     half = ROWS * lax.axis_size("z")
     pooled = ROWS * n_plane
     (spread,) = local(
-        spread_kernel, [((n_plane, rows, width), BF, HBM)], [texts],
-        scratch=[pltpu.VMEM((rows, width), BF), pltpu.SemaphoreType.DMA((n_plane,))],
+        spread_kernel, [((n_plane, rows, width), BF, HBM)], [texts], hbm=1,
+        scratch=[
+            pltpu.VMEM((rows, width), F32),
+            pltpu.VMEM((rows, width), BF),
+            pltpu.SemaphoreType.DMA((n_plane + 1,)),
+        ],
     )
     spread, images = lax.optimization_barrier((spread, images))
     ts = lax.all_to_all(spread, PLANE, 0, 0, tiled=True).reshape(pooled, width)
-    (x,) = local(unit_kernel, [((rows, width), BF, VMEM)], [images])
+    (x,) = local(
+        unit_kernel, [((rows, width), BF, VMEM)], [images], hbm=1,
+        scratch=[pltpu.VMEM((rows, width), F32), pltpu.SemaphoreType.DMA],
+    )
     (xs,) = local(pack_kernel, [((half, width), BF, VMEM)], ring_gather(x))
     xo = shifted(xs, "core", 1)
     place = lax.axis_index(PLANE).astype(jnp.int32).reshape(1)
@@ -201,7 +223,10 @@
     )
     got = near_reduce(rest.reshape(-1, rows, width))
     (grad_images,) = local(finish_kernel, [((rows, width), F32, VMEM)], [scal, images, own] + got, smem=1)
-    (grad_texts,) = local(finish_texts_kernel, [((rows, width), F32, VMEM)], [scal, texts, dyr], smem=1)
+    (grad_texts,) = local(
+        finish_texts_kernel, [((rows, width), F32, HBM)], [scal, texts, dyr], smem=1,
+        scratch=[pltpu.VMEM((rows, width), F32), pltpu.SemaphoreType.DMA((4,))],
+    )
     return (grad_images, grad_texts)
 
 

time: 98.3 us -> 98.5 us (level)
  no operation moved by 1% of the time
where the time goes in v16:
time: 98.5 us; the launch traced here: 98.1 us
  starting transfers between devices  46.1 us (47%)
  waiting for transfers between devices  30.6 us (31%)
  Pallas kernels  16.3 us (17%)
  local copies, waits for them, and re-layouts  2.69 us (3%)
  between operations  2.25 us (2%)
    ppermute x16, starting transfers between devices, shifted(): lax.ppermute(block, axis, [(i, (i + distance) % n) for i in range(n)])  32.1 us
    ppermute x16, waiting for transfers between devices, shifted(): lax.ppermute(block, axis, [(i, (i + distance) % n) for i in range(n)])  29.7 us
    pallas_call x7, Pallas kernels, local(): pl.pallas_call(kernel, out_shape=tuple(((pltpu.HBM if spec is HBM else ja...  16.3 us
    all_to_all x1, starting transfers between devices, on_device(): ts = lax.all_to_all(spread, PLANE, 0, 0, tiled=True).reshape(pooled, width)  7.54 us
    all_to_all x1, starting transfers between devices, on_device(): lax.all_to_all(dy.reshape(n_plane, rows, width), PLANE, 0, 0, tiled=True)  6.48 us
    unnamed x10, local copies, waits for them, and re-layouts  2.63 us
  transfers between devices with their start and end apart: 18, of which 10 were waited for; matrix products, arithmetic and copies ran while one was open for 0% of the time, Pallas kernels for 2%

profile of v16, /device:TPU:8, one launch (start us, length us, event | category | flops | bytes accessed | tf_op | source)
XLA Modules:
  0.0 98.1 jit_solution(13598866469975926742)
XLA Ops:
  1.6 1.8 %shard_map.59 = bf16[16,64,1152]{2,1,0:T(8,128)(2,1)} custom-call(f32[64,1152]{1,0:T(8,128)S(1)} %copy-done.1), custom_call_target="tpu_custom_call" | custom-call | bytes 1048576 | tf_op jit(solution)/shard_map/pallas_call | solution.py:147
  3.4 7.5 %all-to-all-start = ((bf16[16,64,1152]{2,1,0:T(8,128)(2,1)}), bf16[16,64,1152]{2,1,0:T(8,128)(2,1)S(1)}, u32[]{:S(2)}, u32[]{:S(2)}) async-start(bf16[16,64,1152]{2,1,0:T(8,128)(2,1)} %shard_map.59), calls=%async_computation | async-start | bytes 4718592 | tf_op jit(solution)/shard_map/all_to_all | solution.py:194
  11.1 2.0 %collective-permute-start.4 = (bf16[64,1152]{1,0:T(8,128)(2,1)S(1)}, bf16[64,1152]{1,0:T(8,128)(2,1)S(1)}, u32[]{:S(2)}, u32[]{:S(2)}) collective-permute-start(bf16[64,1152]{1,0:T(8,128)(2,1)S(1)} %shard_map.60.refs_0_), channel_id=1, source_target_pairs={{0,1},{1,2},{2,3},{3,4},{4,5},{5,6},{6,7},{7,0},{8,9},{9,10},{10,1... | collective-permute-start | bytes 442376 | tf_op jit(solution)/shard_map/ppermute | solution.py:20
  13.1 4.0 %collective-permute-start = (bf16[64,1152]{1,0:T(8,128)(2,1)S(1)}, bf16[64,1152]{1,0:T(8,128)(2,1)S(1)}, u32[]{:S(2)}, u32[]{:S(2)}) collective-permute-start(bf16[64,1152]{1,0:T(8,128)(2,1)S(1)} %shard_map.60.refs_0_), channel_id=1, source_target_pairs={{0,7},{1,0},{2,1},{3,2},{4,3},{5,4},{6,5},{7,6},{8,15},{9,8},{10,9... | collective-permute-start | bytes 442376 | tf_op jit(solution)/shard_map/ppermute | solution.py:20
  17.2 3.2 %collective-permute-done.4.refs_7_ = bf16[64,1152]{1,0:T(8,128)(2,1)S(1)} collective-permute-done((bf16[64,1152]{1,0:T(8,128)(2,1)S(1)}, bf16[64,1152]{1,0:T(8,128)(2,1)S(1)}, u32[]{:S(2)}, u32[]{:S(2)}) %collective-permute-start.4) | collective-permute-done | bytes 147488 | tf_op jit(solution)/shard_map/ppermute | solution.py:20
  20.4 3.2 %collective-permute-start.1 = (bf16[64,1152]{1,0:T(8,128)(2,1)S(1)}, bf16[64,1152]{1,0:T(8,128)(2,1)S(1)}, u32[]{:S(2)}, u32[]{:S(2)}) collective-permute-start(bf16[64,1152]{1,0:T(8,128)(2,1)S(1)} %collective-permute-done.refs_1_), channel_id=1, source_target_pairs={{0,7},{1,0},{2,1},{3,2},{4,3},{5,4},{6,5},{7,6},{8,15},{9,8},{10,9... | collective-permute-start | bytes 442376 | tf_op jit(solution)/shard_map/ppermute | solution.py:20
  23.6 4.4 %collective-permute-start.3 = (bf16[64,1152]{1,0:T(8,128)(2,1)S(1)}, bf16[64,1152]{1,0:T(8,128)(2,1)S(1)}, u32[]{:S(2)}, u32[]{:S(2)}) collective-permute-start(bf16[64,1152]{1,0:T(8,128)(2,1)S(1)} %shard_map.60.refs_0_), channel_id=1, source_target_pairs={{0,4},{1,5},{2,6},{3,7},{4,0},{5,1},{6,2},{7,3},{8,12},{9,13},{10,... | collective-permute-start | bytes 442376 | tf_op jit(solution)/shard_map/ppermute | solution.py:20
  28.2 4.9 %collective-permute-done.1.refs_2_ = bf16[64,1152]{1,0:T(8,128)(2,1)S(1)} collective-permute-done((bf16[64,1152]{1,0:T(8,128)(2,1)S(1)}, bf16[64,1152]{1,0:T(8,128)(2,1)S(1)}, u32[]{:S(2)}, u32[]{:S(2)}) %collective-permute-start.1) | collective-permute-done | bytes 147488 | tf_op jit(solution)/shard_map/ppermute | solution.py:20
  33.1 3.8 %collective-permute-start.2 = (bf16[64,1152]{1,0:T(8,128)(2,1)S(1)}, bf16[64,1152]{1,0:T(8,128)(2,1)S(1)}, u32[]{:S(2)}, u32[]{:S(2)}) collective-permute-start(bf16[64,1152]{1,0:T(8,128)(2,1)S(1)} %collective-permute-done.1.refs_2_), channel_id=1, source_target_pairs={{0,7},{1,0},{2,1},{3,2},{4,3},{5,4},{6,5},{7,6},{8,15},{9,8},{10,9... | collective-permute-start | bytes 442376 | tf_op jit(solution)/shard_map/ppermute | solution.py:20
  36.9 2.7 %collective-permute-done.2.refs_3_ = bf16[64,1152]{1,0:T(8,128)(2,1)S(1)} collective-permute-done((bf16[64,1152]{1,0:T(8,128)(2,1)S(1)}, bf16[64,1152]{1,0:T(8,128)(2,1)S(1)}, u32[]{:S(2)}, u32[]{:S(2)}) %collective-permute-start.2) | collective-permute-done | bytes 147488 | tf_op jit(solution)/shard_map/ppermute | solution.py:20
  41.4 1.5 %collective-permute-done.7.xo = bf16[512,1152]{1,0:T(8,128)(2,1)} collective-permute-done((bf16[512,1152]{1,0:T(8,128)(2,1)S(1)}, bf16[512,1152]{1,0:T(8,128)(2,1)}, u32[]{:S(2)}, u32[]{:S(2)}) %collective-permute-start.7) | collective-permute-done | bytes 1179680 | tf_op jit(solution)/shard_map/ppermute | solution.py:20
  43.9 10.8 %shard_map.62 = (f32[512,1152]{1,0:T(8,128)}, bf16[512,1152]{1,0:T(8,128)(2,1)}, bf16[1024,1152]{1,0:T(8,128)(2,1)}) custom-call(s32[1]{0:T(128)} %bitcast.place, f32[2]{0:T(128)S(1)} %pad_maximum_fusion.scal, bf16[512,1152]{1,0:T(8,128)(2,1)S(1)} %shard_map.61.xs, bf16[512,1152]{1,0:T(8,128)(2,1)} %collective-permute-done.7.xo, bf16[1024,1152]{1,0:T(8,128)(2,1)S(1)} %bitcast.3), custom_call_target="tpu_custom_call" | custom-call | flops 7247757312 | bytes 9437184 | tf_op jit(solution)/shard_map/pallas_call | solution.py:147
  54.8 6.5 %all-to-all-start.1 = ((bf16[16,64,1152]{2,1,0:T(8,128)(2,1)}), bf16[16,64,1152]{2,1,0:T(8,128)(2,1)S(1)}, u32[]{:S(2)}, u32[]{:S(2)}) async-start(bf16[16,64,1152]{2,1,0:T(8,128)(2,1)} %bitcast.4), calls=%async_computation.1 | async-start | bytes 4718592 | tf_op jit(solution)/shard_map/all_to_all | solution.py:218
  61.3 1.7 %copy-done = f32[512,1152]{1,0:T(8,128)S(1)} copy-done((f32[512,1152]{1,0:T(8,128)S(1)}, f32[512,1152]{1,0:T(8,128)}, u32[]{:S(2)}) %copy-start) | copy-done | bytes 2359320
  63.3 4.4 %collective-permute-start.14 = (bf16[64,1152]{1,0:T(8,128)(2,1)S(1)}, bf16[64,1152]{1,0:T(8,128)(2,1)S(1)}, u32[]{:S(2)}, u32[]{:S(2)}) collective-permute-start(bf16[64,1152]{1,0:T(8,128)(2,1)S(1)} %get-tuple-element.18), channel_id=1, source_target_pairs={{0,7},{1,0},{2,1},{3,2},{4,3},{5,4},{6,5},{7,6},{8,15},{9,8},{10,9... | collective-permute-start | bytes 442376 | tf_op jit(solution)/shard_map/ppermute | solution.py:20
  67.7 2.9 %collective-permute-start.11 = (bf16[64,1152]{1,0:T(8,128)(2,1)S(1)}, bf16[64,1152]{1,0:T(8,128)(2,1)S(1)}, u32[]{:S(2)}, u32[]{:S(2)}) collective-permute-start(bf16[64,1152]{1,0:T(8,128)(2,1)S(1)} %get-tuple-element.20), channel_id=1, source_target_pairs={{0,5},{1,6},{2,7},{3,0},{4,1},{5,2},{6,3},{7,4},{8,13},{9,14},{10,... | collective-permute-start | bytes 442376 | tf_op jit(solution)/shard_map/ppermute | solution.py:20
  71.5 3.4 %collective-permute-start.9 = (bf16[64,1152]{1,0:T(8,128)(2,1)S(1)}, bf16[64,1152]{1,0:T(8,128)(2,1)S(1)}, u32[]{:S(2)}, u32[]{:S(2)}) collective-permute-start(bf16[64,1152]{1,0:T(8,128)(2,1)S(1)} %get-tuple-element.22), channel_id=1, source_target_pairs={{0,4},{1,5},{2,6},{3,7},{4,0},{5,1},{6,2},{7,3},{8,12},{9,13},{10,... | collective-permute-start | bytes 442376 | tf_op jit(solution)/shard_map/ppermute | solution.py:20
  75.0 2.6 %collective-permute-start.15 = (bf16[64,1152]{1,0:T(8,128)(2,1)S(1)}, bf16[64,1152]{1,0:T(8,128)(2,1)S(1)}, u32[]{:S(2)}, u32[]{:S(2)}) collective-permute-start(bf16[64,1152]{1,0:T(8,128)(2,1)S(1)} %get-tuple-element.16), channel_id=1, source_target_pairs={{0,7},{1,0},{2,1},{3,2},{4,3},{5,4},{6,5},{7,6},{8,15},{9,8},{10,9... | collective-permute-start | bytes 442376 | tf_op jit(solution)/shard_map/ppermute | solution.py:20
  77.6 10.0 %collective-permute-done.11.refs_3_ = bf16[64,1152]{1,0:T(8,128)(2,1)S(1)} collective-permute-done((bf16[64,1152]{1,0:T(8,128)(2,1)S(1)}, bf16[64,1152]{1,0:T(8,128)(2,1)S(1)}, u32[]{:S(2)}, u32[]{:S(2)}) %collective-permute-start.11) | collective-permute-done | bytes 147488 | tf_op jit(solution)/shard_map/ppermute | solution.py:20
  87.6 1.0 collective-permute-done.9.refs_1_
  88.5 2.3 %collective-permute-done.15.refs_5_ = bf16[64,1152]{1,0:T(8,128)(2,1)S(1)} collective-permute-done((bf16[64,1152]{1,0:T(8,128)(2,1)S(1)}, bf16[64,1152]{1,0:T(8,128)(2,1)S(1)}, u32[]{:S(2)}, u32[]{:S(2)}) %collective-permute-start.15) | collective-permute-done | bytes 147488 | tf_op jit(solution)/shard_map/ppermute | solution.py:20
  90.8 4.0 %collective-permute-done.13.refs_4_ = bf16[64,1152]{1,0:T(8,128)(2,1)S(1)} collective-permute-done((bf16[64,1152]{1,0:T(8,128)(2,1)S(1)}, bf16[64,1152]{1,0:T(8,128)(2,1)S(1)}, u32[]{:S(2)}, u32[]{:S(2)}) %collective-permute-start.13) | collective-permute-done | bytes 147488 | tf_op jit(solution)/shard_map/ppermute | solution.py:20
  94.8 1.5 %shard_map.64 = f32[64,1152]{1,0:T(8,128)} custom-call(f32[2]{0:T(128)S(1)} %pad_maximum_fusion.scal, f32[64,1152]{1,0:T(8,128)S(1)} %copy-done.4, f32[64,1152]{1,0:T(8,128)S(1)} %get-tuple-element.13.refs_0_, bf16[64,1152]{1,0:T(8,128)(2,1)S(1)} %collective-permute-done.9.refs_1_, bf16[64,1152]{1,0:T(8,128)(2,1)S(1)} %collective-permute-done.10.refs_2_, ...), custom_call_target="tpu_custom_call" | custom-call | bytes 1048576 | tf_op jit(solution)/shard_map/pallas_call | solution.py:147
  96.3 1.7 %shard_map.65 = f32[64,1152]{1,0:T(8,128)} custom-call(f32[2]{0:T(128)S(1)} %pad_maximum_fusion.scal, f32[64,1152]{1,0:T(8,128)S(1)} %copy-done.2, bf16[16,64,1152]{2,1,0:T(8,128)(2,1)S(1)} %all-to-all-done.1.got), custom_call_target="tpu_custom_call" | custom-call | bytes 1048576 | tf_op jit(solution)/shard_map/pallas_call | solution.py:147
  (32 shorter events, 4.2 us)
Async XLA Ops:
  0.6 1.0 copy-start.1
  3.4 7.5 %copy-start.3 = (f32[64,1152]{1,0:T(8,128)S(1)}, f32[64,1152]{1,0:T(8,128)}, u32[]{:S(2)}) copy-start(f32[64,1152]{1,0:T(8,128)} %raw.1) | copy-start | bytes 884740
  3.4 40.5 %all-to-all-start = ((bf16[16,64,1152]{2,1,0:T(8,128)(2,1)}), bf16[16,64,1152]{2,1,0:T(8,128)(2,1)S(1)}, u32[]{:S(2)}, u32[]{:S(2)}) async-start(bf16[16,64,1152]{2,1,0:T(8,128)(2,1)} %shard_map.59), calls=%async_computation | async-start | bytes 4718592 | tf_op jit(solution)/shard_map/all_to_all | solution.py:194
  11.1 9.2 %collective-permute-start.4 = (bf16[64,1152]{1,0:T(8,128)(2,1)S(1)}, bf16[64,1152]{1,0:T(8,128)(2,1)S(1)}, u32[]{:S(2)}, u32[]{:S(2)}) collective-permute-start(bf16[64,1152]{1,0:T(8,128)(2,1)S(1)} %shard_map.60.refs_0_), channel_id=1, source_target_pairs={{0,1},{1,2},{2,3},{3,4},{4,5},{5,6},{6,7},{7,0},{8,9},{9,10},{10,1... | collective-permute-start | bytes 442376 | tf_op jit(solution)/shard_map/ppermute | solution.py:20
  13.1 7.2 %collective-permute-start = (bf16[64,1152]{1,0:T(8,128)(2,1)S(1)}, bf16[64,1152]{1,0:T(8,128)(2,1)S(1)}, u32[]{:S(2)}, u32[]{:S(2)}) collective-permute-start(bf16[64,1152]{1,0:T(8,128)(2,1)S(1)} %shard_map.60.refs_0_), channel_id=1, source_target_pairs={{0,7},{1,0},{2,1},{3,2},{4,3},{5,4},{6,5},{7,6},{8,15},{9,8},{10,9... | collective-permute-start | bytes 442376 | tf_op jit(solution)/shard_map/ppermute | solution.py:20
  20.4 7.9 %collective-permute-start.5 = (bf16[64,1152]{1,0:T(8,128)(2,1)S(1)}, bf16[64,1152]{1,0:T(8,128)(2,1)S(1)}, u32[]{:S(2)}, u32[]{:S(2)}) collective-permute-start(bf16[64,1152]{1,0:T(8,128)(2,1)S(1)} %collective-permute-done.4.refs_7_), channel_id=1, source_target_pairs={{0,1},{1,2},{2,3},{3,4},{4,5},{5,6},{6,7},{7,0},{8,9},{9,10},{10,1... | collective-permute-start | bytes 442376 | tf_op jit(solution)/shard_map/ppermute | solution.py:20
  20.4 12.7 %collective-permute-start.1 = (bf16[64,1152]{1,0:T(8,128)(2,1)S(1)}, bf16[64,1152]{1,0:T(8,128)(2,1)S(1)}, u32[]{:S(2)}, u32[]{:S(2)}) collective-permute-start(bf16[64,1152]{1,0:T(8,128)(2,1)S(1)} %collective-permute-done.refs_1_), channel_id=1, source_target_pairs={{0,7},{1,0},{2,1},{3,2},{4,3},{5,4},{6,5},{7,6},{8,15},{9,8},{10,9... | collective-permute-start | bytes 442376 | tf_op jit(solution)/shard_map/ppermute | solution.py:20
  23.6 13.3 %collective-permute-start.3 = (bf16[64,1152]{1,0:T(8,128)(2,1)S(1)}, bf16[64,1152]{1,0:T(8,128)(2,1)S(1)}, u32[]{:S(2)}, u32[]{:S(2)}) collective-permute-start(bf16[64,1152]{1,0:T(8,128)(2,1)S(1)} %shard_map.60.refs_0_), channel_id=1, source_target_pairs={{0,4},{1,5},{2,6},{3,7},{4,0},{5,1},{6,2},{7,3},{8,12},{9,13},{10,... | collective-permute-start | bytes 442376 | tf_op jit(solution)/shard_map/ppermute | solution.py:20
  28.2 8.7 %collective-permute-start.6 = (bf16[64,1152]{1,0:T(8,128)(2,1)S(1)}, bf16[64,1152]{1,0:T(8,128)(2,1)S(1)}, u32[]{:S(2)}, u32[]{:S(2)}) collective-permute-start(bf16[64,1152]{1,0:T(8,128)(2,1)S(1)} %collective-permute-done.5.refs_6_), channel_id=1, source_target_pairs={{0,1},{1,2},{2,3},{3,4},{4,5},{5,6},{6,7},{7,0},{8,9},{9,10},{10,1... | collective-permute-start | bytes 442376 | tf_op jit(solution)/shard_map/ppermute | solution.py:20
  33.1 6.5 %collective-permute-start.2 = (bf16[64,1152]{1,0:T(8,128)(2,1)S(1)}, bf16[64,1152]{1,0:T(8,128)(2,1)S(1)}, u32[]{:S(2)}, u32[]{:S(2)}) collective-permute-start(bf16[64,1152]{1,0:T(8,128)(2,1)S(1)} %collective-permute-done.1.refs_2_), channel_id=1, source_target_pairs={{0,7},{1,0},{2,1},{3,2},{4,3},{5,4},{6,5},{7,6},{8,15},{9,8},{10,9... | collective-permute-start | bytes 442376 | tf_op jit(solution)/shard_map/ppermute | solution.py:20
  39.7 3.2 %collective-permute-start.7 = (bf16[512,1152]{1,0:T(8,128)(2,1)S(1)}, bf16[512,1152]{1,0:T(8,128)(2,1)}, u32[]{:S(2)}, u32[]{:S(2)}) collective-permute-start(bf16[512,1152]{1,0:T(8,128)(2,1)S(1)} %shard_map.61.xs), channel_id=1, source_target_pairs={{0,16},{16,0},{1,17},{17,1},{2,18},{18,2},{3,19},{19,3},{4,20},{20... | collective-permute-start | bytes 3538952 | tf_op jit(solution)/shard_map/ppermute | solution.py:20
  54.7 6.6 %collective-permute-start.8 = (bf16[512,1152]{1,0:T(8,128)(2,1)}, bf16[512,1152]{1,0:T(8,128)(2,1)S(1)}, u32[]{:S(2)}, u32[]{:S(2)}) collective-permute-start(bf16[512,1152]{1,0:T(8,128)(2,1)} %get-tuple-element.12), channel_id=1, source_target_pairs={{0,16},{16,0},{1,17},{17,1},{2,18},{18,2},{3,19},{19,3},{4,20},{20... | collective-permute-start | bytes 3538952 | tf_op jit(solution)/shard_map/ppermute | solution.py:20
  54.8 41.5 %all-to-all-start.1 = ((bf16[16,64,1152]{2,1,0:T(8,128)(2,1)}), bf16[16,64,1152]{2,1,0:T(8,128)(2,1)S(1)}, u32[]{:S(2)}, u32[]{:S(2)}) async-start(bf16[16,64,1152]{2,1,0:T(8,128)(2,1)} %bitcast.4), calls=%async_computation.1 | async-start | bytes 4718592 | tf_op jit(solution)/shard_map/all_to_all | solution.py:218
  61.2 1.7 %copy-start = (f32[512,1152]{1,0:T(8,128)S(1)}, f32[512,1152]{1,0:T(8,128)}, u32[]{:S(2)}) copy-start(f32[512,1152]{1,0:T(8,128)} %get-tuple-element.11.dxs) | copy-start | bytes 7077892
  62.9 31.9 %copy-start.4 = (f32[64,1152]{1,0:T(8,128)S(1)}, f32[64,1152]{1,0:T(8,128)}, u32[]{:S(2)}) copy-start(f32[64,1152]{1,0:T(8,128)} %raw.1) | copy-start | bytes 884740
  63.2 33.1 %copy-start.2 = (f32[64,1152]{1,0:T(8,128)S(1)}, f32[64,1152]{1,0:T(8,128)}, u32[]{:S(2)}) copy-start(f32[64,1152]{1,0:T(8,128)} %raw.2) | copy-start | bytes 884740
  63.3 11.6 %collective-permute-start.14 = (bf16[64,1152]{1,0:T(8,128)(2,1)S(1)}, bf16[64,1152]{1,0:T(8,128)(2,1)S(1)}, u32[]{:S(2)}, u32[]{:S(2)}) collective-permute-start(bf16[64,1152]{1,0:T(8,128)(2,1)S(1)} %get-tuple-element.18), channel_id=1, source_target_pairs={{0,7},{1,0},{2,1},{3,2},{4,3},{5,4},{6,5},{7,6},{8,15},{9,8},{10,9... | collective-permute-start | bytes 442376 | tf_op jit(solution)/shard_map/ppermute | solution.py:20
  67.7 7.2 %collective-permute-start.12 = (bf16[64,1152]{1,0:T(8,128)(2,1)S(1)}, bf16[64,1152]{1,0:T(8,128)(2,1)S(1)}, u32[]{:S(2)}, u32[]{:S(2)}) collective-permute-start(bf16[64,1152]{1,0:T(8,128)(2,1)S(1)} %get-tuple-element.19), channel_id=1, source_target_pairs={{0,1},{1,2},{2,3},{3,4},{4,5},{5,6},{6,7},{7,0},{8,9},{9,10},{10,1... | collective-permute-start | bytes 442376 | tf_op jit(solution)/shard_map/ppermute | solution.py:20
  67.7 19.9 %collective-permute-start.11 = (bf16[64,1152]{1,0:T(8,128)(2,1)S(1)}, bf16[64,1152]{1,0:T(8,128)(2,1)S(1)}, u32[]{:S(2)}, u32[]{:S(2)}) collective-permute-start(bf16[64,1152]{1,0:T(8,128)(2,1)S(1)} %get-tuple-element.20), channel_id=1, source_target_pairs={{0,5},{1,6},{2,7},{3,0},{4,1},{5,2},{6,3},{7,4},{8,13},{9,14},{10,... | collective-permute-start | bytes 442376 | tf_op jit(solution)/shard_map/ppermute | solution.py:20
  70.6 16.9 %collective-permute-start.10 = (bf16[64,1152]{1,0:T(8,128)(2,1)S(1)}, bf16[64,1152]{1,0:T(8,128)(2,1)S(1)}, u32[]{:S(2)}, u32[]{:S(2)}) collective-permute-start(bf16[64,1152]{1,0:T(8,128)(2,1)S(1)} %get-tuple-element.21), channel_id=1, source_target_pairs={{0,3},{1,4},{2,5},{3,6},{4,7},{5,0},{6,1},{7,2},{8,11},{9,12},{10,... | collective-permute-start | bytes 442376 | tf_op jit(solution)/shard_map/ppermute | solution.py:20
  71.5 17.0 %collective-permute-start.9 = (bf16[64,1152]{1,0:T(8,128)(2,1)S(1)}, bf16[64,1152]{1,0:T(8,128)(2,1)S(1)}, u32[]{:S(2)}, u32[]{:S(2)}) collective-permute-start(bf16[64,1152]{1,0:T(8,128)(2,1)S(1)} %get-tuple-element.22), channel_id=1, source_target_pairs={{0,4},{1,5},{2,6},{3,7},{4,0},{5,1},{6,2},{7,3},{8,12},{9,13},{10,... | collective-permute-start | bytes 442376 | tf_op jit(solution)/shard_map/ppermute | solution.py:20
  75.0 15.8 %collective-permute-start.15 = (bf16[64,1152]{1,0:T(8,128)(2,1)S(1)}, bf16[64,1152]{1,0:T(8,128)(2,1)S(1)}, u32[]{:S(2)}, u32[]{:S(2)}) collective-permute-start(bf16[64,1152]{1,0:T(8,128)(2,1)S(1)} %get-tuple-element.16), channel_id=1, source_target_pairs={{0,7},{1,0},{2,1},{3,2},{4,3},{5,4},{6,5},{7,6},{8,15},{9,8},{10,9... | collective-permute-start | bytes 442376 | tf_op jit(solution)/shard_map/ppermute | solution.py:20
  77.6 17.2 %collective-permute-start.13 = (bf16[64,1152]{1,0:T(8,128)(2,1)S(1)}, bf16[64,1152]{1,0:T(8,128)(2,1)S(1)}, u32[]{:S(2)}, u32[]{:S(2)}) collective-permute-start(bf16[64,1152]{1,0:T(8,128)(2,1)S(1)} %get-tuple-element.17), channel_id=1, source_target_pairs={{0,1},{1,2},{2,3},{3,4},{4,5},{5,6},{6,7},{7,0},{8,9},{9,10},{10,1... | collective-permute-start | bytes 442376 | tf_op jit(solution)/shard_map/ppermute | solution.py:20

commit v17 on v16

--- a/solution.py
+++ b/solution.py
@@ -150,7 +150,7 @@
         in_specs=specs + [VMEM] * (len(args) - len(specs)),
         out_specs=tuple(spec for _, _, spec in outs),
         scratch_shapes=list(scratch),
-        compiler_params=pltpu.CompilerParams(vmem_limit_bytes=vmem * 2**20),
+        compiler_params=pltpu.CompilerParams(vmem_limit_bytes=int(vmem * 2**20)),
         cost_estimate=pl.CostEstimate(flops=flops, bytes_accessed=nbytes, transcendentals=trans),
     )(*args)
 
@@ -183,7 +183,7 @@
     half = ROWS * lax.axis_size("z")
     pooled = ROWS * n_plane
     (spread,) = local(
-        spread_kernel, [((n_plane, rows, width), BF, HBM)], [texts], hbm=1,
+        spread_kernel, [((n_plane, rows, width), BF, HBM)], [texts], hbm=1, vmem=60.5,
         scratch=[
             pltpu.VMEM((rows, width), F32),
             pltpu.VMEM((rows, width), BF),

time: 98.5 us -> 98.4 us (level)
    unnamed x10 -> x8, local copies, waits for them, and re-layouts: 2.63 us -> 1.67 us
where the time goes in v17:
time: 98.4 us; the launch traced here: 98.1 us
  starting transfers between devices  46.1 us (47%)
  waiting for transfers between devices  30.6 us (31%)
  Pallas kernels  17.2 us (17%)
  between operations  2.24 us (2%)
  local copies, waits for them, and re-layouts  1.74 us (2%)
    ppermute x16, starting transfers between devices, shifted(): lax.ppermute(block, axis, [(i, (i + distance) % n) for i in range(n)])  32.1 us
    ppermute x16, waiting for transfers between devices, shifted(): lax.ppermute(block, axis, [(i, (i + distance) % n) for i in range(n)])  29.7 us
    pallas_call x7, Pallas kernels, local(): pl.pallas_call(kernel, out_shape=tuple(((pltpu.HBM if spec is HBM else ja...  17.2 us
    all_to_all x1, starting transfers between devices, on_device(): ts = lax.all_to_all(spread, PLANE, 0, 0, tiled=True).reshape(pooled, width)  7.54 us
    all_to_all x1, starting transfers between devices, on_device(): lax.all_to_all(dy.reshape(n_plane, rows, width), PLANE, 0, 0, tiled=True)  6.47 us
  transfers between devices with their start and end apart: 18, of which 10 were waited for; matrix products, arithmetic and copies ran while one was open for 0% of the time, Pallas kernels for 2%

profile of v17, /device:TPU:8, one launch (start us, length us, event | category | flops | bytes accessed | tf_op | source)
XLA Modules:
  0.0 98.1 jit_solution(7151198110933898017)
XLA Ops:
  0.6 2.7 %shard_map.59 = bf16[16,64,1152]{2,1,0:T(8,128)(2,1)} custom-call(f32[64,1152]{1,0:T(8,128)} %raw.2), custom_call_target="tpu_custom_call" | custom-call | bytes 1048576 | tf_op jit(solution)/shard_map/pallas_call | solution.py:147
  3.3 7.5 %all-to-all-start = ((bf16[16,64,1152]{2,1,0:T(8,128)(2,1)}), bf16[16,64,1152]{2,1,0:T(8,128)(2,1)S(1)}, u32[]{:S(2)}, u32[]{:S(2)}) async-start(bf16[16,64,1152]{2,1,0:T(8,128)(2,1)} %shard_map.59), calls=%async_computation | async-start | bytes 4718592 | tf_op jit(solution)/shard_map/all_to_all | solution.py:194
  11.1 2.0 %collective-permute-start.4 = (bf16[64,1152]{1,0:T(8,128)(2,1)S(1)}, bf16[64,1152]{1,0:T(8,128)(2,1)S(1)}, u32[]{:S(2)}, u32[]{:S(2)}) collective-permute-start(bf16[64,1152]{1,0:T(8,128)(2,1)S(1)} %shard_map.60.refs_0_), channel_id=1, source_target_pairs={{0,1},{1,2},{2,3},{3,4},{4,5},{5,6},{6,7},{7,0},{8,9},{9,10},{10,1... | collective-permute-start | bytes 442376 | tf_op jit(solution)/shard_map/ppermute | solution.py:20
  13.1 4.0 %collective-permute-start = (bf16[64,1152]{1,0:T(8,128)(2,1)S(1)}, bf16[64,1152]{1,0:T(8,128)(2,1)S(1)}, u32[]{:S(2)}, u32[]{:S(2)}) collective-permute-start(bf16[64,1152]{1,0:T(8,128)(2,1)S(1)} %shard_map.60.refs_0_), channel_id=1, source_target_pairs={{0,7},{1,0},{2,1},{3,2},{4,3},{5,4},{6,5},{7,6},{8,15},{9,8},{10,9... | collective-permute-start | bytes 442376 | tf_op jit(solution)/shard_map/ppermute | solution.py:20
  17.1 3.2 %collective-permute-done.4.refs_7_ = bf16[64,1152]{1,0:T(8,128)(2,1)S(1)} collective-permute-done((bf16[64,1152]{1,0:T(8,128)(2,1)S(1)}, bf16[64,1152]{1,0:T(8,128)(2,1)S(1)}, u32[]{:S(2)}, u32[]{:S(2)}) %collective-permute-start.4) | collective-permute-done | bytes 147488 | tf_op jit(solution)/shard_map/ppermute | solution.py:20
  20.3 3.2 %collective-permute-start.1 = (bf16[64,1152]{1,0:T(8,128)(2,1)S(1)}, bf16[64,1152]{1,0:T(8,128)(2,1)S(1)}, u32[]{:S(2)}, u32[]{:S(2)}) collective-permute-start(bf16[64,1152]{1,0:T(8,128)(2,1)S(1)} %collective-permute-done.refs_1_), channel_id=1, source_target_pairs={{0,7},{1,0},{2,1},{3,2},{4,3},{5,4},{6,5},{7,6},{8,15},{9,8},{10,9... | collective-permute-start | bytes 442376 | tf_op jit(solution)/shard_map/ppermute | solution.py:20
  23.5 4.4 %collective-permute-start.3 = (bf16[64,1152]{1,0:T(8,128)(2,1)S(1)}, bf16[64,1152]{1,0:T(8,128)(2,1)S(1)}, u32[]{:S(2)}, u32[]{:S(2)}) collective-permute-start(bf16[64,1152]{1,0:T(8,128)(2,1)S(1)} %shard_map.60.refs_0_), channel_id=1, source_target_pairs={{0,4},{1,5},{2,6},{3,7},{4,0},{5,1},{6,2},{7,3},{8,12},{9,13},{10,... | collective-permute-start | bytes 442376 | tf_op jit(solution)/shard_map/ppermute | solution.py:20
  28.2 4.9 %collective-permute-done.1.refs_2_ = bf16[64,1152]{1,0:T(8,128)(2,1)S(1)} collective-permute-done((bf16[64,1152]{1,0:T(8,128)(2,1)S(1)}, bf16[64,1152]{1,0:T(8,128)(2,1)S(1)}, u32[]{:S(2)}, u32[]{:S(2)}) %collective-permute-start.1) | collective-permute-done | bytes 147488 | tf_op jit(solution)/shard_map/ppermute | solution.py:20
  33.0 3.8 %collective-permute-start.2 = (bf16[64,1152]{1,0:T(8,128)(2,1)S(1)}, bf16[64,1152]{1,0:T(8,128)(2,1)S(1)}, u32[]{:S(2)}, u32[]{:S(2)}) collective-permute-start(bf16[64,1152]{1,0:T(8,128)(2,1)S(1)} %collective-permute-done.1.refs_2_), channel_id=1, source_target_pairs={{0,7},{1,0},{2,1},{3,2},{4,3},{5,4},{6,5},{7,6},{8,15},{9,8},{10,9... | collective-permute-start | bytes 442376 | tf_op jit(solution)/shard_map/ppermute | solution.py:20
  36.9 2.7 %collective-permute-done.2.refs_3_ = bf16[64,1152]{1,0:T(8,128)(2,1)S(1)} collective-permute-done((bf16[64,1152]{1,0:T(8,128)(2,1)S(1)}, bf16[64,1152]{1,0:T(8,128)(2,1)S(1)}, u32[]{:S(2)}, u32[]{:S(2)}) %collective-permute-start.2) | collective-permute-done | bytes 147488 | tf_op jit(solution)/shard_map/ppermute | solution.py:20
  41.3 1.5 %collective-permute-done.7.xo = bf16[512,1152]{1,0:T(8,128)(2,1)} collective-permute-done((bf16[512,1152]{1,0:T(8,128)(2,1)S(1)}, bf16[512,1152]{1,0:T(8,128)(2,1)}, u32[]{:S(2)}, u32[]{:S(2)}) %collective-permute-start.7) | collective-permute-done | bytes 1179680 | tf_op jit(solution)/shard_map/ppermute | solution.py:20
  42.9 0.9 all-to-all-done
  43.8 10.8 %shard_map.62 = (f32[512,1152]{1,0:T(8,128)}, bf16[512,1152]{1,0:T(8,128)(2,1)}, bf16[1024,1152]{1,0:T(8,128)(2,1)}) custom-call(s32[1]{0:T(128)} %bitcast.place, f32[2]{0:T(128)S(1)} %pad_maximum_fusion.scal, bf16[512,1152]{1,0:T(8,128)(2,1)S(1)} %shard_map.61.xs, bf16[512,1152]{1,0:T(8,128)(2,1)} %collective-permute-done.7.xo, bf16[1024,1152]{1,0:T(8,128)(2,1)S(1)} %bitcast.3), custom_call_target="tpu_custom_call" | custom-call | flops 7247757312 | bytes 9437184 | tf_op jit(solution)/shard_map/pallas_call | solution.py:147
  54.7 6.5 %all-to-all-start.1 = ((bf16[16,64,1152]{2,1,0:T(8,128)(2,1)}), bf16[16,64,1152]{2,1,0:T(8,128)(2,1)S(1)}, u32[]{:S(2)}, u32[]{:S(2)}) async-start(bf16[16,64,1152]{2,1,0:T(8,128)(2,1)} %bitcast.4), calls=%async_computation.1 | async-start | bytes 4718592 | tf_op jit(solution)/shard_map/all_to_all | solution.py:218
  61.2 1.7 %copy-done = f32[512,1152]{1,0:T(8,128)S(1)} copy-done((f32[512,1152]{1,0:T(8,128)S(1)}, f32[512,1152]{1,0:T(8,128)}, u32[]{:S(2)}) %copy-start) | copy-done | bytes 2359320
  63.2 4.4 %collective-permute-start.14 = (bf16[64,1152]{1,0:T(8,128)(2,1)S(1)}, bf16[64,1152]{1,0:T(8,128)(2,1)S(1)}, u32[]{:S(2)}, u32[]{:S(2)}) collective-permute-start(bf16[64,1152]{1,0:T(8,128)(2,1)S(1)} %get-tuple-element.18), channel_id=1, source_target_pairs={{0,7},{1,0},{2,1},{3,2},{4,3},{5,4},{6,5},{7,6},{8,15},{9,8},{10,9... | collective-permute-start | bytes 442376 | tf_op jit(solution)/shard_map/ppermute | solution.py:20
  67.6 2.9 %collective-permute-start.11 = (bf16[64,1152]{1,0:T(8,128)(2,1)S(1)}, bf16[64,1152]{1,0:T(8,128)(2,1)S(1)}, u32[]{:S(2)}, u32[]{:S(2)}) collective-permute-start(bf16[64,1152]{1,0:T(8,128)(2,1)S(1)} %get-tuple-element.20), channel_id=1, source_target_pairs={{0,5},{1,6},{2,7},{3,0},{4,1},{5,2},{6,3},{7,4},{8,13},{9,14},{10,... | collective-permute-start | bytes 442376 | tf_op jit(solution)/shard_map/ppermute | solution.py:20
  71.5 3.4 %collective-permute-start.9 = (bf16[64,1152]{1,0:T(8,128)(2,1)S(1)}, bf16[64,1152]{1,0:T(8,128)(2,1)S(1)}, u32[]{:S(2)}, u32[]{:S(2)}) collective-permute-start(bf16[64,1152]{1,0:T(8,128)(2,1)S(1)} %get-tuple-element.22), channel_id=1, source_target_pairs={{0,4},{1,5},{2,6},{3,7},{4,0},{5,1},{6,2},{7,3},{8,12},{9,13},{10,... | collective-permute-start | bytes 442376 | tf_op jit(solution)/shard_map/ppermute | solution.py:20
  74.9 2.6 %collective-permute-start.15 = (bf16[64,1152]{1,0:T(8,128)(2,1)S(1)}, bf16[64,1152]{1,0:T(8,128)(2,1)S(1)}, u32[]{:S(2)}, u32[]{:S(2)}) collective-permute-start(bf16[64,1152]{1,0:T(8,128)(2,1)S(1)} %get-tuple-element.16), channel_id=1, source_target_pairs={{0,7},{1,0},{2,1},{3,2},{4,3},{5,4},{6,5},{7,6},{8,15},{9,8},{10,9... | collective-permute-start | bytes 442376 | tf_op jit(solution)/shard_map/ppermute | solution.py:20
  77.5 10.0 %collective-permute-done.11.refs_3_ = bf16[64,1152]{1,0:T(8,128)(2,1)S(1)} collective-permute-done((bf16[64,1152]{1,0:T(8,128)(2,1)S(1)}, bf16[64,1152]{1,0:T(8,128)(2,1)S(1)}, u32[]{:S(2)}, u32[]{:S(2)}) %collective-permute-start.11) | collective-permute-done | bytes 147488 | tf_op jit(solution)/shard_map/ppermute | solution.py:20
  88.4 2.4 %collective-permute-done.15.refs_5_ = bf16[64,1152]{1,0:T(8,128)(2,1)S(1)} collective-permute-done((bf16[64,1152]{1,0:T(8,128)(2,1)S(1)}, bf16[64,1152]{1,0:T(8,128)(2,1)S(1)}, u32[]{:S(2)}, u32[]{:S(2)}) %collective-permute-start.15) | collective-permute-done | bytes 147488 | tf_op jit(solution)/shard_map/ppermute | solution.py:20
  90.7 4.0 %collective-permute-done.13.refs_4_ = bf16[64,1152]{1,0:T(8,128)(2,1)S(1)} collective-permute-done((bf16[64,1152]{1,0:T(8,128)(2,1)S(1)}, bf16[64,1152]{1,0:T(8,128)(2,1)S(1)}, u32[]{:S(2)}, u32[]{:S(2)}) %collective-permute-start.13) | collective-permute-done | bytes 147488 | tf_op jit(solution)/shard_map/ppermute | solution.py:20
  94.7 1.5 %shard_map.64 = f32[64,1152]{1,0:T(8,128)} custom-call(f32[2]{0:T(128)S(1)} %pad_maximum_fusion.scal, f32[64,1152]{1,0:T(8,128)S(1)} %copy-done.3, f32[64,1152]{1,0:T(8,128)S(1)} %get-tuple-element.13.refs_0_, bf16[64,1152]{1,0:T(8,128)(2,1)S(1)} %collective-permute-done.9.refs_1_, bf16[64,1152]{1,0:T(8,128)(2,1)S(1)} %collective-permute-done.10.refs_2_, ...), custom_call_target="tpu_custom_call" | custom-call | bytes 1048576 | tf_op jit(solution)/shard_map/pallas_call | solution.py:147
  96.2 1.7 %shard_map.65 = f32[64,1152]{1,0:T(8,128)} custom-call(f32[2]{0:T(128)S(1)} %pad_maximum_fusion.scal, f32[64,1152]{1,0:T(8,128)S(1)} %copy-done.1, bf16[16,64,1152]{2,1,0:T(8,128)(2,1)S(1)} %all-to-all-done.1.got), custom_call_target="tpu_custom_call" | custom-call | bytes 1048576 | tf_op jit(solution)/shard_map/pallas_call | solution.py:147
  (30 shorter events, 3.2 us)
Async XLA Ops:
  3.3 7.5 %copy-start.2 = (f32[64,1152]{1,0:T(8,128)S(1)}, f32[64,1152]{1,0:T(8,128)}, u32[]{:S(2)}) copy-start(f32[64,1152]{1,0:T(8,128)} %raw.1) | copy-start | bytes 884740
  3.3 40.5 %all-to-all-start = ((bf16[16,64,1152]{2,1,0:T(8,128)(2,1)}), bf16[16,64,1152]{2,1,0:T(8,128)(2,1)S(1)}, u32[]{:S(2)}, u32[]{:S(2)}) async-start(bf16[16,64,1152]{2,1,0:T(8,128)(2,1)} %shard_map.59), calls=%async_computation | async-start | bytes 4718592 | tf_op jit(solution)/shard_map/all_to_all | solution.py:194
  11.1 9.2 %collective-permute-start.4 = (bf16[64,1152]{1,0:T(8,128)(2,1)S(1)}, bf16[64,1152]{1,0:T(8,128)(2,1)S(1)}, u32[]{:S(2)}, u32[]{:S(2)}) collective-permute-start(bf16[64,1152]{1,0:T(8,128)(2,1)S(1)} %shard_map.60.refs_0_), channel_id=1, source_target_pairs={{0,1},{1,2},{2,3},{3,4},{4,5},{5,6},{6,7},{7,0},{8,9},{9,10},{10,1... | collective-permute-start | bytes 442376 | tf_op jit(solution)/shard_map/ppermute | solution.py:20
  13.1 7.2 %collective-permute-start = (bf16[64,1152]{1,0:T(8,128)(2,1)S(1)}, bf16[64,1152]{1,0:T(8,128)(2,1)S(1)}, u32[]{:S(2)}, u32[]{:S(2)}) collective-permute-start(bf16[64,1152]{1,0:T(8,128)(2,1)S(1)} %shard_map.60.refs_0_), channel_id=1, source_target_pairs={{0,7},{1,0},{2,1},{3,2},{4,3},{5,4},{6,5},{7,6},{8,15},{9,8},{10,9... | collective-permute-start | bytes 442376 | tf_op jit(solution)/shard_map/ppermute | solution.py:20
  20.3 7.9 %collective-permute-start.5 = (bf16[64,1152]{1,0:T(8,128)(2,1)S(1)}, bf16[64,1152]{1,0:T(8,128)(2,1)S(1)}, u32[]{:S(2)}, u32[]{:S(2)}) collective-permute-start(bf16[64,1152]{1,0:T(8,128)(2,1)S(1)} %collective-permute-done.4.refs_7_), channel_id=1, source_target_pairs={{0,1},{1,2},{2,3},{3,4},{4,5},{5,6},{6,7},{7,0},{8,9},{9,10},{10,1... | collective-permute-start | bytes 442376 | tf_op jit(solution)/shard_map/ppermute | solution.py:20
  20.3 12.7 %collective-permute-start.1 = (bf16[64,1152]{1,0:T(8,128)(2,1)S(1)}, bf16[64,1152]{1,0:T(8,128)(2,1)S(1)}, u32[]{:S(2)}, u32[]{:S(2)}) collective-permute-start(bf16[64,1152]{1,0:T(8,128)(2,1)S(1)} %collective-permute-done.refs_1_), channel_id=1, source_target_pairs={{0,7},{1,0},{2,1},{3,2},{4,3},{5,4},{6,5},{7,6},{8,15},{9,8},{10,9... | collective-permute-start | bytes 442376 | tf_op jit(solution)/shard_map/ppermute | solution.py:20
  23.5 13.3 %collective-permute-start.3 = (bf16[64,1152]{1,0:T(8,128)(2,1)S(1)}, bf16[64,1152]{1,0:T(8,128)(2,1)S(1)}, u32[]{:S(2)}, u32[]{:S(2)}) collective-permute-start(bf16[64,1152]{1,0:T(8,128)(2,1)S(1)} %shard_map.60.refs_0_), channel_id=1, source_target_pairs={{0,4},{1,5},{2,6},{3,7},{4,0},{5,1},{6,2},{7,3},{8,12},{9,13},{10,... | collective-permute-start | bytes 442376 | tf_op jit(solution)/shard_map/ppermute | solution.py:20
  28.2 8.7 %collective-permute-start.6 = (bf16[64,1152]{1,0:T(8,128)(2,1)S(1)}, bf16[64,1152]{1,0:T(8,128)(2,1)S(1)}, u32[]{:S(2)}, u32[]{:S(2)}) collective-permute-start(bf16[64,1152]{1,0:T(8,128)(2,1)S(1)} %collective-permute-done.5.refs_6_), channel_id=1, source_target_pairs={{0,1},{1,2},{2,3},{3,4},{4,5},{5,6},{6,7},{7,0},{8,9},{9,10},{10,1... | collective-permute-start | bytes 442376 | tf_op jit(solution)/shard_map/ppermute | solution.py:20
  33.0 6.5 %collective-permute-start.2 = (bf16[64,1152]{1,0:T(8,128)(2,1)S(1)}, bf16[64,1152]{1,0:T(8,128)(2,1)S(1)}, u32[]{:S(2)}, u32[]{:S(2)}) collective-permute-start(bf16[64,1152]{1,0:T(8,128)(2,1)S(1)} %collective-permute-done.1.refs_2_), channel_id=1, source_target_pairs={{0,7},{1,0},{2,1},{3,2},{4,3},{5,4},{6,5},{7,6},{8,15},{9,8},{10,9... | collective-permute-start | bytes 442376 | tf_op jit(solution)/shard_map/ppermute | solution.py:20
  39.6 3.2 %collective-permute-start.7 = (bf16[512,1152]{1,0:T(8,128)(2,1)S(1)}, bf16[512,1152]{1,0:T(8,128)(2,1)}, u32[]{:S(2)}, u32[]{:S(2)}) collective-permute-start(bf16[512,1152]{1,0:T(8,128)(2,1)S(1)} %shard_map.61.xs), channel_id=1, source_target_pairs={{0,16},{16,0},{1,17},{17,1},{2,18},{18,2},{3,19},{19,3},{4,20},{20... | collective-permute-start | bytes 3538952 | tf_op jit(solution)/shard_map/ppermute | solution.py:20
  54.6 6.6 %collective-permute-start.8 = (bf16[512,1152]{1,0:T(8,128)(2,1)}, bf16[512,1152]{1,0:T(8,128)(2,1)S(1)}, u32[]{:S(2)}, u32[]{:S(2)}) collective-permute-start(bf16[512,1152]{1,0:T(8,128)(2,1)} %get-tuple-element.12), channel_id=1, source_target_pairs={{0,16},{16,0},{1,17},{17,1},{2,18},{18,2},{3,19},{19,3},{4,20},{20... | collective-permute-start | bytes 3538952 | tf_op jit(solution)/shard_map/ppermute | solution.py:20
  54.7 41.5 %all-to-all-start.1 = ((bf16[16,64,1152]{2,1,0:T(8,128)(2,1)}), bf16[16,64,1152]{2,1,0:T(8,128)(2,1)S(1)}, u32[]{:S(2)}, u32[]{:S(2)}) async-start(bf16[16,64,1152]{2,1,0:T(8,128)(2,1)} %bitcast.4), calls=%async_computation.1 | async-start | bytes 4718592 | tf_op jit(solution)/shard_map/all_to_all | solution.py:218
  61.2 1.7 %copy-start = (f32[512,1152]{1,0:T(8,128)S(1)}, f32[512,1152]{1,0:T(8,128)}, u32[]{:S(2)}) copy-start(f32[512,1152]{1,0:T(8,128)} %get-tuple-element.11.dxs) | copy-start | bytes 7077892
  62.9 31.9 %copy-start.3 = (f32[64,1152]{1,0:T(8,128)S(1)}, f32[64,1152]{1,0:T(8,128)}, u32[]{:S(2)}) copy-start(f32[64,1152]{1,0:T(8,128)} %raw.1) | copy-start | bytes 884740
  63.1 33.1 %copy-start.1 = (f32[64,1152]{1,0:T(8,128)S(1)}, f32[64,1152]{1,0:T(8,128)}, u32[]{:S(2)}) copy-start(f32[64,1152]{1,0:T(8,128)} %raw.2) | copy-start | bytes 884740
  63.2 11.6 %collective-permute-start.14 = (bf16[64,1152]{1,0:T(8,128)(2,1)S(1)}, bf16[64,1152]{1,0:T(8,128)(2,1)S(1)}, u32[]{:S(2)}, u32[]{:S(2)}) collective-permute-start(bf16[64,1152]{1,0:T(8,128)(2,1)S(1)} %get-tuple-element.18), channel_id=1, source_target_pairs={{0,7},{1,0},{2,1},{3,2},{4,3},{5,4},{6,5},{7,6},{8,15},{9,8},{10,9... | collective-permute-start | bytes 442376 | tf_op jit(solution)/shard_map/ppermute | solution.py:20
  67.6 7.2 %collective-permute-start.12 = (bf16[64,1152]{1,0:T(8,128)(2,1)S(1)}, bf16[64,1152]{1,0:T(8,128)(2,1)S(1)}, u32[]{:S(2)}, u32[]{:S(2)}) collective-permute-start(bf16[64,1152]{1,0:T(8,128)(2,1)S(1)} %get-tuple-element.19), channel_id=1, source_target_pairs={{0,1},{1,2},{2,3},{3,4},{4,5},{5,6},{6,7},{7,0},{8,9},{9,10},{10,1... | collective-permute-start | bytes 442376 | tf_op jit(solution)/shard_map/ppermute | solution.py:20
  67.6 19.9 %collective-permute-start.11 = (bf16[64,1152]{1,0:T(8,128)(2,1)S(1)}, bf16[64,1152]{1,0:T(8,128)(2,1)S(1)}, u32[]{:S(2)}, u32[]{:S(2)}) collective-permute-start(bf16[64,1152]{1,0:T(8,128)(2,1)S(1)} %get-tuple-element.20), channel_id=1, source_target_pairs={{0,5},{1,6},{2,7},{3,0},{4,1},{5,2},{6,3},{7,4},{8,13},{9,14},{10,... | collective-permute-start | bytes 442376 | tf_op jit(solution)/shard_map/ppermute | solution.py:20
  70.5 17.0 %collective-permute-start.10 = (bf16[64,1152]{1,0:T(8,128)(2,1)S(1)}, bf16[64,1152]{1,0:T(8,128)(2,1)S(1)}, u32[]{:S(2)}, u32[]{:S(2)}) collective-permute-start(bf16[64,1152]{1,0:T(8,128)(2,1)S(1)} %get-tuple-element.21), channel_id=1, source_target_pairs={{0,3},{1,4},{2,5},{3,6},{4,7},{5,0},{6,1},{7,2},{8,11},{9,12},{10,... | collective-permute-start | bytes 442376 | tf_op jit(solution)/shard_map/ppermute | solution.py:20
  71.5 16.9 %collective-permute-start.9 = (bf16[64,1152]{1,0:T(8,128)(2,1)S(1)}, bf16[64,1152]{1,0:T(8,128)(2,1)S(1)}, u32[]{:S(2)}, u32[]{:S(2)}) collective-permute-start(bf16[64,1152]{1,0:T(8,128)(2,1)S(1)} %get-tuple-element.22), channel_id=1, source_target_pairs={{0,4},{1,5},{2,6},{3,7},{4,0},{5,1},{6,2},{7,3},{8,12},{9,13},{10,... | collective-permute-start | bytes 442376 | tf_op jit(solution)/shard_map/ppermute | solution.py:20
  74.9 15.8 %collective-permute-start.15 = (bf16[64,1152]{1,0:T(8,128)(2,1)S(1)}, bf16[64,1152]{1,0:T(8,128)(2,1)S(1)}, u32[]{:S(2)}, u32[]{:S(2)}) collective-permute-start(bf16[64,1152]{1,0:T(8,128)(2,1)S(1)} %get-tuple-element.16), channel_id=1, source_target_pairs={{0,7},{1,0},{2,1},{3,2},{4,3},{5,4},{6,5},{7,6},{8,15},{9,8},{10,9... | collective-permute-start | bytes 442376 | tf_op jit(solution)/shard_map/ppermute | solution.py:20
  77.5 17.2 %collective-permute-start.13 = (bf16[64,1152]{1,0:T(8,128)(2,1)S(1)}, bf16[64,1152]{1,0:T(8,128)(2,1)S(1)}, u32[]{:S(2)}, u32[]{:S(2)}) collective-permute-start(bf16[64,1152]{1,0:T(8,128)(2,1)S(1)} %get-tuple-element.17), channel_id=1, source_target_pairs={{0,1},{1,2},{2,3},{3,4},{4,5},{5,6},{6,7},{7,0},{8,9},{9,10},{10,1... | collective-permute-start | bytes 442376 | tf_op jit(solution)/shard_map/ppermute | solution.py:20

commit v18 on v17

--- a/solution.py
+++ b/solution.py
@@ -36,10 +36,16 @@
 
 def spread_kernel(texts, out, raw, unit, sems):
     n = out.shape[0]
-    load = pltpu.make_async_copy(texts, raw, sems.at[n])
-    load.start()
-    load.wait()
-    unit[...] = unit_rows(raw[...])
+    step = 16
+    loads = []
+    for i in range(0, ROWS, step):
+        sl = slice(i, i + step)
+        loads.append(pltpu.make_async_copy(texts.at[sl], raw.at[sl], sems.at[n + len(loads)]))
+        loads[-1].start()
+    for i, load in enumerate(loads):
+        load.wait()
+        sl = slice(i * step, (i + 1) * step)
+        unit[sl] = unit_rows(raw[sl])
     copies = [pltpu.make_async_copy(unit, out.at[k], sems.at[k]) for k in range(n)]
     for copy in copies:
         copy.start()
@@ -63,7 +69,7 @@
     return 1.0 / (1.0 + jnp.exp2(dots * (temp * -LOG2E) + offset * -LOG2E))
 
 
-def pair_kernel(place, scal, xs, xo, ts, dxs, dxo, dy, x, held, mine, theirs, part, sems):
+def pair_kernel(place, scal, xs, xo, ts, coeff, kept, dxo, dy, x, held, theirs, part, sems):
     temp = scal[0]
     offset = scal[1]
     half = xs.shape[0]
@@ -95,12 +101,13 @@
         copies.append(pltpu.make_async_copy(src, dst, sems.at[2 + len(copies)]))
         copies[-1].start()
 
-    for h, (buf, out) in enumerate(((mine, dxs), (theirs, dxo))):
-        for i in range(0, half, wide):
-            cols = slice(h * half + i, h * half + i + wide)
-            dots = lax.dot_general(held[:, cols], ts[...], TN, preferred_element_type=F32)
-            buf[i : i + wide] = dots.astype(buf.dtype)
-            send(buf.at[i : i + wide], out.at[i : i + wide])
+    send(ts, kept)
+    send(held.at[:, 0:half], coeff)
+    for i in range(0, half, wide):
+        cols = slice(half + i, half + i + wide)
+        dots = lax.dot_general(held[:, cols], ts[...], TN, preferred_element_type=F32)
+        theirs[i : i + wide] = dots.astype(BF)
+        send(theirs.at[i : i + wide], dxo.at[i : i + wide])
     for j in range(0, pooled, step):
         part[j : j + step] = jnp.dot(held[j : j + step], x[...], preferred_element_type=F32).astype(BF)
         send(part.at[j : j + step], dy.at[j : j + step])
@@ -108,9 +115,34 @@
         copy.wait()
 
 
-def join_kernel(dxs, other, own, rest):
-    own[...] = dxs[0:ROWS] + other[0:ROWS].astype(F32)
-    rest[...] = (dxs[ROWS:] + other[ROWS:].astype(F32)).astype(BF)
+def join_kernel(coeff, kept, other, own, rest, held, ts, theirs, mine, sums, sems):
+    pooled, half = coeff.shape
+    step = 256
+    pairs = [(coeff.at[j : j + step], held.at[j : j + step]) for j in range(0, pooled, step)]
+    pairs += [(kept.at[j : j + step], ts.at[j : j + step]) for j in range(0, pooled, step)]
+    pairs += [(other, theirs)]
+    loads = [pltpu.make_async_copy(src, dst, sems.at[k]) for k, (src, dst) in enumerate(pairs)]
+    for copy in loads:
+        copy.start()
+    for copy in loads:
+        copy.wait()
+    copies = []
+    for i in range(0, half, step):
+        part = lax.dot_general(held[:, i : i + step], ts[...], TN, preferred_element_type=F32)
+        part += theirs[i : i + step].astype(F32)
+        if i == 0:
+            mine[...] = part[0:ROWS]
+            sums[0 : step - ROWS] = part[ROWS:].astype(BF)
+            sl = slice(0, step - ROWS)
+            copies.append(pltpu.make_async_copy(mine, own, sems.at[len(loads)]))
+            copies[-1].start()
+        else:
+            sl = slice(i - ROWS, i - ROWS + step)
+            sums[sl] = part.astype(BF)
+        copies.append(pltpu.make_async_copy(sums.at[sl], rest.at[sl], sems.at[len(loads) + len(copies)]))
+        copies[-1].start()
+    for copy in copies:
+        copy.wait()
 
 
 def finish_kernel(scal, raw, *refs):
@@ -187,7 +219,7 @@
         scratch=[
             pltpu.VMEM((rows, width), F32),
             pltpu.VMEM((rows, width), BF),
-            pltpu.SemaphoreType.DMA((n_plane + 1,)),
+            pltpu.SemaphoreType.DMA((n_plane + 4,)),
         ],
     )
     spread, images = lax.optimization_barrier((spread, images))
@@ -201,25 +233,32 @@
     place = lax.axis_index(PLANE).astype(jnp.int32).reshape(1)
     scal = jnp.stack([temp, bias[0]])
     unit_flops = 2 * half * pooled * width
-    dxs, dxo, dy = local(
+    coeff, kept, dxo, dy = local(
         pair_kernel,
-        [((half, width), F32, HBM), ((half, width), BF, HBM), ((pooled, width), BF, HBM)],
+        [((pooled, half), BF, HBM), ((pooled, width), BF, HBM), ((half, width), BF, HBM), ((pooled, width), BF, HBM)],
         [place, scal, xs, xo, ts], smem=2, hbm=2,
         scratch=[
             pltpu.VMEM((2 * half, width), BF),
             pltpu.VMEM((pooled, 2 * half), BF),
-            pltpu.VMEM((half, width), F32),
             pltpu.VMEM((half, width), BF),
             pltpu.VMEM((pooled, width), BF),
-            pltpu.SemaphoreType.DMA((8,)),
+            pltpu.SemaphoreType.DMA((9,)),
         ],
-        flops=6 * unit_flops, nbytes=9 * 2**20, trans=4 * half * pooled, vmem=24,
+        flops=5 * unit_flops, nbytes=9 * 2**20, trans=4 * half * pooled, vmem=24,
     )
     dyr = lax.all_to_all(dy.reshape(n_plane, rows, width), PLANE, 0, 0, tiled=True)
     other = shifted(dxo, "core", 1)
     own, rest = local(
-        join_kernel, [((rows, width), F32, VMEM), ((half - rows, width), BF, VMEM)], [dxs, other],
-        nbytes=5 * 2**20, vmem=16,
+        join_kernel, [((rows, width), F32, HBM), ((half - rows, width), BF, HBM)], [coeff, kept, other], hbm=3,
+        scratch=[
+            pltpu.VMEM((pooled, half), BF),
+            pltpu.VMEM((pooled, width), BF),
+            pltpu.VMEM((half, width), BF),
+            pltpu.VMEM((rows, width), F32),
+            pltpu.VMEM((half - rows, width), BF),
+            pltpu.SemaphoreType.DMA((12,)),
+        ],
+        flops=unit_flops, nbytes=6 * 2**20, vmem=60.5,
     )
     got = near_reduce(rest.reshape(-1, rows, width))
     (grad_images,) = local(finish_kernel, [((rows, width), F32, VMEM)], [scal, images, own] + got, smem=1)

time: 98.4 us -> 103 us (1.047)
  Pallas kernels: 17.2 us -> 20.6 us
    pallas_call x7, Pallas kernels: 17.2 us -> 20.6 us  [local(): pl.pallas_call(kernel, out_shape=tuple(((pltpu.HBM if spec is HBM else ja...]
    slice x1, local copies, waits for them, and re-layouts: 0.06 us -> 1.31 us  [near_reduce(): up, down = (shifted(rest[1], 'z', 1), shifted(rest[5], 'z', -1))]
  transfers between devices with their start and end apart: 18 -> 18, of which waited for: 10 -> 10; matrix products, arithmetic and copies ran while one was open for 0% -> 2% of each run, Pallas kernels for 2% -> 7%
where the time goes in v18:
time: 103 us; the launch traced here: 102 us
  starting transfers between devices  46.1 us (45%)
  waiting for transfers between devices  29.7 us (29%)
  Pallas kernels  20.6 us (20%)
  local copies, waits for them, and re-layouts  2.38 us (2%)
  between operations  2.25 us (2%)
  other arithmetic  1.14 us (1%)
    ppermute x16, starting transfers between devices, shifted(): lax.ppermute(block, axis, [(i, (i + distance) % n) for i in range(n)])  32.1 us
    ppermute x16, waiting for transfers between devices, shifted(): lax.ppermute(block, axis, [(i, (i + distance) % n) for i in range(n)])  28.7 us
    pallas_call x7, Pallas kernels, local(): pl.pallas_call(kernel, out_shape=tuple(((pltpu.HBM if spec is HBM else ja...  20.6 us
    all_to_all x1, starting transfers between devices, on_device(): ts = lax.all_to_all(spread, PLANE, 0, 0, tiled=True).reshape(pooled, width)  7.54 us
    all_to_all x1, starting transfers between devices, on_device(): lax.all_to_all(dy.reshape(n_plane, rows, width), PLANE, 0, 0, tiled=True)  6.48 us
  transfers between devices with their start and end apart: 18, of which 10 were waited for; matrix products, arithmetic and copies ran while one was open for 2% of the time, Pallas kernels for 7%

profile of v18, /device:TPU:8, one launch (start us, length us, event | category | flops | bytes accessed | tf_op | source)
XLA Modules:
  0.0 102.2 jit_solution(14031603723998924460)
XLA Ops:
  0.6 2.9 %shard_map.59 = bf16[16,64,1152]{2,1,0:T(8,128)(2,1)} custom-call(f32[64,1152]{1,0:T(8,128)} %raw.2), custom_call_target="tpu_custom_call" | custom-call | bytes 1048576 | tf_op jit(solution)/shard_map/pallas_call | solution.py:179
  3.6 7.5 %all-to-all-start = ((bf16[16,64,1152]{2,1,0:T(8,128)(2,1)}), bf16[16,64,1152]{2,1,0:T(8,128)(2,1)S(1)}, u32[]{:S(2)}, u32[]{:S(2)}) async-start(bf16[16,64,1152]{2,1,0:T(8,128)(2,1)} %shard_map.59), calls=%async_computation | async-start | bytes 4718592 | tf_op jit(solution)/shard_map/all_to_all | solution.py:226
  11.3 2.0 %collective-permute-start.4 = (bf16[64,1152]{1,0:T(8,128)(2,1)S(1)}, bf16[64,1152]{1,0:T(8,128)(2,1)S(1)}, u32[]{:S(2)}, u32[]{:S(2)}) collective-permute-start(bf16[64,1152]{1,0:T(8,128)(2,1)S(1)} %shard_map.60.refs_0_), channel_id=1, source_target_pairs={{0,1},{1,2},{2,3},{3,4},{4,5},{5,6},{6,7},{7,0},{8,9},{9,10},{10,1... | collective-permute-start | bytes 442376 | tf_op jit(solution)/shard_map/ppermute | solution.py:20
  13.3 4.0 %collective-permute-start = (bf16[64,1152]{1,0:T(8,128)(2,1)S(1)}, bf16[64,1152]{1,0:T(8,128)(2,1)S(1)}, u32[]{:S(2)}, u32[]{:S(2)}) collective-permute-start(bf16[64,1152]{1,0:T(8,128)(2,1)S(1)} %shard_map.60.refs_0_), channel_id=1, source_target_pairs={{0,7},{1,0},{2,1},{3,2},{4,3},{5,4},{6,5},{7,6},{8,15},{9,8},{10,9... | collective-permute-start | bytes 442376 | tf_op jit(solution)/shard_map/ppermute | solution.py:20
  17.3 3.2 %collective-permute-done.4.refs_7_ = bf16[64,1152]{1,0:T(8,128)(2,1)S(1)} collective-permute-done((bf16[64,1152]{1,0:T(8,128)(2,1)S(1)}, bf16[64,1152]{1,0:T(8,128)(2,1)S(1)}, u32[]{:S(2)}, u32[]{:S(2)}) %collective-permute-start.4) | collective-permute-done | bytes 147488 | tf_op jit(solution)/shard_map/ppermute | solution.py:20
  20.6 3.2 %collective-permute-start.1 = (bf16[64,1152]{1,0:T(8,128)(2,1)S(1)}, bf16[64,1152]{1,0:T(8,128)(2,1)S(1)}, u32[]{:S(2)}, u32[]{:S(2)}) collective-permute-start(bf16[64,1152]{1,0:T(8,128)(2,1)S(1)} %collective-permute-done.refs_1_), channel_id=1, source_target_pairs={{0,7},{1,0},{2,1},{3,2},{4,3},{5,4},{6,5},{7,6},{8,15},{9,8},{10,9... | collective-permute-start | bytes 442376 | tf_op jit(solution)/shard_map/ppermute | solution.py:20
  23.8 4.4 %collective-permute-start.3 = (bf16[64,1152]{1,0:T(8,128)(2,1)S(1)}, bf16[64,1152]{1,0:T(8,128)(2,1)S(1)}, u32[]{:S(2)}, u32[]{:S(2)}) collective-permute-start(bf16[64,1152]{1,0:T(8,128)(2,1)S(1)} %shard_map.60.refs_0_), channel_id=1, source_target_pairs={{0,4},{1,5},{2,6},{3,7},{4,0},{5,1},{6,2},{7,3},{8,12},{9,13},{10,... | collective-permute-start | bytes 442376 | tf_op jit(solution)/shard_map/ppermute | solution.py:20
  28.4 4.9 %collective-permute-done.1.refs_2_ = bf16[64,1152]{1,0:T(8,128)(2,1)S(1)} collective-permute-done((bf16[64,1152]{1,0:T(8,128)(2,1)S(1)}, bf16[64,1152]{1,0:T(8,128)(2,1)S(1)}, u32[]{:S(2)}, u32[]{:S(2)}) %collective-permute-start.1) | collective-permute-done | bytes 147488 | tf_op jit(solution)/shard_map/ppermute | solution.py:20
  33.3 3.8 %collective-permute-start.2 = (bf16[64,1152]{1,0:T(8,128)(2,1)S(1)}, bf16[64,1152]{1,0:T(8,128)(2,1)S(1)}, u32[]{:S(2)}, u32[]{:S(2)}) collective-permute-start(bf16[64,1152]{1,0:T(8,128)(2,1)S(1)} %collective-permute-done.1.refs_2_), channel_id=1, source_target_pairs={{0,7},{1,0},{2,1},{3,2},{4,3},{5,4},{6,5},{7,6},{8,15},{9,8},{10,9... | collective-permute-start | bytes 442376 | tf_op jit(solution)/shard_map/ppermute | solution.py:20
  37.1 2.7 %collective-permute-done.2.refs_3_ = bf16[64,1152]{1,0:T(8,128)(2,1)S(1)} collective-permute-done((bf16[64,1152]{1,0:T(8,128)(2,1)S(1)}, bf16[64,1152]{1,0:T(8,128)(2,1)S(1)}, u32[]{:S(2)}, u32[]{:S(2)}) %collective-permute-start.2) | collective-permute-done | bytes 147488 | tf_op jit(solution)/shard_map/ppermute | solution.py:20
  41.6 1.5 %collective-permute-done.7.xo = bf16[512,1152]{1,0:T(8,128)(2,1)} collective-permute-done((bf16[512,1152]{1,0:T(8,128)(2,1)S(1)}, bf16[512,1152]{1,0:T(8,128)(2,1)}, u32[]{:S(2)}, u32[]{:S(2)}) %collective-permute-start.7) | collective-permute-done | bytes 1179680 | tf_op jit(solution)/shard_map/ppermute | solution.py:20
  44.1 9.4 %shard_map.62 = (bf16[1024,512]{1,0:T(8,128)(2,1)}, bf16[1024,1152]{1,0:T(8,128)(2,1)}, bf16[512,1152]{1,0:T(8,128)(2,1)}, bf16[1024,1152]{1,0:T(8,128)(2,1)}) custom-call(s32[1]{0:T(128)} %bitcast.place, f32[2]{0:T(128)S(1)} %pad_maximum_fusion.scal, bf16[512,1152]{1,0:T(8,128)(2,1)S(1)} %shard_map.61.xs, bf16[512,1152]{1,0:T(8,128)(2,1)} %collective-permute-done.7.xo, ...), custom_call_target="tpu_custom_call" | custom-call | flops 6039797760 | bytes 9437184 | tf_op jit(solution)/shard_map/pallas_call | solution.py:179
  53.6 6.5 %all-to-all-start.1 = ((bf16[16,64,1152]{2,1,0:T(8,128)(2,1)}), bf16[16,64,1152]{2,1,0:T(8,128)(2,1)S(1)}, u32[]{:S(2)}, u32[]{:S(2)}) async-start(bf16[16,64,1152]{2,1,0:T(8,128)(2,1)} %bitcast.4), calls=%async_computation.1 | async-start | bytes 4718592 | tf_op jit(solution)/shard_map/all_to_all | solution.py:249
  61.1 4.8 %shard_map.63 = (f32[64,1152]{1,0:T(8,128)}, bf16[448,1152]{1,0:T(8,128)(2,1)}) custom-call(bf16[1024,512]{1,0:T(8,128)(2,1)} %get-tuple-element.12.coeff, bf16[1024,1152]{1,0:T(8,128)(2,1)} %get-tuple-element.13.kept, bf16[512,1152]{1,0:T(8,128)(2,1)} %copy-done.4), custom_call_target="tpu_custom_call" | custom-call | flops 1207959552 | bytes 6291456 | tf_op jit(solution)/shard_map/pallas_call | solution.py:179
  66.0 1.3 %fusion = (bf16[64,1152]{1,0:T(8,128)(2,1)S(1)}, bf16[64,1152]{1,0:T(8,128)(2,1)S(1)}, bf16[64,1152]{1,0:T(8,128)(2,1)S(1)}, bf16[64,1152]{1,0:T(8,128)(2,1)S(1)}, bf16[64,1152]{1,0:T(8,128)(2,1)S(1)}) fusion(bf16[448,1152]{1,0:T(8,128)(2,1)} %get-tuple-element.16), kind=kLoop, calls=%fused_computation.3 | loop fusion | bytes 1474560 | tf_op jit(solution)/shard_map/slice | solution.py:206
  67.3 4.5 %collective-permute-start.14 = (bf16[64,1152]{1,0:T(8,128)(2,1)S(1)}, bf16[64,1152]{1,0:T(8,128)(2,1)S(1)}, u32[]{:S(2)}, u32[]{:S(2)}) collective-permute-start(bf16[64,1152]{1,0:T(8,128)(2,1)S(1)} %get-tuple-element.20), channel_id=1, source_target_pairs={{0,7},{1,0},{2,1},{3,2},{4,3},{5,4},{6,5},{7,6},{8,15},{9,8},{10,9... | collective-permute-start | bytes 442376 | tf_op jit(solution)/shard_map/ppermute | solution.py:20
  71.7 2.9 %collective-permute-start.11 = (bf16[64,1152]{1,0:T(8,128)(2,1)S(1)}, bf16[64,1152]{1,0:T(8,128)(2,1)S(1)}, u32[]{:S(2)}, u32[]{:S(2)}) collective-permute-start(bf16[64,1152]{1,0:T(8,128)(2,1)S(1)} %get-tuple-element.22), channel_id=1, source_target_pairs={{0,5},{1,6},{2,7},{3,0},{4,1},{5,2},{6,3},{7,4},{8,13},{9,14},{10,... | collective-permute-start | bytes 442376 | tf_op jit(solution)/shard_map/ppermute | solution.py:20
  75.6 3.4 %collective-permute-start.9 = (bf16[64,1152]{1,0:T(8,128)(2,1)S(1)}, bf16[64,1152]{1,0:T(8,128)(2,1)S(1)}, u32[]{:S(2)}, u32[]{:S(2)}) collective-permute-start(bf16[64,1152]{1,0:T(8,128)(2,1)S(1)} %get-tuple-element.24), channel_id=1, source_target_pairs={{0,4},{1,5},{2,6},{3,7},{4,0},{5,1},{6,2},{7,3},{8,12},{9,13},{10,... | collective-permute-start | bytes 442376 | tf_op jit(solution)/shard_map/ppermute | solution.py:20
  80.0 2.6 %collective-permute-start.15 = (bf16[64,1152]{1,0:T(8,128)(2,1)S(1)}, bf16[64,1152]{1,0:T(8,128)(2,1)S(1)}, u32[]{:S(2)}, u32[]{:S(2)}) collective-permute-start(bf16[64,1152]{1,0:T(8,128)(2,1)S(1)} %get-tuple-element.18), channel_id=1, source_target_pairs={{0,7},{1,0},{2,1},{3,2},{4,3},{5,4},{6,5},{7,6},{8,15},{9,8},{10,9... | collective-permute-start | bytes 442376 | tf_op jit(solution)/shard_map/ppermute | solution.py:20
  82.6 9.0 %collective-permute-done.11.refs_3_ = bf16[64,1152]{1,0:T(8,128)(2,1)S(1)} collective-permute-done((bf16[64,1152]{1,0:T(8,128)(2,1)S(1)}, bf16[64,1152]{1,0:T(8,128)(2,1)S(1)}, u32[]{:S(2)}, u32[]{:S(2)}) %collective-permute-start.11) | collective-permute-done | bytes 147488 | tf_op jit(solution)/shard_map/ppermute | solution.py:20
  92.5 2.3 %collective-permute-done.15.refs_5_ = bf16[64,1152]{1,0:T(8,128)(2,1)S(1)} collective-permute-done((bf16[64,1152]{1,0:T(8,128)(2,1)S(1)}, bf16[64,1152]{1,0:T(8,128)(2,1)S(1)}, u32[]{:S(2)}, u32[]{:S(2)}) %collective-permute-start.15) | collective-permute-done | bytes 147488 | tf_op jit(solution)/shard_map/ppermute | solution.py:20
  94.8 4.0 %collective-permute-done.13.refs_4_ = bf16[64,1152]{1,0:T(8,128)(2,1)S(1)} collective-permute-done((bf16[64,1152]{1,0:T(8,128)(2,1)S(1)}, bf16[64,1152]{1,0:T(8,128)(2,1)S(1)}, u32[]{:S(2)}, u32[]{:S(2)}) %collective-permute-start.13) | collective-permute-done | bytes 147488 | tf_op jit(solution)/shard_map/ppermute | solution.py:20
  98.8 1.5 %shard_map.64 = f32[64,1152]{1,0:T(8,128)} custom-call(f32[2]{0:T(128)S(1)} %pad_maximum_fusion.scal, f32[64,1152]{1,0:T(8,128)S(1)} %copy-done.2, f32[64,1152]{1,0:T(8,128)S(1)} %copy-done.3, bf16[64,1152]{1,0:T(8,128)(2,1)S(1)} %collective-permute-done.9.refs_1_, bf16[64,1152]{1,0:T(8,128)(2,1)S(1)} %collective-permute-done.10.refs_2_, ...), custom_call_target="tpu_custom_call" | custom-call | bytes 1048576 | tf_op jit(solution)/shard_map/pallas_call | solution.py:179
  100.3 1.7 %shard_map.65 = f32[64,1152]{1,0:T(8,128)} custom-call(f32[2]{0:T(128)S(1)} %pad_maximum_fusion.scal, f32[64,1152]{1,0:T(8,128)S(1)} %copy-done, bf16[16,64,1152]{2,1,0:T(8,128)(2,1)S(1)} %all-to-all-done.1.got), custom_call_target="tpu_custom_call" | custom-call | bytes 1048576 | tf_op jit(solution)/shard_map/pallas_call | solution.py:179
  (32 shorter events, 5.9 us)
Async XLA Ops:
  3.6 7.5 %copy-start.1 = (f32[64,1152]{1,0:T(8,128)S(1)}, f32[64,1152]{1,0:T(8,128)}, u32[]{:S(2)}) copy-start(f32[64,1152]{1,0:T(8,128)} %raw.1) | copy-start | bytes 884740
  3.6 40.5 %all-to-all-start = ((bf16[16,64,1152]{2,1,0:T(8,128)(2,1)}), bf16[16,64,1152]{2,1,0:T(8,128)(2,1)S(1)}, u32[]{:S(2)}, u32[]{:S(2)}) async-start(bf16[16,64,1152]{2,1,0:T(8,128)(2,1)} %shard_map.59), calls=%async_computation | async-start | bytes 4718592 | tf_op jit(solution)/shard_map/all_to_all | solution.py:226
  11.3 9.2 %collective-permute-start.4 = (bf16[64,1152]{1,0:T(8,128)(2,1)S(1)}, bf16[64,1152]{1,0:T(8,128)(2,1)S(1)}, u32[]{:S(2)}, u32[]{:S(2)}) collective-permute-start(bf16[64,1152]{1,0:T(8,128)(2,1)S(1)} %shard_map.60.refs_0_), channel_id=1, source_target_pairs={{0,1},{1,2},{2,3},{3,4},{4,5},{5,6},{6,7},{7,0},{8,9},{9,10},{10,1... | collective-permute-start | bytes 442376 | tf_op jit(solution)/shard_map/ppermute | solution.py:20
  13.3 7.2 %collective-permute-start = (bf16[64,1152]{1,0:T(8,128)(2,1)S(1)}, bf16[64,1152]{1,0:T(8,128)(2,1)S(1)}, u32[]{:S(2)}, u32[]{:S(2)}) collective-permute-start(bf16[64,1152]{1,0:T(8,128)(2,1)S(1)} %shard_map.60.refs_0_), channel_id=1, source_target_pairs={{0,7},{1,0},{2,1},{3,2},{4,3},{5,4},{6,5},{7,6},{8,15},{9,8},{10,9... | collective-permute-start | bytes 442376 | tf_op jit(solution)/shard_map/ppermute | solution.py:20
  20.5 7.9 %collective-permute-start.5 = (bf16[64,1152]{1,0:T(8,128)(2,1)S(1)}, bf16[64,1152]{1,0:T(8,128)(2,1)S(1)}, u32[]{:S(2)}, u32[]{:S(2)}) collective-permute-start(bf16[64,1152]{1,0:T(8,128)(2,1)S(1)} %collective-permute-done.4.refs_7_), channel_id=1, source_target_pairs={{0,1},{1,2},{2,3},{3,4},{4,5},{5,6},{6,7},{7,0},{8,9},{9,10},{10,1... | collective-permute-start | bytes 442376 | tf_op jit(solution)/shard_map/ppermute | solution.py:20
  20.6 12.7 %collective-permute-start.1 = (bf16[64,1152]{1,0:T(8,128)(2,1)S(1)}, bf16[64,1152]{1,0:T(8,128)(2,1)S(1)}, u32[]{:S(2)}, u32[]{:S(2)}) collective-permute-start(bf16[64,1152]{1,0:T(8,128)(2,1)S(1)} %collective-permute-done.refs_1_), channel_id=1, source_target_pairs={{0,7},{1,0},{2,1},{3,2},{4,3},{5,4},{6,5},{7,6},{8,15},{9,8},{10,9... | collective-permute-start | bytes 442376 | tf_op jit(solution)/shard_map/ppermute | solution.py:20
  23.8 13.3 %collective-permute-start.3 = (bf16[64,1152]{1,0:T(8,128)(2,1)S(1)}, bf16[64,1152]{1,0:T(8,128)(2,1)S(1)}, u32[]{:S(2)}, u32[]{:S(2)}) collective-permute-start(bf16[64,1152]{1,0:T(8,128)(2,1)S(1)} %shard_map.60.refs_0_), channel_id=1, source_target_pairs={{0,4},{1,5},{2,6},{3,7},{4,0},{5,1},{6,2},{7,3},{8,12},{9,13},{10,... | collective-permute-start | bytes 442376 | tf_op jit(solution)/shard_map/ppermute | solution.py:20
  28.4 8.7 %collective-permute-start.6 = (bf16[64,1152]{1,0:T(8,128)(2,1)S(1)}, bf16[64,1152]{1,0:T(8,128)(2,1)S(1)}, u32[]{:S(2)}, u32[]{:S(2)}) collective-permute-start(bf16[64,1152]{1,0:T(8,128)(2,1)S(1)} %collective-permute-done.5.refs_6_), channel_id=1, source_target_pairs={{0,1},{1,2},{2,3},{3,4},{4,5},{5,6},{6,7},{7,0},{8,9},{9,10},{10,1... | collective-permute-start | bytes 442376 | tf_op jit(solution)/shard_map/ppermute | solution.py:20
  33.3 6.5 %collective-permute-start.2 = (bf16[64,1152]{1,0:T(8,128)(2,1)S(1)}, bf16[64,1152]{1,0:T(8,128)(2,1)S(1)}, u32[]{:S(2)}, u32[]{:S(2)}) collective-permute-start(bf16[64,1152]{1,0:T(8,128)(2,1)S(1)} %collective-permute-done.1.refs_2_), channel_id=1, source_target_pairs={{0,7},{1,0},{2,1},{3,2},{4,3},{5,4},{6,5},{7,6},{8,15},{9,8},{10,9... | collective-permute-start | bytes 442376 | tf_op jit(solution)/shard_map/ppermute | solution.py:20
  39.9 3.2 %collective-permute-start.7 = (bf16[512,1152]{1,0:T(8,128)(2,1)S(1)}, bf16[512,1152]{1,0:T(8,128)(2,1)}, u32[]{:S(2)}, u32[]{:S(2)}) collective-permute-start(bf16[512,1152]{1,0:T(8,128)(2,1)S(1)} %shard_map.61.xs), channel_id=1, source_target_pairs={{0,16},{16,0},{1,17},{17,1},{2,18},{18,2},{3,19},{19,3},{4,20},{20... | collective-permute-start | bytes 3538952 | tf_op jit(solution)/shard_map/ppermute | solution.py:20
  53.5 6.6 %collective-permute-start.8 = (bf16[512,1152]{1,0:T(8,128)(2,1)}, bf16[512,1152]{1,0:T(8,128)(2,1)S(1)}, u32[]{:S(2)}, u32[]{:S(2)}) collective-permute-start(bf16[512,1152]{1,0:T(8,128)(2,1)} %get-tuple-element.14), channel_id=1, source_target_pairs={{0,16},{16,0},{1,17},{17,1},{2,18},{18,2},{3,19},{19,3},{4,20},{20... | collective-permute-start | bytes 3538952 | tf_op jit(solution)/shard_map/ppermute | solution.py:20
  53.6 46.8 %all-to-all-start.1 = ((bf16[16,64,1152]{2,1,0:T(8,128)(2,1)}), bf16[16,64,1152]{2,1,0:T(8,128)(2,1)S(1)}, u32[]{:S(2)}, u32[]{:S(2)}) async-start(bf16[16,64,1152]{2,1,0:T(8,128)(2,1)} %bitcast.4), calls=%async_computation.1 | async-start | bytes 4718592 | tf_op jit(solution)/shard_map/all_to_all | solution.py:249
  60.1 1.1 %copy-start.4 = (bf16[512,1152]{1,0:T(8,128)(2,1)}, bf16[512,1152]{1,0:T(8,128)(2,1)S(1)}, u32[]{:S(2)}) copy-start(bf16[512,1152]{1,0:T(8,128)(2,1)S(1)} %collective-permute-done.8.other) | copy-start | bytes 3538948
  61.1 37.7 %copy-start.2 = (f32[64,1152]{1,0:T(8,128)S(1)}, f32[64,1152]{1,0:T(8,128)}, u32[]{:S(2)}) copy-start(f32[64,1152]{1,0:T(8,128)} %raw.1) | copy-start | bytes 884740
  66.0 32.9 %copy-start.3 = (f32[64,1152]{1,0:T(8,128)S(1)}, f32[64,1152]{1,0:T(8,128)}, u32[]{:S(2)}) copy-start(f32[64,1152]{1,0:T(8,128)} %get-tuple-element.15.refs_0_) | copy-start | bytes 884740
  66.0 34.4 %copy-start = (f32[64,1152]{1,0:T(8,128)S(1)}, f32[64,1152]{1,0:T(8,128)}, u32[]{:S(2)}) copy-start(f32[64,1152]{1,0:T(8,128)} %raw.2) | copy-start | bytes 884740
  67.3 11.6 %collective-permute-start.14 = (bf16[64,1152]{1,0:T(8,128)(2,1)S(1)}, bf16[64,1152]{1,0:T(8,128)(2,1)S(1)}, u32[]{:S(2)}, u32[]{:S(2)}) collective-permute-start(bf16[64,1152]{1,0:T(8,128)(2,1)S(1)} %get-tuple-element.20), channel_id=1, source_target_pairs={{0,7},{1,0},{2,1},{3,2},{4,3},{5,4},{6,5},{7,6},{8,15},{9,8},{10,9... | collective-permute-start | bytes 442376 | tf_op jit(solution)/shard_map/ppermute | solution.py:20
  71.7 7.2 %collective-permute-start.12 = (bf16[64,1152]{1,0:T(8,128)(2,1)S(1)}, bf16[64,1152]{1,0:T(8,128)(2,1)S(1)}, u32[]{:S(2)}, u32[]{:S(2)}) collective-permute-start(bf16[64,1152]{1,0:T(8,128)(2,1)S(1)} %get-tuple-element.21), channel_id=1, source_target_pairs={{0,1},{1,2},{2,3},{3,4},{4,5},{5,6},{6,7},{7,0},{8,9},{9,10},{10,1... | collective-permute-start | bytes 442376 | tf_op jit(solution)/shard_map/ppermute | solution.py:20
  71.7 19.9 %collective-permute-start.11 = (bf16[64,1152]{1,0:T(8,128)(2,1)S(1)}, bf16[64,1152]{1,0:T(8,128)(2,1)S(1)}, u32[]{:S(2)}, u32[]{:S(2)}) collective-permute-start(bf16[64,1152]{1,0:T(8,128)(2,1)S(1)} %get-tuple-element.22), channel_id=1, source_target_pairs={{0,5},{1,6},{2,7},{3,0},{4,1},{5,2},{6,3},{7,4},{8,13},{9,14},{10,... | collective-permute-start | bytes 442376 | tf_op jit(solution)/shard_map/ppermute | solution.py:20
  74.6 17.0 %collective-permute-start.10 = (bf16[64,1152]{1,0:T(8,128)(2,1)S(1)}, bf16[64,1152]{1,0:T(8,128)(2,1)S(1)}, u32[]{:S(2)}, u32[]{:S(2)}) collective-permute-start(bf16[64,1152]{1,0:T(8,128)(2,1)S(1)} %get-tuple-element.23), channel_id=1, source_target_pairs={{0,3},{1,4},{2,5},{3,6},{4,7},{5,0},{6,1},{7,2},{8,11},{9,12},{10,... | collective-permute-start | bytes 442376 | tf_op jit(solution)/shard_map/ppermute | solution.py:20
  75.6 17.0 %collective-permute-start.9 = (bf16[64,1152]{1,0:T(8,128)(2,1)S(1)}, bf16[64,1152]{1,0:T(8,128)(2,1)S(1)}, u32[]{:S(2)}, u32[]{:S(2)}) collective-permute-start(bf16[64,1152]{1,0:T(8,128)(2,1)S(1)} %get-tuple-element.24), channel_id=1, source_target_pairs={{0,4},{1,5},{2,6},{3,7},{4,0},{5,1},{6,2},{7,3},{8,12},{9,13},{10,... | collective-permute-start | bytes 442376 | tf_op jit(solution)/shard_map/ppermute | solution.py:20
  80.0 14.8 %collective-permute-start.15 = (bf16[64,1152]{1,0:T(8,128)(2,1)S(1)}, bf16[64,1152]{1,0:T(8,128)(2,1)S(1)}, u32[]{:S(2)}, u32[]{:S(2)}) collective-permute-start(bf16[64,1152]{1,0:T(8,128)(2,1)S(1)} %get-tuple-element.18), channel_id=1, source_target_pairs={{0,7},{1,0},{2,1},{3,2},{4,3},{5,4},{6,5},{7,6},{8,15},{9,8},{10,9... | collective-permute-start | bytes 442376 | tf_op jit(solution)/shard_map/ppermute | solution.py:20
  82.6 16.2 %collective-permute-start.13 = (bf16[64,1152]{1,0:T(8,128)(2,1)S(1)}, bf16[64,1152]{1,0:T(8,128)(2,1)S(1)}, u32[]{:S(2)}, u32[]{:S(2)}) collective-permute-start(bf16[64,1152]{1,0:T(8,128)(2,1)S(1)} %get-tuple-element.19), channel_id=1, source_target_pairs={{0,1},{1,2},{2,3},{3,4},{4,5},{5,6},{6,7},{7,0},{8,9},{9,10},{10,1... | collective-permute-start | bytes 442376 | tf_op jit(solution)/shard_map/ppermute | solution.py:20

commit v19 on v14

--- a/solution.py
+++ b/solution.py
@@ -106,22 +106,6 @@
     rest[...] = (dxs[ROWS:] + other[ROWS:].astype(F32)).astype(BF)
 
 
-def finish_kernel(scal, raw, *refs):
-    total = refs[0][...].astype(F32)
-    for part in refs[1:-1]:
-        total += part[...].astype(F32)
-    unit, norm = to_unit(raw[...])
-    refs[-1][...] = from_unit(scal[0] * total, unit, norm)
-
-
-def finish_texts_kernel(scal, raw, got, out):
-    total = got[0].astype(F32)
-    for k in range(1, got.shape[0]):
-        total += got[k].astype(F32)
-    unit, norm = to_unit(raw[...])
-    out[...] = from_unit(scal[0] * total, unit, norm)
-
-
 VMEM = pl.BlockSpec(memory_space=pltpu.VMEM)
 SMEM = pl.BlockSpec(memory_space=pltpu.SMEM)
 HBM = pl.BlockSpec(memory_space=pltpu.HBM)
@@ -200,8 +184,11 @@
         nbytes=5 * 2**20, vmem=16,
     )
     got = near_reduce(rest.reshape(-1, rows, width))
-    (grad_images,) = local(finish_kernel, [((rows, width), F32, VMEM)], [scal, images, own] + got, smem=1)
-    (grad_texts,) = local(finish_texts_kernel, [((rows, width), F32, VMEM)], [scal, texts, dyr], smem=1)
+    for part in got:
+        own = own + part.astype(F32)
+    grad_images = from_unit(temp * own, *to_unit(images))
+    text_sum = jnp.sum(dyr.astype(F32), axis=0)
+    grad_texts = from_unit(temp * text_sum, *to_unit(texts))
     return (grad_images, grad_texts)
 
 

time: 98.3 us -> 101 us (1.027)
  other arithmetic: 0.15 us -> 4.53 us
  local copies, waits for them, and re-layouts: 2.69 us -> 1.03 us
  waiting for transfers between devices: 30.7 us -> 29.5 us
    ppermute x16, waiting for transfers between devices: 29.7 us -> 26.2 us  [shifted(): lax.ppermute(block, axis, [(i, (i + distance) % n) for i in range(n)])]
    all_to_all x1, waiting for transfers between devices: 0.01 us -> 3.36 us  [on_device(): lax.all_to_all(dy.reshape(n_plane, rows, width), PLANE, 0, 0, tiled=True)]
    reduce_sum x0 -> x5, other arithmetic: none -> 2.69 us  [the longest x1 2.01 us: on_device(): text_sum = jnp.sum(dyr.astype(F32), axis=0)]
    div x0 -> x2, other arithmetic: none -> 1.67 us  [from_unit(): return (grad - unit * jnp.sum(unit * grad, axis=1, keepdims=True)) / norm]
    unnamed x10 -> x8, local copies, waits for them, and re-layouts: 2.63 us -> 0.97 us
    all_to_all x1, waiting for transfers between devices: 1.03 us -> 0.01 us  [on_device(): ts = lax.all_to_all(spread, PLANE, 0, 0, tiled=True).reshape(pooled, width)]
    pallas_call x7 -> x5, Pallas kernels: 16.2 us -> 16.1 us  [local(): pl.pallas_call(kernel, out_shape=tuple(((pltpu.HBM if spec is HBM else ja...]
  transfers between devices with their start and end apart: 18 -> 18, of which waited for: 10 -> 11; matrix products, arithmetic and copies ran while one was open for 0% -> 2% of each run, Pallas kernels for 2% -> 3%
where the time goes in v19:
time: 101 us; the launch traced here: 100 us
  starting transfers between devices  47.1 us (47%)
  waiting for transfers between devices  29.5 us (29%)
  Pallas kernels  16.1 us (16%)
  other arithmetic  4.53 us (4%)
  between operations  2.08 us (2%)
  local copies, waits for them, and re-layouts  1.03 us (1%)
    ppermute x16, starting transfers between devices, shifted(): lax.ppermute(block, axis, [(i, (i + distance) % n) for i in range(n)])  32.2 us
    ppermute x16, waiting for transfers between devices, shifted(): lax.ppermute(block, axis, [(i, (i + distance) % n) for i in range(n)])  26.2 us
    pallas_call x5, Pallas kernels, local(): pl.pallas_call(kernel, out_shape=tuple(((pltpu.HBM if spec is HBM else ja...  16.1 us
    all_to_all x1, starting transfers between devices, on_device(): ts = lax.all_to_all(spread, PLANE, 0, 0, tiled=True).reshape(pooled, width)  7.54 us
    all_to_all x1, starting transfers between devices, on_device(): lax.all_to_all(dy.reshape(n_plane, rows, width), PLANE, 0, 0, tiled=True)  7.32 us
    all_to_all x1, waiting for transfers between devices, on_device(): lax.all_to_all(dy.reshape(n_plane, rows, width), PLANE, 0, 0, tiled=True)  3.36 us
  transfers between devices with their start and end apart: 18, of which 11 were waited for; matrix products, arithmetic and copies ran while one was open for 2% of the time, Pallas kernels for 3%

profile of v19, /device:TPU:8, one launch (start us, length us, event | category | flops | bytes accessed | tf_op | source)
XLA Modules:
  0.0 100.3 jit_solution(8720918554711717661)
XLA Ops:
  1.6 1.7 %shard_map.59 = bf16[16,64,1152]{2,1,0:T(8,128)(2,1)} custom-call(f32[64,1152]{1,0:T(8,128)S(1)} %copy-done.1), custom_call_target="tpu_custom_call" | custom-call | bytes 1048576 | tf_op jit(solution)/shard_map/pallas_call | solution.py:116
  3.3 7.5 %all-to-all-start = ((bf16[16,64,1152]{2,1,0:T(8,128)(2,1)}), bf16[16,64,1152]{2,1,0:T(8,128)(2,1)S(1)}, u32[]{:S(2)}, u32[]{:S(2)}) async-start(bf16[16,64,1152]{2,1,0:T(8,128)(2,1)} %shard_map.59), calls=%async_computation | async-start | bytes 4718592 | tf_op jit(solution)/shard_map/all_to_all | solution.py:159
  11.0 5.9 %collective-permute-start = (bf16[64,1152]{1,0:T(8,128)(2,1)S(1)}, bf16[64,1152]{1,0:T(8,128)(2,1)S(1)}, u32[]{:S(2)}, u32[]{:S(2)}) collective-permute-start(bf16[64,1152]{1,0:T(8,128)(2,1)S(1)} %shard_map.60.refs_0_), channel_id=1, source_target_pairs={{0,7},{1,0},{2,1},{3,2},{4,3},{5,4},{6,5},{7,6},{8,15},{9,8},{10,9... | collective-permute-start | bytes 442376 | tf_op jit(solution)/shard_map/ppermute | solution.py:20
  16.9 2.7 %collective-permute-done.refs_1_ = bf16[64,1152]{1,0:T(8,128)(2,1)S(1)} collective-permute-done((bf16[64,1152]{1,0:T(8,128)(2,1)S(1)}, bf16[64,1152]{1,0:T(8,128)(2,1)S(1)}, u32[]{:S(2)}, u32[]{:S(2)}) %collective-permute-start) | collective-permute-done | bytes 147488 | tf_op jit(solution)/shard_map/ppermute | solution.py:20
  19.6 3.7 %collective-permute-start.1 = (bf16[64,1152]{1,0:T(8,128)(2,1)S(1)}, bf16[64,1152]{1,0:T(8,128)(2,1)S(1)}, u32[]{:S(2)}, u32[]{:S(2)}) collective-permute-start(bf16[64,1152]{1,0:T(8,128)(2,1)S(1)} %collective-permute-done.refs_1_), channel_id=1, source_target_pairs={{0,7},{1,0},{2,1},{3,2},{4,3},{5,4},{6,5},{7,6},{8,15},{9,8},{10,9... | collective-permute-start | bytes 442376 | tf_op jit(solution)/shard_map/ppermute | solution.py:20
  23.3 2.1 %collective-permute-start.3 = (bf16[64,1152]{1,0:T(8,128)(2,1)S(1)}, bf16[64,1152]{1,0:T(8,128)(2,1)S(1)}, u32[]{:S(2)}, u32[]{:S(2)}) collective-permute-start(bf16[64,1152]{1,0:T(8,128)(2,1)S(1)} %shard_map.60.refs_0_), channel_id=1, source_target_pairs={{0,4},{1,5},{2,6},{3,7},{4,0},{5,1},{6,2},{7,3},{8,12},{9,13},{10,... | collective-permute-start | bytes 442376 | tf_op jit(solution)/shard_map/ppermute | solution.py:20
  25.4 1.6 %collective-permute-done.1.refs_2_ = bf16[64,1152]{1,0:T(8,128)(2,1)S(1)} collective-permute-done((bf16[64,1152]{1,0:T(8,128)(2,1)S(1)}, bf16[64,1152]{1,0:T(8,128)(2,1)S(1)}, u32[]{:S(2)}, u32[]{:S(2)}) %collective-permute-start.1) | collective-permute-done | bytes 147488 | tf_op jit(solution)/shard_map/ppermute | solution.py:20
  27.0 3.7 %collective-permute-start.2 = (bf16[64,1152]{1,0:T(8,128)(2,1)S(1)}, bf16[64,1152]{1,0:T(8,128)(2,1)S(1)}, u32[]{:S(2)}, u32[]{:S(2)}) collective-permute-start(bf16[64,1152]{1,0:T(8,128)(2,1)S(1)} %collective-permute-done.1.refs_2_), channel_id=1, source_target_pairs={{0,7},{1,0},{2,1},{3,2},{4,3},{5,4},{6,5},{7,6},{8,15},{9,8},{10,9... | collective-permute-start | bytes 442376 | tf_op jit(solution)/shard_map/ppermute | solution.py:20
  30.7 3.2 %collective-permute-done.5.refs_6_ = bf16[64,1152]{1,0:T(8,128)(2,1)S(1)} collective-permute-done((bf16[64,1152]{1,0:T(8,128)(2,1)S(1)}, bf16[64,1152]{1,0:T(8,128)(2,1)S(1)}, u32[]{:S(2)}, u32[]{:S(2)}) %collective-permute-start.5) | collective-permute-done | bytes 147488 | tf_op jit(solution)/shard_map/ppermute | solution.py:20
  33.9 2.2 %collective-permute-done.3.refs_4_ = bf16[64,1152]{1,0:T(8,128)(2,1)S(1)} collective-permute-done((bf16[64,1152]{1,0:T(8,128)(2,1)S(1)}, bf16[64,1152]{1,0:T(8,128)(2,1)S(1)}, u32[]{:S(2)}, u32[]{:S(2)}) %collective-permute-start.3) | collective-permute-done | bytes 147488 | tf_op jit(solution)/shard_map/ppermute | solution.py:20
  36.1 4.1 %collective-permute-done.6.refs_5_ = bf16[64,1152]{1,0:T(8,128)(2,1)S(1)} collective-permute-done((bf16[64,1152]{1,0:T(8,128)(2,1)S(1)}, bf16[64,1152]{1,0:T(8,128)(2,1)S(1)}, u32[]{:S(2)}, u32[]{:S(2)}) %collective-permute-start.6) | collective-permute-done | bytes 147488 | tf_op jit(solution)/shard_map/ppermute | solution.py:20
  42.8 1.8 %collective-permute-done.7.xo = bf16[512,1152]{1,0:T(8,128)(2,1)} collective-permute-done((bf16[512,1152]{1,0:T(8,128)(2,1)}, bf16[512,1152]{1,0:T(8,128)(2,1)}, u32[]{:S(2)}, u32[]{:S(2)}) %collective-permute-start.7) | collective-permute-done | bytes 1179680 | tf_op jit(solution)/shard_map/ppermute | solution.py:20
  44.5 11.7 %shard_map.62 = (f32[512,1152]{1,0:T(8,128)}, bf16[512,1152]{1,0:T(8,128)(2,1)}, bf16[1024,1152]{1,0:T(8,128)(2,1)}) custom-call(s32[1]{0:T(128)} %bitcast.1.place, f32[2]{0:T(128)S(1)} %pad_maximum_fusion.scal, bf16[512,1152]{1,0:T(8,128)(2,1)} %shard_map.61.xs, bf16[512,1152]{1,0:T(8,128)(2,1)} %collective-permute-done.7.xo, bf16[1024,1152]{1,0:T(8,128)(2,1)S(1)} %bitcast.4), custom_call_target="tpu_custom_call" | custom-call | flops 7247757312 | bytes 9437184 | tf_op jit(solution)/shard_map/pallas_call | solution.py:116
  56.6 7.3 %all-to-all-start.1 = ((bf16[16,64,1152]{2,1,0:T(8,128)(2,1)}), bf16[16,64,1152]{2,1,0:T(8,128)(2,1)}, u32[]{:S(2)}, u32[]{:S(2)}) async-start(bf16[16,64,1152]{2,1,0:T(8,128)(2,1)} %bitcast.5), calls=%async_computation.1 | async-start | bytes 4718592 | tf_op jit(solution)/shard_map/all_to_all | solution.py:180
  65.5 3.5 %collective-permute-start.14 = (bf16[64,1152]{1,0:T(8,128)(2,1)S(1)}, bf16[64,1152]{1,0:T(8,128)(2,1)S(1)}, u32[]{:S(2)}, u32[]{:S(2)}) collective-permute-start(bf16[64,1152]{1,0:T(8,128)(2,1)S(1)} %get-tuple-element.19), channel_id=1, source_target_pairs={{0,7},{1,0},{2,1},{3,2},{4,3},{5,4},{6,5},{7,6},{8,15},{9,8},{10,9... | collective-permute-start | bytes 442376 | tf_op jit(solution)/shard_map/ppermute | solution.py:20
  69.2 1.9 %collective-permute-start.10 = (bf16[64,1152]{1,0:T(8,128)(2,1)S(1)}, bf16[64,1152]{1,0:T(8,128)(2,1)S(1)}, u32[]{:S(2)}, u32[]{:S(2)}) collective-permute-start(bf16[64,1152]{1,0:T(8,128)(2,1)S(1)} %get-tuple-element.22), channel_id=1, source_target_pairs={{0,3},{1,4},{2,5},{3,6},{4,7},{5,0},{6,1},{7,2},{8,11},{9,12},{10,... | collective-permute-start | bytes 442376 | tf_op jit(solution)/shard_map/ppermute | solution.py:20
  71.1 3.2 %collective-permute-start.11 = (bf16[64,1152]{1,0:T(8,128)(2,1)S(1)}, bf16[64,1152]{1,0:T(8,128)(2,1)S(1)}, u32[]{:S(2)}, u32[]{:S(2)}) collective-permute-start(bf16[64,1152]{1,0:T(8,128)(2,1)S(1)} %get-tuple-element.21), channel_id=1, source_target_pairs={{0,5},{1,6},{2,7},{3,0},{4,1},{5,2},{6,3},{7,4},{8,13},{9,14},{10,... | collective-permute-start | bytes 442376 | tf_op jit(solution)/shard_map/ppermute | solution.py:20
  74.3 4.5 %collective-permute-start.9 = (bf16[64,1152]{1,0:T(8,128)(2,1)S(1)}, bf16[64,1152]{1,0:T(8,128)(2,1)S(1)}, u32[]{:S(2)}, u32[]{:S(2)}) collective-permute-start(bf16[64,1152]{1,0:T(8,128)(2,1)S(1)} %get-tuple-element.18), channel_id=1, source_target_pairs={{0,4},{1,5},{2,6},{3,7},{4,0},{5,1},{6,2},{7,3},{8,12},{9,13},{10,... | collective-permute-start | bytes 442376 | tf_op jit(solution)/shard_map/ppermute | solution.py:20
  79.0 3.2 %collective-permute-start.15 = (bf16[64,1152]{1,0:T(8,128)(2,1)S(1)}, bf16[64,1152]{1,0:T(8,128)(2,1)S(1)}, u32[]{:S(2)}, u32[]{:S(2)}) collective-permute-start(bf16[64,1152]{1,0:T(8,128)(2,1)S(1)} %get-tuple-element.24), channel_id=1, source_target_pairs={{0,7},{1,0},{2,1},{3,2},{4,3},{5,4},{6,5},{7,6},{8,15},{9,8},{10,9... | collective-permute-start | bytes 442376 | tf_op jit(solution)/shard_map/ppermute | solution.py:20
  82.2 5.3 %collective-permute-done.10 = bf16[64,1152]{1,0:T(8,128)(2,1)S(1)} collective-permute-done((bf16[64,1152]{1,0:T(8,128)(2,1)S(1)}, bf16[64,1152]{1,0:T(8,128)(2,1)S(1)}, u32[]{:S(2)}, u32[]{:S(2)}) %collective-permute-start.10) | collective-permute-done | bytes 147488 | tf_op jit(solution)/shard_map/ppermute | solution.py:20
  87.5 2.0 %collective-permute-done.9 = bf16[64,1152]{1,0:T(8,128)(2,1)S(1)} collective-permute-done((bf16[64,1152]{1,0:T(8,128)(2,1)S(1)}, bf16[64,1152]{1,0:T(8,128)(2,1)S(1)}, u32[]{:S(2)}, u32[]{:S(2)}) %collective-permute-start.9) | collective-permute-done | bytes 147488 | tf_op jit(solution)/shard_map/ppermute | solution.py:20
  89.5 3.0 %collective-permute-done.13 = bf16[64,1152]{1,0:T(8,128)(2,1)S(1)} collective-permute-done((bf16[64,1152]{1,0:T(8,128)(2,1)S(1)}, bf16[64,1152]{1,0:T(8,128)(2,1)S(1)}, u32[]{:S(2)}, u32[]{:S(2)}) %collective-permute-start.13) | collective-permute-done | bytes 147488 | tf_op jit(solution)/shard_map/ppermute | solution.py:20
  93.9 3.4 %all-to-all-done.1 = bf16[16,64,1152]{2,1,0:T(8,128)(2,1)} async-done(((bf16[16,64,1152]{2,1,0:T(8,128)(2,1)}), bf16[16,64,1152]{2,1,0:T(8,128)(2,1)}, u32[]{:S(2)}, u32[]{:S(2)}) %all-to-all-start.1) | async-done | bytes 2359328 | tf_op jit(solution)/shard_map/all_to_all | solution.py:180
  97.3 2.0 %convert_reduce_fusion = f32[64,1152]{1,0:T(8,128)S(1)} fusion(bf16[16,64,1152]{2,1,0:T(8,128)(2,1)} %all-to-all-done.1), kind=kLoop, calls=%fused_computation | loop fusion | flops 2285568 | bytes 2654208 | tf_op jit(solution)/shard_map/reduce_sum | solution.py:190
  (37 shorter events, 7.1 us)
Async XLA Ops:
  0.6 1.0 copy-start.1
  3.3 7.5 %copy-start = (f32[64,1152]{1,0:T(8,128)S(1)}, f32[64,1152]{1,0:T(8,128)}, u32[]{:S(2)}) copy-start(f32[64,1152]{1,0:T(8,128)} %raw.2) | copy-start | bytes 884740
  3.3 41.2 %all-to-all-start = ((bf16[16,64,1152]{2,1,0:T(8,128)(2,1)}), bf16[16,64,1152]{2,1,0:T(8,128)(2,1)S(1)}, u32[]{:S(2)}, u32[]{:S(2)}) async-start(bf16[16,64,1152]{2,1,0:T(8,128)(2,1)} %shard_map.59), calls=%async_computation | async-start | bytes 4718592 | tf_op jit(solution)/shard_map/all_to_all | solution.py:159
  11.0 8.6 %collective-permute-start = (bf16[64,1152]{1,0:T(8,128)(2,1)S(1)}, bf16[64,1152]{1,0:T(8,128)(2,1)S(1)}, u32[]{:S(2)}, u32[]{:S(2)}) collective-permute-start(bf16[64,1152]{1,0:T(8,128)(2,1)S(1)} %shard_map.60.refs_0_), channel_id=1, source_target_pairs={{0,7},{1,0},{2,1},{3,2},{4,3},{5,4},{6,5},{7,6},{8,15},{9,8},{10,9... | collective-permute-start | bytes 442376 | tf_op jit(solution)/shard_map/ppermute | solution.py:20
  16.9 6.4 %collective-permute-start.4 = (bf16[64,1152]{1,0:T(8,128)(2,1)S(1)}, bf16[64,1152]{1,0:T(8,128)(2,1)S(1)}, u32[]{:S(2)}, u32[]{:S(2)}) collective-permute-start(bf16[64,1152]{1,0:T(8,128)(2,1)S(1)} %shard_map.60.refs_0_), channel_id=1, source_target_pairs={{0,1},{1,2},{2,3},{3,4},{4,5},{5,6},{6,7},{7,0},{8,9},{9,10},{10,1... | collective-permute-start | bytes 442376 | tf_op jit(solution)/shard_map/ppermute | solution.py:20
  19.6 7.4 %collective-permute-start.1 = (bf16[64,1152]{1,0:T(8,128)(2,1)S(1)}, bf16[64,1152]{1,0:T(8,128)(2,1)S(1)}, u32[]{:S(2)}, u32[]{:S(2)}) collective-permute-start(bf16[64,1152]{1,0:T(8,128)(2,1)S(1)} %collective-permute-done.refs_1_), channel_id=1, source_target_pairs={{0,7},{1,0},{2,1},{3,2},{4,3},{5,4},{6,5},{7,6},{8,15},{9,8},{10,9... | collective-permute-start | bytes 442376 | tf_op jit(solution)/shard_map/ppermute | solution.py:20
  23.3 10.6 %collective-permute-start.5 = (bf16[64,1152]{1,0:T(8,128)(2,1)S(1)}, bf16[64,1152]{1,0:T(8,128)(2,1)S(1)}, u32[]{:S(2)}, u32[]{:S(2)}) collective-permute-start(bf16[64,1152]{1,0:T(8,128)(2,1)S(1)} %collective-permute-done.4.refs_7_), channel_id=1, source_target_pairs={{0,1},{1,2},{2,3},{3,4},{4,5},{5,6},{6,7},{7,0},{8,9},{9,10},{10,1... | collective-permute-start | bytes 442376 | tf_op jit(solution)/shard_map/ppermute | solution.py:20
  23.3 12.8 %collective-permute-start.3 = (bf16[64,1152]{1,0:T(8,128)(2,1)S(1)}, bf16[64,1152]{1,0:T(8,128)(2,1)S(1)}, u32[]{:S(2)}, u32[]{:S(2)}) collective-permute-start(bf16[64,1152]{1,0:T(8,128)(2,1)S(1)} %shard_map.60.refs_0_), channel_id=1, source_target_pairs={{0,4},{1,5},{2,6},{3,7},{4,0},{5,1},{6,2},{7,3},{8,12},{9,13},{10,... | collective-permute-start | bytes 442376 | tf_op jit(solution)/shard_map/ppermute | solution.py:20
  27.0 9.1 %collective-permute-start.2 = (bf16[64,1152]{1,0:T(8,128)(2,1)S(1)}, bf16[64,1152]{1,0:T(8,128)(2,1)S(1)}, u32[]{:S(2)}, u32[]{:S(2)}) collective-permute-start(bf16[64,1152]{1,0:T(8,128)(2,1)S(1)} %collective-permute-done.1.refs_2_), channel_id=1, source_target_pairs={{0,7},{1,0},{2,1},{3,2},{4,3},{5,4},{6,5},{7,6},{8,15},{9,8},{10,9... | collective-permute-start | bytes 442376 | tf_op jit(solution)/shard_map/ppermute | solution.py:20
  33.9 6.4 %collective-permute-start.6 = (bf16[64,1152]{1,0:T(8,128)(2,1)S(1)}, bf16[64,1152]{1,0:T(8,128)(2,1)S(1)}, u32[]{:S(2)}, u32[]{:S(2)}) collective-permute-start(bf16[64,1152]{1,0:T(8,128)(2,1)S(1)} %collective-permute-done.5.refs_6_), channel_id=1, source_target_pairs={{0,1},{1,2},{2,3},{3,4},{4,5},{5,6},{6,7},{7,0},{8,9},{9,10},{10,1... | collective-permute-start | bytes 442376 | tf_op jit(solution)/shard_map/ppermute | solution.py:20
  41.3 3.2 %collective-permute-start.7 = (bf16[512,1152]{1,0:T(8,128)(2,1)}, bf16[512,1152]{1,0:T(8,128)(2,1)}, u32[]{:S(2)}, u32[]{:S(2)}) collective-permute-start(bf16[512,1152]{1,0:T(8,128)(2,1)} %shard_map.61.xs), channel_id=1, source_target_pairs={{0,16},{16,0},{1,17},{17,1},{2,18},{18,2},{3,19},{19,3},{4,20},{20... | collective-permute-start | bytes 3538952 | tf_op jit(solution)/shard_map/ppermute | solution.py:20
  44.5 11.9 %copy-start.2 = (f32[64,1152]{1,0:T(8,128)S(1)}, f32[64,1152]{1,0:T(8,128)}, u32[]{:S(2)}) copy-start(f32[64,1152]{1,0:T(8,128)} %raw.1) | copy-start | bytes 884740
  56.2 7.7 %collective-permute-start.8 = (bf16[512,1152]{1,0:T(8,128)(2,1)}, bf16[512,1152]{1,0:T(8,128)(2,1)}, u32[]{:S(2)}, u32[]{:S(2)}) collective-permute-start(bf16[512,1152]{1,0:T(8,128)(2,1)} %get-tuple-element.12), channel_id=1, source_target_pairs={{0,16},{16,0},{1,17},{17,1},{2,18},{18,2},{3,19},{19,3},{4,20},{20... | collective-permute-start | bytes 3538952 | tf_op jit(solution)/shard_map/ppermute | solution.py:20
  56.6 7.3 %copy-start.3 = (f32[512,1152]{1,0:T(8,128)S(1)}, f32[512,1152]{1,0:T(8,128)}, u32[]{:S(2)}) copy-start(f32[512,1152]{1,0:T(8,128)} %get-tuple-element.11.dxs) | copy-start | bytes 7077892
  56.6 40.7 %all-to-all-start.1 = ((bf16[16,64,1152]{2,1,0:T(8,128)(2,1)}), bf16[16,64,1152]{2,1,0:T(8,128)(2,1)}, u32[]{:S(2)}, u32[]{:S(2)}) async-start(bf16[16,64,1152]{2,1,0:T(8,128)(2,1)} %bitcast.5), calls=%async_computation.1 | async-start | bytes 4718592 | tf_op jit(solution)/shard_map/all_to_all | solution.py:180
  65.4 13.4 %collective-permute-start.12 = (bf16[64,1152]{1,0:T(8,128)(2,1)S(1)}, bf16[64,1152]{1,0:T(8,128)(2,1)S(1)}, u32[]{:S(2)}, u32[]{:S(2)}) collective-permute-start(bf16[64,1152]{1,0:T(8,128)(2,1)S(1)} %get-tuple-element.20), channel_id=1, source_target_pairs={{0,1},{1,2},{2,3},{3,4},{4,5},{5,6},{6,7},{7,0},{8,9},{9,10},{10,1... | collective-permute-start | bytes 442376 | tf_op jit(solution)/shard_map/ppermute | solution.py:20
  65.5 13.3 %collective-permute-start.14 = (bf16[64,1152]{1,0:T(8,128)(2,1)S(1)}, bf16[64,1152]{1,0:T(8,128)(2,1)S(1)}, u32[]{:S(2)}, u32[]{:S(2)}) collective-permute-start(bf16[64,1152]{1,0:T(8,128)(2,1)S(1)} %get-tuple-element.19), channel_id=1, source_target_pairs={{0,7},{1,0},{2,1},{3,2},{4,3},{5,4},{6,5},{7,6},{8,15},{9,8},{10,9... | collective-permute-start | bytes 442376 | tf_op jit(solution)/shard_map/ppermute | solution.py:20
  69.2 18.3 %collective-permute-start.10 = (bf16[64,1152]{1,0:T(8,128)(2,1)S(1)}, bf16[64,1152]{1,0:T(8,128)(2,1)S(1)}, u32[]{:S(2)}, u32[]{:S(2)}) collective-permute-start(bf16[64,1152]{1,0:T(8,128)(2,1)S(1)} %get-tuple-element.22), channel_id=1, source_target_pairs={{0,3},{1,4},{2,5},{3,6},{4,7},{5,0},{6,1},{7,2},{8,11},{9,12},{10,... | collective-permute-start | bytes 442376 | tf_op jit(solution)/shard_map/ppermute | solution.py:20
  71.1 16.4 %collective-permute-start.11 = (bf16[64,1152]{1,0:T(8,128)(2,1)S(1)}, bf16[64,1152]{1,0:T(8,128)(2,1)S(1)}, u32[]{:S(2)}, u32[]{:S(2)}) collective-permute-start(bf16[64,1152]{1,0:T(8,128)(2,1)S(1)} %get-tuple-element.21), channel_id=1, source_target_pairs={{0,5},{1,6},{2,7},{3,0},{4,1},{5,2},{6,3},{7,4},{8,13},{9,14},{10,... | collective-permute-start | bytes 442376 | tf_op jit(solution)/shard_map/ppermute | solution.py:20
  74.3 15.2 %collective-permute-start.9 = (bf16[64,1152]{1,0:T(8,128)(2,1)S(1)}, bf16[64,1152]{1,0:T(8,128)(2,1)S(1)}, u32[]{:S(2)}, u32[]{:S(2)}) collective-permute-start(bf16[64,1152]{1,0:T(8,128)(2,1)S(1)} %get-tuple-element.18), channel_id=1, source_target_pairs={{0,4},{1,5},{2,6},{3,7},{4,0},{5,1},{6,2},{7,3},{8,12},{9,13},{10,... | collective-permute-start | bytes 442376 | tf_op jit(solution)/shard_map/ppermute | solution.py:20
  78.9 13.6 %collective-permute-start.13 = (bf16[64,1152]{1,0:T(8,128)(2,1)S(1)}, bf16[64,1152]{1,0:T(8,128)(2,1)S(1)}, u32[]{:S(2)}, u32[]{:S(2)}) collective-permute-start(bf16[64,1152]{1,0:T(8,128)(2,1)S(1)} %get-tuple-element.23), channel_id=1, source_target_pairs={{0,1},{1,2},{2,3},{3,4},{4,5},{5,6},{6,7},{7,0},{8,9},{9,10},{10,1... | collective-permute-start | bytes 442376 | tf_op jit(solution)/shard_map/ppermute | solution.py:20
  79.0 13.9 %collective-permute-start.15 = (bf16[64,1152]{1,0:T(8,128)(2,1)S(1)}, bf16[64,1152]{1,0:T(8,128)(2,1)S(1)}, u32[]{:S(2)}, u32[]{:S(2)}) collective-permute-start(bf16[64,1152]{1,0:T(8,128)(2,1)S(1)} %get-tuple-element.24), channel_id=1, source_target_pairs={{0,7},{1,0},{2,1},{3,2},{4,3},{5,4},{6,5},{7,6},{8,15},{9,8},{10,9... | collective-permute-start | bytes 442376 | tf_op jit(solution)/shard_map/ppermute | solution.py:20

commit v20 on v19

--- a/solution.py
+++ b/solution.py
@@ -106,6 +106,14 @@
     rest[...] = (dxs[ROWS:] + other[ROWS:].astype(F32)).astype(BF)
 
 
+def finish_texts_kernel(scal, raw, got, out):
+    total = got[0].astype(F32)
+    for k in range(1, got.shape[0]):
+        total += got[k].astype(F32)
+    unit, norm = to_unit(raw[...])
+    out[...] = from_unit(scal[0] * total, unit, norm)
+
+
 VMEM = pl.BlockSpec(memory_space=pltpu.VMEM)
 SMEM = pl.BlockSpec(memory_space=pltpu.SMEM)
 HBM = pl.BlockSpec(memory_space=pltpu.HBM)
@@ -187,8 +195,7 @@
     for part in got:
         own = own + part.astype(F32)
     grad_images = from_unit(temp * own, *to_unit(images))
-    text_sum = jnp.sum(dyr.astype(F32), axis=0)
-    grad_texts = from_unit(temp * text_sum, *to_unit(texts))
+    (grad_texts,) = local(finish_texts_kernel, [((rows, width), F32, VMEM)], [scal, texts, dyr], smem=1)
     return (grad_images, grad_texts)
 
 

time: 101 us -> 99.5 us (0.985)
  other arithmetic: 4.53 us -> 1.36 us
  Pallas kernels: 16.1 us -> 17.9 us
  local copies, waits for them, and re-layouts: 1.03 us -> 2.69 us
  waiting for transfers between devices: 29.5 us -> 28.1 us
    reduce_sum x1 -> x0, other arithmetic: 2.01 us -> none  [on_device(): text_sum = jnp.sum(dyr.astype(F32), axis=0)]
    pallas_call x5 -> x6, Pallas kernels: 16.1 us -> 17.9 us  [local(): pl.pallas_call(kernel, out_shape=tuple(((pltpu.HBM if spec is HBM else ja...]
    unnamed x8, local copies, waits for them, and re-layouts: 0.97 us -> 2.63 us
    all_to_all x1, waiting for transfers between devices: 3.36 us -> 2.2 us  [on_device(): lax.all_to_all(dy.reshape(n_plane, rows, width), PLANE, 0, 0, tiled=True)]
  transfers between devices with their start and end apart: 18 -> 18, of which waited for: 11 -> 11; matrix products, arithmetic and copies ran while one was open for 2% -> 1% of each run, Pallas kernels for 3% -> 3%
where the time goes in v20:
time: 99.5 us; the launch traced here: 98.7 us
  starting transfers between devices  46.5 us (47%)
  waiting for transfers between devices  28.1 us (28%)
  Pallas kernels  17.9 us (18%)
  local copies, waits for them, and re-layouts  2.69 us (3%)
  between operations  2.08 us (2%)
  other arithmetic  1.36 us (1%)
    ppermute x16, starting transfers between devices, shifted(): lax.ppermute(block, axis, [(i, (i + distance) % n) for i in range(n)])  31.8 us
    ppermute x16, waiting for transfers between devices, shifted(): lax.ppermute(block, axis, [(i, (i + distance) % n) for i in range(n)])  25.9 us
    pallas_call x6, Pallas kernels, local(): pl.pallas_call(kernel, out_shape=tuple(((pltpu.HBM if spec is HBM else ja...  17.9 us
    all_to_all x1, starting transfers between devices, on_device(): ts = lax.all_to_all(spread, PLANE, 0, 0, tiled=True).reshape(pooled, width)  7.54 us
    all_to_all x1, starting transfers between devices, on_device(): lax.all_to_all(dy.reshape(n_plane, rows, width), PLANE, 0, 0, tiled=True)  7.18 us
    unnamed x8, local copies, waits for them, and re-layouts  2.63 us
    all_to_all x1, waiting for transfers between devices, on_device(): lax.all_to_all(dy.reshape(n_plane, rows, width), PLANE, 0, 0, tiled=True)  2.2 us
  transfers between devices with their start and end apart: 18, of which 11 were waited for; matrix products, arithmetic and copies ran while one was open for 1% of the time, Pallas kernels for 3%

profile of v20, /device:TPU:8, one launch (start us, length us, event | category | flops | bytes accessed | tf_op | source)
XLA Modules:
  0.0 98.7 jit_solution(18084042735071576062)
XLA Ops:
  1.6 1.7 %shard_map.59 = bf16[16,64,1152]{2,1,0:T(8,128)(2,1)} custom-call(f32[64,1152]{1,0:T(8,128)S(1)} %copy-done.2), custom_call_target="tpu_custom_call" | custom-call | bytes 1048576 | tf_op jit(solution)/shard_map/pallas_call | solution.py:124
  3.3 7.5 %all-to-all-start = ((bf16[16,64,1152]{2,1,0:T(8,128)(2,1)}), bf16[16,64,1152]{2,1,0:T(8,128)(2,1)S(1)}, u32[]{:S(2)}, u32[]{:S(2)}) async-start(bf16[16,64,1152]{2,1,0:T(8,128)(2,1)} %shard_map.59), calls=%async_computation | async-start | bytes 4718592 | tf_op jit(solution)/shard_map/all_to_all | solution.py:167
  11.0 5.9 %collective-permute-start = (bf16[64,1152]{1,0:T(8,128)(2,1)S(1)}, bf16[64,1152]{1,0:T(8,128)(2,1)S(1)}, u32[]{:S(2)}, u32[]{:S(2)}) collective-permute-start(bf16[64,1152]{1,0:T(8,128)(2,1)S(1)} %shard_map.60.refs_0_), channel_id=1, source_target_pairs={{0,7},{1,0},{2,1},{3,2},{4,3},{5,4},{6,5},{7,6},{8,15},{9,8},{10,9... | collective-permute-start | bytes 442376 | tf_op jit(solution)/shard_map/ppermute | solution.py:20
  16.9 2.7 %collective-permute-done.refs_1_ = bf16[64,1152]{1,0:T(8,128)(2,1)S(1)} collective-permute-done((bf16[64,1152]{1,0:T(8,128)(2,1)S(1)}, bf16[64,1152]{1,0:T(8,128)(2,1)S(1)}, u32[]{:S(2)}, u32[]{:S(2)}) %collective-permute-start) | collective-permute-done | bytes 147488 | tf_op jit(solution)/shard_map/ppermute | solution.py:20
  19.6 3.7 %collective-permute-start.1 = (bf16[64,1152]{1,0:T(8,128)(2,1)S(1)}, bf16[64,1152]{1,0:T(8,128)(2,1)S(1)}, u32[]{:S(2)}, u32[]{:S(2)}) collective-permute-start(bf16[64,1152]{1,0:T(8,128)(2,1)S(1)} %collective-permute-done.refs_1_), channel_id=1, source_target_pairs={{0,7},{1,0},{2,1},{3,2},{4,3},{5,4},{6,5},{7,6},{8,15},{9,8},{10,9... | collective-permute-start | bytes 442376 | tf_op jit(solution)/shard_map/ppermute | solution.py:20
  23.3 2.1 %collective-permute-start.3 = (bf16[64,1152]{1,0:T(8,128)(2,1)S(1)}, bf16[64,1152]{1,0:T(8,128)(2,1)S(1)}, u32[]{:S(2)}, u32[]{:S(2)}) collective-permute-start(bf16[64,1152]{1,0:T(8,128)(2,1)S(1)} %shard_map.60.refs_0_), channel_id=1, source_target_pairs={{0,4},{1,5},{2,6},{3,7},{4,0},{5,1},{6,2},{7,3},{8,12},{9,13},{10,... | collective-permute-start | bytes 442376 | tf_op jit(solution)/shard_map/ppermute | solution.py:20
  27.0 3.7 %collective-permute-start.2 = (bf16[64,1152]{1,0:T(8,128)(2,1)S(1)}, bf16[64,1152]{1,0:T(8,128)(2,1)S(1)}, u32[]{:S(2)}, u32[]{:S(2)}) collective-permute-start(bf16[64,1152]{1,0:T(8,128)(2,1)S(1)} %collective-permute-done.1.refs_2_), channel_id=1, source_target_pairs={{0,7},{1,0},{2,1},{3,2},{4,3},{5,4},{6,5},{7,6},{8,15},{9,8},{10,9... | collective-permute-start | bytes 442376 | tf_op jit(solution)/shard_map/ppermute | solution.py:20
  30.7 3.2 %collective-permute-done.5.refs_6_ = bf16[64,1152]{1,0:T(8,128)(2,1)S(1)} collective-permute-done((bf16[64,1152]{1,0:T(8,128)(2,1)S(1)}, bf16[64,1152]{1,0:T(8,128)(2,1)S(1)}, u32[]{:S(2)}, u32[]{:S(2)}) %collective-permute-start.5) | collective-permute-done | bytes 147488 | tf_op jit(solution)/shard_map/ppermute | solution.py:20
  33.9 2.2 %collective-permute-done.3.refs_4_ = bf16[64,1152]{1,0:T(8,128)(2,1)S(1)} collective-permute-done((bf16[64,1152]{1,0:T(8,128)(2,1)S(1)}, bf16[64,1152]{1,0:T(8,128)(2,1)S(1)}, u32[]{:S(2)}, u32[]{:S(2)}) %collective-permute-start.3) | collective-permute-done | bytes 147488 | tf_op jit(solution)/shard_map/ppermute | solution.py:20
  36.1 4.1 %collective-permute-done.6.refs_5_ = bf16[64,1152]{1,0:T(8,128)(2,1)S(1)} collective-permute-done((bf16[64,1152]{1,0:T(8,128)(2,1)S(1)}, bf16[64,1152]{1,0:T(8,128)(2,1)S(1)}, u32[]{:S(2)}, u32[]{:S(2)}) %collective-permute-start.6) | collective-permute-done | bytes 147488 | tf_op jit(solution)/shard_map/ppermute | solution.py:20
  42.8 1.8 %collective-permute-done.7.xo = bf16[512,1152]{1,0:T(8,128)(2,1)} collective-permute-done((bf16[512,1152]{1,0:T(8,128)(2,1)}, bf16[512,1152]{1,0:T(8,128)(2,1)}, u32[]{:S(2)}, u32[]{:S(2)}) %collective-permute-start.7) | collective-permute-done | bytes 1179680 | tf_op jit(solution)/shard_map/ppermute | solution.py:20
  44.6 11.7 %shard_map.62 = (f32[512,1152]{1,0:T(8,128)}, bf16[512,1152]{1,0:T(8,128)(2,1)}, bf16[1024,1152]{1,0:T(8,128)(2,1)}) custom-call(s32[1]{0:T(128)} %bitcast.1.place, f32[2]{0:T(128)S(1)} %pad_maximum_fusion.scal, bf16[512,1152]{1,0:T(8,128)(2,1)} %shard_map.61.xs, bf16[512,1152]{1,0:T(8,128)(2,1)} %collective-permute-done.7.xo, bf16[1024,1152]{1,0:T(8,128)(2,1)S(1)} %bitcast.4), custom_call_target="tpu_custom_call" | custom-call | flops 7247757312 | bytes 9437184 | tf_op jit(solution)/shard_map/pallas_call | solution.py:124
  56.5 7.2 %all-to-all-start.1 = ((bf16[16,64,1152]{2,1,0:T(8,128)(2,1)}), bf16[16,64,1152]{2,1,0:T(8,128)(2,1)S(1)}, u32[]{:S(2)}, u32[]{:S(2)}) async-start(bf16[16,64,1152]{2,1,0:T(8,128)(2,1)} %bitcast.5), calls=%async_computation.1 | async-start | bytes 4718592 | tf_op jit(solution)/shard_map/all_to_all | solution.py:188
  63.7 1.7 %copy-done.1 = f32[512,1152]{1,0:T(8,128)S(1)} copy-done((f32[512,1152]{1,0:T(8,128)S(1)}, f32[512,1152]{1,0:T(8,128)}, u32[]{:S(2)}) %copy-start.1) | copy-done | bytes 2359320
  67.1 3.2 %collective-permute-start.14 = (bf16[64,1152]{1,0:T(8,128)(2,1)S(1)}, bf16[64,1152]{1,0:T(8,128)(2,1)S(1)}, u32[]{:S(2)}, u32[]{:S(2)}) collective-permute-start(bf16[64,1152]{1,0:T(8,128)(2,1)S(1)} %get-tuple-element.19), channel_id=1, source_target_pairs={{0,7},{1,0},{2,1},{3,2},{4,3},{5,4},{6,5},{7,6},{8,15},{9,8},{10,9... | collective-permute-start | bytes 442376 | tf_op jit(solution)/shard_map/ppermute | solution.py:20
  70.4 1.8 %collective-permute-start.10 = (bf16[64,1152]{1,0:T(8,128)(2,1)S(1)}, bf16[64,1152]{1,0:T(8,128)(2,1)S(1)}, u32[]{:S(2)}, u32[]{:S(2)}) collective-permute-start(bf16[64,1152]{1,0:T(8,128)(2,1)S(1)} %get-tuple-element.22), channel_id=1, source_target_pairs={{0,3},{1,4},{2,5},{3,6},{4,7},{5,0},{6,1},{7,2},{8,11},{9,12},{10,... | collective-permute-start | bytes 442376 | tf_op jit(solution)/shard_map/ppermute | solution.py:20
  72.2 3.3 %collective-permute-start.11 = (bf16[64,1152]{1,0:T(8,128)(2,1)S(1)}, bf16[64,1152]{1,0:T(8,128)(2,1)S(1)}, u32[]{:S(2)}, u32[]{:S(2)}) collective-permute-start(bf16[64,1152]{1,0:T(8,128)(2,1)S(1)} %get-tuple-element.21), channel_id=1, source_target_pairs={{0,5},{1,6},{2,7},{3,0},{4,1},{5,2},{6,3},{7,4},{8,13},{9,14},{10,... | collective-permute-start | bytes 442376 | tf_op jit(solution)/shard_map/ppermute | solution.py:20
  75.5 4.4 %collective-permute-start.9 = (bf16[64,1152]{1,0:T(8,128)(2,1)S(1)}, bf16[64,1152]{1,0:T(8,128)(2,1)S(1)}, u32[]{:S(2)}, u32[]{:S(2)}) collective-permute-start(bf16[64,1152]{1,0:T(8,128)(2,1)S(1)} %get-tuple-element.18), channel_id=1, source_target_pairs={{0,4},{1,5},{2,6},{3,7},{4,0},{5,1},{6,2},{7,3},{8,12},{9,13},{10,... | collective-permute-start | bytes 442376 | tf_op jit(solution)/shard_map/ppermute | solution.py:20
  80.1 3.2 %collective-permute-start.15 = (bf16[64,1152]{1,0:T(8,128)(2,1)S(1)}, bf16[64,1152]{1,0:T(8,128)(2,1)S(1)}, u32[]{:S(2)}, u32[]{:S(2)}) collective-permute-start(bf16[64,1152]{1,0:T(8,128)(2,1)S(1)} %get-tuple-element.24), channel_id=1, source_target_pairs={{0,7},{1,0},{2,1},{3,2},{4,3},{5,4},{6,5},{7,6},{8,15},{9,8},{10,9... | collective-permute-start | bytes 442376 | tf_op jit(solution)/shard_map/ppermute | solution.py:20
  83.3 5.4 %collective-permute-done.10 = bf16[64,1152]{1,0:T(8,128)(2,1)S(1)} collective-permute-done((bf16[64,1152]{1,0:T(8,128)(2,1)S(1)}, bf16[64,1152]{1,0:T(8,128)(2,1)S(1)}, u32[]{:S(2)}, u32[]{:S(2)}) %collective-permute-start.10) | collective-permute-done | bytes 147488 | tf_op jit(solution)/shard_map/ppermute | solution.py:20
  88.7 1.8 %collective-permute-done.9 = bf16[64,1152]{1,0:T(8,128)(2,1)S(1)} collective-permute-done((bf16[64,1152]{1,0:T(8,128)(2,1)S(1)}, bf16[64,1152]{1,0:T(8,128)(2,1)S(1)}, u32[]{:S(2)}, u32[]{:S(2)}) %collective-permute-start.9) | collective-permute-done | bytes 147488 | tf_op jit(solution)/shard_map/ppermute | solution.py:20
  90.5 2.8 %collective-permute-done.13 = bf16[64,1152]{1,0:T(8,128)(2,1)S(1)} collective-permute-done((bf16[64,1152]{1,0:T(8,128)(2,1)S(1)}, bf16[64,1152]{1,0:T(8,128)(2,1)S(1)}, u32[]{:S(2)}, u32[]{:S(2)}) %collective-permute-start.13) | collective-permute-done | bytes 147488 | tf_op jit(solution)/shard_map/ppermute | solution.py:20
  94.8 2.2 %all-to-all-done.1.got = bf16[16,64,1152]{2,1,0:T(8,128)(2,1)S(1)} async-done(((bf16[16,64,1152]{2,1,0:T(8,128)(2,1)}), bf16[16,64,1152]{2,1,0:T(8,128)(2,1)S(1)}, u32[]{:S(2)}, u32[]{:S(2)}) %all-to-all-start.1) | async-done | bytes 2359328 | tf_op jit(solution)/shard_map/all_to_all | solution.py:188
  97.0 1.7 %shard_map.64 = f32[64,1152]{1,0:T(8,128)} custom-call(f32[2]{0:T(128)S(1)} %pad_maximum_fusion.scal, f32[64,1152]{1,0:T(8,128)S(1)} %copy-done.3, bf16[16,64,1152]{2,1,0:T(8,128)(2,1)S(1)} %all-to-all-done.1.got), custom_call_target="tpu_custom_call" | custom-call | bytes 1048576 | tf_op jit(solution)/shard_map/pallas_call | solution.py:124
  (33 shorter events, 7.5 us)
Async XLA Ops:
  0.6 1.0 copy-start.2
  3.3 7.5 %copy-start = (f32[64,1152]{1,0:T(8,128)S(1)}, f32[64,1152]{1,0:T(8,128)}, u32[]{:S(2)}) copy-start(f32[64,1152]{1,0:T(8,128)} %raw.3) | copy-start | bytes 884740
  3.3 41.2 %all-to-all-start = ((bf16[16,64,1152]{2,1,0:T(8,128)(2,1)}), bf16[16,64,1152]{2,1,0:T(8,128)(2,1)S(1)}, u32[]{:S(2)}, u32[]{:S(2)}) async-start(bf16[16,64,1152]{2,1,0:T(8,128)(2,1)} %shard_map.59), calls=%async_computation | async-start | bytes 4718592 | tf_op jit(solution)/shard_map/all_to_all | solution.py:167
  11.0 8.6 %collective-permute-start = (bf16[64,1152]{1,0:T(8,128)(2,1)S(1)}, bf16[64,1152]{1,0:T(8,128)(2,1)S(1)}, u32[]{:S(2)}, u32[]{:S(2)}) collective-permute-start(bf16[64,1152]{1,0:T(8,128)(2,1)S(1)} %shard_map.60.refs_0_), channel_id=1, source_target_pairs={{0,7},{1,0},{2,1},{3,2},{4,3},{5,4},{6,5},{7,6},{8,15},{9,8},{10,9... | collective-permute-start | bytes 442376 | tf_op jit(solution)/shard_map/ppermute | solution.py:20
  16.9 6.4 %collective-permute-start.4 = (bf16[64,1152]{1,0:T(8,128)(2,1)S(1)}, bf16[64,1152]{1,0:T(8,128)(2,1)S(1)}, u32[]{:S(2)}, u32[]{:S(2)}) collective-permute-start(bf16[64,1152]{1,0:T(8,128)(2,1)S(1)} %shard_map.60.refs_0_), channel_id=1, source_target_pairs={{0,1},{1,2},{2,3},{3,4},{4,5},{5,6},{6,7},{7,0},{8,9},{9,10},{10,1... | collective-permute-start | bytes 442376 | tf_op jit(solution)/shard_map/ppermute | solution.py:20
  19.6 7.4 %collective-permute-start.1 = (bf16[64,1152]{1,0:T(8,128)(2,1)S(1)}, bf16[64,1152]{1,0:T(8,128)(2,1)S(1)}, u32[]{:S(2)}, u32[]{:S(2)}) collective-permute-start(bf16[64,1152]{1,0:T(8,128)(2,1)S(1)} %collective-permute-done.refs_1_), channel_id=1, source_target_pairs={{0,7},{1,0},{2,1},{3,2},{4,3},{5,4},{6,5},{7,6},{8,15},{9,8},{10,9... | collective-permute-start | bytes 442376 | tf_op jit(solution)/shard_map/ppermute | solution.py:20
  23.3 10.6 %collective-permute-start.5 = (bf16[64,1152]{1,0:T(8,128)(2,1)S(1)}, bf16[64,1152]{1,0:T(8,128)(2,1)S(1)}, u32[]{:S(2)}, u32[]{:S(2)}) collective-permute-start(bf16[64,1152]{1,0:T(8,128)(2,1)S(1)} %collective-permute-done.4.refs_7_), channel_id=1, source_target_pairs={{0,1},{1,2},{2,3},{3,4},{4,5},{5,6},{6,7},{7,0},{8,9},{9,10},{10,1... | collective-permute-start | bytes 442376 | tf_op jit(solution)/shard_map/ppermute | solution.py:20
  23.3 12.8 %collective-permute-start.3 = (bf16[64,1152]{1,0:T(8,128)(2,1)S(1)}, bf16[64,1152]{1,0:T(8,128)(2,1)S(1)}, u32[]{:S(2)}, u32[]{:S(2)}) collective-permute-start(bf16[64,1152]{1,0:T(8,128)(2,1)S(1)} %shard_map.60.refs_0_), channel_id=1, source_target_pairs={{0,4},{1,5},{2,6},{3,7},{4,0},{5,1},{6,2},{7,3},{8,12},{9,13},{10,... | collective-permute-start | bytes 442376 | tf_op jit(solution)/shard_map/ppermute | solution.py:20
  27.0 9.1 %collective-permute-start.2 = (bf16[64,1152]{1,0:T(8,128)(2,1)S(1)}, bf16[64,1152]{1,0:T(8,128)(2,1)S(1)}, u32[]{:S(2)}, u32[]{:S(2)}) collective-permute-start(bf16[64,1152]{1,0:T(8,128)(2,1)S(1)} %collective-permute-done.1.refs_2_), channel_id=1, source_target_pairs={{0,7},{1,0},{2,1},{3,2},{4,3},{5,4},{6,5},{7,6},{8,15},{9,8},{10,9... | collective-permute-start | bytes 442376 | tf_op jit(solution)/shard_map/ppermute | solution.py:20
  33.9 6.4 %collective-permute-start.6 = (bf16[64,1152]{1,0:T(8,128)(2,1)S(1)}, bf16[64,1152]{1,0:T(8,128)(2,1)S(1)}, u32[]{:S(2)}, u32[]{:S(2)}) collective-permute-start(bf16[64,1152]{1,0:T(8,128)(2,1)S(1)} %collective-permute-done.5.refs_6_), channel_id=1, source_target_pairs={{0,1},{1,2},{2,3},{3,4},{4,5},{5,6},{6,7},{7,0},{8,9},{9,10},{10,1... | collective-permute-start | bytes 442376 | tf_op jit(solution)/shard_map/ppermute | solution.py:20
  41.4 3.2 %collective-permute-start.7 = (bf16[512,1152]{1,0:T(8,128)(2,1)}, bf16[512,1152]{1,0:T(8,128)(2,1)}, u32[]{:S(2)}, u32[]{:S(2)}) collective-permute-start(bf16[512,1152]{1,0:T(8,128)(2,1)} %shard_map.61.xs), channel_id=1, source_target_pairs={{0,16},{16,0},{1,17},{17,1},{2,18},{18,2},{3,19},{19,3},{4,20},{20... | collective-permute-start | bytes 3538952 | tf_op jit(solution)/shard_map/ppermute | solution.py:20
  56.3 7.4 %collective-permute-start.8 = (bf16[512,1152]{1,0:T(8,128)(2,1)}, bf16[512,1152]{1,0:T(8,128)(2,1)}, u32[]{:S(2)}, u32[]{:S(2)}) collective-permute-start(bf16[512,1152]{1,0:T(8,128)(2,1)} %get-tuple-element.12), channel_id=1, source_target_pairs={{0,16},{16,0},{1,17},{17,1},{2,18},{18,2},{3,19},{19,3},{4,20},{20... | collective-permute-start | bytes 3538952 | tf_op jit(solution)/shard_map/ppermute | solution.py:20
  56.5 40.5 %all-to-all-start.1 = ((bf16[16,64,1152]{2,1,0:T(8,128)(2,1)}), bf16[16,64,1152]{2,1,0:T(8,128)(2,1)S(1)}, u32[]{:S(2)}, u32[]{:S(2)}) async-start(bf16[16,64,1152]{2,1,0:T(8,128)(2,1)} %bitcast.5), calls=%async_computation.1 | async-start | bytes 4718592 | tf_op jit(solution)/shard_map/all_to_all | solution.py:188
  63.7 1.7 %copy-start.1 = (f32[512,1152]{1,0:T(8,128)S(1)}, f32[512,1152]{1,0:T(8,128)}, u32[]{:S(2)}) copy-start(f32[512,1152]{1,0:T(8,128)} %get-tuple-element.11.dxs) | copy-start | bytes 7077892
  66.9 30.1 %copy-start.3 = (f32[64,1152]{1,0:T(8,128)S(1)}, f32[64,1152]{1,0:T(8,128)}, u32[]{:S(2)}) copy-start(f32[64,1152]{1,0:T(8,128)} %raw.4) | copy-start | bytes 884740
  67.0 12.9 %collective-permute-start.12 = (bf16[64,1152]{1,0:T(8,128)(2,1)S(1)}, bf16[64,1152]{1,0:T(8,128)(2,1)S(1)}, u32[]{:S(2)}, u32[]{:S(2)}) collective-permute-start(bf16[64,1152]{1,0:T(8,128)(2,1)S(1)} %get-tuple-element.20), channel_id=1, source_target_pairs={{0,1},{1,2},{2,3},{3,4},{4,5},{5,6},{6,7},{7,0},{8,9},{9,10},{10,1... | collective-permute-start | bytes 442376 | tf_op jit(solution)/shard_map/ppermute | solution.py:20
  67.1 12.9 %collective-permute-start.14 = (bf16[64,1152]{1,0:T(8,128)(2,1)S(1)}, bf16[64,1152]{1,0:T(8,128)(2,1)S(1)}, u32[]{:S(2)}, u32[]{:S(2)}) collective-permute-start(bf16[64,1152]{1,0:T(8,128)(2,1)S(1)} %get-tuple-element.19), channel_id=1, source_target_pairs={{0,7},{1,0},{2,1},{3,2},{4,3},{5,4},{6,5},{7,6},{8,15},{9,8},{10,9... | collective-permute-start | bytes 442376 | tf_op jit(solution)/shard_map/ppermute | solution.py:20
  70.4 18.3 %collective-permute-start.10 = (bf16[64,1152]{1,0:T(8,128)(2,1)S(1)}, bf16[64,1152]{1,0:T(8,128)(2,1)S(1)}, u32[]{:S(2)}, u32[]{:S(2)}) collective-permute-start(bf16[64,1152]{1,0:T(8,128)(2,1)S(1)} %get-tuple-element.22), channel_id=1, source_target_pairs={{0,3},{1,4},{2,5},{3,6},{4,7},{5,0},{6,1},{7,2},{8,11},{9,12},{10,... | collective-permute-start | bytes 442376 | tf_op jit(solution)/shard_map/ppermute | solution.py:20
  72.2 16.5 %collective-permute-start.11 = (bf16[64,1152]{1,0:T(8,128)(2,1)S(1)}, bf16[64,1152]{1,0:T(8,128)(2,1)S(1)}, u32[]{:S(2)}, u32[]{:S(2)}) collective-permute-start(bf16[64,1152]{1,0:T(8,128)(2,1)S(1)} %get-tuple-element.21), channel_id=1, source_target_pairs={{0,5},{1,6},{2,7},{3,0},{4,1},{5,2},{6,3},{7,4},{8,13},{9,14},{10,... | collective-permute-start | bytes 442376 | tf_op jit(solution)/shard_map/ppermute | solution.py:20
  75.5 15.0 %collective-permute-start.9 = (bf16[64,1152]{1,0:T(8,128)(2,1)S(1)}, bf16[64,1152]{1,0:T(8,128)(2,1)S(1)}, u32[]{:S(2)}, u32[]{:S(2)}) collective-permute-start(bf16[64,1152]{1,0:T(8,128)(2,1)S(1)} %get-tuple-element.18), channel_id=1, source_target_pairs={{0,4},{1,5},{2,6},{3,7},{4,0},{5,1},{6,2},{7,3},{8,12},{9,13},{10,... | collective-permute-start | bytes 442376 | tf_op jit(solution)/shard_map/ppermute | solution.py:20
  80.0 13.3 %collective-permute-start.13 = (bf16[64,1152]{1,0:T(8,128)(2,1)S(1)}, bf16[64,1152]{1,0:T(8,128)(2,1)S(1)}, u32[]{:S(2)}, u32[]{:S(2)}) collective-permute-start(bf16[64,1152]{1,0:T(8,128)(2,1)S(1)} %get-tuple-element.23), channel_id=1, source_target_pairs={{0,1},{1,2},{2,3},{3,4},{4,5},{5,6},{6,7},{7,0},{8,9},{9,10},{10,1... | collective-permute-start | bytes 442376 | tf_op jit(solution)/shard_map/ppermute | solution.py:20
  80.1 13.6 %collective-permute-start.15 = (bf16[64,1152]{1,0:T(8,128)(2,1)S(1)}, bf16[64,1152]{1,0:T(8,128)(2,1)S(1)}, u32[]{:S(2)}, u32[]{:S(2)}) collective-permute-start(bf16[64,1152]{1,0:T(8,128)(2,1)S(1)} %get-tuple-element.24), channel_id=1, source_target_pairs={{0,7},{1,0},{2,1},{3,2},{4,3},{5,4},{6,5},{7,6},{8,15},{9,8},{10,9... | collective-permute-start | bytes 442376 | tf_op jit(solution)/shard_map/ppermute | solution.py:20
